TPU v7x, 256 devices: a whole 4x4x8 slice. The times are simulated.
256 devices in a mesh: hid: 4 (over z_lo), ffn: 64 (over x, z_hi, y, core).
Axes of the slice: x: 4, y: 4, z: 8 (z_hi: 2, z_lo: 4; z = z_hi * 4 + z_lo), core: 2. Of those that a mesh axis runs over, the one named last changes fastest.
Arguments:
- inputs: bfloat16 [512, 8192], P('ffn', 'hid'), may hold values from -3 to 3
- gate_grad: bfloat16 [512, 53248], P('hid', 'ffn'), may hold values from -1.1953125 to 1.1953125
- up_grad: bfloat16 [512, 53248], P('hid', 'ffn'), may hold values from -1.1953125 to 1.1953125
- gate_codes: bfloat16 [8192, 53248], P('hid', 'ffn'), may hold values from -127 to 127, as said below
- up_codes: bfloat16 [8192, 53248], P('hid', 'ffn'), may hold values from -127 to 127, as said below
- gate_scale: float32 [53248], P('ffn'), as said below
- up_scale: float32 [53248], P('ffn'), as said below
- gate_down: float32 [8192, 16], P('hid'), may hold values from -0.0625 to 0.0625
- gate_lift: float32 [16, 53248], P(None, 'ffn'), may hold values from -0.06 to 0.06
- up_down: float32 [8192, 16], P('hid'), may hold values from -0.0625 to 0.0625
- up_lift: float32 [16, 53248], P(None, 'ffn'), may hold values from -0.06 to 0.06
Outputs:
- input_gradient_rows: bfloat16 [512, 8192], P('ffn', 'hid')
- gate_reducer_gradient: float32 [8192, 16], P('hid')
- gate_expander_gradient: float32 [16, 53248], P(None, 'ffn')
- upward_reducer_gradient: float32 [8192, 16], P('hid')
- upward_expander_gradient: float32 [16, 53248], P(None, 'ffn')
Inputs may be any that keep to these rules, and one draw needn't show every extreme that they name: `gate_codes`: whole numbers. `up_codes`: whole numbers. `gate_scale`: between 0.5 and 2 times 1 / (73 sqrt(8192)). `up_scale`: between 0.5 and 2 times 1 / (73 sqrt(8192)).
All inputs are finite; a program needn't handle non-finite values.
Results may differ from a plain program's by a relative error of at most 0.014.
Values may be sent and summed in bfloat16 or wider, within the bound.
No kernel may reach another device: no remote copies, remote signals or barrier semaphores. Data moves between devices by JAX's collectives and lax.ppermute only.
A program may use at most 64 MiB of HBM per device.

v0:
```python
import jax
import jax.numpy as jnp
from jax import lax
from jax.sharding import PartitionSpec as P

ADAPTER_SCALE = 2.0


def precise_product(left, right):
    return jnp.dot(left, right, precision=lax.Precision.HIGHEST, preferred_element_type=jnp.float32)


def against_rows(cotangent, weight):
    return lax.dot_general(
        cotangent, weight, (((1,), (1,)), ((), ())), preferred_element_type=jnp.float32
    )


def per_device(
    inputs,
    gate_grad,
    up_grad,
    gate_codes,
    up_codes,
    gate_scale,
    up_scale,
    gate_down,
    gate_lift,
    up_down,
    up_lift,
):
    gate_all, up_all = (
        lax.all_gather(gate_grad, "hid", axis=0, tiled=True),
        lax.all_gather(up_grad, "hid", axis=0, tiled=True),
    )
    gate_weight = (gate_codes.astype(jnp.float32) * gate_scale).astype(jnp.bfloat16)
    up_weight = (up_codes.astype(jnp.float32) * up_scale).astype(jnp.bfloat16)
    gate_dequantized = gate_all.astype(jnp.float32)
    upward_dequantized = up_all.astype(jnp.float32)
    gate_part = precise_product(gate_dequantized, gate_lift.T)
    up_part = precise_product(upward_dequantized, up_lift.T)
    gate_backward_signal, upward_backward_signal = lax.psum((gate_part, up_part), "ffn")
    own_rows = inputs.shape[0]
    rows_grad = gate_all
    total = against_rows(rows_grad, gate_weight)
    combined_total = lax.psum_scatter(total, "ffn", scatter_dimension=0, tiled=True)
    rows_grad = up_all
    total = against_rows(rows_grad, up_weight)
    combined_total = combined_total + lax.psum_scatter(
        total, "ffn", scatter_dimension=0, tiled=True
    )
    first_row = lax.axis_index("ffn") * own_rows
    gate_mine = lax.dynamic_slice_in_dim(gate_backward_signal, first_row, own_rows, 0)
    up_mine = lax.dynamic_slice_in_dim(upward_backward_signal, first_row, own_rows, 0)
    combined_total = combined_total + ADAPTER_SCALE * (
        precise_product(gate_mine, gate_down.T) + precise_product(up_mine, up_down.T)
    )
    input_gradient_rows = combined_total.astype(jnp.bfloat16)
    input_all = lax.all_gather(inputs, "ffn", axis=0, tiled=True)
    input_widened = input_all.astype(jnp.float32)
    gate_low_part = precise_product(input_widened, gate_down)
    up_low_part = precise_product(input_widened, up_down)
    gate_narrow_activation, upward_narrow_activation = (
        lax.psum(gate_low_part.astype(jnp.bfloat16), "hid").astype(jnp.float32),
        lax.psum(up_low_part.astype(jnp.bfloat16), "hid").astype(jnp.float32),
    )
    gate_expander_gradient = ADAPTER_SCALE * precise_product(
        gate_narrow_activation.T, gate_dequantized
    )
    upward_expander_gradient = ADAPTER_SCALE * precise_product(
        upward_narrow_activation.T, upward_dequantized
    )
    gate_reducer_gradient = ADAPTER_SCALE * precise_product(input_widened.T, gate_backward_signal)
    upward_reducer_gradient = ADAPTER_SCALE * precise_product(
        input_widened.T, upward_backward_signal
    )
    return (
        input_gradient_rows,
        gate_reducer_gradient,
        gate_expander_gradient,
        upward_reducer_gradient,
        upward_expander_gradient,
    )


def solution(mesh):
    placed = (
        P("ffn", "hid"),
        P("hid", "ffn"),
        P("hid", "ffn"),
        P("hid", "ffn"),
        P("hid", "ffn"),
        P("ffn"),
        P("ffn"),
        P("hid", None),
        P(None, "ffn"),
        P("hid", None),
        P(None, "ffn"),
    )
    return jax.shard_map(
        per_device,
        mesh=mesh,
        in_specs=placed,
        out_specs=(P("ffn", "hid"), P("hid", None), P(None, "ffn"), P("hid", None), P(None, "ffn")),
        check_vma=False,
    )
```

profile of v0, /device:TPU:8, one launch (start us, length us, event | category | flops | bytes accessed | tf_op | source)
XLA Modules:
  0.0 1257.3 jit_solution(8035297710752371941)
XLA Ops:
  7.2 0.0 copy-start
  7.2 0.0 copy-start.6
  7.2 0.0 all-reduce.4.cloned.1.call-start
  7.2 20.7 %all_gather.9 = bf16[512,832]{0,1:T(8,128)(2,1)S(1)} all-gather(bf16[128,832]{0,1:T(8,128)(2,1)} %param.12), channel_id=1, replica_groups=mesh['hid'=4,'ffn'=64] {'hid'}, dimensions={0}, use_global_device_ids=true | all-gather | bytes 1064960 | tf_op jit(solution)/shard_map/all_gather | solution.py:33
  27.9 17.9 %all_gather.10 = bf16[512,832]{0,1:T(8,128)(2,1)S(1)} all-gather(bf16[128,832]{0,1:T(8,128)(2,1)} %param.13), channel_id=1, replica_groups=mesh['hid'=4,'ffn'=64] {'hid'}, dimensions={0}, use_global_device_ids=true | all-gather | bytes 1064960 | tf_op jit(solution)/shard_map/all_gather | solution.py:34
  45.8 1.9 fusion.14
  47.7 1.9 fusion.15
  49.6 0.0 all-reduce.4.cloned.1.call-update
  49.6 0.0 all-gather.2.cloned.1.call-start
  49.7 0.7 all-gather.2.cloned.1.call-update
  50.4 0.0 copy-start.7
  50.4 0.0 reduce-scatter.4.cloned.1.call-start
  50.4 0.0 copy-done.6
  50.4 0.0 copy-start.5
  50.5 4.6 fusion
  55.1 4.5 add_bitcast_fusion
  59.6 5.4 copy.20
  65.0 0.0 reduce-scatter.4.cloned.1.call-update
  65.1 693.3 %all-reduce.4.cloned.1.call-done = (f32[512,16]{0,1:T(8,128)}, f32[512,16]{0,1:T(8,128)}) async-done(((f32[512,16]{0,1:T(8,128)}, f32[512,16]{0,1:T(8,128)}), (f32[512,16]{0,1:T(8,128)}, f32[512,16]{0,1:T(8,128)})) %all-reduce.4.cloned.1.call-update) | async-done | bytes 65552 | tf_op jit(solution)/shard_map/psum | solution.py:42
  758.4 0.0 copy-done
  758.4 1.0 fusion.10
  759.4 82.6 %all-gather.2.cloned.1.call-done = bf16[512,2048]{1,0:T(8,128)(2,1)} async-done(((bf16[8,2048]{1,0:T(8,128)(2,1)}), bf16[512,2048]{1,0:T(8,128)(2,1)}) %all-gather.2.cloned.1.call-update) | async-done | bytes 2097168 | tf_op jit(solution)/shard_map/all_gather | solution.py:59
  842.1 3.5 convolution_convert_fusion.1
  845.6 0.0 copy-done.3
  845.6 3.4 convolution_convert_fusion
  849.0 22.6 %all-reduce.1 = (bf16[512,16]{1,0:T(8,128)(2,1)}, bf16[512,16]{1,0:T(8,128)(2,1)}) all-reduce(bf16[512,16]{1,0:T(8,128)(2,1)S(1)} %convolution_convert_fusion.1, bf16[512,16]{1,0:T(8,128)(2,1)S(1)} %convolution_convert_fusion), channel_id=1, replica_groups=mesh['hid'=4,'ffn'=64] {'hid'}, use_global_device_ids=true, to_apply=%region_4.0 | all-reduce | flops 16384 | bytes 65536 | tf_op jit(solution)/shard_map/psum | solution.py:64
  871.5 2.2 convolution_multiply_fusion.3
  873.7 1.9 convolution_multiply_fusion.2
  875.6 2.3 fusion.5
  877.9 1.6 fusion.4
  879.5 369.4 %reduce-scatter.4.cloned.1.call-done = f32[8,2048]{1,0:T(8,128)} async-done(((f32[512,2048]{1,0:T(8,128)}), f32[8,2048]{1,0:T(8,128)}) %reduce-scatter.4.cloned.1.call-update) | async-done | bytes 65552 | tf_op jit(solution)/shard_map/reduce_scatter | solution.py:46
  1249.0 1.8 fusion.8
  (9 shorter events, 0.0 us)
Async XLA Ops:
  7.2 751.2 %copy-start = (f32[2048,16]{0,1:T(8,128)S(1)}, f32[2048,16]{0,1:T(8,128)}, u32[]{:S(2)}) copy-start(f32[2048,16]{0,1:T(8,128)} %param.18) | copy-start | bytes 393220
  7.2 43.3 %copy-start.6 = (f32[832]{0:T(1024)S(1)}, f32[832]{0:T(1024)}, u32[]{:S(2)}) copy-start(f32[832]{0:T(1024)} %param.16) | copy-start | bytes 9988
  7.2 751.2 %all-reduce.4.cloned.1.call-start = ((), (), s32[]{:S(2)}) async-start(), calls=%async_computation.3 | async-start | bytes 131072 | tf_op jit(solution)/shard_map/psum | solution.py:42
  27.9 27.2 %copy-start.2 = (bf16[512,832]{0,1:T(8,128)(2,1)}, bf16[512,832]{0,1:T(8,128)(2,1)S(1)}, u32[]{:S(2)}) copy-start(bf16[512,832]{0,1:T(8,128)(2,1)S(1)} %all_gather.9) | copy-start | bytes 2555908
  49.6 792.4 %all-gather.2.cloned.1.call-start = ((), (), s32[]{:S(2)}) async-start(), calls=%async_computation.1 | async-start | bytes 2129920 | tf_op jit(solution)/shard_map/all_gather | solution.py:59
  50.4 4.7 copy-start.7
  50.4 1198.6 %reduce-scatter.4.cloned.1.call-start = ((), (), s32[]{:S(2)}) async-start(), calls=%async_computation.2 | async-start | bytes 4259840 | tf_op jit(solution)/shard_map/reduce_scatter | solution.py:46
  50.4 4.7 copy-start.5
  65.0 780.6 %copy-start.3 = (f32[2048,16]{0,1:T(8,128)S(1)}, f32[2048,16]{0,1:T(8,128)}, u32[]{:S(2)}) copy-start(f32[2048,16]{0,1:T(8,128)} %param.20) | copy-start | bytes 393220
  842.1 33.5 %copy-start.1 = (bf16[512,2048]{1,0:T(8,128)(2,1)S(1)}, bf16[512,2048]{1,0:T(8,128)(2,1)}, u32[]{:S(2)}) copy-start(bf16[512,2048]{1,0:T(8,128)(2,1)} %all-gather.2.cloned.1.call-done) | copy-start | bytes 6291460
  871.5 6.4 copy-start.4
Sparse Core Ops, SparseCore 0:
  49.7 708.6 all-reduce.3
  762.6 79.4 all-gather.1
  844.7 404.1 reduce-scatter.3
where the time goes:
time: 1270 us; the launch traced here: 1260 us
  waiting for transfers between devices  1150 us (91%)
  blocking collectives  61.1 us (5%)
  matrix products  30.6 us (2%)
  between operations  13.9 us (1%)
    psum x1, waiting for transfers between devices, per_device(): lax.psum((gate_part, up_part), 'ffn')  693 us
    reduce_scatter x1, waiting for transfers between devices, per_device(): lax.psum_scatter(total, 'ffn', scatter_dimension=0, tiled=True)  369 us
    all_gather x1, waiting for transfers between devices, per_device(): input_all = lax.all_gather(inputs, 'ffn', axis=0, tiled=True)  82.6 us
  transfers between devices with their start and end apart: 3, of which 3 were waited for; matrix products, arithmetic and copies ran while one was open for 2% of the time, Pallas kernels for 0%

commit v1 on v0

v1 whole, which is shorter than its diff:
```python
import jax
import jax.numpy as jnp
from jax import lax
from jax.sharding import Mesh, PartitionSpec as P

ADAPTER_SCALE = 2.0
FFN = ("x", "zh", "y", "core")
F32, BF16 = jnp.float32, jnp.bfloat16


def swap(value, axis, mask):
    size = lax.axis_size(axis)
    return lax.ppermute(value, axis, [(i, i ^ mask) for i in range(size)])


def xor_order(value, dim, index):
    size, step = value.shape[dim], 1
    while step < size:
        order = [j ^ step for j in range(size)]
        moved = jnp.concatenate([lax.slice_in_dim(value, j, j + 1, axis=dim) for j in order], dim)
        value = jnp.where((index & step) != 0, moved, value)
        step *= 2
    return value


def pair_first(value, dim, index):
    other = lax.dynamic_index_in_dim(value, 1 - index, dim, keepdims=False)
    own = lax.dynamic_index_in_dim(value, index, dim, keepdims=False)
    return other, own


def dot(left, right, contract):
    return lax.dot_general(left, right, (contract, ((), ())), preferred_element_type=F32)


def sum_over(value, axis):
    size = lax.axis_size(axis)
    parts = [value] + [swap(value, axis, k) for k in range(1, size)]
    total = parts[0]
    for part in parts[1:]:
        total = total + part
    return total


def gather_over(value, axis):
    size = lax.axis_size(axis)
    return jnp.stack([value] + [swap(value, axis, k) for k in range(1, size)])


def per_device(
    inputs, gate_grad, up_grad, gate_codes, up_codes, gate_scale, up_scale,
    gate_down, gate_lift, up_down, up_lift,
):
    hid = lax.axis_index("hid")
    x, zh, y, core = (lax.axis_index(name) for name in FFN)

    scaled = jnp.stack(
        [
            (gate_grad.astype(F32) * gate_scale).astype(BF16),
            (up_grad.astype(F32) * up_scale).astype(BF16),
        ]
    ).reshape(2, 2, 4, 2, 8, 832)
    phases = []
    for half in pair_first(scaled, 1, zh):
        other, own = pair_first(half, 2, core)
        phases.append(jnp.stack([other, own], 1).reshape(2, 64, 832))

    tokens = gather_over(inputs, "zh").reshape(16, 2048)
    tokens = gather_over(tokens, "x").reshape(64, 2048)
    tokens = gather_over(tokens, "y").reshape(256, 2048)

    back = jnp.concatenate(
        [
            dot(gate_grad, gate_lift.astype(BF16), ((1,), (1,))),
            dot(up_grad, up_lift.astype(BF16), ((1,), (1,))),
        ],
        1,
    ).reshape(8, 2, 8, 32)
    other, own = pair_first(back, 1, core)
    back = (own + swap(other, "core", 1)).reshape(64, 32)
    back = sum_over(back, "x")
    back = sum_over(back, "y")
    back = sum_over(back, "zh")
    back = gather_over(back, "hid").reshape(4, 2, 4, 8, 32)
    back = xor_order(xor_order(xor_order(back, 0, hid ^ x), 1, zh), 2, y)
    back = back.transpose(2, 0, 1, 3, 4).reshape(256, 32)
    down = jnp.concatenate([gate_down, up_down], 1).astype(BF16)
    adapter = ADAPTER_SCALE * dot(back[:8].astype(BF16), down, ((1,), (1,)))
    reducer = ADAPTER_SCALE * dot(tokens, back.astype(BF16), ((0,), (0,)))
    reducer = reducer + swap(reducer, "core", 1)

    low = sum_over(dot(tokens, down, ((1,), (0,))).astype(BF16), "hid").astype(BF16)
    low = low.reshape(4, 4, 2, 8, 32)
    low = xor_order(xor_order(low, 0, y), 1, x)
    low = jnp.stack([swap(low, "core", 1), low])
    low = low.transpose(3, 2, 0, 1, 4, 5)[::-1].reshape(2, 256, 32)

    kept = []
    expander = None
    for phase, mine in enumerate(phases):
        grads = lax.all_gather(mine, "hid", axis=1, tiled=True)
        part = dot(grads[0], gate_codes, ((1,), (1,))) + dot(grads[1], up_codes, ((1,), (1,)))
        part = part.astype(BF16).reshape(4, 2, 32, 2048)
        summed = part[:, 1].astype(F32) + swap(part[:, 0], "core", 1).astype(F32)
        summed = summed.astype(BF16).reshape(128, 2048)
        landed = lax.all_to_all(summed, ("x", "y"), split_axis=0, concat_axis=0, tiled=True)
        kept.append(landed.astype(F32).reshape(16, 8, 2048).sum(0))
        term = [
            dot(low[phase, :, 16 * k : 16 * k + 16], grads[k], ((0,), (0,))) for k in range(2)
        ]
        expander = term if expander is None else [a + b for a, b in zip(expander, term)]
    arrived = swap(kept[0].astype(BF16), "zh", 1)
    rows = (kept[1] + arrived.astype(F32) + adapter).astype(BF16)
    return (
        rows,
        reducer[:, :16],
        ADAPTER_SCALE * expander[0] / gate_scale,
        reducer[:, 16:],
        ADAPTER_SCALE * expander[1] / up_scale,
    )


def solution(mesh):
    whole = Mesh(mesh.devices.reshape(4, 4, 2, 4, 2), ("hid",) + FFN)
    placed = (
        P(FFN, "hid"), P("hid", FFN), P("hid", FFN), P("hid", FFN), P("hid", FFN),
        P(FFN), P(FFN), P("hid", None), P(None, FFN), P("hid", None), P(None, FFN),
    )
    return jax.shard_map(
        per_device,
        mesh=whole,
        in_specs=placed,
        out_specs=(P(FFN, "hid"), P("hid", None), P(None, FFN), P("hid", None), P(None, FFN)),
        check_vma=False,
    )
```

time: 1270 us -> 162 us (0.13)
  waiting for transfers between devices: 1150 us -> 31.7 us
  starting transfers between devices: 0.12 us -> 45.5 us
  blocking collectives: 61.1 us -> 42.3 us
  other arithmetic: 0 us -> 15.8 us
  matrix products: 30.6 us -> 16.6 us
  between operations: 13.9 us -> 1.07 us
    psum x1 -> x0, waiting for transfers between devices: 693 us -> none  [per_device(): lax.psum((gate_part, up_part), 'ffn')]
    reduce_scatter x1 -> x0, waiting for transfers between devices: 369 us -> none  [per_device(): lax.psum_scatter(total, 'ffn', scatter_dimension=0, tiled=True)]
    all_gather x1 -> x0, waiting for transfers between devices: 82.6 us -> none  [per_device(): input_all = lax.all_gather(inputs, 'ffn', axis=0, tiled=True)]
    ppermute x0 -> x26, starting transfers between devices: none -> 33.7 us  [swap(): return lax.ppermute(value, axis, [(i, i ^ mask) for i in range(size)])]
    ppermute x0 -> x26, waiting for transfers between devices: none -> 23.7 us  [swap(): return lax.ppermute(value, axis, [(i, i ^ mask) for i in range(size)])]
    psum x1 -> x0, blocking collectives: 22.6 us -> none  [per_device(): lax.psum(gate_low_part.astype(jnp.bfloat16), 'hid').astype(jnp.float32)]
    dot_general x12 -> x13, matrix products: 30.6 us -> 16.6 us  [dot(): lax.dot_general(left, right, (contract, ((), ())), preferred_element_type...]
  transfers between devices with their start and end apart: 3 -> 28, of which waited for: 3 -> 17; matrix products, arithmetic and copies ran while one was open for 2% -> 23% of each run, Pallas kernels for 0% -> 0%
where the time goes in v1:
time: 162 us; the launch traced here: 161 us
  starting transfers between devices  45.5 us (28%)
  blocking collectives  42.3 us (26%)
  waiting for transfers between devices  31.7 us (20%)
  matrix products  16.6 us (10%)
  other arithmetic  15.8 us (10%)
  local copies, waits for them, and re-layouts  8.45 us (5%)
    all_gather x2, blocking collectives, per_device(): grads = lax.all_gather(mine, 'hid', axis=1, tiled=True)  42.3 us
    ppermute x26, starting transfers between devices, swap(): return lax.ppermute(value, axis, [(i, i ^ mask) for i in range(size)])  33.7 us
    ppermute x26, waiting for transfers between devices, swap(): return lax.ppermute(value, axis, [(i, i ^ mask) for i in range(size)])  23.7 us
    dot_general x13, matrix products, dot(): lax.dot_general(left, right, (contract, ((), ())), preferred_element_type...  16.6 us
    all_to_all x2, starting transfers between devices, per_device(): lax.all_to_all(summed, ('x', 'y'), split_axis=0, concat_axis=0, tiled=True)  11.8 us
    all_to_all x2, waiting for transfers between devices, per_device(): lax.all_to_all(summed, ('x', 'y'), split_axis=0, concat_axis=0, tiled=True)  7.93 us
    convert_element_type x2, other arithmetic, per_device(): summed = summed.astype(BF16).reshape(128, 2048)  4.28 us
    unnamed x18, local copies, waits for them, and re-layouts  3.55 us
  transfers between devices with their start and end apart: 28, of which 17 were waited for; matrix products, arithmetic and copies ran while one was open for 23% of the time, Pallas kernels for 0%

profile of v1, /device:TPU:8, one launch (start us, length us, event | category | flops | bytes accessed | tf_op | source)
XLA Modules:
  0.0 161.3 jit_solution(3921049487513368464)
XLA Ops:
  3.3 1.8 %copy.32 = bf16[128,832]{1,0:T(8,128)(2,1)} copy(bf16[128,832]{0,1:T(8,128)(2,1)} %param.12) | data formatting | bytes 425984 | tf_op args[1]
  5.0 1.8 %copy.33 = bf16[128,832]{1,0:T(8,128)(2,1)} copy(bf16[128,832]{0,1:T(8,128)(2,1)} %param.13) | data formatting | bytes 425984 | tf_op args[2]
  9.0 22.4 %all_gather.6 = bf16[2,256,832]{2,1,0:T(8,128)(2,1)S(1)} all-gather(bf16[2,64,832]{2,1,0:T(8,128)(2,1)S(1)} %bitcast.167), channel_id=1, replica_groups=mesh['hid'=4,'x'=4,'zh'=2,'y'=4,'core'=2] {'hid'}, dimensions={1}, use_global_device_ids=true | all-gather | bytes 1064960 | tf_op jit(solution)/shard_map/all_gather | solution.py:101
  34.8 4.9 %collective-permute-start.14 = (bf16[8,2048]{1,0:T(8,128)(2,1)}, bf16[8,2048]{1,0:T(8,128)(2,1)}, u32[]{:S(2)}, u32[]{:S(2)}) collective-permute-start(bf16[8,2048]{1,0:T(8,128)(2,1)} %param.11), channel_id=1, source_target_pairs={{0,8},{8,0},{1,9},{9,1},{2,10},{10,2},{3,11},{11,3},{4,12},{12,4},... | collective-permute-start | bytes 98312 | tf_op jit(solution)/shard_map/ppermute | solution.py:13
  39.7 19.9 %all_gather.7 = bf16[2,256,832]{2,1,0:T(8,128)(2,1)S(1)} all-gather(bf16[2,64,832]{2,1,0:T(8,128)(2,1)S(1)} %bitcast.168), channel_id=1, replica_groups=mesh['hid'=4,'x'=4,'zh'=2,'y'=4,'core'=2] {'hid'}, dimensions={1}, use_global_device_ids=true | all-gather | bytes 1064960 | tf_op jit(solution)/shard_map/all_gather | solution.py:101
  59.6 2.8 %collective-permute-start.6 = (f32[64,32]{1,0:T(8,128)S(1)}, f32[64,32]{1,0:T(8,128)S(1)}, u32[]{:S(2)}, u32[]{:S(2)}) collective-permute-start(f32[64,32]{1,0:T(8,128)S(1)} %fusion.24), channel_id=1, source_target_pairs={{0,48},{16,32},{32,16},{48,0},{1,49},{17,33},{33,17},{49,1},{2,50}... | collective-permute-start | bytes 24584 | tf_op jit(solution)/shard_map/ppermute | solution.py:13
  65.1 2.8 %collective-permute-done.5 = f32[64,32]{1,0:T(8,128)S(1)} collective-permute-done((f32[64,32]{1,0:T(8,128)S(1)}, f32[64,32]{1,0:T(8,128)S(1)}, u32[]{:S(2)}, u32[]{:S(2)}) %collective-permute-start.5) | collective-permute-done | bytes 8224 | tf_op jit(solution)/shard_map/ppermute | solution.py:13
  67.9 1.7 %collective-permute-start.9 = (f32[64,32]{1,0:T(8,128)S(1)}, f32[64,32]{1,0:T(8,128)S(1)}, u32[]{:S(2)}, u32[]{:S(2)}) collective-permute-start(f32[64,32]{1,0:T(8,128)S(1)} %add_add_fusion.1), channel_id=1, source_target_pairs={{0,6},{2,4},{4,2},{6,0},{1,7},{3,5},{5,3},{7,1},{8,14},{10,12},{12... | collective-permute-start | bytes 24584 | tf_op jit(solution)/shard_map/ppermute | solution.py:13
  70.5 1.6 collective-permute-start.7
  73.4 1.6 collective-permute-done.8
  75.6 1.6 collective-permute-start.10
  79.9 3.8 %collective-permute-done.10 = f32[64,32]{1,0:T(8,128)} collective-permute-done((f32[64,32]{1,0:T(8,128)}, f32[64,32]{1,0:T(8,128)}, u32[]{:S(2)}, u32[]{:S(2)}) %collective-permute-start.10) | collective-permute-done | bytes 8224 | tf_op jit(solution)/shard_map/ppermute | solution.py:13
  85.4 1.8 %collective-permute-start.12 = (bf16[64,32]{1,0:T(8,128)(2,1)S(1)}, bf16[64,32]{1,0:T(8,128)(2,1)S(1)}, u32[]{:S(2)}, u32[]{:S(2)}) collective-permute-start(bf16[64,32]{1,0:T(8,128)(2,1)S(1)} %add.121), channel_id=1, source_target_pairs={{0,192},{64,128},{128,64},{192,0},{1,193},{65,129},{129,65},{193,1... | collective-permute-start | bytes 12296 | tf_op jit(solution)/shard_map/ppermute | solution.py:13
  91.1 2.0 %collective-permute-start.16 = (bf16[16,2048]{1,0:T(8,128)(2,1)S(1)}, bf16[16,2048]{1,0:T(8,128)(2,1)S(1)}, u32[]{:S(2)}, u32[]{:S(2)}) collective-permute-start(bf16[16,2048]{1,0:T(8,128)(2,1)S(1)} %get-tuple-element.28), channel_id=1, source_target_pairs={{0,32},{16,48},{32,0},{48,16},{1,33},{17,49},{33,1},{49,17},{2,34}... | collective-permute-start | bytes 196616 | tf_op jit(solution)/shard_map/ppermute | solution.py:13
  94.7 2.2 %collective-permute-done.16 = bf16[16,2048]{1,0:T(8,128)(2,1)S(1)} collective-permute-done((bf16[16,2048]{1,0:T(8,128)(2,1)S(1)}, bf16[16,2048]{1,0:T(8,128)(2,1)S(1)}, u32[]{:S(2)}, u32[]{:S(2)}) %collective-permute-start.16) | collective-permute-done | bytes 65568 | tf_op jit(solution)/shard_map/ppermute | solution.py:13
  97.4 1.9 %collective-permute-start.20 = (bf16[64,2048]{1,0:T(8,128)(2,1)S(1)}, bf16[64,2048]{1,0:T(8,128)(2,1)S(1)}, u32[]{:S(2)}, u32[]{:S(2)}) collective-permute-start(bf16[64,2048]{1,0:T(8,128)(2,1)S(1)} %bitcast.161), channel_id=1, source_target_pairs={{0,6},{2,4},{4,2},{6,0},{1,7},{3,5},{5,3},{7,1},{8,14},{10,12},{12... | collective-permute-start | bytes 786440 | tf_op jit(solution)/shard_map/ppermute | solution.py:13
  99.3 2.1 %collective-permute-start.19 = (bf16[64,2048]{1,0:T(8,128)(2,1)S(1)}, bf16[64,2048]{1,0:T(8,128)(2,1)S(1)}, u32[]{:S(2)}, u32[]{:S(2)}) collective-permute-start(bf16[64,2048]{1,0:T(8,128)(2,1)S(1)} %bitcast.162), channel_id=1, source_target_pairs={{0,4},{2,6},{4,0},{6,2},{1,5},{3,7},{5,1},{7,3},{8,12},{10,14},{12... | collective-permute-start | bytes 786440 | tf_op jit(solution)/shard_map/ppermute | solution.py:13
  102.4 3.6 %collective-permute-done.20 = bf16[64,2048]{1,0:T(8,128)(2,1)S(1)} collective-permute-done((bf16[64,2048]{1,0:T(8,128)(2,1)S(1)}, bf16[64,2048]{1,0:T(8,128)(2,1)S(1)}, u32[]{:S(2)}, u32[]{:S(2)}) %collective-permute-start.20) | collective-permute-done | bytes 262176 | tf_op jit(solution)/shard_map/ppermute | solution.py:13
  107.2 1.6 collective-permute-done.18
  109.3 1.7 %collective-permute-start.24 = (bf16[256,32]{0,1:T(8,128)(2,1)S(1)}, bf16[256,32]{0,1:T(8,128)(2,1)S(1)}, u32[]{:S(2)}, u32[]{:S(2)}) collective-permute-start(bf16[256,32]{0,1:T(8,128)(2,1)S(1)} %convolution_convert_fusion), channel_id=1, source_target_pairs={{0,192},{64,128},{128,64},{192,0},{1,193},{65,129},{129,65},{193,1... | collective-permute-start | bytes 49160 | tf_op jit(solution)/shard_map/ppermute | solution.py:13
  111.0 2.7 %collective-permute-start.22 = (bf16[256,32]{0,1:T(8,128)(2,1)S(1)}, bf16[256,32]{0,1:T(8,128)(2,1)S(1)}, u32[]{:S(2)}, u32[]{:S(2)}) collective-permute-start(bf16[256,32]{0,1:T(8,128)(2,1)S(1)} %convolution_convert_fusion), channel_id=1, source_target_pairs={{0,64},{64,0},{128,192},{192,128},{1,65},{65,1},{129,193},{193,129... | collective-permute-start | bytes 49160 | tf_op jit(solution)/shard_map/ppermute | solution.py:13
  120.7 1.9 %fusion.3 = f32[16,832]{1,0:T(8,128)} fusion(f32[16,832]{1,0:T(8,128)S(1)} %fusion.9, bf16[2,256,832]{2,1,0:T(8,128)(2,1)} %copy-done.5, bf16[2,256,32]{2,1,0:T(8,128)(2,1)S(1)} %bitcast.170, f32[832]{0:T(1024)S(1)} %copy-done.6), kind=kOutput, calls=%fused_computation.9 | convolution fusion | flops 6855680 | bytes 638976 | tf_op jit(solution)/shard_map/dot_general | solution.py:33
  122.6 2.1 %fusion.6 = bf16[4,32,2048]{2,1,0:T(8,128)(2,1)} fusion(bf16[4,32,2048]{2,1,0:T(8,128)(2,1)} %collective-permute-done.1, bf16[4,2,32,2048]{3,2,1,0:T(8,128)(2,1)} %bitcast.155), kind=kLoop, calls=%fused_computation.15 | loop fusion | flops 1048576 | bytes 1572864 | tf_op jit(solution)/shard_map/convert_element_type | solution.py:105
  124.7 6.3 %all-to-all-start.1 = ((bf16[16,8,2048]{2,1,0:T(8,128)(2,1)}), bf16[16,8,2048]{2,1,0:T(8,128)(2,1)}, u32[]{:S(2)}, u32[]{:S(2)}) async-start(bf16[16,8,2048]{2,1,0:T(8,128)(2,1)} %bitcast.157), calls=%async_computation.1 | async-start | bytes 1048576 | tf_op jit(solution)/shard_map/all_to_all | solution.py:106
  131.1 1.9 %fusion.11 = f32[16,832]{1,0:T(8,128)} fusion(bf16[2,256,832]{2,1,0:T(8,128)(2,1)} %copy-done.2, bf16[2,256,32]{2,1,0:T(8,128)(2,1)S(1)} %bitcast.171), kind=kOutput, calls=%fused_computation.40 | convolution fusion | flops 6815744 | bytes 577536 | tf_op jit(solution)/shard_map/dot_general | solution.py:33
  133.0 2.1 %fusion.7 = bf16[4,32,2048]{2,1,0:T(8,128)(2,1)} fusion(bf16[4,32,2048]{2,1,0:T(8,128)(2,1)} %collective-permute-done, bf16[4,2,32,2048]{3,2,1,0:T(8,128)(2,1)} %bitcast.153), kind=kLoop, calls=%fused_computation.17 | loop fusion | flops 1048576 | bytes 1572864 | tf_op jit(solution)/shard_map/convert_element_type | solution.py:105
  135.1 6.5 %all-to-all-done.1 = bf16[16,8,2048]{2,1,0:T(8,128)(2,1)} async-done(((bf16[16,8,2048]{2,1,0:T(8,128)(2,1)}), bf16[16,8,2048]{2,1,0:T(8,128)(2,1)}, u32[]{:S(2)}, u32[]{:S(2)}) %all-to-all-start.1) | async-done | bytes 524320 | tf_op jit(solution)/shard_map/all_to_all | solution.py:106
  141.6 5.4 %all-to-all-start = ((bf16[16,8,2048]{2,1,0:T(8,128)(2,1)}), bf16[16,8,2048]{2,1,0:T(8,128)(2,1)}, u32[]{:S(2)}, u32[]{:S(2)}) async-start(bf16[16,8,2048]{2,1,0:T(8,128)(2,1)} %bitcast.156), calls=%async_computation | async-start | bytes 1048576 | tf_op jit(solution)/shard_map/all_to_all | solution.py:106
  147.1 1.9 %fusion.5 = f32[16,832]{1,0:T(8,128)} fusion(f32[16,832]{1,0:T(8,128)} %fusion.11, bf16[2,256,832]{2,1,0:T(8,128)(2,1)} %copy-done.5, bf16[2,256,32]{2,1,0:T(8,128)(2,1)S(1)} %bitcast.172, f32[832]{0:T(1024)S(1)} %copy-done.7), kind=kOutput, calls=%fused_computation.11 | convolution fusion | flops 6855680 | bytes 638976 | tf_op jit(solution)/shard_map/dot_general | solution.py:33
  151.9 2.9 %collective-permute-start.2 = (bf16[8,2048]{1,0:T(8,128)(2,1)S(1)}, bf16[8,2048]{1,0:T(8,128)(2,1)S(1)}, u32[]{:S(2)}, u32[]{:S(2)}) collective-permute-start(bf16[8,2048]{1,0:T(8,128)(2,1)S(1)} %reduce_sum.22), channel_id=1, source_target_pairs={{0,8},{8,0},{1,9},{9,1},{2,10},{10,2},{3,11},{11,3},{4,12},{12,4},... | collective-permute-start | bytes 98312 | tf_op jit(solution)/shard_map/ppermute | solution.py:13
  157.4 2.4 %collective-permute-done.2 = bf16[8,2048]{1,0:T(8,128)(2,1)S(1)} collective-permute-done((bf16[8,2048]{1,0:T(8,128)(2,1)S(1)}, bf16[8,2048]{1,0:T(8,128)(2,1)S(1)}, u32[]{:S(2)}, u32[]{:S(2)}) %collective-permute-start.2) | collective-permute-done | bytes 32800 | tf_op jit(solution)/shard_map/ppermute | solution.py:13
  159.8 1.5 add_convert_fusion
  (112 shorter events, 38.9 us)
Async XLA Ops:
  0.6 30.7 %copy-start = (bf16[2048,832]{0,1:T(8,128)(2,1)S(1)}, bf16[2048,832]{0,1:T(8,128)(2,1)}, u32[]{:S(2)}) copy-start(bf16[2048,832]{0,1:T(8,128)(2,1)} %param.14) | copy-start | bytes 10223620
  3.2 56.5 %collective-permute-start.3 = (f32[8,8,32]{2,1,0:T(8,128)S(1)}, f32[8,8,32]{2,1,0:T(8,128)S(1)}, u32[]{:S(2)}, u32[]{:S(2)}) collective-permute-start(f32[8,8,32]{2,1,0:T(8,128)S(1)} %dynamic-slice_bitcast_fusion), channel_id=1, source_target_pairs={{0,1},{1,0},{2,3},{3,2},{4,5},{5,4},{6,7},{7,6},{8,9},{9,8},{10,11... | collective-permute-start | bytes 24584 | tf_op jit(solution)/shard_map/ppermute | solution.py:13
  8.9 23.7 %copy-start.1 = (bf16[2048,832]{0,1:T(8,128)(2,1)S(1)}, bf16[2048,832]{0,1:T(8,128)(2,1)}, u32[]{:S(2)}) copy-start(bf16[2048,832]{0,1:T(8,128)(2,1)} %param.15) | copy-start | bytes 10223620
  33.9 29.4 %copy-start.3 = (bf16[256,2048]{1,0:T(8,128)(2,1)}, bf16[256,2048]{1,0:T(8,128)(2,1)S(1)}, u32[]{:S(2)}) copy-start(bf16[256,2048]{1,0:T(8,128)(2,1)S(1)} %fusion) | copy-start | bytes 3145732
  34.8 98.2 %collective-permute-start = (bf16[4,32,2048]{2,1,0:T(8,128)(2,1)}, bf16[4,32,2048]{2,1,0:T(8,128)(2,1)}, u32[]{:S(2)}, u32[]{:S(2)}) collective-permute-start(bf16[4,32,2048]{2,1,0:T(8,128)(2,1)} %slice_bitcast_fusion.2), channel_id=1, source_target_pairs={{0,1},{1,0},{2,3},{3,2},{4,5},{5,4},{6,7},{7,6},{8,9},{9,8},{10,11... | collective-permute-start | bytes 1572872 | tf_op jit(solution)/shard_map/ppermute | solution.py:13
  34.8 52.3 %collective-permute-start.14 = (bf16[8,2048]{1,0:T(8,128)(2,1)}, bf16[8,2048]{1,0:T(8,128)(2,1)}, u32[]{:S(2)}, u32[]{:S(2)}) collective-permute-start(bf16[8,2048]{1,0:T(8,128)(2,1)} %param.11), channel_id=1, source_target_pairs={{0,8},{8,0},{1,9},{9,1},{2,10},{10,2},{3,11},{11,3},{4,12},{12,4},... | collective-permute-start | bytes 98312 | tf_op jit(solution)/shard_map/ppermute | solution.py:13
  59.6 5.5 %collective-permute-start.6 = (f32[64,32]{1,0:T(8,128)S(1)}, f32[64,32]{1,0:T(8,128)S(1)}, u32[]{:S(2)}, u32[]{:S(2)}) collective-permute-start(f32[64,32]{1,0:T(8,128)S(1)} %fusion.24), channel_id=1, source_target_pairs={{0,48},{16,32},{32,16},{48,0},{1,49},{17,33},{33,17},{49,1},{2,50}... | collective-permute-start | bytes 24584 | tf_op jit(solution)/shard_map/ppermute | solution.py:13
  62.5 5.4 %collective-permute-start.5 = (f32[64,32]{1,0:T(8,128)S(1)}, f32[64,32]{1,0:T(8,128)S(1)}, u32[]{:S(2)}, u32[]{:S(2)}) collective-permute-start(f32[64,32]{1,0:T(8,128)S(1)} %fusion.24), channel_id=1, source_target_pairs={{0,32},{16,48},{32,0},{48,16},{1,33},{17,49},{33,1},{49,17},{2,34}... | collective-permute-start | bytes 24584 | tf_op jit(solution)/shard_map/ppermute | solution.py:13
  63.3 4.6 %collective-permute-start.4 = (f32[64,32]{1,0:T(8,128)S(1)}, f32[64,32]{1,0:T(8,128)S(1)}, u32[]{:S(2)}, u32[]{:S(2)}) collective-permute-start(f32[64,32]{1,0:T(8,128)S(1)} %fusion.24), channel_id=1, source_target_pairs={{0,16},{16,0},{32,48},{48,32},{1,17},{17,1},{33,49},{49,33},{2,18}... | collective-permute-start | bytes 24584 | tf_op jit(solution)/shard_map/ppermute | solution.py:13
  67.9 5.5 %collective-permute-start.9 = (f32[64,32]{1,0:T(8,128)S(1)}, f32[64,32]{1,0:T(8,128)S(1)}, u32[]{:S(2)}, u32[]{:S(2)}) collective-permute-start(f32[64,32]{1,0:T(8,128)S(1)} %add_add_fusion.1), channel_id=1, source_target_pairs={{0,6},{2,4},{4,2},{6,0},{1,7},{3,5},{5,3},{7,1},{8,14},{10,12},{12... | collective-permute-start | bytes 24584 | tf_op jit(solution)/shard_map/ppermute | solution.py:13
  69.6 5.4 %collective-permute-start.8 = (f32[64,32]{1,0:T(8,128)S(1)}, f32[64,32]{1,0:T(8,128)S(1)}, u32[]{:S(2)}, u32[]{:S(2)}) collective-permute-start(f32[64,32]{1,0:T(8,128)S(1)} %add_add_fusion.1), channel_id=1, source_target_pairs={{0,4},{2,6},{4,0},{6,2},{1,5},{3,7},{5,1},{7,3},{8,12},{10,14},{12... | collective-permute-start | bytes 24584 | tf_op jit(solution)/shard_map/ppermute | solution.py:13
  70.5 4.5 %collective-permute-start.7 = (f32[64,32]{1,0:T(8,128)S(1)}, f32[64,32]{1,0:T(8,128)S(1)}, u32[]{:S(2)}, u32[]{:S(2)}) collective-permute-start(f32[64,32]{1,0:T(8,128)S(1)} %add_add_fusion.1), channel_id=1, source_target_pairs={{0,2},{2,0},{4,6},{6,4},{1,3},{3,1},{5,7},{7,5},{8,10},{10,8},{12,... | collective-permute-start | bytes 24584 | tf_op jit(solution)/shard_map/ppermute | solution.py:13
  75.6 8.1 %collective-permute-start.10 = (f32[64,32]{1,0:T(8,128)}, f32[64,32]{1,0:T(8,128)}, u32[]{:S(2)}, u32[]{:S(2)}) collective-permute-start(f32[64,32]{1,0:T(8,128)} %add_add_fusion), channel_id=1, source_target_pairs={{0,8},{8,0},{1,9},{9,1},{2,10},{10,2},{3,11},{11,3},{4,12},{12,4},... | collective-permute-start | bytes 24584 | tf_op jit(solution)/shard_map/ppermute | solution.py:13
  78.1 44.5 %collective-permute-start.1 = (bf16[4,32,2048]{2,1,0:T(8,128)(2,1)}, bf16[4,32,2048]{2,1,0:T(8,128)(2,1)}, u32[]{:S(2)}, u32[]{:S(2)}) collective-permute-start(bf16[4,32,2048]{2,1,0:T(8,128)(2,1)} %slice_bitcast_fusion), channel_id=1, source_target_pairs={{0,1},{1,0},{2,3},{3,2},{4,5},{5,4},{6,7},{7,6},{8,9},{9,8},{10,11... | collective-permute-start | bytes 1572872 | tf_op jit(solution)/shard_map/ppermute | solution.py:13
  84.5 4.6 %collective-permute-start.13 = (bf16[64,32]{1,0:T(8,128)(2,1)S(1)}, bf16[64,32]{1,0:T(8,128)(2,1)S(1)}, u32[]{:S(2)}, u32[]{:S(2)}) collective-permute-start(bf16[64,32]{1,0:T(8,128)(2,1)S(1)} %add.121), channel_id=1, source_target_pairs={{0,128},{64,192},{128,0},{192,64},{1,129},{65,193},{129,1},{193,65... | collective-permute-start | bytes 12296 | tf_op jit(solution)/shard_map/ppermute | solution.py:13
  85.4 5.6 %collective-permute-start.12 = (bf16[64,32]{1,0:T(8,128)(2,1)S(1)}, bf16[64,32]{1,0:T(8,128)(2,1)S(1)}, u32[]{:S(2)}, u32[]{:S(2)}) collective-permute-start(bf16[64,32]{1,0:T(8,128)(2,1)S(1)} %add.121), channel_id=1, source_target_pairs={{0,192},{64,128},{128,64},{192,0},{1,193},{65,129},{129,65},{193,1... | collective-permute-start | bytes 12296 | tf_op jit(solution)/shard_map/ppermute | solution.py:13
  87.2 5.9 %collective-permute-start.11 = (bf16[64,32]{1,0:T(8,128)(2,1)S(1)}, bf16[64,32]{1,0:T(8,128)(2,1)S(1)}, u32[]{:S(2)}, u32[]{:S(2)}) collective-permute-start(bf16[64,32]{1,0:T(8,128)(2,1)S(1)} %add.121), channel_id=1, source_target_pairs={{0,64},{64,0},{128,192},{192,128},{1,65},{65,1},{129,193},{193,129... | collective-permute-start | bytes 12296 | tf_op jit(solution)/shard_map/ppermute | solution.py:13
  89.2 5.5 %collective-permute-start.17 = (bf16[16,2048]{1,0:T(8,128)(2,1)S(1)}, bf16[16,2048]{1,0:T(8,128)(2,1)S(1)}, u32[]{:S(2)}, u32[]{:S(2)}) collective-permute-start(bf16[16,2048]{1,0:T(8,128)(2,1)S(1)} %get-tuple-element.28), channel_id=1, source_target_pairs={{0,48},{16,32},{32,16},{48,0},{1,49},{17,33},{33,17},{49,1},{2,50}... | collective-permute-start | bytes 196616 | tf_op jit(solution)/shard_map/ppermute | solution.py:13
  91.1 5.8 %collective-permute-start.16 = (bf16[16,2048]{1,0:T(8,128)(2,1)S(1)}, bf16[16,2048]{1,0:T(8,128)(2,1)S(1)}, u32[]{:S(2)}, u32[]{:S(2)}) collective-permute-start(bf16[16,2048]{1,0:T(8,128)(2,1)S(1)} %get-tuple-element.28), channel_id=1, source_target_pairs={{0,32},{16,48},{32,0},{48,16},{1,33},{17,49},{33,1},{49,17},{2,34}... | collective-permute-start | bytes 196616 | tf_op jit(solution)/shard_map/ppermute | solution.py:13
  93.1 4.3 %collective-permute-start.15 = (bf16[16,2048]{1,0:T(8,128)(2,1)S(1)}, bf16[16,2048]{1,0:T(8,128)(2,1)S(1)}, u32[]{:S(2)}, u32[]{:S(2)}) collective-permute-start(bf16[16,2048]{1,0:T(8,128)(2,1)S(1)} %get-tuple-element.28), channel_id=1, source_target_pairs={{0,16},{16,0},{32,48},{48,32},{1,17},{17,1},{33,49},{49,33},{2,18}... | collective-permute-start | bytes 196616 | tf_op jit(solution)/shard_map/ppermute | solution.py:13
  97.4 8.6 %collective-permute-start.20 = (bf16[64,2048]{1,0:T(8,128)(2,1)S(1)}, bf16[64,2048]{1,0:T(8,128)(2,1)S(1)}, u32[]{:S(2)}, u32[]{:S(2)}) collective-permute-start(bf16[64,2048]{1,0:T(8,128)(2,1)S(1)} %bitcast.161), channel_id=1, source_target_pairs={{0,6},{2,4},{4,2},{6,0},{1,7},{3,5},{5,3},{7,1},{8,14},{10,12},{12... | collective-permute-start | bytes 786440 | tf_op jit(solution)/shard_map/ppermute | solution.py:13
  99.3 7.9 %collective-permute-start.19 = (bf16[64,2048]{1,0:T(8,128)(2,1)S(1)}, bf16[64,2048]{1,0:T(8,128)(2,1)S(1)}, u32[]{:S(2)}, u32[]{:S(2)}) collective-permute-start(bf16[64,2048]{1,0:T(8,128)(2,1)S(1)} %bitcast.162), channel_id=1, source_target_pairs={{0,4},{2,6},{4,0},{6,2},{1,5},{3,7},{5,1},{7,3},{8,12},{10,14},{12... | collective-permute-start | bytes 786440 | tf_op jit(solution)/shard_map/ppermute | solution.py:13
  101.4 7.3 %collective-permute-start.18 = (bf16[64,2048]{1,0:T(8,128)(2,1)S(1)}, bf16[64,2048]{1,0:T(8,128)(2,1)S(1)}, u32[]{:S(2)}, u32[]{:S(2)}) collective-permute-start(bf16[64,2048]{1,0:T(8,128)(2,1)S(1)} %bitcast.163), channel_id=1, source_target_pairs={{0,2},{2,0},{4,6},{6,4},{1,3},{3,1},{5,7},{7,5},{8,10},{10,8},{12,... | collective-permute-start | bytes 786440 | tf_op jit(solution)/shard_map/ppermute | solution.py:13
  109.3 5.6 %collective-permute-start.24 = (bf16[256,32]{0,1:T(8,128)(2,1)S(1)}, bf16[256,32]{0,1:T(8,128)(2,1)S(1)}, u32[]{:S(2)}, u32[]{:S(2)}) collective-permute-start(bf16[256,32]{0,1:T(8,128)(2,1)S(1)} %convolution_convert_fusion), channel_id=1, source_target_pairs={{0,192},{64,128},{128,64},{192,0},{1,193},{65,129},{129,65},{193,1... | collective-permute-start | bytes 49160 | tf_op jit(solution)/shard_map/ppermute | solution.py:13
  111.0 4.6 %collective-permute-start.23 = (bf16[256,32]{0,1:T(8,128)(2,1)S(1)}, bf16[256,32]{0,1:T(8,128)(2,1)S(1)}, u32[]{:S(2)}, u32[]{:S(2)}) collective-permute-start(bf16[256,32]{0,1:T(8,128)(2,1)S(1)} %convolution_convert_fusion), channel_id=1, source_target_pairs={{0,128},{64,192},{128,0},{192,64},{1,129},{65,193},{129,1},{193,65... | collective-permute-start | bytes 49160 | tf_op jit(solution)/shard_map/ppermute | solution.py:13
  111.0 4.6 %collective-permute-start.22 = (bf16[256,32]{0,1:T(8,128)(2,1)S(1)}, bf16[256,32]{0,1:T(8,128)(2,1)S(1)}, u32[]{:S(2)}, u32[]{:S(2)}) collective-permute-start(bf16[256,32]{0,1:T(8,128)(2,1)S(1)} %convolution_convert_fusion), channel_id=1, source_target_pairs={{0,64},{64,0},{128,192},{192,128},{1,65},{65,1},{129,193},{193,129... | collective-permute-start | bytes 49160 | tf_op jit(solution)/shard_map/ppermute | solution.py:13
  114.9 34.1 %collective-permute-start.21 = (f32[2048,32]{0,1:T(8,128)}, f32[2048,32]{0,1:T(8,128)}, u32[]{:S(2)}, u32[]{:S(2)}) collective-permute-start(f32[2048,32]{0,1:T(8,128)} %convolution_multiply_fusion), channel_id=1, source_target_pairs={{0,1},{1,0},{2,3},{3,2},{4,5},{5,4},{6,7},{7,6},{8,9},{9,8},{10,11... | collective-permute-start | bytes 786440 | tf_op jit(solution)/shard_map/ppermute | solution.py:13
  116.5 1.3 collective-permute-start.25
  120.7 26.4 %copy-start.7 = (f32[832]{0:T(1024)S(1)}, f32[832]{0:T(1024)}, u32[]{:S(2)}) copy-start(f32[832]{0:T(1024)} %param.17) | copy-start | bytes 9988
  124.7 16.9 %all-to-all-start.1 = ((bf16[16,8,2048]{2,1,0:T(8,128)(2,1)}), bf16[16,8,2048]{2,1,0:T(8,128)(2,1)}, u32[]{:S(2)}, u32[]{:S(2)}) async-start(bf16[16,8,2048]{2,1,0:T(8,128)(2,1)} %bitcast.157), calls=%async_computation.1 | async-start | bytes 1048576 | tf_op jit(solution)/shard_map/all_to_all | solution.py:106
  141.6 14.6 %all-to-all-start = ((bf16[16,8,2048]{2,1,0:T(8,128)(2,1)}), bf16[16,8,2048]{2,1,0:T(8,128)(2,1)}, u32[]{:S(2)}, u32[]{:S(2)}) async-start(bf16[16,8,2048]{2,1,0:T(8,128)(2,1)} %bitcast.156), calls=%async_computation | async-start | bytes 1048576 | tf_op jit(solution)/shard_map/all_to_all | solution.py:106
  151.9 7.9 %collective-permute-start.2 = (bf16[8,2048]{1,0:T(8,128)(2,1)S(1)}, bf16[8,2048]{1,0:T(8,128)(2,1)S(1)}, u32[]{:S(2)}, u32[]{:S(2)}) collective-permute-start(bf16[8,2048]{1,0:T(8,128)(2,1)S(1)} %reduce_sum.22), channel_id=1, source_target_pairs={{0,8},{8,0},{1,9},{9,1},{2,10},{10,2},{3,11},{11,3},{4,12},{12,4},... | collective-permute-start | bytes 98312 | tf_op jit(solution)/shard_map/ppermute | solution.py:13
  (4 other events, 32.0 us)

commit v2 on v1

v2 whole, which is shorter than its diff:
```python
import jax
import jax.numpy as jnp
from jax import lax
from jax.experimental import pallas as pl
from jax.experimental.pallas import tpu as pltpu
from jax.sharding import Mesh, PartitionSpec as P

ADAPTER_SCALE = 2.0
FFN = ("x", "zh", "y", "core")
F32, BF16 = jnp.float32, jnp.bfloat16
UNITS, FEATS, STEP = 832, 2048, 256
BY_ROWS = (((1,), (1,)), ((), ()))
BY_COLUMNS = (((0,), (0,)), ((), ()))
SMEM = pl.BlockSpec(memory_space=pltpu.SMEM)
VMEM = pl.BlockSpec(memory_space=pltpu.VMEM)


def swap(value, axis, mask):
    size = lax.axis_size(axis)
    return lax.ppermute(value, axis, [(i, i ^ mask) for i in range(size)])


def gather_over(value, axis):
    return [value] + [swap(value, axis, k) for k in range(1, lax.axis_size(axis))]


def xor_order(value, dim, index):
    size, step = value.shape[dim], 1
    while step < size:
        order = [j ^ step for j in range(size)]
        moved = jnp.concatenate([lax.slice_in_dim(value, j, j + 1, axis=dim) for j in order], dim)
        value = jnp.where((index & step) != 0, moved, value)
        step *= 2
    return value


def dot(left, right, how):
    return lax.dot_general(left, right, how, preferred_element_type=F32)


def prep_kernel(place, gate, up, gate_scale, up_scale, gate_lift, up_lift, far, near, back_other, back_own):
    zh, core = place[0], place[1]
    for k, (grad, scale) in enumerate(((gate, gate_scale), (up, up_scale))):
        rows = (grad[...].astype(F32) * scale[...]).reshape(2, 4, 2, 8, UNITS)
        first, second = rows[0], rows[1]
        for out, half in (
            (far, jnp.where(zh == 0, second, first)),
            (near, jnp.where(zh == 0, first, second)),
        ):
            other = jnp.where(core == 0, half[:, 1], half[:, 0]).reshape(32, UNITS)
            own = jnp.where(core == 0, half[:, 0], half[:, 1]).reshape(32, UNITS)
            out[k, 0] = other.astype(BF16)
            out[k, 1] = own.astype(BF16)
    none = jnp.zeros((16, UNITS), F32)
    back = dot(gate[...], jnp.concatenate([gate_lift[...], none], 0).astype(BF16), BY_ROWS)
    back += dot(up[...], jnp.concatenate([none, up_lift[...]], 0).astype(BF16), BY_ROWS)
    back = back.reshape(8, 2, 8, 32)
    back_other[...] = jnp.where(core == 0, back[:, 1], back[:, 0]).reshape(64, 32)
    back_own[...] = jnp.where(core == 0, back[:, 0], back[:, 1]).reshape(64, 32)


def prep(place, *arrays):
    half = jax.ShapeDtypeStruct((2, 2, 32, UNITS), BF16)
    back = jax.ShapeDtypeStruct((64, 32), F32)
    return pl.pallas_call(
        prep_kernel,
        out_shape=(half, half, back, back),
        in_specs=[SMEM] + [VMEM] * 6,
        out_specs=(VMEM,) * 4,
        cost_estimate=pl.CostEstimate(flops=14_000_000, bytes_accessed=1_200_000, transcendentals=0),
        name="prep",
    )(place, *arrays)


def product_kernel(place, r0, r1, r2, r3a, r3b, gate_codes, up_codes, out, grads):
    @pl.when(pl.program_id(0) == 0)
    def _():
        for k in range(2):
            for c in range(2):
                for j, block in enumerate((r0, r1, r2)):
                    grads[k, c, place[0] ^ j] = block[k, c]
                grads[k, c, place[0] ^ 3] = r3a[k, c] + r3b[k, c]

    total = dot(grads[0].reshape(256, UNITS), gate_codes[...], BY_ROWS)
    total += dot(grads[1].reshape(256, UNITS), up_codes[...], BY_ROWS)
    out[...] = total.astype(BF16).reshape(2, 128, STEP)


def product(place, blocks, gate_codes, up_codes):
    whole = pl.BlockSpec((2, 2, 32, UNITS), lambda i: (0, 0, 0, 0))
    codes = pl.BlockSpec((STEP, UNITS), lambda i: (i, 0))
    return pl.pallas_call(
        product_kernel,
        grid=(FEATS // STEP,),
        out_shape=(
            jax.ShapeDtypeStruct((2, 128, FEATS), BF16),
            jax.ShapeDtypeStruct((2, 2, 4, 32, UNITS), BF16),
        ),
        in_specs=[SMEM] + [whole] * 5 + [codes] * 2,
        out_specs=(
            pl.BlockSpec((2, 128, STEP), lambda i: (0, 0, i)),
            pl.BlockSpec((2, 2, 4, 32, UNITS), lambda i: (0, 0, 0, 0, 0)),
        ),
        compiler_params=pltpu.CompilerParams(vmem_limit_bytes=32 << 20),
        cost_estimate=pl.CostEstimate(flops=1_750_000_000, bytes_accessed=9_700_000, transcendentals=0),
        name="product",
    )(place, *blocks, gate_codes, up_codes)


def expander_kernel(low, far, near, gate_scale, up_scale, gate_out, up_out):
    for k, (out, scale) in enumerate(((gate_out, gate_scale), (up_out, up_scale))):
        total = dot(low[0], far[k].reshape(256, UNITS), BY_COLUMNS)
        total += dot(low[1], near[k].reshape(256, UNITS), BY_COLUMNS)
        out[...] = ADAPTER_SCALE * total[16 * k : 16 * k + 16] / scale[...]


def expander(*arrays):
    out = jax.ShapeDtypeStruct((16, UNITS), F32)
    return pl.pallas_call(
        expander_kernel,
        out_shape=(out, out),
        in_specs=[VMEM] * 5,
        out_specs=(VMEM, VMEM),
        compiler_params=pltpu.CompilerParams(vmem_limit_bytes=32 << 20),
        cost_estimate=pl.CostEstimate(flops=55_000_000, bytes_accessed=2_000_000, transcendentals=0),
        name="expander",
    )(*arrays)


def gather_hid(value):
    two = swap(value, "hid", 2)
    one = swap(value, "hid", 1)
    middle = lax.ppermute(value, "hid", [(1, 2), (2, 1)])
    ends = lax.ppermute(two, "hid", [(1, 0), (2, 3)])
    return value, one, two, middle, ends


def per_device(
    inputs, gate_grad, up_grad, gate_codes, up_codes, gate_scale, up_scale,
    gate_down, gate_lift, up_down, up_lift,
):
    hid = lax.axis_index("hid")
    x, zh, y, core = (lax.axis_index(name) for name in FFN)
    gate_scale, up_scale = gate_scale.reshape(1, UNITS), up_scale.reshape(1, UNITS)

    far, near, back_other, back_own = prep(
        jnp.stack([zh, core]), gate_grad, up_grad, gate_scale, up_scale, gate_lift, up_lift
    )
    far_blocks = gather_hid(far)
    near_blocks = gather_hid(near)

    tokens = jnp.concatenate(gather_over(inputs, "zh"), 0)
    back = (back_own + swap(back_other, "core", 1)).reshape(16, 128)
    parts = gather_over(jnp.concatenate([tokens, back.astype(BF16)], 1), "x")
    tokens = jnp.concatenate([part[:, :FEATS] for part in parts], 0)
    back = sum(part[:, FEATS:].astype(F32) for part in parts)
    back = jnp.pad(back.astype(BF16), ((0, 48), (0, 0)))
    parts = gather_over(jnp.concatenate([tokens, back], 1), "y")
    tokens = jnp.concatenate([part[:, :FEATS] for part in parts], 0)
    back = sum(part[:16, FEATS:].astype(F32) for part in parts)
    back = (back + swap(back, "zh", 1)).reshape(64, 32)

    down = jnp.concatenate([gate_down, up_down], 1).astype(BF16)
    low = dot(tokens, down, (((1,), (0,)), ((), ())))
    parts = gather_over(jnp.concatenate([low, back], 0).astype(BF16), "hid")
    low = sum(part[:256].astype(F32) for part in parts).astype(BF16)
    back = jnp.stack([part[256:] for part in parts]).reshape(4, 2, 4, 8, 32)
    back = xor_order(xor_order(xor_order(back, 0, hid ^ x), 1, zh), 2, y)
    back = back.transpose(2, 0, 1, 3, 4).reshape(256, 32)

    adapter = ADAPTER_SCALE * dot(back[:8], down, BY_ROWS)
    reducer = ADAPTER_SCALE * dot(tokens, back, BY_COLUMNS)
    reducer = reducer + swap(reducer, "core", 1)

    low = low.reshape(4, 4, 2, 8, 32)
    low = xor_order(xor_order(low, 0, y), 1, x)
    low = jnp.stack([swap(low, "core", 1), low])
    low = low.transpose(3, 0, 2, 1, 4, 5)[::-1].reshape(2, 256, 32)

    kept, grads = [], []
    for blocks in (far_blocks, near_blocks):
        part, assembled = product(hid.reshape(1), blocks, gate_codes, up_codes)
        grads.append(assembled)
        summed = part[1].astype(F32) + swap(part[0], "core", 1).astype(F32)
        landed = lax.all_to_all(
            summed.astype(BF16), ("x", "y"), split_axis=0, concat_axis=0, tiled=True
        )
        kept.append(landed.astype(F32).reshape(16, 8, FEATS).sum(0))
    gate_expander, up_expander = expander(low, *grads, gate_scale, up_scale)
    arrived = swap(kept[0].astype(BF16), "zh", 1)
    rows = (kept[1] + arrived.astype(F32) + adapter).astype(BF16)
    return rows, reducer[:, :16], gate_expander, reducer[:, 16:], up_expander


def solution(mesh):
    whole = Mesh(mesh.devices.reshape(4, 4, 2, 4, 2), ("hid",) + FFN)
    placed = (
        P(FFN, "hid"), P("hid", FFN), P("hid", FFN), P("hid", FFN), P("hid", FFN),
        P(FFN), P(FFN), P("hid", None), P(None, FFN), P("hid", None), P(None, FFN),
    )
    return jax.shard_map(
        per_device,
        mesh=whole,
        in_specs=placed,
        out_specs=(P(FFN, "hid"), P("hid", None), P(None, FFN), P("hid", None), P(None, FFN)),
        check_vma=False,
    )
```

time: 162 us -> 136 us (0.84)
  blocking collectives: 42.3 us -> 0 us
  local copies, waits for them, and re-layouts: 8.45 us -> 28.9 us
  matrix products: 16.6 us -> 2.23 us
  Pallas kernels: 0 us -> 10.9 us
  starting transfers between devices: 45.5 us -> 53.8 us
  waiting for transfers between devices: 31.7 us -> 25.3 us
  other arithmetic: 15.8 us -> 12.2 us
    all_gather x2 -> x0, blocking collectives: 42.3 us -> none  [per_device(): grads = lax.all_gather(mine, 'hid', axis=1, tiled=True)]
    unnamed x18 -> x31, local copies, waits for them, and re-layouts: 3.55 us -> 21.5 us
    dot_general x13 -> x3, matrix products: 16.6 us -> 2.23 us  [dot(): return lax.dot_general(left, right, how, preferred_element_type=F32)]
    pallas_call x0 -> x4, Pallas kernels: none -> 10.9 us  [the longest x2 7.63 us: product(): pl.pallas_call(product_kernel, grid=(FEATS // STEP,), out_shape=(jax.Shap...]
    ppermute x26 -> x21, waiting for transfers between devices: 23.7 us -> 16.1 us  [swap(): return lax.ppermute(value, axis, [(i, i ^ mask) for i in range(size)])]
    convert_element_type x4 -> x3, other arithmetic: 6.25 us -> 0.79 us  [the longest x1 0.76 us: per_device(): parts = gather_over(jnp.concatenate([tokens, back.astype(BF16)], 1), 'x')]
    ppermute x0 -> x4, starting transfers between devices: none -> 3.91 us  [the longest x2 2.58 us: gather_hid(): ends = lax.ppermute(two, 'hid', [(1, 0), (2, 3)])]
    ppermute x26 -> x21, starting transfers between devices: 33.7 us -> 37.5 us  [swap(): return lax.ppermute(value, axis, [(i, i ^ mask) for i in range(size)])]
  transfers between devices with their start and end apart: 28 -> 27, of which waited for: 17 -> 11; matrix products, arithmetic and copies ran while one was open for 23% -> 22% of each run, Pallas kernels for 0% -> 6%
where the time goes in v2:
time: 136 us; the launch traced here: 134 us
  starting transfers between devices  53.8 us (40%)
  local copies, waits for them, and re-layouts  28.9 us (21%)
  waiting for transfers between devices  25.3 us (19%)
  other arithmetic  12.2 us (9%)
  Pallas kernels  10.9 us (8%)
  matrix products  2.23 us (2%)
    ppermute x21, starting transfers between devices, swap(): return lax.ppermute(value, axis, [(i, i ^ mask) for i in range(size)])  37.5 us
    unnamed x31, local copies, waits for them, and re-layouts  21.5 us
    ppermute x21, waiting for transfers between devices, swap(): return lax.ppermute(value, axis, [(i, i ^ mask) for i in range(size)])  16.1 us
    all_to_all x2, starting transfers between devices, per_device(): lax.all_to_all(summed.astype(BF16), ('x', 'y'), split_axis=0, concat_axis...  12.4 us
    all_to_all x2, waiting for transfers between devices, per_device(): lax.all_to_all(summed.astype(BF16), ('x', 'y'), split_axis=0, concat_axis...  8.05 us
    pallas_call x2, Pallas kernels, product(): pl.pallas_call(product_kernel, grid=(FEATS // STEP,), out_shape=(jax.Shap...  7.63 us
    all_to_all x2, other arithmetic, per_device(): lax.all_to_all(summed.astype(BF16), ('x', 'y'), split_axis=0, concat_axis...  2.98 us
  transfers between devices with their start and end apart: 27, of which 11 were waited for; matrix products, arithmetic and copies ran while one was open for 22% of the time, Pallas kernels for 6%

profile of v2, /device:TPU:8, one launch (start us, length us, event | category | flops | bytes accessed | tf_op | source)
XLA Modules:
  0.0 134.5 jit_solution(11021072175010639193)
XLA Ops:
  0.6 1.8 %copy.44.gate = bf16[128,832]{1,0:T(8,128)(2,1)} copy(bf16[128,832]{0,1:T(8,128)(2,1)} %param.12) | data formatting | bytes 425984 | tf_op args[1]
  2.4 1.8 %copy.45.up = bf16[128,832]{1,0:T(8,128)(2,1)} copy(bf16[128,832]{0,1:T(8,128)(2,1)} %param.13) | data formatting | bytes 425984 | tf_op args[2]
  7.3 2.2 %prep.1 = (bf16[2,2,32,832]{3,2,1,0:T(8,128)(2,1)}, bf16[2,2,32,832]{3,2,1,0:T(8,128)(2,1)}, f32[64,32]{1,0:T(8,128)}, f32[64,32]{1,0:T(8,128)}) custom-call(s32[2]{0:T(128)} %pad_add_fusion.place, bf16[128,832]{1,0:T(8,128)(2,1)} %copy.44.gate, bf16[128,832]{1,0:T(8,128)(2,1)} %copy.45.up, f32[1,832]{1,0:T(1,128)} %reshape.249.gate_scale, ...), custom_call_target="tpu_custom_call" | custom-call | flops 14000000 | bytes 1200000 | tf_op jit(solution)/shard_map/prep/pallas_call | solution.py:65
  9.6 7.3 %collective-permute-start.11 = (bf16[8,2048]{1,0:T(8,128)(2,1)}, bf16[8,2048]{1,0:T(8,128)(2,1)S(1)}, u32[]{:S(2)}, u32[]{:S(2)}) collective-permute-start(bf16[8,2048]{1,0:T(8,128)(2,1)} %param.11), channel_id=1, source_target_pairs={{0,8},{8,0},{1,9},{9,1},{2,10},{10,2},{3,11},{11,3},{4,12},{12,4},... | collective-permute-start | bytes 98312 | tf_op jit(solution)/shard_map/ppermute | solution.py:20
  20.0 2.8 %collective-permute-start.15 = (bf16[16,2176]{1,0:T(8,128)(2,1)S(1)}, bf16[16,2176]{1,0:T(8,128)(2,1)S(1)}, u32[]{:S(2)}, u32[]{:S(2)}) collective-permute-start(bf16[16,2176]{1,0:T(8,128)(2,1)S(1)} %pad_maximum_fusion.3), channel_id=1, source_target_pairs={{0,48},{16,32},{32,16},{48,0},{1,49},{17,33},{33,17},{49,1},{2,50}... | collective-permute-start | bytes 208904 | tf_op jit(solution)/shard_map/ppermute | solution.py:20
  24.1 1.4 %collective-permute-done.15 = bf16[16,2176]{1,0:T(8,128)(2,1)S(1)} collective-permute-done((bf16[16,2176]{1,0:T(8,128)(2,1)S(1)}, bf16[16,2176]{1,0:T(8,128)(2,1)S(1)}, u32[]{:S(2)}, u32[]{:S(2)}) %collective-permute-start.15) | collective-permute-done | bytes 69664 | tf_op jit(solution)/shard_map/ppermute | solution.py:20
  25.5 3.1 %collective-permute-done.14 = bf16[16,2176]{1,0:T(8,128)(2,1)S(1)} collective-permute-done((bf16[16,2176]{1,0:T(8,128)(2,1)S(1)}, bf16[16,2176]{1,0:T(8,128)(2,1)S(1)}, u32[]{:S(2)}, u32[]{:S(2)}) %collective-permute-start.14) | collective-permute-done | bytes 69664 | tf_op jit(solution)/shard_map/ppermute | solution.py:20
  28.6 1.7 %collective-permute-start.18 = (bf16[64,2176]{1,0:T(8,128)(2,1)S(1)}, bf16[64,2176]{1,0:T(8,128)(2,1)S(1)}, u32[]{:S(2)}, u32[]{:S(2)}) collective-permute-start(bf16[64,2176]{1,0:T(8,128)(2,1)S(1)} %fusion.5), channel_id=1, source_target_pairs={{0,6},{2,4},{4,2},{6,0},{1,7},{3,5},{5,3},{7,1},{8,14},{10,12},{12... | collective-permute-start | bytes 835592 | tf_op jit(solution)/shard_map/ppermute | solution.py:20
  31.2 1.6 %collective-permute-start.16 = (bf16[64,2176]{1,0:T(8,128)(2,1)S(1)}, bf16[64,2176]{1,0:T(8,128)(2,1)S(1)}, u32[]{:S(2)}, u32[]{:S(2)}) collective-permute-start(bf16[64,2176]{1,0:T(8,128)(2,1)S(1)} %fusion.5), channel_id=1, source_target_pairs={{0,2},{2,0},{4,6},{6,4},{1,3},{3,1},{5,7},{7,5},{8,10},{10,8},{12,... | collective-permute-start | bytes 835592 | tf_op jit(solution)/shard_map/ppermute | solution.py:20
  32.8 2.5 %collective-permute-start.6 = (bf16[2,2,32,832]{3,2,1,0:T(8,128)(2,1)}, bf16[2,2,32,832]{3,2,1,0:T(8,128)(2,1)S(1)}, u32[]{:S(2)}, u32[]{:S(2)}) collective-permute-start(bf16[2,2,32,832]{3,2,1,0:T(8,128)(2,1)} %get-tuple-element.17.r0), channel_id=1, source_target_pairs={{0,128},{64,192},{128,0},{192,64},{1,129},{65,193},{129,1},{193,65... | collective-permute-start | bytes 638984 | tf_op jit(solution)/shard_map/ppermute | solution.py:20
  37.2 4.4 %collective-permute-done.18 = bf16[64,2176]{1,0:T(8,128)(2,1)S(1)} collective-permute-done((bf16[64,2176]{1,0:T(8,128)(2,1)S(1)}, bf16[64,2176]{1,0:T(8,128)(2,1)S(1)}, u32[]{:S(2)}, u32[]{:S(2)}) %collective-permute-start.18) | collective-permute-done | bytes 278560 | tf_op jit(solution)/shard_map/ppermute | solution.py:20
  41.6 1.8 %collective-permute-done.16 = bf16[64,2176]{1,0:T(8,128)(2,1)S(1)} collective-permute-done((bf16[64,2176]{1,0:T(8,128)(2,1)S(1)}, bf16[64,2176]{1,0:T(8,128)(2,1)S(1)}, u32[]{:S(2)}, u32[]{:S(2)}) %collective-permute-start.16) | collective-permute-done | bytes 278560 | tf_op jit(solution)/shard_map/ppermute | solution.py:20
  43.4 5.3 %collective-permute-start.19 = (f32[16,128]{1,0:T(8,128)S(1)}, f32[16,128]{1,0:T(8,128)S(1)}, u32[]{:S(2)}, u32[]{:S(2)}) collective-permute-start(f32[16,128]{1,0:T(8,128)S(1)} %convert_add_fusion.2), channel_id=1, source_target_pairs={{0,8},{8,0},{1,9},{9,1},{2,10},{10,2},{3,11},{11,3},{4,12},{12,4},... | collective-permute-start | bytes 24584 | tf_op jit(solution)/shard_map/ppermute | solution.py:20
  49.2 1.8 %collective-permute-done.19 = f32[16,128]{1,0:T(8,128)S(1)} collective-permute-done((f32[16,128]{1,0:T(8,128)S(1)}, f32[16,128]{1,0:T(8,128)S(1)}, u32[]{:S(2)}, u32[]{:S(2)}) %collective-permute-start.19) | collective-permute-done | bytes 8224 | tf_op jit(solution)/shard_map/ppermute | solution.py:20
  51.1 1.8 %collective-permute-start.22 = (bf16[320,32]{0,1:T(8,128)(2,1)S(1)}, bf16[320,32]{0,1:T(8,128)(2,1)S(1)}, u32[]{:S(2)}, u32[]{:S(2)}) collective-permute-start(bf16[320,32]{0,1:T(8,128)(2,1)S(1)} %pad_maximum_fusion.5), channel_id=1, source_target_pairs={{0,128},{64,192},{128,0},{192,64},{1,129},{65,193},{129,1},{193,65... | collective-permute-start | bytes 61448 | tf_op jit(solution)/shard_map/ppermute | solution.py:20
  52.9 1.7 %collective-permute-start.21 = (bf16[320,32]{0,1:T(8,128)(2,1)S(1)}, bf16[320,32]{0,1:T(8,128)(2,1)S(1)}, u32[]{:S(2)}, u32[]{:S(2)}) collective-permute-start(bf16[320,32]{0,1:T(8,128)(2,1)S(1)} %pad_maximum_fusion.5), channel_id=1, source_target_pairs={{0,192},{64,128},{128,64},{192,0},{1,193},{65,129},{129,65},{193,1... | collective-permute-start | bytes 61448 | tf_op jit(solution)/shard_map/ppermute | solution.py:20
  54.7 1.9 %collective-permute-start = (bf16[2,2,32,832]{3,2,1,0:T(8,128)(2,1)S(1)}, bf16[2,2,32,832]{3,2,1,0:T(8,128)(2,1)S(1)}, u32[]{:S(2)}, u32[]{:S(2)}) collective-permute-start(bf16[2,2,32,832]{3,2,1,0:T(8,128)(2,1)S(1)} %copy-done.3), channel_id=1, source_target_pairs={{0,64},{64,0},{128,192},{192,128},{1,65},{65,1},{129,193},{193,129... | collective-permute-start | bytes 638984 | tf_op jit(solution)/shard_map/ppermute | solution.py:20
  56.6 6.0 %copy.46.gate_codes = bf16[2048,832]{1,0:T(8,128)(2,1)} copy(bf16[2048,832]{0,1:T(8,128)(2,1)} %param.14) | data formatting | bytes 6815744 | tf_op args[3]
  62.6 6.0 %copy.47.up_codes = bf16[2048,832]{1,0:T(8,128)(2,1)} copy(bf16[2048,832]{0,1:T(8,128)(2,1)} %param.15) | data formatting | bytes 6815744 | tf_op args[4]
  68.8 1.5 %collective-permute-start.1 = (bf16[2,2,32,832]{3,2,1,0:T(8,128)(2,1)S(1)}, bf16[2,2,32,832]{3,2,1,0:T(8,128)(2,1)S(1)}, u32[]{:S(2)}, u32[]{:S(2)}) collective-permute-start(bf16[2,2,32,832]{3,2,1,0:T(8,128)(2,1)S(1)} %copy-done.3), channel_id=1, source_target_pairs={{0,128},{64,192},{128,0},{192,64},{1,129},{65,193},{129,1},{193,65... | collective-permute-start | bytes 638984 | tf_op jit(solution)/shard_map/ppermute | solution.py:20
  70.2 1.3 collective-permute-start.5
  83.6 2.0 %copy-done = bf16[2048,832]{1,0:T(8,128)(2,1)S(1)} copy-done((bf16[2048,832]{1,0:T(8,128)(2,1)S(1)}, bf16[2048,832]{1,0:T(8,128)(2,1)}, u32[]{:S(2)}) %copy-start) | copy-done | bytes 3407896
  85.7 2.0 %copy-done.2 = bf16[2048,832]{1,0:T(8,128)(2,1)S(1)} copy-done((bf16[2048,832]{1,0:T(8,128)(2,1)S(1)}, bf16[2048,832]{1,0:T(8,128)(2,1)}, u32[]{:S(2)}) %copy-start.2) | copy-done | bytes 3407896
  87.7 3.8 %product.3 = (bf16[2,128,2048]{2,1,0:T(8,128)(2,1)S(1)}, bf16[2,2,4,32,832]{4,3,2,1,0:T(8,128)(2,1)S(1)}) custom-call(s32[1]{0:T(128)} %bitcast.place, bf16[2,2,32,832]{3,2,1,0:T(8,128)(2,1)S(1)} %copy-done.4, bf16[2,2,32,832]{3,2,1,0:T(8,128)(2,1)S(1)} %collective-permute-done.5.r1, bf16[2,2,32,832]{3,2,1,0:T(8,128)(2,1)S(1)} %collective-permute-done.6.r2, ...), custom_call_target="tpu_custom_call" | custom-call | flops 1750000000 | bytes 9700000 | tf_op jit(solution)/shard_map/product/pallas_call | solution.py:92
  93.1 3.8 %product.2 = (bf16[2,128,2048]{2,1,0:T(8,128)(2,1)S(1)}, bf16[2,2,4,32,832]{4,3,2,1,0:T(8,128)(2,1)S(1)}) custom-call(s32[1]{0:T(128)} %bitcast.place, bf16[2,2,32,832]{3,2,1,0:T(8,128)(2,1)S(1)} %copy-done.3, bf16[2,2,32,832]{3,2,1,0:T(8,128)(2,1)S(1)} %collective-permute-done.r1, bf16[2,2,32,832]{3,2,1,0:T(8,128)(2,1)S(1)} %copy-done.6, ...), custom_call_target="tpu_custom_call" | custom-call | flops 1750000000 | bytes 9700000 | tf_op jit(solution)/shard_map/product/pallas_call | solution.py:92
  98.8 7.6 %all-to-all-start.1 = ((bf16[16,8,2048]{2,1,0:T(8,128)(2,1)}), bf16[16,8,2048]{2,1,0:T(8,128)(2,1)S(1)}, u32[]{:S(2)}, u32[]{:S(2)}) async-start(bf16[16,8,2048]{2,1,0:T(8,128)(2,1)} %fusion.4), calls=%async_computation.1 | async-start | bytes 1048576 | tf_op jit(solution)/shard_map/all_to_all | solution.py:185
  106.4 1.6 %maximum_select_fusion.8 = bf16[1,4,4,2,8,32]{5,4,3,2,1,0:T(8,128)(2,1)} fusion(bf16[1,4,2,2,8,32]{5,4,3,2,1,0:T(8,128)(2,1)} %get-tuple-element.35, bf16[1,4,2,2,8,32]{5,4,3,2,1,0:T(8,128)(2,1)} %get-tuple-element.34, bf16[1,4,1,2,8,32]{5,4,3,2,1,0:T(8,128)(2,1)} %get-tuple-element.44, bf16[1,4,1,2,8,32]{5,4,3,2,1,0:T(8,128)(2,1)} %get-tuple-element.43, ...), kind=kLoop, calls=%fused_computation.31 | loop fusion | flops 98304 | bytes 98308 | tf_op jit(solution)/shard_map/jit(_where)/select_n | solution.py:32
  108.0 2.0 %fusion.3 = bf16[16,8,2048]{2,1,0:T(8,128)(2,1)} fusion(bf16[128,2048]{1,0:T(8,128)(2,1)} %collective-permute-done.4, bf16[2,128,2048]{2,1,0:T(8,128)(2,1)S(1)} %get-tuple-element.16), kind=kLoop, calls=%fused_computation.10 | loop fusion | flops 1048576 | bytes 1572864 | tf_op jit(solution)/shard_map/all_to_all | solution.py:185
  110.0 7.1 %all-to-all-done.1 = bf16[16,8,2048]{2,1,0:T(8,128)(2,1)S(1)} async-done(((bf16[16,8,2048]{2,1,0:T(8,128)(2,1)}), bf16[16,8,2048]{2,1,0:T(8,128)(2,1)S(1)}, u32[]{:S(2)}, u32[]{:S(2)}) %all-to-all-start.1) | async-done | bytes 524320 | tf_op jit(solution)/shard_map/all_to_all | solution.py:185
  117.2 4.8 %all-to-all-start = ((bf16[16,8,2048]{2,1,0:T(8,128)(2,1)}), bf16[16,8,2048]{2,1,0:T(8,128)(2,1)S(1)}, u32[]{:S(2)}, u32[]{:S(2)}) async-start(bf16[16,8,2048]{2,1,0:T(8,128)(2,1)} %fusion.3), calls=%async_computation | async-start | bytes 1048576 | tf_op jit(solution)/shard_map/all_to_all | solution.py:185
  125.9 4.8 %collective-permute-start.10 = (bf16[8,2048]{1,0:T(8,128)(2,1)S(1)}, bf16[8,2048]{1,0:T(8,128)(2,1)S(1)}, u32[]{:S(2)}, u32[]{:S(2)}) collective-permute-start(bf16[8,2048]{1,0:T(8,128)(2,1)S(1)} %reduce_sum.22), channel_id=1, source_target_pairs={{0,8},{8,0},{1,9},{9,1},{2,10},{10,2},{3,11},{11,3},{4,12},{12,4},... | collective-permute-start | bytes 98312 | tf_op jit(solution)/shard_map/ppermute | solution.py:20
  131.8 2.1 %collective-permute-done.10 = bf16[8,2048]{1,0:T(8,128)(2,1)S(1)} collective-permute-done((bf16[8,2048]{1,0:T(8,128)(2,1)S(1)}, bf16[8,2048]{1,0:T(8,128)(2,1)S(1)}, u32[]{:S(2)}, u32[]{:S(2)}) %collective-permute-start.10) | collective-permute-done | bytes 32800 | tf_op jit(solution)/shard_map/ppermute | solution.py:20
  (120 shorter events, 32.1 us)
Async XLA Ops:
  9.5 45.2 %copy-start.3 = (bf16[2,2,32,832]{3,2,1,0:T(8,128)(2,1)S(1)}, bf16[2,2,32,832]{3,2,1,0:T(8,128)(2,1)}, u32[]{:S(2)}) copy-start(bf16[2,2,32,832]{3,2,1,0:T(8,128)(2,1)} %get-tuple-element.15.r0) | copy-start | bytes 638980
  9.5 8.2 %collective-permute-start.12 = (f32[64,32]{1,0:T(8,128)}, f32[64,32]{1,0:T(8,128)S(1)}, u32[]{:S(2)}, u32[]{:S(2)}) collective-permute-start(f32[64,32]{1,0:T(8,128)} %get-tuple-element.20), channel_id=1, source_target_pairs={{0,1},{1,0},{2,3},{3,2},{4,5},{5,4},{6,7},{7,6},{8,9},{9,8},{10,11... | collective-permute-start | bytes 24584 | tf_op jit(solution)/shard_map/ppermute | solution.py:20
  9.6 9.5 %collective-permute-start.11 = (bf16[8,2048]{1,0:T(8,128)(2,1)}, bf16[8,2048]{1,0:T(8,128)(2,1)S(1)}, u32[]{:S(2)}, u32[]{:S(2)}) collective-permute-start(bf16[8,2048]{1,0:T(8,128)(2,1)} %param.11), channel_id=1, source_target_pairs={{0,8},{8,0},{1,9},{9,1},{2,10},{10,2},{3,11},{11,3},{4,12},{12,4},... | collective-permute-start | bytes 98312 | tf_op jit(solution)/shard_map/ppermute | solution.py:20
  20.0 5.5 %collective-permute-start.15 = (bf16[16,2176]{1,0:T(8,128)(2,1)S(1)}, bf16[16,2176]{1,0:T(8,128)(2,1)S(1)}, u32[]{:S(2)}, u32[]{:S(2)}) collective-permute-start(bf16[16,2176]{1,0:T(8,128)(2,1)S(1)} %pad_maximum_fusion.3), channel_id=1, source_target_pairs={{0,48},{16,32},{32,16},{48,0},{1,49},{17,33},{33,17},{49,1},{2,50}... | collective-permute-start | bytes 208904 | tf_op jit(solution)/shard_map/ppermute | solution.py:20
  22.7 5.8 %collective-permute-start.14 = (bf16[16,2176]{1,0:T(8,128)(2,1)S(1)}, bf16[16,2176]{1,0:T(8,128)(2,1)S(1)}, u32[]{:S(2)}, u32[]{:S(2)}) collective-permute-start(bf16[16,2176]{1,0:T(8,128)(2,1)S(1)} %pad_maximum_fusion.3), channel_id=1, source_target_pairs={{0,32},{16,48},{32,0},{48,16},{1,33},{17,49},{33,1},{49,17},{2,34}... | collective-permute-start | bytes 208904 | tf_op jit(solution)/shard_map/ppermute | solution.py:20
  23.5 5.0 %collective-permute-start.13 = (bf16[16,2176]{1,0:T(8,128)(2,1)S(1)}, bf16[16,2176]{1,0:T(8,128)(2,1)S(1)}, u32[]{:S(2)}, u32[]{:S(2)}) collective-permute-start(bf16[16,2176]{1,0:T(8,128)(2,1)S(1)} %pad_maximum_fusion.3), channel_id=1, source_target_pairs={{0,16},{16,0},{32,48},{48,32},{1,17},{17,1},{33,49},{49,33},{2,18}... | collective-permute-start | bytes 208904 | tf_op jit(solution)/shard_map/ppermute | solution.py:20
  28.6 12.9 %collective-permute-start.18 = (bf16[64,2176]{1,0:T(8,128)(2,1)S(1)}, bf16[64,2176]{1,0:T(8,128)(2,1)S(1)}, u32[]{:S(2)}, u32[]{:S(2)}) collective-permute-start(bf16[64,2176]{1,0:T(8,128)(2,1)S(1)} %fusion.5), channel_id=1, source_target_pairs={{0,6},{2,4},{4,2},{6,0},{1,7},{3,5},{5,3},{7,1},{8,14},{10,12},{12... | collective-permute-start | bytes 835592 | tf_op jit(solution)/shard_map/ppermute | solution.py:20
  30.3 11.3 %collective-permute-start.17 = (bf16[64,2176]{1,0:T(8,128)(2,1)S(1)}, bf16[64,2176]{1,0:T(8,128)(2,1)S(1)}, u32[]{:S(2)}, u32[]{:S(2)}) collective-permute-start(bf16[64,2176]{1,0:T(8,128)(2,1)S(1)} %fusion.5), channel_id=1, source_target_pairs={{0,4},{2,6},{4,0},{6,2},{1,5},{3,7},{5,1},{7,3},{8,12},{10,14},{12... | collective-permute-start | bytes 835592 | tf_op jit(solution)/shard_map/ppermute | solution.py:20
  31.2 12.1 %collective-permute-start.16 = (bf16[64,2176]{1,0:T(8,128)(2,1)S(1)}, bf16[64,2176]{1,0:T(8,128)(2,1)S(1)}, u32[]{:S(2)}, u32[]{:S(2)}) collective-permute-start(bf16[64,2176]{1,0:T(8,128)(2,1)S(1)} %fusion.5), channel_id=1, source_target_pairs={{0,2},{2,0},{4,6},{6,4},{1,3},{3,1},{5,7},{7,5},{8,10},{10,8},{12,... | collective-permute-start | bytes 835592 | tf_op jit(solution)/shard_map/ppermute | solution.py:20
  32.8 35.9 %collective-permute-start.6 = (bf16[2,2,32,832]{3,2,1,0:T(8,128)(2,1)}, bf16[2,2,32,832]{3,2,1,0:T(8,128)(2,1)S(1)}, u32[]{:S(2)}, u32[]{:S(2)}) collective-permute-start(bf16[2,2,32,832]{3,2,1,0:T(8,128)(2,1)} %get-tuple-element.17.r0), channel_id=1, source_target_pairs={{0,128},{64,192},{128,0},{192,64},{1,129},{65,193},{129,1},{193,65... | collective-permute-start | bytes 638984 | tf_op jit(solution)/shard_map/ppermute | solution.py:20
  43.4 7.6 %collective-permute-start.19 = (f32[16,128]{1,0:T(8,128)S(1)}, f32[16,128]{1,0:T(8,128)S(1)}, u32[]{:S(2)}, u32[]{:S(2)}) collective-permute-start(f32[16,128]{1,0:T(8,128)S(1)} %convert_add_fusion.2), channel_id=1, source_target_pairs={{0,8},{8,0},{1,9},{9,1},{2,10},{10,2},{3,11},{11,3},{4,12},{12,4},... | collective-permute-start | bytes 24584 | tf_op jit(solution)/shard_map/ppermute | solution.py:20
  51.1 19.1 %collective-permute-start.22 = (bf16[320,32]{0,1:T(8,128)(2,1)S(1)}, bf16[320,32]{0,1:T(8,128)(2,1)S(1)}, u32[]{:S(2)}, u32[]{:S(2)}) collective-permute-start(bf16[320,32]{0,1:T(8,128)(2,1)S(1)} %pad_maximum_fusion.5), channel_id=1, source_target_pairs={{0,128},{64,192},{128,0},{192,64},{1,129},{65,193},{129,1},{193,65... | collective-permute-start | bytes 61448 | tf_op jit(solution)/shard_map/ppermute | solution.py:20
  52.9 18.6 %collective-permute-start.21 = (bf16[320,32]{0,1:T(8,128)(2,1)S(1)}, bf16[320,32]{0,1:T(8,128)(2,1)S(1)}, u32[]{:S(2)}, u32[]{:S(2)}) collective-permute-start(bf16[320,32]{0,1:T(8,128)(2,1)S(1)} %pad_maximum_fusion.5), channel_id=1, source_target_pairs={{0,192},{64,128},{128,64},{192,0},{1,193},{65,129},{129,65},{193,1... | collective-permute-start | bytes 61448 | tf_op jit(solution)/shard_map/ppermute | solution.py:20
  54.6 17.6 %collective-permute-start.20 = (bf16[320,32]{0,1:T(8,128)(2,1)S(1)}, bf16[320,32]{0,1:T(8,128)(2,1)S(1)}, u32[]{:S(2)}, u32[]{:S(2)}) collective-permute-start(bf16[320,32]{0,1:T(8,128)(2,1)S(1)} %pad_maximum_fusion.5), channel_id=1, source_target_pairs={{0,64},{64,0},{128,192},{192,128},{1,65},{65,1},{129,193},{193,129... | collective-permute-start | bytes 61448 | tf_op jit(solution)/shard_map/ppermute | solution.py:20
  54.7 36.9 %collective-permute-start = (bf16[2,2,32,832]{3,2,1,0:T(8,128)(2,1)S(1)}, bf16[2,2,32,832]{3,2,1,0:T(8,128)(2,1)S(1)}, u32[]{:S(2)}, u32[]{:S(2)}) collective-permute-start(bf16[2,2,32,832]{3,2,1,0:T(8,128)(2,1)S(1)} %copy-done.3), channel_id=1, source_target_pairs={{0,64},{64,0},{128,192},{192,128},{1,65},{65,1},{129,193},{193,129... | collective-permute-start | bytes 638984 | tf_op jit(solution)/shard_map/ppermute | solution.py:20
  68.8 11.4 %collective-permute-start.1 = (bf16[2,2,32,832]{3,2,1,0:T(8,128)(2,1)S(1)}, bf16[2,2,32,832]{3,2,1,0:T(8,128)(2,1)S(1)}, u32[]{:S(2)}, u32[]{:S(2)}) collective-permute-start(bf16[2,2,32,832]{3,2,1,0:T(8,128)(2,1)S(1)} %copy-done.3), channel_id=1, source_target_pairs={{0,128},{64,192},{128,0},{192,64},{1,129},{65,193},{129,1},{193,65... | collective-permute-start | bytes 638984 | tf_op jit(solution)/shard_map/ppermute | solution.py:20
  70.2 10.6 %collective-permute-start.5 = (bf16[2,2,32,832]{3,2,1,0:T(8,128)(2,1)S(1)}, bf16[2,2,32,832]{3,2,1,0:T(8,128)(2,1)S(1)}, u32[]{:S(2)}, u32[]{:S(2)}) collective-permute-start(bf16[2,2,32,832]{3,2,1,0:T(8,128)(2,1)S(1)} %copy-done.4), channel_id=1, source_target_pairs={{0,64},{64,0},{128,192},{192,128},{1,65},{65,1},{129,193},{193,129... | collective-permute-start | bytes 638984 | tf_op jit(solution)/shard_map/ppermute | solution.py:20
  71.6 10.6 %collective-permute-start.7 = (bf16[2,2,32,832]{3,2,1,0:T(8,128)(2,1)S(1)}, bf16[2,2,32,832]{3,2,1,0:T(8,128)(2,1)S(1)}, u32[]{:S(2)}, u32[]{:S(2)}) collective-permute-start(bf16[2,2,32,832]{3,2,1,0:T(8,128)(2,1)S(1)} %copy-done.4), channel_id=1, source_target_pairs={{64,128},{128,64},{65,129},{129,65},{66,130},{130,66},{67,131},{13... | collective-permute-start | bytes 638984 | tf_op jit(solution)/shard_map/ppermute | solution.py:133
  72.2 11.4 %collective-permute-start.8 = (bf16[2,2,32,832]{3,2,1,0:T(8,128)(2,1)S(1)}, bf16[2,2,32,832]{3,2,1,0:T(8,128)(2,1)S(1)}, u32[]{:S(2)}, u32[]{:S(2)}) collective-permute-start(bf16[2,2,32,832]{3,2,1,0:T(8,128)(2,1)S(1)} %collective-permute-done.6.r2), channel_id=1, source_target_pairs={{64,0},{128,192},{65,1},{129,193},{66,2},{130,194},{67,3},{131,195... | collective-permute-start | bytes 638984 | tf_op jit(solution)/shard_map/ppermute | solution.py:134
  80.2 11.4 %copy-start.5 = (bf16[2,2,32,832]{3,2,1,0:T(8,128)(2,1)}, bf16[2,2,32,832]{3,2,1,0:T(8,128)(2,1)S(1)}, u32[]{:S(2)}) copy-start(bf16[2,2,32,832]{3,2,1,0:T(8,128)(2,1)S(1)} %collective-permute-done.1.r2) | copy-start | bytes 638980
  80.2 12.0 %collective-permute-start.2 = (bf16[2,2,32,832]{3,2,1,0:T(8,128)(2,1)S(1)}, bf16[2,2,32,832]{3,2,1,0:T(8,128)(2,1)S(1)}, u32[]{:S(2)}, u32[]{:S(2)}) collective-permute-start(bf16[2,2,32,832]{3,2,1,0:T(8,128)(2,1)S(1)} %copy-done.3), channel_id=1, source_target_pairs={{64,128},{128,64},{65,129},{129,65},{66,130},{130,66},{67,131},{13... | collective-permute-start | bytes 638984 | tf_op jit(solution)/shard_map/ppermute | solution.py:133
  80.8 11.3 %collective-permute-start.3 = (bf16[2,2,32,832]{3,2,1,0:T(8,128)(2,1)S(1)}, bf16[2,2,32,832]{3,2,1,0:T(8,128)(2,1)S(1)}, u32[]{:S(2)}, u32[]{:S(2)}) collective-permute-start(bf16[2,2,32,832]{3,2,1,0:T(8,128)(2,1)S(1)} %collective-permute-done.1.r2), channel_id=1, source_target_pairs={{64,0},{128,192},{65,1},{129,193},{66,2},{130,194},{67,3},{131,195... | collective-permute-start | bytes 638984 | tf_op jit(solution)/shard_map/ppermute | solution.py:134
  82.2 41.9 %collective-permute-start.23 = (f32[2048,32]{0,1:T(8,128)}, f32[2048,32]{0,1:T(8,128)}, u32[]{:S(2)}, u32[]{:S(2)}) collective-permute-start(f32[2048,32]{0,1:T(8,128)} %convolution_multiply_fusion), channel_id=1, source_target_pairs={{0,1},{1,0},{2,3},{3,2},{4,5},{5,4},{6,7},{7,6},{8,9},{9,8},{10,11... | collective-permute-start | bytes 786440 | tf_op jit(solution)/shard_map/ppermute | solution.py:20
  83.6 38.4 %collective-permute-start.24 = (bf16[4,4,2,8,32]{4,3,2,1,0:T(8,128)(2,1)}, bf16[4,4,2,8,32]{4,3,2,1,0:T(8,128)(2,1)}, u32[]{:S(2)}, u32[]{:S(2)}) collective-permute-start(bf16[4,4,2,8,32]{4,3,2,1,0:T(8,128)(2,1)} %maximum_select_fusion.7), channel_id=1, source_target_pairs={{0,1},{1,0},{2,3},{3,2},{4,5},{5,4},{6,7},{7,6},{8,9},{9,8},{10,11... | collective-permute-start | bytes 49160 | tf_op jit(solution)/shard_map/ppermute | solution.py:20
  91.6 6.3 %collective-permute-start.9 = (bf16[128,2048]{1,0:T(8,128)(2,1)S(1)}, bf16[128,2048]{1,0:T(8,128)(2,1)S(1)}, u32[]{:S(2)}, u32[]{:S(2)}) collective-permute-start(bf16[128,2048]{1,0:T(8,128)(2,1)S(1)} %slice_bitcast_fusion), channel_id=1, source_target_pairs={{0,1},{1,0},{2,3},{3,2},{4,5},{5,4},{6,7},{7,6},{8,9},{9,8},{10,11... | collective-permute-start | bytes 1572872 | tf_op jit(solution)/shard_map/ppermute | solution.py:20
  97.0 26.0 %copy-start.7 = (f32[1,832]{1,0:T(1,128)S(1)}, f32[1,832]{1,0:T(1,128)}, u32[]{:S(2)}) copy-start(f32[1,832]{1,0:T(1,128)} %reshape.249.gate_scale) | copy-start | bytes 9988
  97.0 26.0 %copy-start.8 = (f32[1,832]{1,0:T(1,128)S(1)}, f32[1,832]{1,0:T(1,128)}, u32[]{:S(2)}) copy-start(f32[1,832]{1,0:T(1,128)} %reshape.250.up_scale) | copy-start | bytes 9988
  97.9 10.2 %collective-permute-start.4 = (bf16[128,2048]{1,0:T(8,128)(2,1)}, bf16[128,2048]{1,0:T(8,128)(2,1)}, u32[]{:S(2)}, u32[]{:S(2)}) collective-permute-start(bf16[128,2048]{1,0:T(8,128)(2,1)} %slice_bitcast_fusion.1), channel_id=1, source_target_pairs={{0,1},{1,0},{2,3},{3,2},{4,5},{5,4},{6,7},{7,6},{8,9},{9,8},{10,11... | collective-permute-start | bytes 1572872 | tf_op jit(solution)/shard_map/ppermute | solution.py:20
  98.8 18.4 %all-to-all-start.1 = ((bf16[16,8,2048]{2,1,0:T(8,128)(2,1)}), bf16[16,8,2048]{2,1,0:T(8,128)(2,1)S(1)}, u32[]{:S(2)}, u32[]{:S(2)}) async-start(bf16[16,8,2048]{2,1,0:T(8,128)(2,1)} %fusion.4), calls=%async_computation.1 | async-start | bytes 1048576 | tf_op jit(solution)/shard_map/all_to_all | solution.py:185
  108.0 25.8 %copy-start.9 = (f32[8,2048]{1,0:T(8,128)S(1)}, f32[8,2048]{1,0:T(8,128)}, u32[]{:S(2)}) copy-start(f32[8,2048]{1,0:T(8,128)} %convolution_multiply_fusion.1) | copy-start | bytes 196612
  117.2 14.5 %all-to-all-start = ((bf16[16,8,2048]{2,1,0:T(8,128)(2,1)}), bf16[16,8,2048]{2,1,0:T(8,128)(2,1)S(1)}, u32[]{:S(2)}, u32[]{:S(2)}) async-start(bf16[16,8,2048]{2,1,0:T(8,128)(2,1)} %fusion.3), calls=%async_computation | async-start | bytes 1048576 | tf_op jit(solution)/shard_map/all_to_all | solution.py:185
  125.9 7.9 %collective-permute-start.10 = (bf16[8,2048]{1,0:T(8,128)(2,1)S(1)}, bf16[8,2048]{1,0:T(8,128)(2,1)S(1)}, u32[]{:S(2)}, u32[]{:S(2)}) collective-permute-start(bf16[8,2048]{1,0:T(8,128)(2,1)S(1)} %reduce_sum.22), channel_id=1, source_target_pairs={{0,8},{8,0},{1,9},{9,1},{2,10},{10,2},{3,11},{11,3},{4,12},{12,4},... | collective-permute-start | bytes 98312 | tf_op jit(solution)/shard_map/ppermute | solution.py:20
  (5 other events, 17.1 us)

commit v3 on v2

v3 whole, which is shorter than its diff:
```python
import jax
import jax.numpy as jnp
from jax import lax
from jax.experimental import pallas as pl
from jax.experimental.pallas import tpu as pltpu
from jax.sharding import Mesh, PartitionSpec as P

ADAPTER_SCALE = 2.0
FFN = ("x", "zh", "y", "core")
F32, BF16 = jnp.float32, jnp.bfloat16
UNITS, FEATS, STEP = 832, 2048, 256
PLAIN = (((1,), (0,)), ((), ()))
BY_ROWS = (((1,), (1,)), ((), ()))
BY_COLUMNS = (((0,), (0,)), ((), ()))
SMEM = pl.BlockSpec(memory_space=pltpu.SMEM)
VMEM = pl.BlockSpec(memory_space=pltpu.VMEM)


def swap(value, axis, mask):
    size = lax.axis_size(axis)
    return lax.ppermute(value, axis, [(i, i ^ mask) for i in range(size)])


def gather_over(value, axis):
    return [value] + [swap(value, axis, k) for k in range(1, lax.axis_size(axis))]


def after(values, others):
    return lax.optimization_barrier((values, others))[0]


def dot(left, right, how):
    return lax.dot_general(left, right, how, preferred_element_type=F32)


def one_hot(rows, columns, source):
    row = lax.broadcasted_iota(jnp.int32, (rows, columns), 0)
    column = lax.broadcasted_iota(jnp.int32, (rows, columns), 1)
    return (column == source(row)).astype(F32).astype(BF16)


def prep_kernel(place, gate, up, gate_scale, up_scale, gate_lift, up_lift, far, near, back_other, back_own):
    zh, core = place[0], place[1]

    def source(row):
        half, side = 1 - row // 64, 1 - row // 32 % 2
        return (half ^ zh) * 64 + row // 8 % 4 * 16 + (side ^ core) * 8 + row % 8

    order = one_hot(128, 128, source)
    none = jnp.zeros((16, UNITS), F32)
    lifts = (
        jnp.concatenate([gate_lift[...], none], 0).astype(BF16),
        jnp.concatenate([none, up_lift[...]], 0).astype(BF16),
    )
    back = jnp.zeros((128, 32), F32)
    for k, (grad, scale) in enumerate(((gate, gate_scale), (up, up_scale))):
        rows = dot(order, grad[...], BY_ROWS)
        back += dot(rows.astype(BF16), lifts[k], BY_ROWS)
        rows = (rows * scale[...].reshape(1, UNITS)).astype(BF16).reshape(2, 2, 32, UNITS)
        far[k] = rows[0]
        near[k] = rows[1]
    back = back.reshape(2, 2, 32, 32)
    back_other[...] = back[:, 0].reshape(64, 32)
    back_own[...] = back[:, 1].reshape(64, 32)


def prep(place, *arrays):
    half = jax.ShapeDtypeStruct((2, 2, 32, UNITS), BF16)
    back = jax.ShapeDtypeStruct((64, 32), F32)
    return pl.pallas_call(
        prep_kernel,
        out_shape=(half, half, back, back),
        in_specs=[SMEM] + [VMEM] * 6,
        out_specs=(VMEM,) * 4,
        cost_estimate=pl.CostEstimate(flops=14_000_000, bytes_accessed=1_200_000, transcendentals=0),
        name="prep",
    )(place, *arrays)


def product_kernel(place, r0, r1, r2, r3a, r3b, gate_codes, up_codes, other, own, grads):
    @pl.when(pl.program_id(0) == 0)
    def _():
        for k in range(2):
            for c in range(2):
                for j, block in enumerate((r0, r1, r2)):
                    grads[k, c, place[0] ^ j] = block[k, c]
                grads[k, c, place[0] ^ 3] = r3a[k, c] + r3b[k, c]

    total = dot(grads[0].reshape(256, UNITS), gate_codes[...], PLAIN)
    total += dot(grads[1].reshape(256, UNITS), up_codes[...], PLAIN)
    other[...] = total[:128].astype(BF16)
    own[...] = total[128:].astype(BF16)


def product(place, blocks, gate_codes, up_codes):
    whole = pl.BlockSpec((2, 2, 32, UNITS), lambda i: (0, 0, 0, 0))
    codes = pl.BlockSpec((UNITS, STEP), lambda i: (0, i))
    part = pl.BlockSpec((128, STEP), lambda i: (0, i))
    return pl.pallas_call(
        product_kernel,
        grid=(FEATS // STEP,),
        out_shape=(
            jax.ShapeDtypeStruct((128, FEATS), BF16),
            jax.ShapeDtypeStruct((128, FEATS), BF16),
            jax.ShapeDtypeStruct((2, 2, 4, 32, UNITS), BF16),
        ),
        in_specs=[SMEM] + [whole] * 5 + [codes] * 2,
        out_specs=(part, part, pl.BlockSpec((2, 2, 4, 32, UNITS), lambda i: (0, 0, 0, 0, 0))),
        compiler_params=pltpu.CompilerParams(vmem_limit_bytes=32 << 20),
        cost_estimate=pl.CostEstimate(flops=1_750_000_000, bytes_accessed=9_700_000, transcendentals=0),
        name="product",
    )(place, *blocks, gate_codes, up_codes)


def joined_kernel(place, p0, p1, p2, p3, tokens, down, low_out, adapter, reducer):
    hid_x, y = place[2] ^ place[3], place[4]
    parts = [part[...] for part in (p0, p1, p2, p3)]
    low = sum(part[:256].astype(F32) for part in parts)
    low_out[...] = low.astype(BF16)
    back = jnp.concatenate([part[256:] for part in parts], 0)

    def source(row):
        rel_y, rel_x, half = row // 64, row // 16 % 4, row // 8 % 2
        return ((rel_x ^ hid_x) * 2 + 1 - half) * 32 + (rel_y ^ y) * 8 + row % 8

    back = (ADAPTER_SCALE * dot(one_hot(256, 256, source), back, PLAIN)).astype(BF16)
    adapter[...] = dot(back[:16], down[...], PLAIN)[:8]
    reducer[...] = dot(back, tokens[...], BY_COLUMNS)


def joined(place, parts, tokens, down):
    return pl.pallas_call(
        joined_kernel,
        out_shape=(
            jax.ShapeDtypeStruct((256, 32), BF16),
            jax.ShapeDtypeStruct((8, FEATS), F32),
            jax.ShapeDtypeStruct((32, FEATS), F32),
        ),
        in_specs=[SMEM] + [VMEM] * 6,
        out_specs=(VMEM,) * 3,
        compiler_params=pltpu.CompilerParams(vmem_limit_bytes=32 << 20),
        cost_estimate=pl.CostEstimate(flops=40_000_000, bytes_accessed=1_700_000, transcendentals=0),
        name="joined",
    )(place, *parts, tokens, down)


def expander_kernel(place, low_other, low_own, far, near, gate_scale, up_scale, gate_out, up_out):
    x, y = place[3], place[4]
    lows = []
    for half in (1, 0):
        order = one_hot(
            128,
            256,
            lambda row: (((row // 8 % 4) ^ y) * 4 + ((row // 32) ^ x)) * 16 + half * 8 + row % 8,
        )
        lows.append([dot(order, low[...], PLAIN).astype(BF16) for low in (low_other, low_own)])
    for k, (out, scale) in enumerate(((gate_out, gate_scale), (up_out, up_scale))):
        total = jnp.zeros((32, UNITS), F32)
        for half, grads in enumerate((far, near)):
            for c in range(2):
                total += dot(lows[half][c], grads[k, c].reshape(128, UNITS), BY_COLUMNS)
        out[...] = ADAPTER_SCALE * total[16 * k : 16 * k + 16] / scale[...].reshape(1, UNITS)


def expander(*arrays):
    out = jax.ShapeDtypeStruct((16, UNITS), F32)
    return pl.pallas_call(
        expander_kernel,
        out_shape=(out, out),
        in_specs=[SMEM] + [VMEM] * 6,
        out_specs=(VMEM, VMEM),
        compiler_params=pltpu.CompilerParams(vmem_limit_bytes=32 << 20),
        cost_estimate=pl.CostEstimate(flops=55_000_000, bytes_accessed=2_000_000, transcendentals=0),
        name="expander",
    )(*arrays)


def direct(value):
    middle = lax.ppermute(value, "hid", [(1, 2), (2, 1)])
    return swap(value, "hid", 2), swap(value, "hid", 1), middle


def relay(two):
    return lax.ppermute(two, "hid", [(1, 0), (2, 3)])


def per_device(
    inputs, gate_grad, up_grad, gate_codes, up_codes, gate_scale, up_scale,
    gate_down, gate_lift, up_down, up_lift,
):
    hid = lax.axis_index("hid")
    x, zh, y, core = (lax.axis_index(name) for name in FFN)
    place = jnp.stack([zh, core, hid, x, y])
    down = jnp.concatenate([gate_down.T, up_down.T], 0).astype(BF16)
    down_columns = jnp.concatenate([gate_down, up_down], 1).astype(BF16)

    far, near, back_other, back_own = prep(
        place, gate_grad.T, up_grad.T, gate_scale, up_scale, gate_lift, up_lift
    )
    far_two, far_one, far_middle = direct(far)
    back = (back_own + swap(back_other, "core", 1)).reshape(2, 4, 256)
    payload = jnp.concatenate([inputs, back.reshape(8, 256).astype(BF16)], 1)
    arrived = swap(payload, "zh", 1)
    back = back + arrived[:, FEATS:].astype(F32).reshape(2, 4, 256)[::-1]
    tokens = jnp.concatenate([inputs, arrived[:, :FEATS]], 0)

    payload = jnp.concatenate(
        [tokens, jnp.pad(back.reshape(8, 256).astype(BF16), ((0, 8), (0, 0)))], 1
    )
    payload, near_sent, far_relayed = after(
        (payload, near, far_two), (far_one, far_middle)
    )
    far_ends = relay(far_relayed)
    near_two, near_one, near_middle = direct(near_sent)
    parts = gather_over(payload, "x")
    tokens = jnp.concatenate([part[:, :FEATS] for part in parts], 0)
    back = sum(part[:8, FEATS:].astype(F32) for part in parts)

    payload = jnp.concatenate([tokens, jnp.pad(back.astype(BF16), ((0, 56), (0, 0)))], 1)
    payload, near_relayed = after((payload, near_two), (near_one, near_middle, far_ends))
    near_ends = relay(near_relayed)
    parts = gather_over(payload, "y")
    tokens = jnp.concatenate([part[:, :FEATS] for part in parts], 0)
    back = sum(part[:8, FEATS:].astype(F32) for part in parts).reshape(64, 32)

    low = dot(tokens, down_columns, PLAIN)
    parts = gather_over(jnp.concatenate([low, back], 0).astype(BF16), "hid")
    low, adapter, reducer = joined(place, parts, tokens, down)
    reducer = reducer + swap(reducer, "core", 1)
    low_other = swap(low, "core", 1)

    kept, grads = [], []
    for blocks in (
        (far, far_one, far_two, far_middle, far_ends),
        (near, near_one, near_two, near_middle, near_ends),
    ):
        other, own, assembled = product(hid.reshape(1), blocks, gate_codes.T, up_codes.T)
        grads.append(assembled)
        summed = own.astype(F32) + swap(other, "core", 1).astype(F32)
        landed = lax.all_to_all(
            summed.astype(BF16), ("x", "y"), split_axis=0, concat_axis=0, tiled=True
        )
        kept.append(landed.astype(F32).reshape(16, 8, FEATS).sum(0))
    gate_expander, up_expander = expander(place, low_other, low, *grads, gate_scale, up_scale)
    arrived = swap(kept[0].astype(BF16), "zh", 1)
    rows = (kept[1] + arrived.astype(F32) + adapter).astype(BF16)
    return rows, reducer[:16].T, gate_expander, reducer[16:].T, up_expander


def solution(mesh):
    whole = Mesh(mesh.devices.reshape(4, 4, 2, 4, 2), ("hid",) + FFN)
    placed = (
        P(FFN, "hid"), P("hid", FFN), P("hid", FFN), P("hid", FFN), P("hid", FFN),
        P(FFN), P(FFN), P("hid", None), P(None, FFN), P("hid", None), P(None, FFN),
    )
    return jax.shard_map(
        per_device,
        mesh=whole,
        in_specs=placed,
        out_specs=(P(FFN, "hid"), P("hid", None), P(None, FFN), P("hid", None), P(None, FFN)),
        check_vma=False,
    )
```

time: 136 us -> 128 us (0.941)
  local copies, waits for them, and re-layouts: 28.9 us -> 13 us
  Pallas kernels: 10.9 us -> 18.5 us
  starting transfers between devices: 53.8 us -> 46.9 us
  other arithmetic: 12.2 us -> 17.3 us
  waiting for transfers between devices: 25.3 us -> 29.6 us
  matrix products: 2.23 us -> 0.41 us
    unnamed x31 -> x50, local copies, waits for them, and re-layouts: 21.5 us -> 7.49 us
    ppermute x21 -> x20, starting transfers between devices: 37.5 us -> 30 us  [swap(): return lax.ppermute(value, axis, [(i, i ^ mask) for i in range(size)])]
    ppermute x21 -> x20, waiting for transfers between devices: 16.1 us -> 22.1 us  [swap(): return lax.ppermute(value, axis, [(i, i ^ mask) for i in range(size)])]
    pallas_call x2, Pallas kernels: 7.63 us -> 11.8 us  [product(): pl.pallas_call(product_kernel, grid=(FEATS // STEP,), out_shape=(jax.Shap...]
    all_to_all x2, waiting for transfers between devices: 8.05 us -> 4.08 us  [per_device(): lax.all_to_all(summed.astype(BF16), ('x', 'y'), split_axis=0, concat_axis...]
    pallas_call x1 -> x2, Pallas kernels: 1.05 us -> 4.19 us  [the longest x1 2.41 us: joined(): pl.pallas_call(joined_kernel, out_shape=(jax.ShapeDtypeStruct((256, 32),...]
    concatenate x2 -> x5, other arithmetic: 0.78 us -> 3.49 us  [the longest x1 1.05 us: per_device(): tokens = jnp.concatenate([part[:, :FEATS] for part in parts], 0)]
    reshape x4 -> x3, local copies, waits for them, and re-layouts: 2.72 us -> 0.18 us  [the longest x1 0.09 us: per_device(): back = sum((part[:8, FEATS:].astype(F32) for part in parts)).reshape(64, 32)]
  transfers between devices with their start and end apart: 27 -> 26, of which waited for: 11 -> 7; matrix products, arithmetic and copies ran while one was open for 22% -> 17% of each run, Pallas kernels for 6% -> 13%
where the time goes in v3:
time: 128 us; the launch traced here: 127 us
  starting transfers between devices  46.9 us (37%)
  waiting for transfers between devices  29.6 us (23%)
  Pallas kernels  18.5 us (14%)
  other arithmetic  17.3 us (14%)
  local copies, waits for them, and re-layouts  13 us (10%)
    ppermute x20, starting transfers between devices, swap(): return lax.ppermute(value, axis, [(i, i ^ mask) for i in range(size)])  30 us
    ppermute x20, waiting for transfers between devices, swap(): return lax.ppermute(value, axis, [(i, i ^ mask) for i in range(size)])  22.1 us
    all_to_all x2, starting transfers between devices, per_device(): lax.all_to_all(summed.astype(BF16), ('x', 'y'), split_axis=0, concat_axis...  12.2 us
    pallas_call x2, Pallas kernels, product(): pl.pallas_call(product_kernel, grid=(FEATS // STEP,), out_shape=(jax.Shap...  11.8 us
    unnamed x50, local copies, waits for them, and re-layouts  7.49 us
    all_to_all x2, waiting for transfers between devices, per_device(): lax.all_to_all(summed.astype(BF16), ('x', 'y'), split_axis=0, concat_axis...  4.08 us
    all_to_all x2, other arithmetic, per_device(): lax.all_to_all(summed.astype(BF16), ('x', 'y'), split_axis=0, concat_axis...  3.99 us
    slice x8, local copies, waits for them, and re-layouts, per_device(): tokens = jnp.concatenate([part[:, :FEATS] for part in parts], 0)  3.7 us
  transfers between devices with their start and end apart: 26, of which 7 were waited for; matrix products, arithmetic and copies ran while one was open for 17% of the time, Pallas kernels for 13%

profile of v3, /device:TPU:8, one launch (start us, length us, event | category | flops | bytes accessed | tf_op | source)
XLA Modules:
  0.0 126.6 jit_solution(2429283744616152566)
XLA Ops:
  1.3 2.5 %prep.1 = (bf16[2,2,32,832]{3,2,1,0:T(8,128)(2,1)}, bf16[2,2,32,832]{3,2,1,0:T(8,128)(2,1)}, f32[64,32]{1,0:T(8,128)}, f32[64,32]{1,0:T(8,128)}) custom-call(s32[5]{0:T(128)} %stack.20.place, bf16[832,128]{1,0:T(8,128)(2,1)} %bitcast.26, bf16[832,128]{1,0:T(8,128)(2,1)} %bitcast.27, f32[832]{0:T(1024)} %gate_scale.3, f32[832]{0:T(1024)} %up_scale.3, ...), custom_call_target="tpu_custom_call" | custom-call | flops 14000000 | bytes 1200000 | tf_op jit(solution)/shard_map/prep/pallas_call | solution.py:70
  3.8 3.3 %collective-permute-start.2 = (bf16[2,2,32,832]{3,2,1,0:T(8,128)(2,1)}, bf16[2,2,32,832]{3,2,1,0:T(8,128)(2,1)}, u32[]{:S(2)}, u32[]{:S(2)}) collective-permute-start(bf16[2,2,32,832]{3,2,1,0:T(8,128)(2,1)} %get-tuple-element.28.r0), channel_id=1, source_target_pairs={{0,128},{64,192},{128,0},{192,64},{1,129},{65,193},{129,1},{193,65... | collective-permute-start | bytes 638984 | tf_op jit(solution)/shard_map/ppermute | solution.py:21
  7.2 1.9 %collective-permute-start.3 = (bf16[2,2,32,832]{3,2,1,0:T(8,128)(2,1)}, bf16[2,2,32,832]{3,2,1,0:T(8,128)(2,1)}, u32[]{:S(2)}, u32[]{:S(2)}) collective-permute-start(bf16[2,2,32,832]{3,2,1,0:T(8,128)(2,1)} %get-tuple-element.28.r0), channel_id=1, source_target_pairs={{0,64},{64,0},{128,192},{192,128},{1,65},{65,1},{129,193},{193,129... | collective-permute-start | bytes 638984 | tf_op jit(solution)/shard_map/ppermute | solution.py:21
  9.1 1.3 %collective-permute-start.4 = (bf16[2,2,32,832]{3,2,1,0:T(8,128)(2,1)}, bf16[2,2,32,832]{3,2,1,0:T(8,128)(2,1)}, u32[]{:S(2)}, u32[]{:S(2)}) collective-permute-start(bf16[2,2,32,832]{3,2,1,0:T(8,128)(2,1)} %get-tuple-element.28.r0), channel_id=1, source_target_pairs={{64,128},{128,64},{65,129},{129,65},{66,130},{130,66},{67,131},{13... | collective-permute-start | bytes 638984 | tf_op jit(solution)/shard_map/ppermute | solution.py:179
  12.1 4.5 %collective-permute-start.1 = (bf16[8,2304]{1,0:T(8,128)(2,1)S(1)}, bf16[8,2304]{1,0:T(8,128)(2,1)S(1)}, u32[]{:S(2)}, u32[]{:S(2)}) collective-permute-start(bf16[8,2304]{1,0:T(8,128)(2,1)S(1)} %pad_maximum_fusion.3), channel_id=1, source_target_pairs={{0,8},{8,0},{1,9},{9,1},{2,10},{10,2},{3,11},{11,3},{4,12},{12,4},... | collective-permute-start | bytes 110600 | tf_op jit(solution)/shard_map/ppermute | solution.py:21
  16.5 1.5 %convert_bitcast_fusion.1 = bf16[16,2048]{1,0:T(8,128)(2,1)} fusion(f32[2048,16]{0,1:T(8,128)} %param.20), kind=kLoop, calls=%fused_computation.29 | loop fusion | flops 32768 | bytes 196608 | tf_op jit(solution)/shard_map/transpose | solution.py:194
  18.2 6.8 %collective-permute-done.1 = bf16[8,2304]{1,0:T(8,128)(2,1)S(1)} collective-permute-done((bf16[8,2304]{1,0:T(8,128)(2,1)S(1)}, bf16[8,2304]{1,0:T(8,128)(2,1)S(1)}, u32[]{:S(2)}, u32[]{:S(2)}) %collective-permute-start.1) | collective-permute-done | bytes 36896 | tf_op jit(solution)/shard_map/ppermute | solution.py:21
  25.8 2.8 %collective-permute-start.10 = (bf16[16,2304]{1,0:T(8,128)(2,1)S(1)}, bf16[16,2304]{1,0:T(8,128)(2,1)S(1)}, u32[]{:S(2)}, u32[]{:S(2)}) collective-permute-start(bf16[16,2304]{1,0:T(8,128)(2,1)S(1)} %fusion.8), channel_id=1, source_target_pairs={{0,48},{16,32},{32,16},{48,0},{1,49},{17,33},{33,17},{49,1},{2,50}... | collective-permute-start | bytes 221192 | tf_op jit(solution)/shard_map/ppermute | solution.py:21
  30.9 1.9 %collective-permute-start.6 = (bf16[2,2,32,832]{3,2,1,0:T(8,128)(2,1)}, bf16[2,2,32,832]{3,2,1,0:T(8,128)(2,1)S(1)}, u32[]{:S(2)}, u32[]{:S(2)}) collective-permute-start(bf16[2,2,32,832]{3,2,1,0:T(8,128)(2,1)} %get-tuple-element.29.r0), channel_id=1, source_target_pairs={{0,128},{64,192},{128,0},{192,64},{1,129},{65,193},{129,1},{193,65... | collective-permute-start | bytes 638984 | tf_op jit(solution)/shard_map/ppermute | solution.py:21
  34.5 1.3 %collective-permute-start.11 = (bf16[2,2,32,832]{3,2,1,0:T(8,128)(2,1)}, bf16[2,2,32,832]{3,2,1,0:T(8,128)(2,1)S(1)}, u32[]{:S(2)}, u32[]{:S(2)}) collective-permute-start(bf16[2,2,32,832]{3,2,1,0:T(8,128)(2,1)} %collective-permute-done.2.r2), channel_id=1, source_target_pairs={{64,0},{128,192},{65,1},{129,193},{66,2},{130,194},{67,3},{131,195... | collective-permute-start | bytes 638984 | tf_op jit(solution)/shard_map/ppermute | solution.py:184
  35.9 7.3 %collective-permute-done.6.r2 = bf16[2,2,32,832]{3,2,1,0:T(8,128)(2,1)S(1)} collective-permute-done((bf16[2,2,32,832]{3,2,1,0:T(8,128)(2,1)}, bf16[2,2,32,832]{3,2,1,0:T(8,128)(2,1)S(1)}, u32[]{:S(2)}, u32[]{:S(2)}) %collective-permute-start.6) | collective-permute-done | bytes 213024 | tf_op jit(solution)/shard_map/ppermute | solution.py:21
  43.3 2.4 %collective-permute-done.5.r1 = bf16[2,2,32,832]{3,2,1,0:T(8,128)(2,1)S(1)} collective-permute-done((bf16[2,2,32,832]{3,2,1,0:T(8,128)(2,1)}, bf16[2,2,32,832]{3,2,1,0:T(8,128)(2,1)S(1)}, u32[]{:S(2)}, u32[]{:S(2)}) %collective-permute-start.5) | collective-permute-done | bytes 213024 | tf_op jit(solution)/shard_map/ppermute | solution.py:21
  45.7 3.4 %collective-permute-done.11.r3b = bf16[2,2,32,832]{3,2,1,0:T(8,128)(2,1)S(1)} collective-permute-done((bf16[2,2,32,832]{3,2,1,0:T(8,128)(2,1)}, bf16[2,2,32,832]{3,2,1,0:T(8,128)(2,1)S(1)}, u32[]{:S(2)}, u32[]{:S(2)}) %collective-permute-start.11) | collective-permute-done | bytes 213024 | tf_op jit(solution)/shard_map/ppermute | solution.py:184
  49.1 1.3 %collective-permute-start.12 = (bf16[2,2,32,832]{3,2,1,0:T(8,128)(2,1)S(1)}, bf16[2,2,32,832]{3,2,1,0:T(8,128)(2,1)S(1)}, u32[]{:S(2)}, u32[]{:S(2)}) collective-permute-start(bf16[2,2,32,832]{3,2,1,0:T(8,128)(2,1)S(1)} %collective-permute-done.6.r2), channel_id=1, source_target_pairs={{64,0},{128,192},{65,1},{129,193},{66,2},{130,194},{67,3},{131,195... | collective-permute-start | bytes 638984 | tf_op jit(solution)/shard_map/ppermute | solution.py:184
  51.2 1.5 %convert.20 = bf16[2048,16]{0,1:T(8,128)(2,1)} convert(f32[2048,16]{0,1:T(8,128)} %param.20) | non-fusion elementwise | flops 32768 | bytes 196608 | tf_op jit(solution)/shard_map/convert.10
  52.8 1.5 %convert.19 = bf16[2048,16]{0,1:T(8,128)(2,1)} convert(f32[2048,16]{0,1:T(8,128)} %param.18) | non-fusion elementwise | flops 32768 | bytes 196608 | tf_op jit(solution)/shard_map/convert.9
  54.3 1.6 %collective-permute-start.18 = (bf16[64,2304]{1,0:T(8,128)(2,1)S(1)}, bf16[64,2304]{1,0:T(8,128)(2,1)S(1)}, u32[]{:S(2)}, u32[]{:S(2)}) collective-permute-start(bf16[64,2304]{1,0:T(8,128)(2,1)S(1)} %fusion.3), channel_id=1, source_target_pairs={{0,6},{2,4},{4,2},{6,0},{1,7},{3,5},{5,3},{7,1},{8,14},{10,12},{12... | collective-permute-start | bytes 884744 | tf_op jit(solution)/shard_map/ppermute | solution.py:21
  56.6 1.8 %collective-permute-start.16 = (bf16[64,2304]{1,0:T(8,128)(2,1)S(1)}, bf16[64,2304]{1,0:T(8,128)(2,1)S(1)}, u32[]{:S(2)}, u32[]{:S(2)}) collective-permute-start(bf16[64,2304]{1,0:T(8,128)(2,1)S(1)} %fusion.3), channel_id=1, source_target_pairs={{0,2},{2,0},{4,6},{6,4},{1,3},{3,1},{5,7},{7,5},{8,10},{10,8},{12,... | collective-permute-start | bytes 884744 | tf_op jit(solution)/shard_map/ppermute | solution.py:21
  59.1 2.0 %copy-done.1 = bf16[2048,832]{0,1:T(8,128)(2,1)S(1)} copy-done((bf16[2048,832]{0,1:T(8,128)(2,1)S(1)}, bf16[2048,832]{0,1:T(8,128)(2,1)}, u32[]{:S(2)}) %copy-start.1) | copy-done | bytes 3407896
  61.1 6.5 %product.3 = (bf16[128,2048]{1,0:T(8,128)(2,1)}, bf16[128,2048]{1,0:T(8,128)(2,1)S(1)}, bf16[2,2,4,32,832]{4,3,2,1,0:T(8,128)(2,1)S(1)}) custom-call(s32[1]{0:T(128)} %bitcast.place, bf16[2,2,32,832]{3,2,1,0:T(8,128)(2,1)S(1)} %copy-done.12, bf16[2,2,32,832]{3,2,1,0:T(8,128)(2,1)} %collective-permute-done.3.r1, ...), custom_call_target="tpu_custom_call" | custom-call | flops 1750000000 | bytes 9700000 | tf_op jit(solution)/shard_map/product/pallas_call | solution.py:99
  68.6 5.3 %product.2 = (bf16[128,2048]{1,0:T(8,128)(2,1)}, bf16[128,2048]{1,0:T(8,128)(2,1)S(1)}, bf16[2,2,4,32,832]{4,3,2,1,0:T(8,128)(2,1)S(1)}) custom-call(s32[1]{0:T(128)} %bitcast.place, bf16[2,2,32,832]{3,2,1,0:T(8,128)(2,1)S(1)} %copy-done.11, bf16[2,2,32,832]{3,2,1,0:T(8,128)(2,1)S(1)} %collective-permute-done.5.r1, ...), custom_call_target="tpu_custom_call" | custom-call | flops 1750000000 | bytes 9700000 | tf_op jit(solution)/shard_map/product/pallas_call | solution.py:99
  83.0 2.6 %collective-permute-start.19 = (bf16[320,32]{1,0:T(8,128)(2,1)}, bf16[320,32]{1,0:T(8,128)(2,1)}, u32[]{:S(2)}, u32[]{:S(2)}) collective-permute-start(bf16[320,32]{1,0:T(8,128)(2,1)} %pad_maximum_fusion.2.p0), channel_id=1, source_target_pairs={{0,64},{64,0},{128,192},{192,128},{1,65},{65,1},{129,193},{193,129... | collective-permute-start | bytes 61448 | tf_op jit(solution)/shard_map/ppermute | solution.py:21
  85.7 2.4 %collective-permute-start.21 = (bf16[320,32]{1,0:T(8,128)(2,1)}, bf16[320,32]{1,0:T(8,128)(2,1)}, u32[]{:S(2)}, u32[]{:S(2)}) collective-permute-start(bf16[320,32]{1,0:T(8,128)(2,1)} %pad_maximum_fusion.2.p0), channel_id=1, source_target_pairs={{0,192},{64,128},{128,64},{192,0},{1,193},{65,129},{129,65},{193,1... | collective-permute-start | bytes 61448 | tf_op jit(solution)/shard_map/ppermute | solution.py:21
  88.0 2.0 %fusion.2 = bf16[16,8,2048]{2,1,0:T(8,128)(2,1)} fusion(bf16[128,2048]{1,0:T(8,128)(2,1)} %collective-permute-done.14, bf16[128,2048]{1,0:T(8,128)(2,1)S(1)} %copy-done.10), kind=kLoop, calls=%fused_computation.8 | loop fusion | flops 1048576 | bytes 1572864 | tf_op jit(solution)/shard_map/all_to_all | solution.py:240
  90.0 7.4 %all-to-all-start.1 = ((bf16[16,8,2048]{2,1,0:T(8,128)(2,1)}), bf16[16,8,2048]{2,1,0:T(8,128)(2,1)}, u32[]{:S(2)}, u32[]{:S(2)}) async-start(bf16[16,8,2048]{2,1,0:T(8,128)(2,1)} %fusion.2), calls=%async_computation.1 | async-start | bytes 1048576 | tf_op jit(solution)/shard_map/all_to_all | solution.py:240
  97.5 2.4 %joined.1 = (bf16[256,32]{1,0:T(8,128)(2,1)S(1)}, f32[8,2048]{1,0:T(8,128)S(1)}, f32[32,2048]{1,0:T(8,128)}) custom-call(s32[5]{0:T(128)S(1)} %copy-done.19, bf16[320,32]{1,0:T(8,128)(2,1)} %pad_maximum_fusion.2.p0, bf16[320,32]{1,0:T(8,128)(2,1)} %collective-permute-done.19.p1, bf16[320,32]{1,0:T(8,128)(2,1)} %collective-permute-done.20.p2, ...), custom_call_target="tpu_custom_call" | custom-call | flops 40000000 | bytes 1700000 | tf_op jit(solution)/shard_map/joined/pallas_call | solution.py:132
  101.2 2.0 %fusion.1 = bf16[16,8,2048]{2,1,0:T(8,128)(2,1)} fusion(bf16[128,2048]{1,0:T(8,128)(2,1)} %collective-permute-done.13, bf16[128,2048]{1,0:T(8,128)(2,1)S(1)} %copy-done.8), kind=kLoop, calls=%fused_computation.7 | loop fusion | flops 1048576 | bytes 1572864 | tf_op jit(solution)/shard_map/all_to_all | solution.py:240
  103.2 4.1 %all-to-all-done.1 = bf16[16,8,2048]{2,1,0:T(8,128)(2,1)} async-done(((bf16[16,8,2048]{2,1,0:T(8,128)(2,1)}), bf16[16,8,2048]{2,1,0:T(8,128)(2,1)}, u32[]{:S(2)}, u32[]{:S(2)}) %all-to-all-start.1) | async-done | bytes 524320 | tf_op jit(solution)/shard_map/all_to_all | solution.py:240
  107.3 4.9 %all-to-all-start = ((bf16[16,8,2048]{2,1,0:T(8,128)(2,1)}), bf16[16,8,2048]{2,1,0:T(8,128)(2,1)S(1)}, u32[]{:S(2)}, u32[]{:S(2)}) async-start(bf16[16,8,2048]{2,1,0:T(8,128)(2,1)} %fusion.1), calls=%async_computation | async-start | bytes 1048576 | tf_op jit(solution)/shard_map/all_to_all | solution.py:240
  113.5 1.8 %expander.1 = (f32[16,832]{1,0:T(8,128)}, f32[16,832]{1,0:T(8,128)}) custom-call(s32[5]{0:T(128)S(1)} %copy-done.19, bf16[256,32]{1,0:T(8,128)(2,1)S(1)} %collective-permute-done.23.low_other, bf16[256,32]{1,0:T(8,128)(2,1)S(1)} %copy-done.16, bf16[2,2,4,32,832]{4,3,2,1,0:T(8,128)(2,1)S(1)} %copy-done.4, bf16[2,2,4,32,832]{4,3,2,1,0:T(8,128)(2,1)S(1)} %copy-done.6, ...), custom_call_target="tpu_custom_call" | custom-call | flops 55000000 | bytes 2000000 | tf_op jit(solution)/shard_map/expander/pallas_call | solution.py:167
  118.1 3.5 %collective-permute-start.15 = (bf16[8,2048]{1,0:T(8,128)(2,1)S(1)}, bf16[8,2048]{1,0:T(8,128)(2,1)S(1)}, u32[]{:S(2)}, u32[]{:S(2)}) collective-permute-start(bf16[8,2048]{1,0:T(8,128)(2,1)S(1)} %reduce_sum.22), channel_id=1, source_target_pairs={{0,8},{8,0},{1,9},{9,1},{2,10},{10,2},{3,11},{11,3},{4,12},{12,4},... | collective-permute-start | bytes 98312 | tf_op jit(solution)/shard_map/ppermute | solution.py:21
  121.7 4.3 %collective-permute-done.15 = bf16[8,2048]{1,0:T(8,128)(2,1)S(1)} collective-permute-done((bf16[8,2048]{1,0:T(8,128)(2,1)S(1)}, bf16[8,2048]{1,0:T(8,128)(2,1)S(1)}, u32[]{:S(2)}, u32[]{:S(2)}) %collective-permute-start.15) | collective-permute-done | bytes 32800 | tf_op jit(solution)/shard_map/ppermute | solution.py:21
  (114 shorter events, 25.7 us)
Async XLA Ops:
  0.6 58.5 %copy-start = (bf16[2048,832]{0,1:T(8,128)(2,1)S(1)}, bf16[2048,832]{0,1:T(8,128)(2,1)}, u32[]{:S(2)}) copy-start(bf16[2048,832]{0,1:T(8,128)(2,1)} %param.14) | copy-start | bytes 10223620
  3.8 6.6 %collective-permute-start = (f32[64,32]{1,0:T(8,128)}, f32[64,32]{1,0:T(8,128)S(1)}, u32[]{:S(2)}, u32[]{:S(2)}) collective-permute-start(f32[64,32]{1,0:T(8,128)} %get-tuple-element.27), channel_id=1, source_target_pairs={{0,1},{1,0},{2,3},{3,2},{4,5},{5,4},{6,7},{7,6},{8,9},{9,8},{10,11... | collective-permute-start | bytes 24584 | tf_op jit(solution)/shard_map/ppermute | solution.py:21
  3.8 22.0 %collective-permute-start.2 = (bf16[2,2,32,832]{3,2,1,0:T(8,128)(2,1)}, bf16[2,2,32,832]{3,2,1,0:T(8,128)(2,1)}, u32[]{:S(2)}, u32[]{:S(2)}) collective-permute-start(bf16[2,2,32,832]{3,2,1,0:T(8,128)(2,1)} %get-tuple-element.28.r0), channel_id=1, source_target_pairs={{0,128},{64,192},{128,0},{192,64},{1,129},{65,193},{129,1},{193,65... | collective-permute-start | bytes 638984 | tf_op jit(solution)/shard_map/ppermute | solution.py:21
  7.2 18.6 %collective-permute-start.3 = (bf16[2,2,32,832]{3,2,1,0:T(8,128)(2,1)}, bf16[2,2,32,832]{3,2,1,0:T(8,128)(2,1)}, u32[]{:S(2)}, u32[]{:S(2)}) collective-permute-start(bf16[2,2,32,832]{3,2,1,0:T(8,128)(2,1)} %get-tuple-element.28.r0), channel_id=1, source_target_pairs={{0,64},{64,0},{128,192},{192,128},{1,65},{65,1},{129,193},{193,129... | collective-permute-start | bytes 638984 | tf_op jit(solution)/shard_map/ppermute | solution.py:21
  9.1 16.7 %collective-permute-start.4 = (bf16[2,2,32,832]{3,2,1,0:T(8,128)(2,1)}, bf16[2,2,32,832]{3,2,1,0:T(8,128)(2,1)}, u32[]{:S(2)}, u32[]{:S(2)}) collective-permute-start(bf16[2,2,32,832]{3,2,1,0:T(8,128)(2,1)} %get-tuple-element.28.r0), channel_id=1, source_target_pairs={{64,128},{128,64},{65,129},{129,65},{66,130},{130,66},{67,131},{13... | collective-permute-start | bytes 638984 | tf_op jit(solution)/shard_map/ppermute | solution.py:179
  12.1 12.9 %collective-permute-start.1 = (bf16[8,2304]{1,0:T(8,128)(2,1)S(1)}, bf16[8,2304]{1,0:T(8,128)(2,1)S(1)}, u32[]{:S(2)}, u32[]{:S(2)}) collective-permute-start(bf16[8,2304]{1,0:T(8,128)(2,1)S(1)} %pad_maximum_fusion.3), channel_id=1, source_target_pairs={{0,8},{8,0},{1,9},{9,1},{2,10},{10,2},{3,11},{11,3},{4,12},{12,4},... | collective-permute-start | bytes 110600 | tf_op jit(solution)/shard_map/ppermute | solution.py:21
  25.0 34.2 %copy-start.12 = (bf16[2,2,32,832]{3,2,1,0:T(8,128)(2,1)S(1)}, bf16[2,2,32,832]{3,2,1,0:T(8,128)(2,1)}, u32[]{:S(2)}) copy-start(bf16[2,2,32,832]{3,2,1,0:T(8,128)(2,1)} %get-tuple-element.28.r0) | copy-start | bytes 638980
  25.8 8.0 %collective-permute-start.10 = (bf16[16,2304]{1,0:T(8,128)(2,1)S(1)}, bf16[16,2304]{1,0:T(8,128)(2,1)S(1)}, u32[]{:S(2)}, u32[]{:S(2)}) collective-permute-start(bf16[16,2304]{1,0:T(8,128)(2,1)S(1)} %fusion.8), channel_id=1, source_target_pairs={{0,48},{16,32},{32,16},{48,0},{1,49},{17,33},{33,17},{49,1},{2,50}... | collective-permute-start | bytes 221192 | tf_op jit(solution)/shard_map/ppermute | solution.py:21
  28.6 5.9 %collective-permute-start.9 = (bf16[16,2304]{1,0:T(8,128)(2,1)S(1)}, bf16[16,2304]{1,0:T(8,128)(2,1)S(1)}, u32[]{:S(2)}, u32[]{:S(2)}) collective-permute-start(bf16[16,2304]{1,0:T(8,128)(2,1)S(1)} %fusion.8), channel_id=1, source_target_pairs={{0,32},{16,48},{32,0},{48,16},{1,33},{17,49},{33,1},{49,17},{2,34}... | collective-permute-start | bytes 221192 | tf_op jit(solution)/shard_map/ppermute | solution.py:21
  29.5 6.4 %collective-permute-start.8 = (bf16[16,2304]{1,0:T(8,128)(2,1)S(1)}, bf16[16,2304]{1,0:T(8,128)(2,1)S(1)}, u32[]{:S(2)}, u32[]{:S(2)}) collective-permute-start(bf16[16,2304]{1,0:T(8,128)(2,1)S(1)} %fusion.8), channel_id=1, source_target_pairs={{0,16},{16,0},{32,48},{48,32},{1,17},{17,1},{33,49},{49,33},{2,18}... | collective-permute-start | bytes 221192 | tf_op jit(solution)/shard_map/ppermute | solution.py:21
  30.9 12.4 %collective-permute-start.6 = (bf16[2,2,32,832]{3,2,1,0:T(8,128)(2,1)}, bf16[2,2,32,832]{3,2,1,0:T(8,128)(2,1)S(1)}, u32[]{:S(2)}, u32[]{:S(2)}) collective-permute-start(bf16[2,2,32,832]{3,2,1,0:T(8,128)(2,1)} %get-tuple-element.29.r0), channel_id=1, source_target_pairs={{0,128},{64,192},{128,0},{192,64},{1,129},{65,193},{129,1},{193,65... | collective-permute-start | bytes 638984 | tf_op jit(solution)/shard_map/ppermute | solution.py:21
  32.8 12.8 %collective-permute-start.5 = (bf16[2,2,32,832]{3,2,1,0:T(8,128)(2,1)}, bf16[2,2,32,832]{3,2,1,0:T(8,128)(2,1)S(1)}, u32[]{:S(2)}, u32[]{:S(2)}) collective-permute-start(bf16[2,2,32,832]{3,2,1,0:T(8,128)(2,1)} %get-tuple-element.29.r0), channel_id=1, source_target_pairs={{0,64},{64,0},{128,192},{192,128},{1,65},{65,1},{129,193},{193,129... | collective-permute-start | bytes 638984 | tf_op jit(solution)/shard_map/ppermute | solution.py:21
  33.8 11.8 %collective-permute-start.7 = (bf16[2,2,32,832]{3,2,1,0:T(8,128)(2,1)}, bf16[2,2,32,832]{3,2,1,0:T(8,128)(2,1)S(1)}, u32[]{:S(2)}, u32[]{:S(2)}) collective-permute-start(bf16[2,2,32,832]{3,2,1,0:T(8,128)(2,1)} %get-tuple-element.29.r0), channel_id=1, source_target_pairs={{64,128},{128,64},{65,129},{129,65},{66,130},{130,66},{67,131},{13... | collective-permute-start | bytes 638984 | tf_op jit(solution)/shard_map/ppermute | solution.py:179
  34.5 14.5 %collective-permute-start.11 = (bf16[2,2,32,832]{3,2,1,0:T(8,128)(2,1)}, bf16[2,2,32,832]{3,2,1,0:T(8,128)(2,1)S(1)}, u32[]{:S(2)}, u32[]{:S(2)}) collective-permute-start(bf16[2,2,32,832]{3,2,1,0:T(8,128)(2,1)} %collective-permute-done.2.r2), channel_id=1, source_target_pairs={{64,0},{128,192},{65,1},{129,193},{66,2},{130,194},{67,3},{131,195... | collective-permute-start | bytes 638984 | tf_op jit(solution)/shard_map/ppermute | solution.py:184
  49.1 19.5 %collective-permute-start.12 = (bf16[2,2,32,832]{3,2,1,0:T(8,128)(2,1)S(1)}, bf16[2,2,32,832]{3,2,1,0:T(8,128)(2,1)S(1)}, u32[]{:S(2)}, u32[]{:S(2)}) collective-permute-start(bf16[2,2,32,832]{3,2,1,0:T(8,128)(2,1)S(1)} %collective-permute-done.6.r2), channel_id=1, source_target_pairs={{64,0},{128,192},{65,1},{129,193},{66,2},{130,194},{67,3},{131,195... | collective-permute-start | bytes 638984 | tf_op jit(solution)/shard_map/ppermute | solution.py:184
  54.3 21.8 %collective-permute-start.18 = (bf16[64,2304]{1,0:T(8,128)(2,1)S(1)}, bf16[64,2304]{1,0:T(8,128)(2,1)S(1)}, u32[]{:S(2)}, u32[]{:S(2)}) collective-permute-start(bf16[64,2304]{1,0:T(8,128)(2,1)S(1)} %fusion.3), channel_id=1, source_target_pairs={{0,6},{2,4},{4,2},{6,0},{1,7},{3,5},{5,3},{7,1},{8,14},{10,12},{12... | collective-permute-start | bytes 884744 | tf_op jit(solution)/shard_map/ppermute | solution.py:21
  55.9 20.2 %collective-permute-start.17 = (bf16[64,2304]{1,0:T(8,128)(2,1)S(1)}, bf16[64,2304]{1,0:T(8,128)(2,1)S(1)}, u32[]{:S(2)}, u32[]{:S(2)}) collective-permute-start(bf16[64,2304]{1,0:T(8,128)(2,1)S(1)} %fusion.3), channel_id=1, source_target_pairs={{0,4},{2,6},{4,0},{6,2},{1,5},{3,7},{5,1},{7,3},{8,12},{10,14},{12... | collective-permute-start | bytes 884744 | tf_op jit(solution)/shard_map/ppermute | solution.py:21
  56.6 19.5 %collective-permute-start.16 = (bf16[64,2304]{1,0:T(8,128)(2,1)S(1)}, bf16[64,2304]{1,0:T(8,128)(2,1)S(1)}, u32[]{:S(2)}, u32[]{:S(2)}) collective-permute-start(bf16[64,2304]{1,0:T(8,128)(2,1)S(1)} %fusion.3), channel_id=1, source_target_pairs={{0,2},{2,0},{4,6},{6,4},{1,3},{3,1},{5,7},{7,5},{8,10},{10,8},{12,... | collective-permute-start | bytes 884744 | tf_op jit(solution)/shard_map/ppermute | solution.py:21
  68.5 19.5 %collective-permute-start.14 = (bf16[128,2048]{1,0:T(8,128)(2,1)}, bf16[128,2048]{1,0:T(8,128)(2,1)}, u32[]{:S(2)}, u32[]{:S(2)}) collective-permute-start(bf16[128,2048]{1,0:T(8,128)(2,1)} %get-tuple-element.36), channel_id=1, source_target_pairs={{0,1},{1,0},{2,3},{3,2},{4,5},{5,4},{6,7},{7,6},{8,9},{9,8},{10,11... | collective-permute-start | bytes 1572872 | tf_op jit(solution)/shard_map/ppermute | solution.py:21
  75.6 25.5 %collective-permute-start.13 = (bf16[128,2048]{1,0:T(8,128)(2,1)}, bf16[128,2048]{1,0:T(8,128)(2,1)}, u32[]{:S(2)}, u32[]{:S(2)}) collective-permute-start(bf16[128,2048]{1,0:T(8,128)(2,1)} %get-tuple-element.34), channel_id=1, source_target_pairs={{0,1},{1,0},{2,3},{3,2},{4,5},{5,4},{6,7},{7,6},{8,9},{9,8},{10,11... | collective-permute-start | bytes 1572872 | tf_op jit(solution)/shard_map/ppermute | solution.py:21
  83.0 18.2 %copy-start.8 = (bf16[128,2048]{1,0:T(8,128)(2,1)S(1)}, bf16[128,2048]{1,0:T(8,128)(2,1)}, u32[]{:S(2)}) copy-start(bf16[128,2048]{1,0:T(8,128)(2,1)} %copy-done.7) | copy-start | bytes 1572868
  83.0 14.4 %collective-permute-start.19 = (bf16[320,32]{1,0:T(8,128)(2,1)}, bf16[320,32]{1,0:T(8,128)(2,1)}, u32[]{:S(2)}, u32[]{:S(2)}) collective-permute-start(bf16[320,32]{1,0:T(8,128)(2,1)} %pad_maximum_fusion.2.p0), channel_id=1, source_target_pairs={{0,64},{64,0},{128,192},{192,128},{1,65},{65,1},{129,193},{193,129... | collective-permute-start | bytes 61448 | tf_op jit(solution)/shard_map/ppermute | solution.py:21
  85.7 11.8 %collective-permute-start.20 = (bf16[320,32]{1,0:T(8,128)(2,1)}, bf16[320,32]{1,0:T(8,128)(2,1)}, u32[]{:S(2)}, u32[]{:S(2)}) collective-permute-start(bf16[320,32]{1,0:T(8,128)(2,1)} %pad_maximum_fusion.2.p0), channel_id=1, source_target_pairs={{0,128},{64,192},{128,0},{192,64},{1,129},{65,193},{129,1},{193,65... | collective-permute-start | bytes 61448 | tf_op jit(solution)/shard_map/ppermute | solution.py:21
  85.7 11.8 %collective-permute-start.21 = (bf16[320,32]{1,0:T(8,128)(2,1)}, bf16[320,32]{1,0:T(8,128)(2,1)}, u32[]{:S(2)}, u32[]{:S(2)}) collective-permute-start(bf16[320,32]{1,0:T(8,128)(2,1)} %pad_maximum_fusion.2.p0), channel_id=1, source_target_pairs={{0,192},{64,128},{128,64},{192,0},{1,193},{65,129},{129,65},{193,1... | collective-permute-start | bytes 61448 | tf_op jit(solution)/shard_map/ppermute | solution.py:21
  90.0 17.3 %all-to-all-start.1 = ((bf16[16,8,2048]{2,1,0:T(8,128)(2,1)}), bf16[16,8,2048]{2,1,0:T(8,128)(2,1)}, u32[]{:S(2)}, u32[]{:S(2)}) async-start(bf16[16,8,2048]{2,1,0:T(8,128)(2,1)} %fusion.2), calls=%async_computation.1 | async-start | bytes 1048576 | tf_op jit(solution)/shard_map/all_to_all | solution.py:240
  97.4 16.1 %copy-start.4 = (bf16[2,2,4,32,832]{4,3,2,1,0:T(8,128)(2,1)S(1)}, bf16[2,2,4,32,832]{4,3,2,1,0:T(8,128)(2,1)}, u32[]{:S(2)}) copy-start(bf16[2,2,4,32,832]{4,3,2,1,0:T(8,128)(2,1)} %copy-done.3) | copy-start | bytes 2555908
  97.4 16.1 %copy-start.6 = (bf16[2,2,4,32,832]{4,3,2,1,0:T(8,128)(2,1)S(1)}, bf16[2,2,4,32,832]{4,3,2,1,0:T(8,128)(2,1)}, u32[]{:S(2)}) copy-start(bf16[2,2,4,32,832]{4,3,2,1,0:T(8,128)(2,1)} %copy-done.5) | copy-start | bytes 2555908
  97.4 16.1 %copy-start.17 = (f32[832]{0:T(1024)S(1)}, f32[832]{0:T(1024)}, u32[]{:S(2)}) copy-start(f32[832]{0:T(1024)} %gate_scale.3) | copy-start | bytes 9988
  101.2 14.1 %collective-permute-start.22 = (f32[32,2048]{1,0:T(8,128)}, f32[32,2048]{1,0:T(8,128)S(1)}, u32[]{:S(2)}, u32[]{:S(2)}) collective-permute-start(f32[32,2048]{1,0:T(8,128)} %get-tuple-element.39), channel_id=1, source_target_pairs={{0,1},{1,0},{2,3},{3,2},{4,5},{5,4},{6,7},{7,6},{8,9},{9,8},{10,11... | collective-permute-start | bytes 786440 | tf_op jit(solution)/shard_map/ppermute | solution.py:21
  107.3 14.3 %all-to-all-start = ((bf16[16,8,2048]{2,1,0:T(8,128)(2,1)}), bf16[16,8,2048]{2,1,0:T(8,128)(2,1)S(1)}, u32[]{:S(2)}, u32[]{:S(2)}) async-start(bf16[16,8,2048]{2,1,0:T(8,128)(2,1)} %fusion.1), calls=%async_computation | async-start | bytes 1048576 | tf_op jit(solution)/shard_map/all_to_all | solution.py:240
  112.1 1.3 %collective-permute-start.23 = (bf16[256,32]{1,0:T(8,128)(2,1)S(1)}, bf16[256,32]{1,0:T(8,128)(2,1)S(1)}, u32[]{:S(2)}, u32[]{:S(2)}) collective-permute-start(bf16[256,32]{1,0:T(8,128)(2,1)S(1)} %copy-done.16), channel_id=1, source_target_pairs={{0,1},{1,0},{2,3},{3,2},{4,5},{5,4},{6,7},{7,6},{8,9},{9,8},{10,11... | collective-permute-start | bytes 49160 | tf_op jit(solution)/shard_map/ppermute | solution.py:21
  118.1 7.9 %collective-permute-start.15 = (bf16[8,2048]{1,0:T(8,128)(2,1)S(1)}, bf16[8,2048]{1,0:T(8,128)(2,1)S(1)}, u32[]{:S(2)}, u32[]{:S(2)}) collective-permute-start(bf16[8,2048]{1,0:T(8,128)(2,1)S(1)} %reduce_sum.22), channel_id=1, source_target_pairs={{0,8},{8,0},{1,9},{9,1},{2,10},{10,2},{3,11},{11,3},{4,12},{12,4},... | collective-permute-start | bytes 98312 | tf_op jit(solution)/shard_map/ppermute | solution.py:21
  (19 other events, 104.4 us)

commit v4 on v3

v4 whole, which is shorter than its diff:
```python
import functools

import jax
import jax.numpy as jnp
from jax import lax
from jax.experimental import pallas as pl
from jax.experimental.pallas import tpu as pltpu
from jax.sharding import Mesh, PartitionSpec as P

ADAPTER_SCALE = 2.0
FFN = ("x", "zh", "y", "core")
F32, BF16 = jnp.float32, jnp.bfloat16
UNITS, FEATS, STEP = 832, 2048, 256
PLAIN = (((1,), (0,)), ((), ()))
BY_ROWS = (((1,), (1,)), ((), ()))
BY_COLUMNS = (((0,), (0,)), ((), ()))
SMEM = pl.BlockSpec(memory_space=pltpu.SMEM)
VMEM = pl.BlockSpec(memory_space=pltpu.VMEM)


def swap(value, axis, mask):
    size = lax.axis_size(axis)
    return lax.ppermute(value, axis, [(i, i ^ mask) for i in range(size)])


def gather_over(value, axis):
    return [value] + [swap(value, axis, k) for k in range(1, lax.axis_size(axis))]


def after(values, others):
    return lax.optimization_barrier((values, others))[0]


def dot(left, right, how):
    return lax.dot_general(left, right, how, preferred_element_type=F32)


def one_hot(rows, columns, source):
    row = lax.broadcasted_iota(jnp.int32, (rows, columns), 0)
    column = lax.broadcasted_iota(jnp.int32, (rows, columns), 1)
    return (column == source(row)).astype(F32).astype(BF16)


def prep_kernel(place, gate, up, gate_scale, up_scale, gate_lift, up_lift, both, back_other, back_own):
    zh, core = place[0], place[1]

    def source(row):
        half, side = 1 - row // 64, 1 - row // 32 % 2
        return (half ^ zh) * 64 + row // 8 % 4 * 16 + (side ^ core) * 8 + row % 8

    order = one_hot(128, 128, source)
    none = jnp.zeros((16, UNITS), F32)
    lifts = (
        jnp.concatenate([gate_lift[...], none], 0).astype(BF16),
        jnp.concatenate([none, up_lift[...]], 0).astype(BF16),
    )
    back = jnp.zeros((128, 32), F32)
    for k, (grad, scale) in enumerate(((gate, gate_scale), (up, up_scale))):
        rows = dot(order, grad[...], BY_ROWS)
        back += dot(rows.astype(BF16), lifts[k], BY_ROWS)
        rows = (rows * scale[...].reshape(1, UNITS)).astype(BF16).reshape(2, 2, 32, UNITS)
        both[0, k] = rows[0]
        both[1, k] = rows[1]
    back = back.reshape(2, 2, 32, 32)
    back_other[...] = back[:, 0].reshape(64, 32)
    back_own[...] = back[:, 1].reshape(64, 32)


def prep(place, *arrays):
    both = jax.ShapeDtypeStruct((2, 2, 2, 32, UNITS), BF16)
    back = jax.ShapeDtypeStruct((64, 32), F32)
    return pl.pallas_call(
        prep_kernel,
        out_shape=(both, back, back),
        in_specs=[SMEM] + [VMEM] * 6,
        out_specs=(VMEM,) * 3,
        compiler_params=pltpu.CompilerParams(vmem_limit_bytes=6 << 20),
        cost_estimate=pl.CostEstimate(flops=14_000_000, bytes_accessed=1_200_000, transcendentals=0),
        name="prep",
    )(place, *arrays)


def product_kernel(pairs, *refs):
    blocks, (gate_codes, up_codes, other, own, grads) = refs[:-5], refs[-5:]
    count = len(blocks) // pairs
    for k in range(2):
        for c in range(2):
            for half in range(2):
                for j in range(count):
                    value = blocks[j * pairs][half, k, c]
                    if pairs == 2:
                        value += blocks[j * pairs + 1][half, k, c]
                    row = ((c * 2 + half) * count + j) * 32
                    grads[k, row : row + 32] = value
    gate, up, cut = grads[0], grads[1], 64 * count
    for start in range(0, FEATS, STEP):
        columns = slice(start, start + STEP)
        total = dot(gate, gate_codes[:, columns], PLAIN) + dot(up, up_codes[:, columns], PLAIN)
        other[:, columns] = total[:cut].astype(BF16)
        own[:, columns] = total[cut:].astype(BF16)


def product(blocks, pairs, gate_codes, up_codes):
    count = len(blocks) // pairs
    part = jax.ShapeDtypeStruct((64 * count, FEATS), BF16)
    return pl.pallas_call(
        functools.partial(product_kernel, pairs),
        out_shape=(part, part, jax.ShapeDtypeStruct((2, 128 * count, UNITS), BF16)),
        in_specs=[VMEM] * (len(blocks) + 2),
        out_specs=(VMEM,) * 3,
        compiler_params=pltpu.CompilerParams(vmem_limit_bytes=24 << 20),
        cost_estimate=pl.CostEstimate(
            flops=900_000_000 * count, bytes_accessed=8_000_000, transcendentals=0
        ),
        name="product",
    )(*blocks, gate_codes, up_codes)


def pairs_kernel(place, own1, theirs1, own2, theirs2, far, near):
    for half, out in enumerate((far, near)):
        for j in range(4):
            own, theirs, row = (own1, theirs1, (half * 3 + j) * 32) if j < 3 else (own2, theirs2, half * 32)
            rows = slice(row, row + 32)
            total = own[rows].astype(F32) + theirs[rows].astype(F32)
            out[place[2] ^ j] = total.astype(BF16)


def add_pairs(*arrays):
    out = jax.ShapeDtypeStruct((4, 32, FEATS), BF16)
    return pl.pallas_call(
        pairs_kernel,
        out_shape=(out, out),
        in_specs=[SMEM] + [VMEM] * 4,
        out_specs=(VMEM, VMEM),
        compiler_params=pltpu.CompilerParams(vmem_limit_bytes=8 << 20),
        cost_estimate=pl.CostEstimate(flops=600_000, bytes_accessed=3_200_000, transcendentals=0),
        name="add_pairs",
    )(*arrays)


def spread_kernel(inputs, back, arrived, out):
    tokens = jnp.concatenate([inputs[...].astype(F32), arrived[:, :FEATS].astype(F32)], 0)
    theirs = arrived[:, FEATS:].astype(F32)
    back = back[...] + jnp.concatenate([theirs[4:], theirs[:4]], 0)
    back = jnp.concatenate([back, jnp.zeros((8, 256), F32)], 0)
    for i in range(16):
        out[i, :, :FEATS] = tokens.astype(BF16)
        out[i, :, FEATS:] = back.astype(BF16)


def spread(*arrays):
    return pl.pallas_call(
        spread_kernel,
        out_shape=jax.ShapeDtypeStruct((16, 16, FEATS + 256), BF16),
        in_specs=[VMEM] * 3,
        out_specs=VMEM,
        compiler_params=pltpu.CompilerParams(vmem_limit_bytes=6 << 20),
        cost_estimate=pl.CostEstimate(flops=100_000, bytes_accessed=1_300_000, transcendentals=0),
        name="spread",
    )(*arrays)


def narrow_kernel(landed, gate_down, up_down, out):
    down = jnp.concatenate([gate_down[...], up_down[...]], 0).astype(BF16)
    low = dot(down, landed[:, :, :FEATS].reshape(256, FEATS), BY_ROWS)
    back = jnp.zeros((16, 256), F32)
    for i in range(16):
        back += landed[i, :, FEATS:].astype(F32)
    out[...] = jnp.concatenate([low, back], 0).astype(BF16)


def narrow(*arrays):
    return pl.pallas_call(
        narrow_kernel,
        out_shape=jax.ShapeDtypeStruct((48, 256), BF16),
        in_specs=[VMEM] * 3,
        out_specs=VMEM,
        compiler_params=pltpu.CompilerParams(vmem_limit_bytes=8 << 20),
        cost_estimate=pl.CostEstimate(flops=34_000_000, bytes_accessed=1_500_000, transcendentals=0),
        name="narrow",
    )(*arrays)


def joined_kernel(place, p0, p1, p2, p3, landed, gate_down, up_down, low_out, adapter, reducer):
    hid, x, y = place[2], place[3], place[4]
    parts = [part[...].astype(F32) for part in (p0, p1, p2, p3)]
    low_out[...] = sum(part[:32] for part in parts).astype(BF16)
    back = jnp.concatenate(
        [part[32:40, 32 * i : 32 * i + 32] for part in parts for i in range(8)], 0
    ).astype(BF16)

    def source(row):
        return ((row // 64) ^ hid) * 64 + row % 8 * 8 + (1 - row // 8 % 2) * 4 + row // 16 % 4

    mine = dot(one_hot(16, 256, lambda row: source(x * 64 + y * 16 + row)), back, PLAIN)
    back = (ADAPTER_SCALE * dot(one_hot(256, 256, source), back, PLAIN)).astype(BF16)
    down = jnp.concatenate([gate_down[...], up_down[...]], 0).astype(BF16)
    adapter[...] = ADAPTER_SCALE * dot(mine.astype(BF16), down, PLAIN)[:8]
    reducer[...] = dot(back, landed[:, :, :FEATS].reshape(256, FEATS), BY_COLUMNS)


def joined(place, parts, *arrays):
    return pl.pallas_call(
        joined_kernel,
        out_shape=(
            jax.ShapeDtypeStruct((32, 256), BF16),
            jax.ShapeDtypeStruct((8, FEATS), F32),
            jax.ShapeDtypeStruct((32, FEATS), F32),
        ),
        in_specs=[SMEM] + [VMEM] * 7,
        out_specs=(VMEM,) * 3,
        compiler_params=pltpu.CompilerParams(vmem_limit_bytes=8 << 20),
        cost_estimate=pl.CostEstimate(flops=40_000_000, bytes_accessed=1_700_000, transcendentals=0),
        name="joined",
    )(place, *parts, *arrays)


def expander_kernel(place, low_other, low_own, grads1, grads2, gate_scale, up_scale, gate_out, up_out):
    hid = place[2]
    low = jnp.concatenate([low_other[...], low_own[...]], 1)

    def order(blocks):
        pieces = [
            one_hot(
                32 * len(blocks),
                512,
                lambda row: c * 256 + ((row // 32 + blocks[0]) ^ hid) * 64 + row // 8 % 4 * 16 + (1 - half) * 8 + row % 8,
            )
            for c in range(2)
            for half in range(2)
        ]
        return jnp.concatenate(pieces, 0)

    low1 = dot(low, order((0, 1, 2)), BY_ROWS).astype(BF16)
    low2 = dot(low, order((3,)), BY_ROWS).astype(BF16)
    for k, (out, scale) in enumerate(((gate_out, gate_scale), (up_out, up_scale))):
        total = dot(low1, grads1[k], PLAIN) + dot(low2, grads2[k], PLAIN)
        out[...] = ADAPTER_SCALE * total[16 * k : 16 * k + 16] / scale[...].reshape(1, UNITS)


def expander(*arrays):
    out = jax.ShapeDtypeStruct((16, UNITS), F32)
    return pl.pallas_call(
        expander_kernel,
        out_shape=(out, out),
        in_specs=[SMEM] + [VMEM] * 6,
        out_specs=(VMEM, VMEM),
        compiler_params=pltpu.CompilerParams(vmem_limit_bytes=12 << 20),
        cost_estimate=pl.CostEstimate(flops=55_000_000, bytes_accessed=2_000_000, transcendentals=0),
        name="expander",
    )(*arrays)


def plane(value):
    return lax.all_to_all(value, ("x", "y"), split_axis=0, concat_axis=0, tiled=True)


def per_device(
    inputs, gate_grad, up_grad, gate_codes, up_codes, gate_scale, up_scale,
    gate_down, gate_lift, up_down, up_lift,
):
    hid = lax.axis_index("hid")
    x, zh, y, core = (lax.axis_index(name) for name in FFN)
    place = jnp.stack([zh, core, hid, x, y])
    downs = gate_down.T, up_down.T

    both, back_other, back_own = prep(
        place, gate_grad.T, up_grad.T, gate_scale, up_scale, gate_lift, up_lift
    )
    two, one = swap(both, "hid", 2), swap(both, "hid", 1)
    back = (back_own + swap(back_other, "core", 1)).reshape(8, 256)
    arrived = swap(jnp.concatenate([inputs, back.astype(BF16)], 1), "zh", 1)
    sent, relayed = after((both, two), (one, arrived))
    middle = lax.ppermute(sent, "hid", [(1, 2), (2, 1)])
    ends = lax.ppermute(relayed, "hid", [(1, 0), (2, 3)])

    landed = plane(spread(inputs, back, arrived))
    parts = gather_over(narrow(landed, *downs), "hid")
    low, adapter, reducer = joined(place, parts, landed, *downs)
    reducer = reducer + swap(reducer, "core", 1)
    low_other = swap(low, "core", 1)

    codes = gate_codes.T, up_codes.T
    other1, own1, grads1 = product((both, one, two), 1, *codes)
    other2, own2, grads2 = product((middle, ends), 2, *codes)
    other1 = after(other1, (middle, ends))
    sums = add_pairs(place, own1, swap(other1, "core", 1), own2, swap(other2, "core", 1))
    kept = [plane(half.reshape(16, 8, FEATS)).astype(F32).sum(0) for half in sums]
    gate_expander, up_expander = expander(
        place, low_other, low, grads1, grads2, gate_scale, up_scale
    )
    arrived = swap(kept[0].astype(BF16), "zh", 1)
    rows = (kept[1] + arrived.astype(F32) + adapter).astype(BF16)
    return rows, reducer[:16].T, gate_expander, reducer[16:].T, up_expander


def solution(mesh):
    whole = Mesh(mesh.devices.reshape(4, 4, 2, 4, 2), ("hid",) + FFN)
    placed = (
        P(FFN, "hid"), P("hid", FFN), P("hid", FFN), P("hid", FFN), P("hid", FFN),
        P(FFN), P(FFN), P("hid", None), P(None, FFN), P("hid", None), P(None, FFN),
    )
    return jax.shard_map(
        per_device,
        mesh=whole,
        in_specs=placed,
        out_specs=(P(FFN, "hid"), P("hid", None), P(None, FFN), P("hid", None), P(None, FFN)),
        check_vma=False,
    )
```

time: 128 us -> 109 us (0.85)
  other arithmetic: 17.3 us -> 2.63 us
  starting transfers between devices: 46.9 us -> 42 us
  Pallas kernels: 18.5 us -> 13.8 us
  local copies, waits for them, and re-layouts: 13 us -> 17.7 us
  waiting for transfers between devices: 29.6 us -> 31.1 us
    ppermute x20 -> x12, starting transfers between devices: 30 us -> 18.2 us  [swap(): return lax.ppermute(value, axis, [(i, i ^ mask) for i in range(size)])]
    all_to_all x2 -> x3, starting transfers between devices: 12.2 us -> 21.9 us  [plane(): lax.all_to_all(value, ('x', 'y'), split_axis=0, concat_axis=0, tiled=True)]
    unnamed x50 -> x52, local copies, waits for them, and re-layouts: 7.49 us -> 16.9 us
    ppermute x20 -> x12, waiting for transfers between devices: 22.1 us -> 30.1 us  [swap(): return lax.ppermute(value, axis, [(i, i ^ mask) for i in range(size)])]
    pallas_call x4 -> x7, Pallas kernels: 16.7 us -> 12 us  [the longest x2 5.98 us: product(): pl.pallas_call(functools.partial(product_kernel, pairs), out_shape=(part,...]
    all_to_all x2 -> x0, other arithmetic: 3.99 us -> none  [per_device(): lax.all_to_all(summed.astype(BF16), ('x', 'y'), split_axis=0, concat_axis...]
    slice x9 -> x0, local copies, waits for them, and re-layouts: 3.7 us -> none  [the longest x8 3.7 us: per_device(): tokens = jnp.concatenate([part[:, :FEATS] for part in parts], 0)]
    ppermute x4 -> x2, waiting for transfers between devices: 3.42 us -> 0.01 us  [the longest x1 0.01 us: per_device(): middle = lax.ppermute(sent, 'hid', [(1, 2), (2, 1)])]
  transfers between devices with their start and end apart: 26 -> 17, of which waited for: 7 -> 8; matrix products, arithmetic and copies ran while one was open for 17% -> 3% of each run, Pallas kernels for 13% -> 11%
where the time goes in v4:
time: 109 us; the launch traced here: 108 us
  starting transfers between devices  42 us (39%)
  waiting for transfers between devices  31.1 us (29%)
  local copies, waits for them, and re-layouts  17.7 us (16%)
  Pallas kernels  13.8 us (13%)
  other arithmetic  2.63 us (2%)
    ppermute x12, waiting for transfers between devices, swap(): return lax.ppermute(value, axis, [(i, i ^ mask) for i in range(size)])  30.1 us
    all_to_all x3, starting transfers between devices, plane(): lax.all_to_all(value, ('x', 'y'), split_axis=0, concat_axis=0, tiled=True)  21.9 us
    ppermute x12, starting transfers between devices, swap(): return lax.ppermute(value, axis, [(i, i ^ mask) for i in range(size)])  18.2 us
    unnamed x52, local copies, waits for them, and re-layouts  16.9 us
    pallas_call x2, Pallas kernels, product(): pl.pallas_call(functools.partial(product_kernel, pairs), out_shape=(part,...  5.98 us
  transfers between devices with their start and end apart: 17, of which 8 were waited for; matrix products, arithmetic and copies ran while one was open for 3% of the time, Pallas kernels for 11%

profile of v4, /device:TPU:8, one launch (start us, length us, event | category | flops | bytes accessed | tf_op | source)
XLA Modules:
  0.0 108.2 jit_solution(1458790703299817546)
XLA Ops:
  0.7 0.9 copy-done.10
  5.6 1.6 %prep.1 = (bf16[2,2,2,32,832]{4,3,2,1,0:T(8,128)(2,1)}, f32[64,32]{1,0:T(8,128)S(1)}, f32[64,32]{1,0:T(8,128)S(1)}) custom-call(s32[5]{0:T(128)S(1)} %stack.23.place, bf16[832,128]{1,0:T(8,128)(2,1)S(1)} %bitcast.25, bf16[832,128]{1,0:T(8,128)(2,1)S(1)} %bitcast.26, f32[832]{0:T(1024)S(1)} %copy-done.17, f32[832]{0:T(1024)S(1)} %copy-done.19, ...), custom_call_target="tpu_custom_call" | custom-call | flops 14000000 | bytes 1200000 | tf_op jit(solution)/shard_map/prep/pallas_call | solution.py:72
  7.2 1.9 %collective-permute-start = (bf16[2,2,2,32,832]{4,3,2,1,0:T(8,128)(2,1)}, bf16[2,2,2,32,832]{4,3,2,1,0:T(8,128)(2,1)S(1)}, u32[]{:S(2)}, u32[]{:S(2)}) collective-permute-start(bf16[2,2,2,32,832]{4,3,2,1,0:T(8,128)(2,1)} %get-tuple-element.29.refs_0_), channel_id=1, source_target_pairs={{0,64},{64,0},{128,192},{192,128},{1,65},{65,1},{129,193},{193,129... | collective-permute-start | bytes 1277960 | tf_op jit(solution)/shard_map/ppermute | solution.py:23
  9.2 3.3 %collective-permute-start.1 = (bf16[2,2,2,32,832]{4,3,2,1,0:T(8,128)(2,1)}, bf16[2,2,2,32,832]{4,3,2,1,0:T(8,128)(2,1)}, u32[]{:S(2)}, u32[]{:S(2)}) collective-permute-start(bf16[2,2,2,32,832]{4,3,2,1,0:T(8,128)(2,1)} %get-tuple-element.29.refs_0_), channel_id=1, source_target_pairs={{0,128},{64,192},{128,0},{192,64},{1,129},{65,193},{129,1},{193,65... | collective-permute-start | bytes 1277960 | tf_op jit(solution)/shard_map/ppermute | solution.py:23
  12.4 1.2 %collective-permute-done.2 = f32[64,32]{1,0:T(8,128)S(1)} collective-permute-done((f32[64,32]{1,0:T(8,128)S(1)}, f32[64,32]{1,0:T(8,128)S(1)}, u32[]{:S(2)}, u32[]{:S(2)}) %collective-permute-start.2) | collective-permute-done | bytes 8224 | tf_op jit(solution)/shard_map/ppermute | solution.py:23
  14.5 4.5 %collective-permute-start.3 = (bf16[8,2304]{1,0:T(8,128)(2,1)S(1)}, bf16[8,2304]{1,0:T(8,128)(2,1)S(1)}, u32[]{:S(2)}, u32[]{:S(2)}) collective-permute-start(bf16[8,2304]{1,0:T(8,128)(2,1)S(1)} %pad_maximum_fusion), channel_id=1, source_target_pairs={{0,8},{8,0},{1,9},{9,1},{2,10},{10,2},{3,11},{11,3},{4,12},{12,4},... | collective-permute-start | bytes 110600 | tf_op jit(solution)/shard_map/ppermute | solution.py:23
  19.0 18.4 %collective-permute-done.3.arrived = bf16[8,2304]{1,0:T(8,128)(2,1)S(1)} collective-permute-done((bf16[8,2304]{1,0:T(8,128)(2,1)S(1)}, bf16[8,2304]{1,0:T(8,128)(2,1)S(1)}, u32[]{:S(2)}, u32[]{:S(2)}) %collective-permute-start.3) | collective-permute-done | bytes 36896 | tf_op jit(solution)/shard_map/ppermute | solution.py:23
  38.1 1.3 %collective-permute-start.5 = (bf16[2,2,2,32,832]{4,3,2,1,0:T(8,128)(2,1)}, bf16[2,2,2,32,832]{4,3,2,1,0:T(8,128)(2,1)S(1)}, u32[]{:S(2)}, u32[]{:S(2)}) collective-permute-start(bf16[2,2,2,32,832]{4,3,2,1,0:T(8,128)(2,1)} %collective-permute-done.1.refs_2_), channel_id=1, source_target_pairs={{64,0},{128,192},{65,1},{129,193},{66,2},{130,194},{67,3},{131,195... | collective-permute-start | bytes 1277960 | tf_op jit(solution)/shard_map/ppermute | solution.py:275
  40.2 1.1 %spread.1 = bf16[16,16,2304]{2,1,0:T(8,128)(2,1)} custom-call(bf16[8,2048]{1,0:T(8,128)(2,1)S(1)} %copy-done.12, f32[8,256]{1,0:T(8,128)S(1)} %reshape.19.back, bf16[8,2304]{1,0:T(8,128)(2,1)S(1)} %collective-permute-done.3.arrived), custom_call_target="tpu_custom_call" | custom-call | flops 100000 | bytes 1300000 | tf_op jit(solution)/shard_map/spread/pallas_call | solution.py:152
  41.3 7.4 %all-to-all-start.2 = ((bf16[16,16,2304]{2,1,0:T(8,128)(2,1)}), bf16[16,16,2304]{2,1,0:T(8,128)(2,1)S(1)}, u32[]{:S(2)}, u32[]{:S(2)}) async-start(bf16[16,16,2304]{2,1,0:T(8,128)(2,1)} %spread.1), calls=%async_computation.2 | async-start | bytes 2359296 | tf_op jit(solution)/shard_map/all_to_all | solution.py:255
  48.7 2.0 %copy-done = bf16[2048,832]{0,1:T(8,128)(2,1)S(1)} copy-done((bf16[2048,832]{0,1:T(8,128)(2,1)S(1)}, bf16[2048,832]{0,1:T(8,128)(2,1)}, u32[]{:S(2)}) %copy-start) | copy-done | bytes 3407896
  50.7 2.0 %copy-done.2 = bf16[2048,832]{0,1:T(8,128)(2,1)S(1)} copy-done((bf16[2048,832]{0,1:T(8,128)(2,1)S(1)}, bf16[2048,832]{0,1:T(8,128)(2,1)}, u32[]{:S(2)}) %copy-start.2) | copy-done | bytes 3407896
  52.6 1.0 copy-done.25
  53.7 4.7 %product.2 = (bf16[192,2048]{1,0:T(8,128)(2,1)S(1)}, bf16[192,2048]{1,0:T(8,128)(2,1)S(1)}, bf16[2,384,832]{2,1,0:T(8,128)(2,1)S(1)}) custom-call(bf16[2,2,2,32,832]{4,3,2,1,0:T(8,128)(2,1)} %get-tuple-element.29.refs_0_, bf16[2,2,2,32,832]{4,3,2,1,0:T(8,128)(2,1)S(1)} %copy-done.25, bf16[2,2,2,32,832]{4,3,2,1,0:T(8,128)(2,1)} %collective-permute-done.1.refs_2_, ...), custom_call_target="tpu_custom_call" | custom-call | flops 2700000000 | bytes 8000000 | tf_op jit(solution)/shard_map/product/pallas_call | solution.py:106
  60.0 1.0 copy-done.7
  61.0 1.0 copy-done.9
  62.0 1.3 %product.3 = (bf16[64,2048]{1,0:T(8,128)(2,1)S(1)}, bf16[64,2048]{1,0:T(8,128)(2,1)S(1)}, bf16[2,128,832]{2,1,0:T(8,128)(2,1)S(1)}) custom-call(bf16[2,2,2,32,832]{4,3,2,1,0:T(8,128)(2,1)S(1)} %copy-done.7, bf16[2,2,2,32,832]{4,3,2,1,0:T(8,128)(2,1)S(1)} %copy-done.9, bf16[832,2048]{1,0:T(8,128)(2,1)S(1)} %bitcast.18, bf16[832,2048]{1,0:T(8,128)(2,1)S(1)} %bitcast.20), custom_call_target="tpu_custom_call" | custom-call | flops 900000000 | bytes 8000000 | tf_op jit(solution)/shard_map/product/pallas_call | solution.py:106
  63.9 1.2 %collective-permute-done.7.theirs2 = bf16[64,2048]{1,0:T(8,128)(2,1)S(1)} collective-permute-done((bf16[64,2048]{1,0:T(8,128)(2,1)S(1)}, bf16[64,2048]{1,0:T(8,128)(2,1)S(1)}, u32[]{:S(2)}, u32[]{:S(2)}) %collective-permute-start.7) | collective-permute-done | bytes 262176 | tf_op jit(solution)/shard_map/ppermute | solution.py:23
  65.1 1.7 %add_pairs.1 = (bf16[4,32,2048]{2,1,0:T(8,128)(2,1)}, bf16[4,32,2048]{2,1,0:T(8,128)(2,1)}) custom-call(s32[5]{0:T(128)S(1)} %stack.23.place, bf16[192,2048]{1,0:T(8,128)(2,1)S(1)} %get-tuple-element.25.own1, bf16[192,2048]{1,0:T(8,128)(2,1)S(1)} %collective-permute-done.6.theirs1, bf16[64,2048]{1,0:T(8,128)(2,1)S(1)} %get-tuple-element.32.own2, ...), custom_call_target="tpu_custom_call" | custom-call | flops 600000 | bytes 3200000 | tf_op jit(solution)/shard_map/add_pairs/pallas_call | solution.py:130
  66.8 7.3 %all-to-all-start.1 = ((bf16[16,8,2048]{2,1,0:T(8,128)(2,1)}), bf16[16,8,2048]{2,1,0:T(8,128)(2,1)}, u32[]{:S(2)}, u32[]{:S(2)}) async-start(bf16[16,8,2048]{2,1,0:T(8,128)(2,1)} %bitcast.10), calls=%async_computation.1 | async-start | bytes 1048576 | tf_op jit(solution)/shard_map/all_to_all | solution.py:255
  74.5 2.7 %collective-permute-start.9 = (bf16[48,256]{1,0:T(8,128)(2,1)S(1)}, bf16[48,256]{1,0:T(8,128)(2,1)S(1)}, u32[]{:S(2)}, u32[]{:S(2)}) collective-permute-start(bf16[48,256]{1,0:T(8,128)(2,1)S(1)} %narrow.1.p0), channel_id=1, source_target_pairs={{0,64},{64,0},{128,192},{192,128},{1,65},{65,1},{129,193},{193,129... | collective-permute-start | bytes 73736 | tf_op jit(solution)/shard_map/ppermute | solution.py:23
  77.7 1.9 %collective-permute-start.11 = (bf16[48,256]{1,0:T(8,128)(2,1)S(1)}, bf16[48,256]{1,0:T(8,128)(2,1)S(1)}, u32[]{:S(2)}, u32[]{:S(2)}) collective-permute-start(bf16[48,256]{1,0:T(8,128)(2,1)S(1)} %narrow.1.p0), channel_id=1, source_target_pairs={{0,192},{64,128},{128,64},{192,0},{1,193},{65,129},{129,65},{193,1... | collective-permute-start | bytes 73736 | tf_op jit(solution)/shard_map/ppermute | solution.py:23
  79.6 2.5 %collective-permute-done.10.p2 = bf16[48,256]{1,0:T(8,128)(2,1)S(1)} collective-permute-done((bf16[48,256]{1,0:T(8,128)(2,1)S(1)}, bf16[48,256]{1,0:T(8,128)(2,1)S(1)}, u32[]{:S(2)}, u32[]{:S(2)}) %collective-permute-start.10) | collective-permute-done | bytes 24608 | tf_op jit(solution)/shard_map/ppermute | solution.py:23
  82.2 1.2 %collective-permute-done.11.p3 = bf16[48,256]{1,0:T(8,128)(2,1)S(1)} collective-permute-done((bf16[48,256]{1,0:T(8,128)(2,1)S(1)}, bf16[48,256]{1,0:T(8,128)(2,1)S(1)}, u32[]{:S(2)}, u32[]{:S(2)}) %collective-permute-start.11) | collective-permute-done | bytes 24608 | tf_op jit(solution)/shard_map/ppermute | solution.py:23
  83.4 1.1 %joined.1 = (bf16[32,256]{1,0:T(8,128)(2,1)S(1)}, f32[8,2048]{1,0:T(8,128)S(1)}, f32[32,2048]{1,0:T(8,128)S(1)}) custom-call(s32[5]{0:T(128)S(1)} %copy-done.22, bf16[48,256]{1,0:T(8,128)(2,1)S(1)} %narrow.1.p0, bf16[48,256]{1,0:T(8,128)(2,1)S(1)} %collective-permute-done.9.p1, bf16[48,256]{1,0:T(8,128)(2,1)S(1)} %collective-permute-done.10.p2, ...), custom_call_target="tpu_custom_call" | custom-call | flops 40000000 | bytes 1700000 | tf_op jit(solution)/shard_map/joined/pallas_call | solution.py:203
  85.1 7.2 %all-to-all-start = ((bf16[16,8,2048]{2,1,0:T(8,128)(2,1)}), bf16[16,8,2048]{2,1,0:T(8,128)(2,1)S(1)}, u32[]{:S(2)}, u32[]{:S(2)}) async-start(bf16[16,8,2048]{2,1,0:T(8,128)(2,1)} %bitcast.9), calls=%async_computation | async-start | bytes 1048576 | tf_op jit(solution)/shard_map/all_to_all | solution.py:255
  92.3 1.2 %collective-permute-done.13.low_other = bf16[32,256]{1,0:T(8,128)(2,1)S(1)} collective-permute-done((bf16[32,256]{1,0:T(8,128)(2,1)S(1)}, bf16[32,256]{1,0:T(8,128)(2,1)S(1)}, u32[]{:S(2)}, u32[]{:S(2)}) %collective-permute-start.13) | collective-permute-done | bytes 16416 | tf_op jit(solution)/shard_map/ppermute | solution.py:23
  95.5 1.9 %expander.1 = (f32[16,832]{1,0:T(8,128)}, f32[16,832]{1,0:T(8,128)}) custom-call(s32[5]{0:T(128)S(1)} %copy-done.23, bf16[32,256]{1,0:T(8,128)(2,1)S(1)} %collective-permute-done.13.low_other, bf16[32,256]{1,0:T(8,128)(2,1)S(1)} %get-tuple-element.38.low_own, bf16[2,384,832]{2,1,0:T(8,128)(2,1)S(1)} %get-tuple-element.39.grads1, ...), custom_call_target="tpu_custom_call" | custom-call | flops 55000000 | bytes 2000000 | tf_op jit(solution)/shard_map/expander/pallas_call | solution.py:243
  98.2 1.1 %reduce_sum.22 = bf16[8,2048]{1,0:T(8,128)(2,1)S(1)} reduce(bf16[16,8,2048]{2,1,0:T(8,128)(2,1)} %all-to-all-done.1, bf16[]{:T(256)} %constant.22.clone.1), dimensions={0}, to_apply=%region_1.0 | reduce | flops 245760 | bytes 557058 | tf_op jit(solution)/shard_map/reduce_sum | solution.py:288
  99.3 2.8 %collective-permute-start.8 = (bf16[8,2048]{1,0:T(8,128)(2,1)S(1)}, bf16[8,2048]{1,0:T(8,128)(2,1)S(1)}, u32[]{:S(2)}, u32[]{:S(2)}) collective-permute-start(bf16[8,2048]{1,0:T(8,128)(2,1)S(1)} %reduce_sum.22), channel_id=1, source_target_pairs={{0,8},{8,0},{1,9},{9,1},{2,10},{10,2},{3,11},{11,3},{4,12},{12,4},... | collective-permute-start | bytes 98312 | tf_op jit(solution)/shard_map/ppermute | solution.py:23
  102.0 1.1 all-to-all-done
  103.2 4.4 %collective-permute-done.8 = bf16[8,2048]{1,0:T(8,128)(2,1)S(1)} collective-permute-done((bf16[8,2048]{1,0:T(8,128)(2,1)S(1)}, bf16[8,2048]{1,0:T(8,128)(2,1)S(1)}, u32[]{:S(2)}, u32[]{:S(2)}) %collective-permute-start.8) | collective-permute-done | bytes 32800 | tf_op jit(solution)/shard_map/ppermute | solution.py:23
  (72 shorter events, 13.6 us)
Async XLA Ops:
  0.7 64.3 %copy-start.21 = (s32[5]{0:T(128)}, s32[5]{0:T(128)S(1)}, u32[]{:S(2)}) copy-start(s32[5]{0:T(128)S(1)} %stack.23.place) | copy-start | bytes 64
  0.7 0.9 copy-start.10
  1.7 0.9 copy-start.11
  7.2 30.2 %collective-permute-start = (bf16[2,2,2,32,832]{4,3,2,1,0:T(8,128)(2,1)}, bf16[2,2,2,32,832]{4,3,2,1,0:T(8,128)(2,1)S(1)}, u32[]{:S(2)}, u32[]{:S(2)}) collective-permute-start(bf16[2,2,2,32,832]{4,3,2,1,0:T(8,128)(2,1)} %get-tuple-element.29.refs_0_), channel_id=1, source_target_pairs={{0,64},{64,0},{128,192},{192,128},{1,65},{65,1},{129,193},{193,129... | collective-permute-start | bytes 1277960 | tf_op jit(solution)/shard_map/ppermute | solution.py:23
  9.2 28.3 %collective-permute-start.1 = (bf16[2,2,2,32,832]{4,3,2,1,0:T(8,128)(2,1)}, bf16[2,2,2,32,832]{4,3,2,1,0:T(8,128)(2,1)}, u32[]{:S(2)}, u32[]{:S(2)}) collective-permute-start(bf16[2,2,2,32,832]{4,3,2,1,0:T(8,128)(2,1)} %get-tuple-element.29.refs_0_), channel_id=1, source_target_pairs={{0,128},{64,192},{128,0},{192,64},{1,129},{65,193},{129,1},{193,65... | collective-permute-start | bytes 1277960 | tf_op jit(solution)/shard_map/ppermute | solution.py:23
  12.4 1.2 %collective-permute-start.2 = (f32[64,32]{1,0:T(8,128)S(1)}, f32[64,32]{1,0:T(8,128)S(1)}, u32[]{:S(2)}, u32[]{:S(2)}) collective-permute-start(f32[64,32]{1,0:T(8,128)S(1)} %get-tuple-element.28), channel_id=1, source_target_pairs={{0,1},{1,0},{2,3},{3,2},{4,5},{5,4},{6,7},{7,6},{8,9},{9,8},{10,11... | collective-permute-start | bytes 24584 | tf_op jit(solution)/shard_map/ppermute | solution.py:23
  14.5 22.9 %collective-permute-start.3 = (bf16[8,2304]{1,0:T(8,128)(2,1)S(1)}, bf16[8,2304]{1,0:T(8,128)(2,1)S(1)}, u32[]{:S(2)}, u32[]{:S(2)}) collective-permute-start(bf16[8,2304]{1,0:T(8,128)(2,1)S(1)} %pad_maximum_fusion), channel_id=1, source_target_pairs={{0,8},{8,0},{1,9},{9,1},{2,10},{10,2},{3,11},{11,3},{4,12},{12,4},... | collective-permute-start | bytes 110600 | tf_op jit(solution)/shard_map/ppermute | solution.py:23
  37.4 3.9 %copy-start.24 = (bf16[2,2,2,32,832]{4,3,2,1,0:T(8,128)(2,1)}, bf16[2,2,2,32,832]{4,3,2,1,0:T(8,128)(2,1)S(1)}, u32[]{:S(2)}) copy-start(bf16[2,2,2,32,832]{4,3,2,1,0:T(8,128)(2,1)S(1)} %collective-permute-done.refs_1_) | copy-start | bytes 1277956
  37.4 21.0 %collective-permute-start.4 = (bf16[2,2,2,32,832]{4,3,2,1,0:T(8,128)(2,1)}, bf16[2,2,2,32,832]{4,3,2,1,0:T(8,128)(2,1)S(1)}, u32[]{:S(2)}, u32[]{:S(2)}) collective-permute-start(bf16[2,2,2,32,832]{4,3,2,1,0:T(8,128)(2,1)} %get-tuple-element.29.refs_0_), channel_id=1, source_target_pairs={{64,128},{128,64},{65,129},{129,65},{66,130},{130,66},{67,131},{13... | collective-permute-start | bytes 1277960 | tf_op jit(solution)/shard_map/ppermute | solution.py:274
  38.1 21.0 %collective-permute-start.5 = (bf16[2,2,2,32,832]{4,3,2,1,0:T(8,128)(2,1)}, bf16[2,2,2,32,832]{4,3,2,1,0:T(8,128)(2,1)S(1)}, u32[]{:S(2)}, u32[]{:S(2)}) collective-permute-start(bf16[2,2,2,32,832]{4,3,2,1,0:T(8,128)(2,1)} %collective-permute-done.1.refs_2_), channel_id=1, source_target_pairs={{64,0},{128,192},{65,1},{129,193},{66,2},{130,194},{67,3},{131,195... | collective-permute-start | bytes 1277960 | tf_op jit(solution)/shard_map/ppermute | solution.py:275
  41.3 25.5 %all-to-all-start.2 = ((bf16[16,16,2304]{2,1,0:T(8,128)(2,1)}), bf16[16,16,2304]{2,1,0:T(8,128)(2,1)S(1)}, u32[]{:S(2)}, u32[]{:S(2)}) async-start(bf16[16,16,2304]{2,1,0:T(8,128)(2,1)} %spread.1), calls=%async_computation.2 | async-start | bytes 2359296 | tf_op jit(solution)/shard_map/all_to_all | solution.py:255
  48.7 2.0 %copy-start = (bf16[2048,832]{0,1:T(8,128)(2,1)S(1)}, bf16[2048,832]{0,1:T(8,128)(2,1)}, u32[]{:S(2)}) copy-start(bf16[2048,832]{0,1:T(8,128)(2,1)} %param.14) | copy-start | bytes 10223620
  50.7 2.0 %copy-start.2 = (bf16[2048,832]{0,1:T(8,128)(2,1)S(1)}, bf16[2048,832]{0,1:T(8,128)(2,1)}, u32[]{:S(2)}) copy-start(bf16[2048,832]{0,1:T(8,128)(2,1)} %param.15) | copy-start | bytes 10223620
  52.6 1.0 copy-start.25
  53.6 6.3 %copy-start.1 = (bf16[2048,832]{0,1:T(8,128)(2,1)S(1)}, bf16[2048,832]{0,1:T(8,128)(2,1)}, u32[]{:S(2)}) copy-start(bf16[2048,832]{0,1:T(8,128)(2,1)} %param.14) | copy-start | bytes 10223620
  53.7 6.3 %copy-start.3 = (bf16[2048,832]{0,1:T(8,128)(2,1)S(1)}, bf16[2048,832]{0,1:T(8,128)(2,1)}, u32[]{:S(2)}) copy-start(bf16[2048,832]{0,1:T(8,128)(2,1)} %param.15) | copy-start | bytes 10223620
  60.0 5.1 %collective-permute-start.6 = (bf16[192,2048]{1,0:T(8,128)(2,1)S(1)}, bf16[192,2048]{1,0:T(8,128)(2,1)S(1)}, u32[]{:S(2)}, u32[]{:S(2)}) collective-permute-start(bf16[192,2048]{1,0:T(8,128)(2,1)S(1)} %get-tuple-element.31), channel_id=1, source_target_pairs={{0,1},{1,0},{2,3},{3,2},{4,5},{5,4},{6,7},{7,6},{8,9},{9,8},{10,11... | collective-permute-start | bytes 2359304 | tf_op jit(solution)/shard_map/ppermute | solution.py:23
  60.0 1.0 copy-start.7
  61.0 1.0 copy-start.9
  63.3 1.7 %collective-permute-start.7 = (bf16[64,2048]{1,0:T(8,128)(2,1)S(1)}, bf16[64,2048]{1,0:T(8,128)(2,1)S(1)}, u32[]{:S(2)}, u32[]{:S(2)}) collective-permute-start(bf16[64,2048]{1,0:T(8,128)(2,1)S(1)} %get-tuple-element.33), channel_id=1, source_target_pairs={{0,1},{1,0},{2,3},{3,2},{4,5},{5,4},{6,7},{7,6},{8,9},{9,8},{10,11... | collective-permute-start | bytes 786440 | tf_op jit(solution)/shard_map/ppermute | solution.py:23
  65.1 9.0 %copy-start.4 = (f32[2048,16]{0,1:T(8,128)S(1)}, f32[2048,16]{0,1:T(8,128)}, u32[]{:S(2)}) copy-start(f32[2048,16]{0,1:T(8,128)} %param.18) | copy-start | bytes 393220
  65.1 9.0 %copy-start.5 = (f32[2048,16]{0,1:T(8,128)S(1)}, f32[2048,16]{0,1:T(8,128)}, u32[]{:S(2)}) copy-start(f32[2048,16]{0,1:T(8,128)} %param.20) | copy-start | bytes 393220
  66.8 18.3 %all-to-all-start.1 = ((bf16[16,8,2048]{2,1,0:T(8,128)(2,1)}), bf16[16,8,2048]{2,1,0:T(8,128)(2,1)}, u32[]{:S(2)}, u32[]{:S(2)}) async-start(bf16[16,8,2048]{2,1,0:T(8,128)(2,1)} %bitcast.10), calls=%async_computation.1 | async-start | bytes 1048576 | tf_op jit(solution)/shard_map/all_to_all | solution.py:255
  74.0 9.3 %copy-start.22 = (s32[5]{0:T(128)S(1)}, s32[5]{0:T(128)}, u32[]{:S(2)}) copy-start(s32[5]{0:T(128)} %copy-done.21) | copy-start | bytes 64
  74.5 5.2 %collective-permute-start.9 = (bf16[48,256]{1,0:T(8,128)(2,1)S(1)}, bf16[48,256]{1,0:T(8,128)(2,1)S(1)}, u32[]{:S(2)}, u32[]{:S(2)}) collective-permute-start(bf16[48,256]{1,0:T(8,128)(2,1)S(1)} %narrow.1.p0), channel_id=1, source_target_pairs={{0,64},{64,0},{128,192},{192,128},{1,65},{65,1},{129,193},{193,129... | collective-permute-start | bytes 73736 | tf_op jit(solution)/shard_map/ppermute | solution.py:23
  77.2 5.0 %collective-permute-start.10 = (bf16[48,256]{1,0:T(8,128)(2,1)S(1)}, bf16[48,256]{1,0:T(8,128)(2,1)S(1)}, u32[]{:S(2)}, u32[]{:S(2)}) collective-permute-start(bf16[48,256]{1,0:T(8,128)(2,1)S(1)} %narrow.1.p0), channel_id=1, source_target_pairs={{0,128},{64,192},{128,0},{192,64},{1,129},{65,193},{129,1},{193,65... | collective-permute-start | bytes 73736 | tf_op jit(solution)/shard_map/ppermute | solution.py:23
  77.7 5.6 %collective-permute-start.11 = (bf16[48,256]{1,0:T(8,128)(2,1)S(1)}, bf16[48,256]{1,0:T(8,128)(2,1)S(1)}, u32[]{:S(2)}, u32[]{:S(2)}) collective-permute-start(bf16[48,256]{1,0:T(8,128)(2,1)S(1)} %narrow.1.p0), channel_id=1, source_target_pairs={{0,192},{64,128},{128,64},{192,0},{1,193},{65,129},{129,65},{193,1... | collective-permute-start | bytes 73736 | tf_op jit(solution)/shard_map/ppermute | solution.py:23
  85.1 12.3 %collective-permute-start.12 = (f32[32,2048]{1,0:T(8,128)S(1)}, f32[32,2048]{1,0:T(8,128)S(1)}, u32[]{:S(2)}, u32[]{:S(2)}) collective-permute-start(f32[32,2048]{1,0:T(8,128)S(1)} %get-tuple-element.37), channel_id=1, source_target_pairs={{0,1},{1,0},{2,3},{3,2},{4,5},{5,4},{6,7},{7,6},{8,9},{9,8},{10,11... | collective-permute-start | bytes 786440 | tf_op jit(solution)/shard_map/ppermute | solution.py:23
  85.1 18.0 %all-to-all-start = ((bf16[16,8,2048]{2,1,0:T(8,128)(2,1)}), bf16[16,8,2048]{2,1,0:T(8,128)(2,1)S(1)}, u32[]{:S(2)}, u32[]{:S(2)}) async-start(bf16[16,8,2048]{2,1,0:T(8,128)(2,1)} %bitcast.9), calls=%async_computation | async-start | bytes 1048576 | tf_op jit(solution)/shard_map/all_to_all | solution.py:255
  92.3 1.2 %collective-permute-start.13 = (bf16[32,256]{1,0:T(8,128)(2,1)S(1)}, bf16[32,256]{1,0:T(8,128)(2,1)S(1)}, u32[]{:S(2)}, u32[]{:S(2)}) collective-permute-start(bf16[32,256]{1,0:T(8,128)(2,1)S(1)} %get-tuple-element.38.low_own), channel_id=1, source_target_pairs={{0,1},{1,0},{2,3},{3,2},{4,5},{5,4},{6,7},{7,6},{8,9},{9,8},{10,11... | collective-permute-start | bytes 49160 | tf_op jit(solution)/shard_map/ppermute | solution.py:23
  97.4 10.1 %copy-start.14 = (f32[8,2048]{1,0:T(8,128)S(1)}, f32[8,2048]{1,0:T(8,128)}, u32[]{:S(2)}) copy-start(f32[8,2048]{1,0:T(8,128)} %copy-done.13) | copy-start | bytes 196612
  99.3 8.3 %collective-permute-start.8 = (bf16[8,2048]{1,0:T(8,128)(2,1)S(1)}, bf16[8,2048]{1,0:T(8,128)(2,1)S(1)}, u32[]{:S(2)}, u32[]{:S(2)}) collective-permute-start(bf16[8,2048]{1,0:T(8,128)(2,1)S(1)} %reduce_sum.22), channel_id=1, source_target_pairs={{0,8},{8,0},{1,9},{9,1},{2,10},{10,2},{3,11},{11,3},{4,12},{12,4},... | collective-permute-start | bytes 98312 | tf_op jit(solution)/shard_map/ppermute | solution.py:23
  (11 other events, 8.0 us)

commit v5 on v4

v5 whole, which is shorter than its diff:
```python
import functools

import jax
import jax.numpy as jnp
from jax import lax
from jax.experimental import pallas as pl
from jax.experimental.pallas import tpu as pltpu
from jax.sharding import Mesh, PartitionSpec as P

ADAPTER_SCALE = 2.0
FFN = ("x", "zh", "y", "core")
F32, BF16 = jnp.float32, jnp.bfloat16
UNITS, FEATS, STEP = 832, 2048, 256
PLAIN = (((1,), (0,)), ((), ()))
BY_ROWS = (((1,), (1,)), ((), ()))
BY_COLUMNS = (((0,), (0,)), ((), ()))
SMEM = pl.BlockSpec(memory_space=pltpu.SMEM)
VMEM = pl.BlockSpec(memory_space=pltpu.VMEM)


def swap(value, axis, mask):
    size = lax.axis_size(axis)
    return lax.ppermute(value, axis, [(i, i ^ mask) for i in range(size)])


def gather_over(value, axis):
    return [value] + [swap(value, axis, k) for k in range(1, lax.axis_size(axis))]


def dot(left, right, how):
    return lax.dot_general(left, right, how, preferred_element_type=F32)


def one_hot(rows, columns, source):
    row = lax.broadcasted_iota(jnp.int32, (rows, columns), 0)
    column = lax.broadcasted_iota(jnp.int32, (rows, columns), 1)
    return (column == source(row)).astype(F32).astype(BF16)


def prep_kernel(place, gate, up, gate_scale, up_scale, gate_lift, up_lift, both, back_other, back_own):
    zh, core = place[0], place[1]

    def source(row):
        half, side = 1 - row // 64, 1 - row // 32 % 2
        return (half ^ zh) * 64 + row // 8 % 4 * 16 + (side ^ core) * 8 + row % 8

    order = one_hot(128, 128, source)
    none = jnp.zeros((16, UNITS), F32)
    lifts = (
        jnp.concatenate([gate_lift[...], none], 0).astype(BF16),
        jnp.concatenate([none, up_lift[...]], 0).astype(BF16),
    )
    back = jnp.zeros((128, 32), F32)
    for k, (grad, scale) in enumerate(((gate, gate_scale), (up, up_scale))):
        rows = dot(order, grad[...], BY_ROWS)
        back += dot(rows.astype(BF16), lifts[k], BY_ROWS)
        rows = (rows * scale[...].reshape(1, UNITS)).astype(BF16).reshape(2, 2, 32, UNITS)
        both[0, k] = rows[0]
        both[1, k] = rows[1]

    def packed(row):
        return row // 4 % 2 * 64 + row // 8 % 2 * 32 + row % 4 * 8 + row // 16

    back = dot(one_hot(128, 128, packed), back.astype(BF16), PLAIN)
    back_other[...] = jnp.concatenate([back[16 * i : 16 * i + 8] for i in range(8)], 1)
    back_own[...] = jnp.concatenate([back[16 * i + 8 : 16 * i + 16] for i in range(8)], 1)


def prep(place, *arrays):
    both = jax.ShapeDtypeStruct((2, 2, 2, 32, UNITS), BF16)
    back = jax.ShapeDtypeStruct((8, 256), F32)
    return pl.pallas_call(
        prep_kernel,
        out_shape=(both, back, back),
        in_specs=[SMEM] + [VMEM] * 6,
        out_specs=(VMEM,) * 3,
        cost_estimate=pl.CostEstimate(flops=14_000_000, bytes_accessed=1_200_000, transcendentals=0),
        name="prep",
    )(place, *arrays)


def product_kernel(pairs, *refs):
    blocks, (gate_codes, up_codes, other, own, grads, gate_held, up_held, sems) = refs[:-8], refs[-8:]
    count = len(blocks) // pairs
    copies = []
    for i, start in enumerate(range(0, FEATS, STEP)):
        columns = pl.ds(start, STEP)
        copies.append(
            [
                pltpu.make_async_copy(source.at[:, columns], held.at[:, columns], sems.at[k, i])
                for k, (source, held) in enumerate(((gate_codes, gate_held), (up_codes, up_held)))
            ]
        )
        for copy in copies[-1]:
            copy.start()
    for k in range(2):
        for c in range(2):
            for half in range(2):
                for j in range(count):
                    value = blocks[j * pairs][half, k, c]
                    if pairs == 2:
                        value += blocks[j * pairs + 1][half, k, c]
                    row = ((c * 2 + half) * count + j) * 32
                    grads[k, row : row + 32] = value
    gate, up, cut = grads[0], grads[1], 64 * count
    for i, start in enumerate(range(0, FEATS, STEP)):
        columns = slice(start, start + STEP)
        for copy in copies[i]:
            copy.wait()
        total = dot(gate, gate_held[:, columns], PLAIN) + dot(up, up_held[:, columns], PLAIN)
        other[:, columns] = total[:cut].astype(BF16)
        own[:, columns] = total[cut:].astype(BF16)


def product(blocks, pairs, gate_codes, up_codes):
    count = len(blocks) // pairs
    part = jax.ShapeDtypeStruct((64 * count, FEATS), BF16)
    anywhere = pl.BlockSpec(memory_space=pl.ANY)
    return pl.pallas_call(
        functools.partial(product_kernel, pairs),
        out_shape=(part, part, jax.ShapeDtypeStruct((2, 128 * count, UNITS), BF16)),
        in_specs=[VMEM] * len(blocks) + [anywhere] * 2,
        out_specs=(VMEM,) * 3,
        scratch_shapes=[
            pltpu.VMEM((UNITS, FEATS), BF16),
            pltpu.VMEM((UNITS, FEATS), BF16),
            pltpu.SemaphoreType.DMA((2, FEATS // STEP)),
        ],
        compiler_params=pltpu.CompilerParams(vmem_limit_bytes=20 << 20),
        cost_estimate=pl.CostEstimate(
            flops=900_000_000 * count, bytes_accessed=8_000_000, transcendentals=0
        ),
        name="product",
    )(*blocks, gate_codes, up_codes)


def pairs_kernel(place, own1, theirs1, own2, theirs2, out):
    for j in range(4):
        halves = []
        for half in range(2):
            own, theirs, row = (own1, theirs1, (half * 3 + j) * 32) if j < 3 else (own2, theirs2, half * 32)
            rows = slice(row, row + 32)
            halves.append(own[rows].astype(F32) + theirs[rows].astype(F32))
        for k in range(4):
            rows = slice(8 * k, 8 * k + 8)
            out[place[2] ^ j, k] = jnp.concatenate([half[rows] for half in halves], 0).astype(BF16)


def add_pairs(*arrays):
    return pl.pallas_call(
        pairs_kernel,
        out_shape=jax.ShapeDtypeStruct((4, 4, 16, FEATS), BF16),
        in_specs=[SMEM] + [VMEM] * 4,
        out_specs=VMEM,
        compiler_params=pltpu.CompilerParams(vmem_limit_bytes=8 << 20),
        cost_estimate=pl.CostEstimate(flops=600_000, bytes_accessed=3_200_000, transcendentals=0),
        name="add_pairs",
    )(*arrays)


def mark_kernel(one, two, out):
    out[...] = jnp.zeros((8, 128), F32)


def mark(*arrays):
    return pl.pallas_call(
        mark_kernel,
        out_shape=jax.ShapeDtypeStruct((8, 128), F32),
        in_specs=[pl.BlockSpec(memory_space=pl.ANY)] * 2,
        out_specs=VMEM,
        compiler_params=pltpu.CompilerParams(vmem_limit_bytes=1 << 20),
        cost_estimate=pl.CostEstimate(flops=100_000_000_000, bytes_accessed=4096, transcendentals=0),
        name="mark",
    )(*arrays)


def spread_kernel(inputs, back_own, back_theirs, out):
    rows = jnp.concatenate([inputs[...].astype(F32), back_own[...] + back_theirs[...]], 1)
    rows = jnp.concatenate([rows, rows], 0).astype(BF16)
    for i in range(8):
        out[16 * i : 16 * i + 16] = rows


def spread(*arrays):
    return pl.pallas_call(
        spread_kernel,
        out_shape=jax.ShapeDtypeStruct((128, FEATS + 256), BF16),
        in_specs=[VMEM] * 3,
        out_specs=VMEM,
        compiler_params=pltpu.CompilerParams(vmem_limit_bytes=4 << 20),
        cost_estimate=pl.CostEstimate(flops=40_000_000_000, bytes_accessed=700_000, transcendentals=0),
        name="spread",
    )(*arrays)


def narrow_kernel(marked, landed, gate_down, up_down, out):
    down = jnp.concatenate([gate_down[...], up_down[...]], 0).astype(BF16)
    low = dot(down, landed[:, :FEATS], BY_ROWS)
    back = landed[:, FEATS:].astype(F32).reshape(16, 8, 256).sum(0)
    low = jnp.concatenate([low, jnp.zeros((32, 128), F32)], 1)
    out[...] = jnp.concatenate([low, back, jnp.zeros((8, 256), F32)], 0).astype(BF16)


def narrow(*arrays):
    return pl.pallas_call(
        narrow_kernel,
        out_shape=jax.ShapeDtypeStruct((48, 256), BF16),
        in_specs=[pl.BlockSpec(memory_space=pl.ANY)] + [VMEM] * 3,
        out_specs=VMEM,
        compiler_params=pltpu.CompilerParams(vmem_limit_bytes=6 << 20),
        cost_estimate=pl.CostEstimate(flops=17_000_000, bytes_accessed=900_000, transcendentals=0),
        name="narrow",
    )(*arrays)


def halves_kernel(own, theirs, out):
    mine, other = own[...].astype(F32), theirs[...].astype(F32)
    low = jnp.concatenate([mine[:32, :128], other[:32, :128]], 1)
    back = mine[32:40] + jnp.concatenate([other[36:40], other[32:36]], 0)
    out[...] = jnp.concatenate([low, back, jnp.zeros((8, 256), F32)], 0).astype(BF16)


def join_halves(*arrays):
    return pl.pallas_call(
        halves_kernel,
        out_shape=jax.ShapeDtypeStruct((48, 256), BF16),
        in_specs=[VMEM] * 2,
        out_specs=VMEM,
        compiler_params=pltpu.CompilerParams(vmem_limit_bytes=2 << 20),
        cost_estimate=pl.CostEstimate(flops=10_000, bytes_accessed=80_000, transcendentals=0),
        name="join_halves",
    )(*arrays)


def joined_kernel(marked, place, p0, p1, p2, p3, landed, gate_down, up_down, low_out, adapter, keep, give):
    core, hid, x, y = place[1], place[2], place[3], place[4]
    parts = [part[...].astype(F32) for part in (p0, p1, p2, p3)]
    low_out[...] = sum(part[:32] for part in parts).astype(BF16)
    back = jnp.concatenate(
        [part[32:40, 32 * i : 32 * i + 32] for part in parts for i in range(8)], 0
    ).astype(BF16)

    def source(row):
        return ((row // 32) ^ hid) * 64 + row % 8 * 8 + 4 + row // 8 % 4

    mine = dot(one_hot(16, 256, lambda row: source(x * 32 + y * 8 + row % 8)), back, PLAIN)
    back = (ADAPTER_SCALE * dot(one_hot(128, 256, source), back, PLAIN)).astype(BF16)
    down = jnp.concatenate([gate_down[...], up_down[...]], 0).astype(BF16)
    adapter[...] = ADAPTER_SCALE * dot(mine.astype(BF16), down, PLAIN)[:8]
    reducer = dot(back, landed[:, :FEATS], BY_COLUMNS)
    keep[...] = jnp.where(core == 0, reducer[:16], reducer[16:])
    give[...] = jnp.where(core == 0, reducer[16:], reducer[:16])


def joined(marked, place, parts, *arrays):
    half = jax.ShapeDtypeStruct((16, FEATS), F32)
    return pl.pallas_call(
        joined_kernel,
        out_shape=(
            jax.ShapeDtypeStruct((32, 256), BF16),
            jax.ShapeDtypeStruct((8, FEATS), F32),
            half,
            half,
        ),
        in_specs=[pl.BlockSpec(memory_space=pl.ANY), SMEM] + [VMEM] * 7,
        out_specs=(VMEM,) * 4,
        compiler_params=pltpu.CompilerParams(vmem_limit_bytes=6 << 20),
        cost_estimate=pl.CostEstimate(flops=100_000_000_000, bytes_accessed=1_000_000, transcendentals=0),
        name="joined",
    )(marked, place, *parts, *arrays)


def expander_kernel(place, low_other, low_own, grads1, grads2, gate_scale, up_scale, gate_out, up_out):
    hid = place[2]
    low = jnp.concatenate([low_other[...], low_own[...]], 1)

    def order(blocks):
        pieces = [
            one_hot(
                32 * len(blocks),
                512,
                lambda row: c * 256 + (1 - half) * 128 + ((row // 32 + blocks[0]) ^ hid) * 32 + row % 32,
            )
            for c in range(2)
            for half in range(2)
        ]
        return jnp.concatenate(pieces, 0)

    low1 = dot(low, order((0, 1, 2)), BY_ROWS).astype(BF16)
    low2 = dot(low, order((3,)), BY_ROWS).astype(BF16)
    for k, (out, scale) in enumerate(((gate_out, gate_scale), (up_out, up_scale))):
        total = dot(low1, grads1[k], PLAIN) + dot(low2, grads2[k], PLAIN)
        out[...] = ADAPTER_SCALE * total[16 * k : 16 * k + 16] / scale[...].reshape(1, UNITS)


def expander(*arrays):
    out = jax.ShapeDtypeStruct((16, UNITS), F32)
    return pl.pallas_call(
        expander_kernel,
        out_shape=(out, out),
        in_specs=[SMEM] + [VMEM] * 6,
        out_specs=(VMEM, VMEM),
        compiler_params=pltpu.CompilerParams(vmem_limit_bytes=8 << 20),
        cost_estimate=pl.CostEstimate(flops=55_000_000, bytes_accessed=2_000_000, transcendentals=0),
        name="expander",
    )(*arrays)


def plane(value):
    return lax.all_to_all(value, ("x", "y"), split_axis=0, concat_axis=0, tiled=True)


def per_device(
    inputs, gate_grad, up_grad, gate_codes, up_codes, gate_scale, up_scale,
    gate_down, gate_lift, up_down, up_lift,
):
    hid = lax.axis_index("hid")
    x, zh, y, core = (lax.axis_index(name) for name in FFN)
    place = jnp.stack([zh, core, hid, x, y])
    downs = gate_down.T, up_down.T

    both, back_other, back_own = prep(
        place, gate_grad.T, up_grad.T, gate_scale, up_scale, gate_lift, up_lift
    )
    two, one = swap(both, "hid", 2), swap(both, "hid", 1)
    gathered = spread(inputs, back_own, swap(back_other, "core", 1))

    landed = plane(gathered)
    both, two, one, landed, marked = lax.optimization_barrier(
        (both, two, one, landed, mark(one, two))
    )
    middle = lax.ppermute(both, "hid", [(1, 2), (2, 1)])
    ends = lax.ppermute(two, "hid", [(1, 0), (2, 3)])

    codes = gate_codes.T, up_codes.T
    small = narrow(marked, landed, *downs)
    small_theirs = swap(small, "zh", 1)
    other1, own1, grads1 = product((both, one, two), 1, *codes)
    other1, middle, ends, marked = lax.optimization_barrier(
        (other1, middle, ends, mark(middle, ends))
    )
    other2, own2, grads2 = product((middle, ends), 2, *codes)
    sums = add_pairs(place, own1, swap(other1, "core", 1), own2, swap(other2, "core", 1))
    kept = plane(sums.reshape(256, FEATS)).astype(F32).reshape(16, 16, FEATS).sum(0)

    small = join_halves(small, small_theirs)
    low, adapter, keep, give = joined(marked, place, gather_over(small, "hid"), landed, *downs)
    low_other = swap(low, "core", 1)
    half = (keep + swap(give, "core", 1)).astype(BF16)
    mine = half.astype(F32) + swap(half, "zh", 1).astype(F32)
    theirs = swap(mine, "core", 1)
    gate_reducer, up_reducer = (jnp.where(core == k, mine, theirs) for k in range(2))
    gate_expander, up_expander = expander(
        place, low_other, low, grads1, grads2, gate_scale, up_scale
    )
    arrived = swap(kept[:8].astype(BF16), "zh", 1)
    rows = (kept[8:] + arrived.astype(F32) + adapter).astype(BF16)
    return rows, gate_reducer.T, gate_expander, up_reducer.T, up_expander


def solution(mesh):
    whole = Mesh(mesh.devices.reshape(4, 4, 2, 4, 2), ("hid",) + FFN)
    placed = (
        P(FFN, "hid"), P("hid", FFN), P("hid", FFN), P("hid", FFN), P("hid", FFN),
        P(FFN), P(FFN), P("hid", None), P(None, FFN), P("hid", None), P(None, FFN),
    )
    return jax.shard_map(
        per_device,
        mesh=whole,
        in_specs=placed,
        out_specs=(P(FFN, "hid"), P("hid", None), P(None, FFN), P("hid", None), P(None, FFN)),
        check_vma=False,
    )
```

time: 109 us -> 101 us (0.927)
  local copies, waits for them, and re-layouts: 17.7 us -> 6.01 us
  Pallas kernels: 13.8 us -> 25.2 us
  starting transfers between devices: 42 us -> 34.4 us
  waiting for transfers between devices: 31.1 us -> 32.5 us
    unnamed x52 -> x30, local copies, waits for them, and re-layouts: 16.9 us -> 5.39 us
    pallas_call x2, Pallas kernels: 5.98 us -> 15.4 us  [product(): pl.pallas_call(functools.partial(product_kernel, pairs), out_shape=(part,...]
    all_to_all x3 -> x2, waiting for transfers between devices: 1.08 us -> 9.08 us  [plane(): lax.all_to_all(value, ('x', 'y'), split_axis=0, concat_axis=0, tiled=True)]
    all_to_all x3 -> x2, starting transfers between devices: 21.9 us -> 14.8 us  [plane(): lax.all_to_all(value, ('x', 'y'), split_axis=0, concat_axis=0, tiled=True)]
    ppermute x12 -> x14, waiting for transfers between devices: 30.1 us -> 23.4 us  [swap(): return lax.ppermute(value, axis, [(i, i ^ mask) for i in range(size)])]
    ppermute x12 -> x14, starting transfers between devices: 18.2 us -> 17.7 us  [swap(): return lax.ppermute(value, axis, [(i, i ^ mask) for i in range(size)])]
    pallas_call x2 -> x5, Pallas kernels: 2.84 us -> 2.61 us  [the longest x1 1.75 us: add_pairs(): pl.pallas_call(pairs_kernel, out_shape=jax.ShapeDtypeStruct((4, 4, 16, FE...]
  transfers between devices with their start and end apart: 17 -> 18, of which waited for: 8 -> 7; matrix products, arithmetic and copies ran while one was open for 3% -> 1% of each run, Pallas kernels for 11% -> 23%
where the time goes in v5:
time: 101 us
  starting transfers between devices  34.4 us (34%)
  waiting for transfers between devices  32.5 us (32%)
  Pallas kernels  25.2 us (25%)
  local copies, waits for them, and re-layouts  6.01 us (6%)
  other arithmetic  1.54 us (2%)
    ppermute x14, waiting for transfers between devices, swap(): return lax.ppermute(value, axis, [(i, i ^ mask) for i in range(size)])  23.4 us
    ppermute x14, starting transfers between devices, swap(): return lax.ppermute(value, axis, [(i, i ^ mask) for i in range(size)])  17.7 us
    pallas_call x2, Pallas kernels, product(): pl.pallas_call(functools.partial(product_kernel, pairs), out_shape=(part,...  15.4 us
    all_to_all x2, starting transfers between devices, plane(): lax.all_to_all(value, ('x', 'y'), split_axis=0, concat_axis=0, tiled=True)  14.8 us
    all_to_all x2, waiting for transfers between devices, plane(): lax.all_to_all(value, ('x', 'y'), split_axis=0, concat_axis=0, tiled=True)  9.08 us
    unnamed x30, local copies, waits for them, and re-layouts  5.39 us
    pallas_call x1, Pallas kernels, prep(): pl.pallas_call(prep_kernel, out_shape=(both, back, back), in_specs=[SMEM]...  2.41 us
  transfers between devices with their start and end apart: 18, of which 7 were waited for; matrix products, arithmetic and copies ran while one was open for 1% of the time, Pallas kernels for 23%

profile of v5, /device:TPU:8, one launch (start us, length us, event | category | flops | bytes accessed | tf_op | source)
XLA Modules:
  0.0 100.6 jit_solution(5778334143971742656)
XLA Ops:
  0.6 0.6 stack.23.place
  1.3 2.4 %prep.1 = (bf16[2,2,2,32,832]{4,3,2,1,0:T(8,128)(2,1)}, f32[8,256]{1,0:T(8,128)}, f32[8,256]{1,0:T(8,128)}) custom-call(s32[5]{0:T(128)} %stack.23.place, bf16[832,128]{1,0:T(8,128)(2,1)} %bitcast.26, bf16[832,128]{1,0:T(8,128)(2,1)} %bitcast.27, f32[832]{0:T(1024)} %gate_scale.3, f32[832]{0:T(1024)} %up_scale.3, f32[16,832]{1,0:T(8,128)} %gate_lift.1, ...), custom_call_target="tpu_custom_call" | custom-call | flops 14000000 | bytes 1200000 | tf_op jit(solution)/shard_map/prep/pallas_call | solution.py:72
  3.7 3.3 %collective-permute-start = (bf16[2,2,2,32,832]{4,3,2,1,0:T(8,128)(2,1)}, bf16[2,2,2,32,832]{4,3,2,1,0:T(8,128)(2,1)}, u32[]{:S(2)}, u32[]{:S(2)}) collective-permute-start(bf16[2,2,2,32,832]{4,3,2,1,0:T(8,128)(2,1)} %get-tuple-element.32.refs_0_), channel_id=1, source_target_pairs={{0,128},{64,192},{128,0},{192,64},{1,129},{65,193},{129,1},{193,65... | collective-permute-start | bytes 1277960 | tf_op jit(solution)/shard_map/ppermute | solution.py:23
  6.9 1.9 %collective-permute-start.1 = (bf16[2,2,2,32,832]{4,3,2,1,0:T(8,128)(2,1)}, bf16[2,2,2,32,832]{4,3,2,1,0:T(8,128)(2,1)}, u32[]{:S(2)}, u32[]{:S(2)}) collective-permute-start(bf16[2,2,2,32,832]{4,3,2,1,0:T(8,128)(2,1)} %get-tuple-element.32.refs_0_), channel_id=1, source_target_pairs={{0,64},{64,0},{128,192},{192,128},{1,65},{65,1},{129,193},{193,129... | collective-permute-start | bytes 1277960 | tf_op jit(solution)/shard_map/ppermute | solution.py:23
  8.9 0.8 copy-done.13
  9.6 0.7 copy-done.14
  10.3 0.8 spread.1
  11.2 7.4 %all-to-all-start = ((bf16[16,8,2304]{2,1,0:T(8,128)(2,1)}), bf16[16,8,2304]{2,1,0:T(8,128)(2,1)}, u32[]{:S(2)}, u32[]{:S(2)}) async-start(bf16[16,8,2304]{2,1,0:T(8,128)(2,1)} %bitcast.7), calls=%async_computation | async-start | bytes 1179648 | tf_op jit(solution)/shard_map/all_to_all | solution.py:310
  18.6 9.8 %collective-permute-done.two.refs_2_ = bf16[2,2,2,32,832]{4,3,2,1,0:T(8,128)(2,1)} collective-permute-done((bf16[2,2,2,32,832]{4,3,2,1,0:T(8,128)(2,1)}, bf16[2,2,2,32,832]{4,3,2,1,0:T(8,128)(2,1)}, u32[]{:S(2)}, u32[]{:S(2)}) %collective-permute-start) | collective-permute-done | bytes 426016 | tf_op jit(solution)/shard_map/ppermute | solution.py:23
  28.5 1.1 %all-to-all-done = bf16[16,8,2304]{2,1,0:T(8,128)(2,1)} async-done(((bf16[16,8,2304]{2,1,0:T(8,128)(2,1)}), bf16[16,8,2304]{2,1,0:T(8,128)(2,1)}, u32[]{:S(2)}, u32[]{:S(2)}) %all-to-all-start) | async-done | bytes 589856 | tf_op jit(solution)/shard_map/all_to_all | solution.py:310
  29.6 0.7 collective-permute-start.3
  30.3 1.3 %collective-permute-start.4 = (bf16[2,2,2,32,832]{4,3,2,1,0:T(8,128)(2,1)}, bf16[2,2,2,32,832]{4,3,2,1,0:T(8,128)(2,1)S(1)}, u32[]{:S(2)}, u32[]{:S(2)}) collective-permute-start(bf16[2,2,2,32,832]{4,3,2,1,0:T(8,128)(2,1)} %collective-permute-done.two.refs_2_), channel_id=1, source_target_pairs={{64,0},{128,192},{65,1},{129,193},{66,2},{130,194},{67,3},{131,195... | collective-permute-start | bytes 1277960 | tf_op jit(solution)/shard_map/ppermute | solution.py:333
  31.6 0.9 copy-done.7
  32.5 1.3 %narrow.1.own = bf16[48,256]{1,0:T(8,128)(2,1)S(1)} custom-call(f32[8,128]{1,0:T(8,128)S(1)} %mark.2.marked, bf16[128,2304]{1,0:T(8,128)(2,1)} %bitcast.8.landed, f32[16,2048]{1,0:T(8,128)S(1)} %bitcast.22, f32[16,2048]{1,0:T(8,128)S(1)} %bitcast.24), custom_call_target="tpu_custom_call" | custom-call | flops 17000000 | bytes 900000 | tf_op jit(solution)/shard_map/narrow/pallas_call | solution.py:205
  33.8 5.3 %collective-permute-start.8 = (bf16[48,256]{1,0:T(8,128)(2,1)S(1)}, bf16[48,256]{1,0:T(8,128)(2,1)S(1)}, u32[]{:S(2)}, u32[]{:S(2)}) collective-permute-start(bf16[48,256]{1,0:T(8,128)(2,1)S(1)} %narrow.1.own), channel_id=1, source_target_pairs={{0,8},{8,0},{1,9},{9,1},{2,10},{10,2},{3,11},{11,3},{4,12},{12,4},... | collective-permute-start | bytes 73736 | tf_op jit(solution)/shard_map/ppermute | solution.py:23
  39.1 2.0 %copy-done.1 = bf16[2048,832]{0,1:T(8,128)(2,1)S(1)} copy-done((bf16[2048,832]{0,1:T(8,128)(2,1)S(1)}, bf16[2048,832]{0,1:T(8,128)(2,1)}, u32[]{:S(2)}) %copy-start.1) | copy-done | bytes 3407896
  41.1 1.0 %copy-done.12 = bf16[2,2,2,32,832]{4,3,2,1,0:T(8,128)(2,1)S(1)} copy-done((bf16[2,2,2,32,832]{4,3,2,1,0:T(8,128)(2,1)S(1)}, bf16[2,2,2,32,832]{4,3,2,1,0:T(8,128)(2,1)}, u32[]{:S(2)}) %copy-start.12) | copy-done | bytes 426008
  42.1 10.5 %product.2 = (bf16[192,2048]{1,0:T(8,128)(2,1)S(1)}, bf16[192,2048]{1,0:T(8,128)(2,1)S(1)}, bf16[2,384,832]{2,1,0:T(8,128)(2,1)S(1)}) custom-call(bf16[2,2,2,32,832]{4,3,2,1,0:T(8,128)(2,1)S(1)} %copy-done.12, bf16[2,2,2,32,832]{4,3,2,1,0:T(8,128)(2,1)} %collective-permute-done.1.one.refs_1_, bf16[2,2,2,32,832]{4,3,2,1,0:T(8,128)(2,1)} %collective-permute-done.two.refs_2_, ...), custom_call_target="tpu_custom_call" | custom-call | flops 2700000000 | bytes 8000000 | tf_op jit(solution)/shard_map/product/pallas_call | solution.py:119
  52.6 2.9 %collective-permute-start.9 = (bf16[48,256]{1,0:T(8,128)(2,1)S(1)}, bf16[48,256]{1,0:T(8,128)(2,1)S(1)}, u32[]{:S(2)}, u32[]{:S(2)}) collective-permute-start(bf16[48,256]{1,0:T(8,128)(2,1)S(1)} %join_halves.1.p0), channel_id=1, source_target_pairs={{0,64},{64,0},{128,192},{192,128},{1,65},{65,1},{129,193},{193,129... | collective-permute-start | bytes 73736 | tf_op jit(solution)/shard_map/ppermute | solution.py:23
  56.1 1.9 %collective-permute-start.11 = (bf16[48,256]{1,0:T(8,128)(2,1)S(1)}, bf16[48,256]{1,0:T(8,128)(2,1)S(1)}, u32[]{:S(2)}, u32[]{:S(2)}) collective-permute-start(bf16[48,256]{1,0:T(8,128)(2,1)S(1)} %join_halves.1.p0), channel_id=1, source_target_pairs={{0,192},{64,128},{128,64},{192,0},{1,193},{65,129},{129,65},{193,1... | collective-permute-start | bytes 73736 | tf_op jit(solution)/shard_map/ppermute | solution.py:23
  58.4 4.9 %product.3 = (bf16[64,2048]{1,0:T(8,128)(2,1)S(1)}, bf16[64,2048]{1,0:T(8,128)(2,1)S(1)}, bf16[2,128,832]{2,1,0:T(8,128)(2,1)S(1)}) custom-call(bf16[2,2,2,32,832]{4,3,2,1,0:T(8,128)(2,1)S(1)} %collective-permute-done.3.one.refs_0_, bf16[2,2,2,32,832]{4,3,2,1,0:T(8,128)(2,1)S(1)} %collective-permute-done.4.two.refs_1_, bf16[832,2048]{1,0:T(8,128)(2,1)S(1)} %bitcast.19, ...), custom_call_target="tpu_custom_call" | custom-call | flops 900000000 | bytes 8000000 | tf_op jit(solution)/shard_map/product/pallas_call | solution.py:119
  63.3 0.6 collective-permute-start.6
  64.0 1.6 %joined.1 = (bf16[32,256]{1,0:T(8,128)(2,1)S(1)}, f32[8,2048]{1,0:T(8,128)S(1)}, f32[16,2048]{1,0:T(8,128)S(1)}, f32[16,2048]{1,0:T(8,128)S(1)}) custom-call(f32[8,128]{1,0:T(8,128)S(1)} %mark.3.marked, s32[5]{0:T(128)S(1)} %copy-done.11, bf16[48,256]{1,0:T(8,128)(2,1)S(1)} %join_halves.1.p0, bf16[48,256]{1,0:T(8,128)(2,1)S(1)} %collective-permute-done.9.p1, ...), custom_call_target="tpu_custom_call" | custom-call | flops 99999997952 | bytes 1000000 | tf_op jit(solution)/shard_map/joined/pallas_call | solution.py:257
  65.7 1.8 %add_pairs.1 = bf16[4,4,16,2048]{3,2,1,0:T(8,128)(2,1)} custom-call(s32[5]{0:T(128)S(1)} %copy-done.11, bf16[192,2048]{1,0:T(8,128)(2,1)S(1)} %get-tuple-element.35.own1, bf16[192,2048]{1,0:T(8,128)(2,1)S(1)} %collective-permute-done.5.theirs1, bf16[64,2048]{1,0:T(8,128)(2,1)S(1)} %get-tuple-element.40.own2, bf16[64,2048]{1,0:T(8,128)(2,1)S(1)} %collective-permute-done.6.theirs2), custom_call_target="tpu_custom_call" | custom-call | flops 600000 | bytes 3200000 | tf_op jit(solution)/shard_map/add_pairs/pallas_call | solution.py:150
  67.4 7.4 %all-to-all-start.1 = ((bf16[16,16,2048]{2,1,0:T(8,128)(2,1)}), bf16[16,16,2048]{2,1,0:T(8,128)(2,1)S(1)}, u32[]{:S(2)}, u32[]{:S(2)}) async-start(bf16[16,16,2048]{2,1,0:T(8,128)(2,1)} %bitcast.11), calls=%async_computation.1 | async-start | bytes 2097152 | tf_op jit(solution)/shard_map/all_to_all | solution.py:310
  75.2 1.2 %collective-permute-done.15.low_other = bf16[32,256]{1,0:T(8,128)(2,1)S(1)} collective-permute-done((bf16[32,256]{1,0:T(8,128)(2,1)S(1)}, bf16[32,256]{1,0:T(8,128)(2,1)S(1)}, u32[]{:S(2)}, u32[]{:S(2)}) %collective-permute-start.15) | collective-permute-done | bytes 16416 | tf_op jit(solution)/shard_map/ppermute | solution.py:23
  76.4 1.9 %expander.1 = (f32[16,832]{1,0:T(8,128)}, f32[16,832]{1,0:T(8,128)}) custom-call(s32[5]{0:T(128)S(1)} %copy-done.11, bf16[32,256]{1,0:T(8,128)(2,1)S(1)} %collective-permute-done.15.low_other, bf16[32,256]{1,0:T(8,128)(2,1)S(1)} %get-tuple-element.48.low_own, bf16[2,384,832]{2,1,0:T(8,128)(2,1)S(1)} %copy-done.3, bf16[2,128,832]{2,1,0:T(8,128)(2,1)S(1)} %copy-done.5, ...), custom_call_target="tpu_custom_call" | custom-call | flops 55000000 | bytes 2000000 | tf_op jit(solution)/shard_map/expander/pallas_call | solution.py:298
  78.3 5.5 %collective-permute-done.13 = bf16[16,2048]{1,0:T(8,128)(2,1)S(1)} collective-permute-done((bf16[16,2048]{1,0:T(8,128)(2,1)S(1)}, bf16[16,2048]{1,0:T(8,128)(2,1)S(1)}, u32[]{:S(2)}, u32[]{:S(2)}) %collective-permute-start.13) | collective-permute-done | bytes 65568 | tf_op jit(solution)/shard_map/ppermute | solution.py:23
  83.9 8.0 %all-to-all-done.1 = bf16[16,16,2048]{2,1,0:T(8,128)(2,1)S(1)} async-done(((bf16[16,16,2048]{2,1,0:T(8,128)(2,1)}), bf16[16,16,2048]{2,1,0:T(8,128)(2,1)S(1)}, u32[]{:S(2)}, u32[]{:S(2)}) %all-to-all-start.1) | async-done | bytes 1048608 | tf_op jit(solution)/shard_map/all_to_all | solution.py:310
  92.4 0.7 select_bitcast_fusion
  93.2 6.8 %collective-permute-done.7 = bf16[8,2048]{1,0:T(8,128)(2,1)S(1)} collective-permute-done((bf16[8,2048]{1,0:T(8,128)(2,1)S(1)}, bf16[8,2048]{1,0:T(8,128)(2,1)S(1)}, u32[]{:S(2)}, u32[]{:S(2)}) %collective-permute-start.7) | collective-permute-done | bytes 32800 | tf_op jit(solution)/shard_map/ppermute | solution.py:23
  100.0 0.6 fusion.1
  (52 shorter events, 2.2 us)
Async XLA Ops:
  3.7 5.2 %collective-permute-start.2 = (f32[8,256]{1,0:T(8,128)}, f32[8,256]{1,0:T(8,128)S(1)}, u32[]{:S(2)}, u32[]{:S(2)}) collective-permute-start(f32[8,256]{1,0:T(8,128)} %get-tuple-element.31), channel_id=1, source_target_pairs={{0,1},{1,0},{2,3},{3,2},{4,5},{5,4},{6,7},{7,6},{8,9},{9,8},{10,11... | collective-permute-start | bytes 24584 | tf_op jit(solution)/shard_map/ppermute | solution.py:23
  3.7 24.7 %collective-permute-start = (bf16[2,2,2,32,832]{4,3,2,1,0:T(8,128)(2,1)}, bf16[2,2,2,32,832]{4,3,2,1,0:T(8,128)(2,1)}, u32[]{:S(2)}, u32[]{:S(2)}) collective-permute-start(bf16[2,2,2,32,832]{4,3,2,1,0:T(8,128)(2,1)} %get-tuple-element.32.refs_0_), channel_id=1, source_target_pairs={{0,128},{64,192},{128,0},{192,64},{1,129},{65,193},{129,1},{193,65... | collective-permute-start | bytes 1277960 | tf_op jit(solution)/shard_map/ppermute | solution.py:23
  6.9 21.5 %collective-permute-start.1 = (bf16[2,2,2,32,832]{4,3,2,1,0:T(8,128)(2,1)}, bf16[2,2,2,32,832]{4,3,2,1,0:T(8,128)(2,1)}, u32[]{:S(2)}, u32[]{:S(2)}) collective-permute-start(bf16[2,2,2,32,832]{4,3,2,1,0:T(8,128)(2,1)} %get-tuple-element.32.refs_0_), channel_id=1, source_target_pairs={{0,64},{64,0},{128,192},{192,128},{1,65},{65,1},{129,193},{193,129... | collective-permute-start | bytes 1277960 | tf_op jit(solution)/shard_map/ppermute | solution.py:23
  8.9 0.8 copy-start.13
  11.2 18.4 %all-to-all-start = ((bf16[16,8,2304]{2,1,0:T(8,128)(2,1)}), bf16[16,8,2304]{2,1,0:T(8,128)(2,1)}, u32[]{:S(2)}, u32[]{:S(2)}) async-start(bf16[16,8,2304]{2,1,0:T(8,128)(2,1)} %bitcast.7), calls=%async_computation | async-start | bytes 1179648 | tf_op jit(solution)/shard_map/all_to_all | solution.py:310
  18.6 13.0 %copy-start.6 = (f32[2048,16]{0,1:T(8,128)S(1)}, f32[2048,16]{0,1:T(8,128)}, u32[]{:S(2)}) copy-start(f32[2048,16]{0,1:T(8,128)} %param.18) | copy-start | bytes 393220
  18.6 20.6 %copy-start = (bf16[2048,832]{0,1:T(8,128)(2,1)S(1)}, bf16[2048,832]{0,1:T(8,128)(2,1)}, u32[]{:S(2)}) copy-start(bf16[2048,832]{0,1:T(8,128)(2,1)} %param.14) | copy-start | bytes 10223620
  29.6 28.5 %collective-permute-start.3 = (bf16[2,2,2,32,832]{4,3,2,1,0:T(8,128)(2,1)}, bf16[2,2,2,32,832]{4,3,2,1,0:T(8,128)(2,1)S(1)}, u32[]{:S(2)}, u32[]{:S(2)}) collective-permute-start(bf16[2,2,2,32,832]{4,3,2,1,0:T(8,128)(2,1)} %get-tuple-element.32.refs_0_), channel_id=1, source_target_pairs={{64,128},{128,64},{65,129},{129,65},{66,130},{130,66},{67,131},{13... | collective-permute-start | bytes 1277960 | tf_op jit(solution)/shard_map/ppermute | solution.py:332
  30.3 27.8 %collective-permute-start.4 = (bf16[2,2,2,32,832]{4,3,2,1,0:T(8,128)(2,1)}, bf16[2,2,2,32,832]{4,3,2,1,0:T(8,128)(2,1)S(1)}, u32[]{:S(2)}, u32[]{:S(2)}) collective-permute-start(bf16[2,2,2,32,832]{4,3,2,1,0:T(8,128)(2,1)} %collective-permute-done.two.refs_2_), channel_id=1, source_target_pairs={{64,0},{128,192},{65,1},{129,193},{66,2},{130,194},{67,3},{131,195... | collective-permute-start | bytes 1277960 | tf_op jit(solution)/shard_map/ppermute | solution.py:333
  31.6 0.9 copy-start.7
  33.8 18.8 %collective-permute-start.8 = (bf16[48,256]{1,0:T(8,128)(2,1)S(1)}, bf16[48,256]{1,0:T(8,128)(2,1)S(1)}, u32[]{:S(2)}, u32[]{:S(2)}) collective-permute-start(bf16[48,256]{1,0:T(8,128)(2,1)S(1)} %narrow.1.own), channel_id=1, source_target_pairs={{0,8},{8,0},{1,9},{9,1},{2,10},{10,2},{3,11},{11,3},{4,12},{12,4},... | collective-permute-start | bytes 73736 | tf_op jit(solution)/shard_map/ppermute | solution.py:23
  39.1 2.0 %copy-start.1 = (bf16[2048,832]{0,1:T(8,128)(2,1)S(1)}, bf16[2048,832]{0,1:T(8,128)(2,1)}, u32[]{:S(2)}) copy-start(bf16[2048,832]{0,1:T(8,128)(2,1)} %param.15) | copy-start | bytes 10223620
  41.1 1.0 %copy-start.12 = (bf16[2,2,2,32,832]{4,3,2,1,0:T(8,128)(2,1)S(1)}, bf16[2,2,2,32,832]{4,3,2,1,0:T(8,128)(2,1)}, u32[]{:S(2)}) copy-start(bf16[2,2,2,32,832]{4,3,2,1,0:T(8,128)(2,1)} %get-tuple-element.32.refs_0_) | copy-start | bytes 1277956
  52.6 5.5 %copy-start.2 = (bf16[2,384,832]{2,1,0:T(8,128)(2,1)}, bf16[2,384,832]{2,1,0:T(8,128)(2,1)S(1)}, u32[]{:S(2)}) copy-start(bf16[2,384,832]{2,1,0:T(8,128)(2,1)S(1)} %get-tuple-element.49.grads1) | copy-start | bytes 3833860
  52.6 11.3 %collective-permute-start.9 = (bf16[48,256]{1,0:T(8,128)(2,1)S(1)}, bf16[48,256]{1,0:T(8,128)(2,1)S(1)}, u32[]{:S(2)}, u32[]{:S(2)}) collective-permute-start(bf16[48,256]{1,0:T(8,128)(2,1)S(1)} %join_halves.1.p0), channel_id=1, source_target_pairs={{0,64},{64,0},{128,192},{192,128},{1,65},{65,1},{129,193},{193,129... | collective-permute-start | bytes 73736 | tf_op jit(solution)/shard_map/ppermute | solution.py:23
  55.6 8.3 %collective-permute-start.10 = (bf16[48,256]{1,0:T(8,128)(2,1)S(1)}, bf16[48,256]{1,0:T(8,128)(2,1)S(1)}, u32[]{:S(2)}, u32[]{:S(2)}) collective-permute-start(bf16[48,256]{1,0:T(8,128)(2,1)S(1)} %join_halves.1.p0), channel_id=1, source_target_pairs={{0,128},{64,192},{128,0},{192,64},{1,129},{65,193},{129,1},{193,65... | collective-permute-start | bytes 73736 | tf_op jit(solution)/shard_map/ppermute | solution.py:23
  56.1 7.8 %collective-permute-start.11 = (bf16[48,256]{1,0:T(8,128)(2,1)S(1)}, bf16[48,256]{1,0:T(8,128)(2,1)S(1)}, u32[]{:S(2)}, u32[]{:S(2)}) collective-permute-start(bf16[48,256]{1,0:T(8,128)(2,1)S(1)} %join_halves.1.p0), channel_id=1, source_target_pairs={{0,192},{64,128},{128,64},{192,0},{1,193},{65,129},{129,65},{193,1... | collective-permute-start | bytes 73736 | tf_op jit(solution)/shard_map/ppermute | solution.py:23
  58.1 5.9 %copy-start.8 = (f32[2048,16]{0,1:T(8,128)S(1)}, f32[2048,16]{0,1:T(8,128)}, u32[]{:S(2)}) copy-start(f32[2048,16]{0,1:T(8,128)} %param.20) | copy-start | bytes 393220
  58.1 5.9 %copy-start.11 = (s32[5]{0:T(128)S(1)}, s32[5]{0:T(128)}, u32[]{:S(2)}) copy-start(s32[5]{0:T(128)} %stack.23.place) | copy-start | bytes 64
  58.1 7.6 %collective-permute-start.5 = (bf16[192,2048]{1,0:T(8,128)(2,1)S(1)}, bf16[192,2048]{1,0:T(8,128)(2,1)S(1)}, u32[]{:S(2)}, u32[]{:S(2)}) collective-permute-start(bf16[192,2048]{1,0:T(8,128)(2,1)S(1)} %get-tuple-element.37), channel_id=1, source_target_pairs={{0,1},{1,0},{2,3},{3,2},{4,5},{5,4},{6,7},{7,6},{8,9},{9,8},{10,11... | collective-permute-start | bytes 2359304 | tf_op jit(solution)/shard_map/ppermute | solution.py:23
  63.3 2.2 %copy-start.4 = (bf16[2,128,832]{2,1,0:T(8,128)(2,1)}, bf16[2,128,832]{2,1,0:T(8,128)(2,1)S(1)}, u32[]{:S(2)}) copy-start(bf16[2,128,832]{2,1,0:T(8,128)(2,1)S(1)} %get-tuple-element.50.grads2) | copy-start | bytes 1277956
  63.3 2.3 %collective-permute-start.6 = (bf16[64,2048]{1,0:T(8,128)(2,1)S(1)}, bf16[64,2048]{1,0:T(8,128)(2,1)S(1)}, u32[]{:S(2)}, u32[]{:S(2)}) collective-permute-start(bf16[64,2048]{1,0:T(8,128)(2,1)S(1)} %get-tuple-element.41), channel_id=1, source_target_pairs={{0,1},{1,0},{2,3},{3,2},{4,5},{5,4},{6,7},{7,6},{8,9},{9,8},{10,11... | collective-permute-start | bytes 786440 | tf_op jit(solution)/shard_map/ppermute | solution.py:23
  65.5 10.9 %copy-start.3 = (bf16[2,384,832]{2,1,0:T(8,128)(2,1)S(1)}, bf16[2,384,832]{2,1,0:T(8,128)(2,1)}, u32[]{:S(2)}) copy-start(bf16[2,384,832]{2,1,0:T(8,128)(2,1)} %copy-done.2) | copy-start | bytes 3833860
  65.5 10.9 %copy-start.9 = (f32[832]{0:T(1024)S(1)}, f32[832]{0:T(1024)}, u32[]{:S(2)}) copy-start(f32[832]{0:T(1024)} %gate_scale.3) | copy-start | bytes 9988
  65.5 10.9 %copy-start.10 = (f32[832]{0:T(1024)S(1)}, f32[832]{0:T(1024)}, u32[]{:S(2)}) copy-start(f32[832]{0:T(1024)} %up_scale.3) | copy-start | bytes 9988
  65.5 10.9 %copy-start.5 = (bf16[2,128,832]{2,1,0:T(8,128)(2,1)S(1)}, bf16[2,128,832]{2,1,0:T(8,128)(2,1)}, u32[]{:S(2)}) copy-start(bf16[2,128,832]{2,1,0:T(8,128)(2,1)} %copy-done.4) | copy-start | bytes 1277956
  65.6 9.3 %collective-permute-start.12 = (f32[16,2048]{1,0:T(8,128)S(1)}, f32[16,2048]{1,0:T(8,128)S(1)}, u32[]{:S(2)}, u32[]{:S(2)}) collective-permute-start(f32[16,2048]{1,0:T(8,128)S(1)} %get-tuple-element.47), channel_id=1, source_target_pairs={{0,1},{1,0},{2,3},{3,2},{4,5},{5,4},{6,7},{7,6},{8,9},{9,8},{10,11... | collective-permute-start | bytes 393224 | tf_op jit(solution)/shard_map/ppermute | solution.py:23
  67.4 24.5 %all-to-all-start.1 = ((bf16[16,16,2048]{2,1,0:T(8,128)(2,1)}), bf16[16,16,2048]{2,1,0:T(8,128)(2,1)S(1)}, u32[]{:S(2)}, u32[]{:S(2)}) async-start(bf16[16,16,2048]{2,1,0:T(8,128)(2,1)} %bitcast.11), calls=%async_computation.1 | async-start | bytes 2097152 | tf_op jit(solution)/shard_map/all_to_all | solution.py:310
  74.9 9.0 %collective-permute-start.13 = (bf16[16,2048]{1,0:T(8,128)(2,1)S(1)}, bf16[16,2048]{1,0:T(8,128)(2,1)S(1)}, u32[]{:S(2)}, u32[]{:S(2)}) collective-permute-start(bf16[16,2048]{1,0:T(8,128)(2,1)S(1)} %add_convert_fusion), channel_id=1, source_target_pairs={{0,8},{8,0},{1,9},{9,1},{2,10},{10,2},{3,11},{11,3},{4,12},{12,4},... | collective-permute-start | bytes 196616 | tf_op jit(solution)/shard_map/ppermute | solution.py:23
  75.2 1.2 %collective-permute-start.15 = (bf16[32,256]{1,0:T(8,128)(2,1)S(1)}, bf16[32,256]{1,0:T(8,128)(2,1)S(1)}, u32[]{:S(2)}, u32[]{:S(2)}) collective-permute-start(bf16[32,256]{1,0:T(8,128)(2,1)S(1)} %get-tuple-element.48.low_own), channel_id=1, source_target_pairs={{0,1},{1,0},{2,3},{3,2},{4,5},{5,4},{6,7},{7,6},{8,9},{9,8},{10,11... | collective-permute-start | bytes 49160 | tf_op jit(solution)/shard_map/ppermute | solution.py:23
  83.8 8.6 %collective-permute-start.14 = (f32[16,2048]{1,0:T(8,128)S(1)}, f32[16,2048]{1,0:T(8,128)S(1)}, u32[]{:S(2)}, u32[]{:S(2)}) collective-permute-start(f32[16,2048]{1,0:T(8,128)S(1)} %convert_add_fusion), channel_id=1, source_target_pairs={{0,1},{1,0},{2,3},{3,2},{4,5},{5,4},{6,7},{7,6},{8,9},{9,8},{10,11... | collective-permute-start | bytes 393224 | tf_op jit(solution)/shard_map/ppermute | solution.py:23
  92.1 7.9 %collective-permute-start.7 = (bf16[8,2048]{1,0:T(8,128)(2,1)S(1)}, bf16[8,2048]{1,0:T(8,128)(2,1)S(1)}, u32[]{:S(2)}, u32[]{:S(2)}) collective-permute-start(bf16[8,2048]{1,0:T(8,128)(2,1)S(1)} %slice.17), channel_id=1, source_target_pairs={{0,8},{8,0},{1,9},{9,1},{2,10},{10,2},{3,11},{11,3},{4,12},{12,4},... | collective-permute-start | bytes 98312 | tf_op jit(solution)/shard_map/ppermute | solution.py:23
  (1 other events, 0.7 us)

commit v6 on v5

--- a/solution.py
+++ b/solution.py
@@ -10,7 +10,7 @@
 ADAPTER_SCALE = 2.0
 FFN = ("x", "zh", "y", "core")
 F32, BF16 = jnp.float32, jnp.bfloat16
-UNITS, FEATS, STEP = 832, 2048, 256
+UNITS, FEATS, STEP, CHUNK = 832, 2048, 256, 512
 PLAIN = (((1,), (0,)), ((), ()))
 BY_ROWS = (((1,), (1,)), ((), ()))
 BY_COLUMNS = (((0,), (0,)), ((), ()))
@@ -21,6 +21,10 @@
 def swap(value, axis, mask):
     size = lax.axis_size(axis)
     return lax.ppermute(value, axis, [(i, i ^ mask) for i in range(size)])
+
+
+def swap_each(values, axis):
+    return [swap(value, axis, k) if k else value for k, value in enumerate(values)]
 
 
 def gather_over(value, axis):
@@ -82,17 +86,15 @@
 def product_kernel(pairs, *refs):
     blocks, (gate_codes, up_codes, other, own, grads, gate_held, up_held, sems) = refs[:-8], refs[-8:]
     count = len(blocks) // pairs
-    copies = []
-    for i, start in enumerate(range(0, FEATS, STEP)):
-        columns = pl.ds(start, STEP)
-        copies.append(
-            [
-                pltpu.make_async_copy(source.at[:, columns], held.at[:, columns], sems.at[k, i])
-                for k, (source, held) in enumerate(((gate_codes, gate_held), (up_codes, up_held)))
-            ]
-        )
-        for copy in copies[-1]:
-            copy.start()
+    def copies(i):
+        columns = pl.ds(i * CHUNK, CHUNK)
+        return [
+            pltpu.make_async_copy(source.at[:, columns], held.at[:, columns], sems.at[k, i])
+            for k, (source, held) in enumerate(((gate_codes, gate_held), (up_codes, up_held)))
+        ]
+
+    for copy in copies(0) + copies(1):
+        copy.start()
     for k in range(2):
         for c in range(2):
             for half in range(2):
@@ -103,10 +105,15 @@
                     row = ((c * 2 + half) * count + j) * 32
                     grads[k, row : row + 32] = value
     gate, up, cut = grads[0], grads[1], 64 * count
-    for i, start in enumerate(range(0, FEATS, STEP)):
+    for start in range(0, FEATS, STEP):
         columns = slice(start, start + STEP)
-        for copy in copies[i]:
-            copy.wait()
+        if start % CHUNK == 0:
+            i = start // CHUNK
+            for copy in copies(i):
+                copy.wait()
+            if i + 2 < FEATS // CHUNK:
+                for copy in copies(i + 2):
+                    copy.start()
         total = dot(gate, gate_held[:, columns], PLAIN) + dot(up, up_held[:, columns], PLAIN)
         other[:, columns] = total[:cut].astype(BF16)
         own[:, columns] = total[cut:].astype(BF16)
@@ -124,9 +131,9 @@
         scratch_shapes=[
             pltpu.VMEM((UNITS, FEATS), BF16),
             pltpu.VMEM((UNITS, FEATS), BF16),
-            pltpu.SemaphoreType.DMA((2, FEATS // STEP)),
+            pltpu.SemaphoreType.DMA((2, FEATS // CHUNK)),
         ],
-        compiler_params=pltpu.CompilerParams(vmem_limit_bytes=20 << 20),
+        compiler_params=pltpu.CompilerParams(vmem_limit_bytes=44 << 20),
         cost_estimate=pl.CostEstimate(
             flops=900_000_000 * count, bytes_accessed=8_000_000, transcendentals=0
         ),
@@ -134,27 +141,53 @@
     )(*blocks, gate_codes, up_codes)
 
 
-def pairs_kernel(place, own1, theirs1, own2, theirs2, out):
-    for j in range(4):
-        halves = []
-        for half in range(2):
+def pairs_kernel(place, own1, theirs1, own2, theirs2, *refs):
+    outs, sums = refs[:8], refs[8]
+    hid_x, y = place[2] ^ place[3], place[4]
+    for half in range(2):
+        for j in range(4):
             own, theirs, row = (own1, theirs1, (half * 3 + j) * 32) if j < 3 else (own2, theirs2, half * 32)
             rows = slice(row, row + 32)
-            halves.append(own[rows].astype(F32) + theirs[rows].astype(F32))
-        for k in range(4):
-            rows = slice(8 * k, 8 * k + 8)
-            out[place[2] ^ j, k] = jnp.concatenate([half[rows] for half in halves], 0).astype(BF16)
+            sums[half, j] = own[rows].astype(F32) + theirs[rows].astype(F32)
+    for k in range(4):
+        outs[k][...] = sums[0, hid_x ^ k].astype(BF16)
+        rows = pl.ds(pl.multiple_of((y ^ k) * 8, 8), 8)
+        outs[4 + k][...] = jnp.concatenate([sums[1, j, rows] for j in range(4)], 0).astype(BF16)
 
 
 def add_pairs(*arrays):
     return pl.pallas_call(
         pairs_kernel,
-        out_shape=jax.ShapeDtypeStruct((4, 4, 16, FEATS), BF16),
+        out_shape=(jax.ShapeDtypeStruct((32, FEATS), BF16),) * 8,
         in_specs=[SMEM] + [VMEM] * 4,
-        out_specs=VMEM,
-        compiler_params=pltpu.CompilerParams(vmem_limit_bytes=8 << 20),
+        out_specs=(VMEM,) * 8,
+        scratch_shapes=[pltpu.VMEM((2, 4, 32, FEATS), F32)],
+        compiler_params=pltpu.CompilerParams(vmem_limit_bytes=12 << 20),
         cost_estimate=pl.CostEstimate(flops=600_000, bytes_accessed=3_200_000, transcendentals=0),
         name="add_pairs",
+    )(*arrays)
+
+
+def turn_kernel(place, *refs):
+    parts, outs, far, near = refs[:8], refs[8:16], refs[16], refs[17]
+    hid_x, y = place[2] ^ place[3], place[4]
+    far[...] = sum(part[...].astype(F32) for part in parts[:4])
+    near[...] = sum(part[...].astype(F32) for part in parts[4:]).reshape(4, 8, FEATS)
+    for k in range(4):
+        outs[k][...] = far[pl.ds(pl.multiple_of((y ^ k) * 8, 8), 8)]
+        outs[4 + k][...] = near[hid_x ^ k]
+
+
+def turn(*arrays):
+    return pl.pallas_call(
+        turn_kernel,
+        out_shape=(jax.ShapeDtypeStruct((8, FEATS), F32),) * 8,
+        in_specs=[SMEM] + [VMEM] * 8,
+        out_specs=(VMEM,) * 8,
+        scratch_shapes=[pltpu.VMEM((32, FEATS), F32), pltpu.VMEM((4, 8, FEATS), F32)],
+        compiler_params=pltpu.CompilerParams(vmem_limit_bytes=8 << 20),
+        cost_estimate=pl.CostEstimate(flops=600_000, bytes_accessed=2_000_000, transcendentals=0),
+        name="turn",
     )(*arrays)
 
 
@@ -341,7 +374,8 @@
     )
     other2, own2, grads2 = product((middle, ends), 2, *codes)
     sums = add_pairs(place, own1, swap(other1, "core", 1), own2, swap(other2, "core", 1))
-    kept = plane(sums.reshape(256, FEATS)).astype(F32).reshape(16, 16, FEATS).sum(0)
+    sums = turn(place, *swap_each(sums[:4], "x"), *swap_each(sums[4:], "y"))
+    kept = sum(swap_each(sums[:4], "y")), sum(swap_each(sums[4:], "x"))
 
     small = join_halves(small, small_theirs)
     low, adapter, keep, give = joined(marked, place, gather_over(small, "hid"), landed, *downs)
@@ -353,8 +387,8 @@
     gate_expander, up_expander = expander(
         place, low_other, low, grads1, grads2, gate_scale, up_scale
     )
-    arrived = swap(kept[:8].astype(BF16), "zh", 1)
-    rows = (kept[8:] + arrived.astype(F32) + adapter).astype(BF16)
+    arrived = swap(kept[0].astype(BF16), "zh", 1)
+    rows = (kept[1] + arrived.astype(F32) + adapter).astype(BF16)
     return rows, gate_reducer.T, gate_expander, up_reducer.T, up_expander
 
 

time: 101 us -> 96.9 us (0.959)
  the two profiles are of different devices: /device:TPU:8 before, /device:TPU:6 now
where the time goes in v6:
time: 96.9 us; the launch traced here: 96.3 us
  starting transfers between devices  46.7 us (48%)
  waiting for transfers between devices  21.5 us (22%)
  Pallas kernels  19.5 us (20%)
  local copies, waits for them, and re-layouts  6.24 us (6%)
  other arithmetic  1.42 us (1%)
    ppermute x26, starting transfers between devices, swap(): return lax.ppermute(value, axis, [(i, i ^ mask) for i in range(size)])  37.3 us
    ppermute x26, waiting for transfers between devices, swap(): return lax.ppermute(value, axis, [(i, i ^ mask) for i in range(size)])  21.1 us
    pallas_call x2, Pallas kernels, product(): pl.pallas_call(functools.partial(product_kernel, pairs), out_shape=(part,...  9.88 us
    all_to_all x1, starting transfers between devices, plane(): lax.all_to_all(value, ('x', 'y'), split_axis=0, concat_axis=0, tiled=True)  7.42 us
    unnamed x30, local copies, waits for them, and re-layouts  5.56 us
    pallas_call x1, Pallas kernels, prep(): pl.pallas_call(prep_kernel, out_shape=(both, back, back), in_specs=[SMEM]...  2.41 us
  transfers between devices with their start and end apart: 29, of which 10 were waited for; matrix products, arithmetic and copies ran while one was open for 1% of the time, Pallas kernels for 18%

profile of v6, /device:TPU:6, one launch (start us, length us, event | category | flops | bytes accessed | tf_op | source)
XLA Modules:
  0.0 96.3 jit_solution(6543249479246912044)
XLA Ops:
  1.3 2.4 %prep.1 = (bf16[2,2,2,32,832]{4,3,2,1,0:T(8,128)(2,1)}, f32[8,256]{1,0:T(8,128)}, f32[8,256]{1,0:T(8,128)}) custom-call(s32[5]{0:T(128)} %stack.23.place, bf16[832,128]{1,0:T(8,128)(2,1)} %bitcast.25, bf16[832,128]{1,0:T(8,128)(2,1)} %bitcast.26, f32[832]{0:T(1024)} %gate_scale.3, f32[832]{0:T(1024)} %up_scale.3, f32[16,832]{1,0:T(8,128)} %gate_lift.1, ...), custom_call_target="tpu_custom_call" | custom-call | flops 14000000 | bytes 1200000 | tf_op jit(solution)/shard_map/prep/pallas_call | solution.py:76
  3.7 3.3 %collective-permute-start = (bf16[2,2,2,32,832]{4,3,2,1,0:T(8,128)(2,1)}, bf16[2,2,2,32,832]{4,3,2,1,0:T(8,128)(2,1)}, u32[]{:S(2)}, u32[]{:S(2)}) collective-permute-start(bf16[2,2,2,32,832]{4,3,2,1,0:T(8,128)(2,1)} %get-tuple-element.48.refs_0_), channel_id=1, source_target_pairs={{0,128},{64,192},{128,0},{192,64},{1,129},{65,193},{129,1},{193,65... | collective-permute-start | bytes 1277960 | tf_op jit(solution)/shard_map/ppermute | solution.py:23
  7.0 1.9 %collective-permute-start.1 = (bf16[2,2,2,32,832]{4,3,2,1,0:T(8,128)(2,1)}, bf16[2,2,2,32,832]{4,3,2,1,0:T(8,128)(2,1)}, u32[]{:S(2)}, u32[]{:S(2)}) collective-permute-start(bf16[2,2,2,32,832]{4,3,2,1,0:T(8,128)(2,1)} %get-tuple-element.48.refs_0_), channel_id=1, source_target_pairs={{0,64},{64,0},{128,192},{192,128},{1,65},{65,1},{129,193},{193,129... | collective-permute-start | bytes 1277960 | tf_op jit(solution)/shard_map/ppermute | solution.py:23
  11.2 7.4 %all-to-all-start = ((bf16[16,8,2304]{2,1,0:T(8,128)(2,1)}), bf16[16,8,2304]{2,1,0:T(8,128)(2,1)}, u32[]{:S(2)}, u32[]{:S(2)}) async-start(bf16[16,8,2304]{2,1,0:T(8,128)(2,1)} %bitcast.7), calls=%async_computation | async-start | bytes 1179648 | tf_op jit(solution)/shard_map/all_to_all | solution.py:343
  18.7 9.7 %collective-permute-done.two.refs_2_ = bf16[2,2,2,32,832]{4,3,2,1,0:T(8,128)(2,1)} collective-permute-done((bf16[2,2,2,32,832]{4,3,2,1,0:T(8,128)(2,1)}, bf16[2,2,2,32,832]{4,3,2,1,0:T(8,128)(2,1)}, u32[]{:S(2)}, u32[]{:S(2)}) %collective-permute-start) | collective-permute-done | bytes 426016 | tf_op jit(solution)/shard_map/ppermute | solution.py:23
  29.7 1.3 %collective-permute-start.4 = (bf16[2,2,2,32,832]{4,3,2,1,0:T(8,128)(2,1)}, bf16[2,2,2,32,832]{4,3,2,1,0:T(8,128)(2,1)S(1)}, u32[]{:S(2)}, u32[]{:S(2)}) collective-permute-start(bf16[2,2,2,32,832]{4,3,2,1,0:T(8,128)(2,1)} %collective-permute-done.two.refs_2_), channel_id=1, source_target_pairs={{64,0},{128,192},{65,1},{129,193},{66,2},{130,194},{67,3},{131,195... | collective-permute-start | bytes 1277960 | tf_op jit(solution)/shard_map/ppermute | solution.py:366
  31.0 0.9 copy-done.7
  31.9 1.3 %narrow.1.own = bf16[48,256]{1,0:T(8,128)(2,1)S(1)} custom-call(f32[8,128]{1,0:T(8,128)S(1)} %mark.2.marked, bf16[128,2304]{1,0:T(8,128)(2,1)} %bitcast.8.landed, f32[16,2048]{1,0:T(8,128)S(1)} %bitcast.21, f32[16,2048]{1,0:T(8,128)S(1)} %bitcast.23), custom_call_target="tpu_custom_call" | custom-call | flops 17000000 | bytes 900000 | tf_op jit(solution)/shard_map/narrow/pallas_call | solution.py:238
  33.2 6.0 %collective-permute-start.20 = (bf16[48,256]{1,0:T(8,128)(2,1)S(1)}, bf16[48,256]{1,0:T(8,128)(2,1)S(1)}, u32[]{:S(2)}, u32[]{:S(2)}) collective-permute-start(bf16[48,256]{1,0:T(8,128)(2,1)S(1)} %narrow.1.own), channel_id=1, source_target_pairs={{0,8},{8,0},{1,9},{9,1},{2,10},{10,2},{3,11},{11,3},{4,12},{12,4},... | collective-permute-start | bytes 73736 | tf_op jit(solution)/shard_map/ppermute | solution.py:23
  39.2 1.0 %copy-done.12 = bf16[2,2,2,32,832]{4,3,2,1,0:T(8,128)(2,1)S(1)} copy-done((bf16[2,2,2,32,832]{4,3,2,1,0:T(8,128)(2,1)S(1)}, bf16[2,2,2,32,832]{4,3,2,1,0:T(8,128)(2,1)}, u32[]{:S(2)}) %copy-start.12) | copy-done | bytes 426008
  40.2 6.7 %product.2 = (bf16[192,2048]{1,0:T(8,128)(2,1)S(1)}, bf16[192,2048]{1,0:T(8,128)(2,1)S(1)}, bf16[2,384,832]{2,1,0:T(8,128)(2,1)S(1)}) custom-call(bf16[2,2,2,32,832]{4,3,2,1,0:T(8,128)(2,1)S(1)} %copy-done.12, bf16[2,2,2,32,832]{4,3,2,1,0:T(8,128)(2,1)} %collective-permute-done.1.one.refs_1_, bf16[2,2,2,32,832]{4,3,2,1,0:T(8,128)(2,1)} %collective-permute-done.two.refs_2_, ...), custom_call_target="tpu_custom_call" | custom-call | flops 2700000000 | bytes 8000000 | tf_op jit(solution)/shard_map/product/pallas_call | solution.py:126
  46.9 1.1 %copy-done.2 = bf16[2,384,832]{2,1,0:T(8,128)(2,1)} copy-done((bf16[2,384,832]{2,1,0:T(8,128)(2,1)}, bf16[2,384,832]{2,1,0:T(8,128)(2,1)S(1)}, u32[]{:S(2)}) %copy-start.2) | copy-done | bytes 1277976
  48.0 3.2 %collective-permute-start.21 = (bf16[48,256]{1,0:T(8,128)(2,1)S(1)}, bf16[48,256]{1,0:T(8,128)(2,1)S(1)}, u32[]{:S(2)}, u32[]{:S(2)}) collective-permute-start(bf16[48,256]{1,0:T(8,128)(2,1)S(1)} %join_halves.1.p0), channel_id=1, source_target_pairs={{0,64},{64,0},{128,192},{192,128},{1,65},{65,1},{129,193},{193,129... | collective-permute-start | bytes 73736 | tf_op jit(solution)/shard_map/ppermute | solution.py:23
  51.8 1.9 %collective-permute-start.23 = (bf16[48,256]{1,0:T(8,128)(2,1)S(1)}, bf16[48,256]{1,0:T(8,128)(2,1)S(1)}, u32[]{:S(2)}, u32[]{:S(2)}) collective-permute-start(bf16[48,256]{1,0:T(8,128)(2,1)S(1)} %join_halves.1.p0), channel_id=1, source_target_pairs={{0,192},{64,128},{128,64},{192,0},{1,193},{65,129},{129,65},{193,1... | collective-permute-start | bytes 73736 | tf_op jit(solution)/shard_map/ppermute | solution.py:23
  53.8 3.2 %product.3 = (bf16[64,2048]{1,0:T(8,128)(2,1)S(1)}, bf16[64,2048]{1,0:T(8,128)(2,1)S(1)}, bf16[2,128,832]{2,1,0:T(8,128)(2,1)S(1)}) custom-call(bf16[2,2,2,32,832]{4,3,2,1,0:T(8,128)(2,1)S(1)} %collective-permute-done.3.one.refs_0_, bf16[2,2,2,32,832]{4,3,2,1,0:T(8,128)(2,1)S(1)} %collective-permute-done.4.two.refs_1_, bf16[832,2048]{1,0:T(8,128)(2,1)S(1)} %bitcast.18, ...), custom_call_target="tpu_custom_call" | custom-call | flops 900000000 | bytes 8000000 | tf_op jit(solution)/shard_map/product/pallas_call | solution.py:126
  57.7 1.5 %joined.1 = (bf16[32,256]{1,0:T(8,128)(2,1)S(1)}, f32[8,2048]{1,0:T(8,128)S(1)}, f32[16,2048]{1,0:T(8,128)S(1)}, f32[16,2048]{1,0:T(8,128)S(1)}) custom-call(f32[8,128]{1,0:T(8,128)S(1)} %mark.3.marked, s32[5]{0:T(128)S(1)} %copy-done.11, bf16[48,256]{1,0:T(8,128)(2,1)S(1)} %join_halves.1.p0, bf16[48,256]{1,0:T(8,128)(2,1)S(1)} %collective-permute-done.21.p1, ...), custom_call_target="tpu_custom_call" | custom-call | flops 99999997952 | bytes 1000000 | tf_op jit(solution)/shard_map/joined/pallas_call | solution.py:290
  59.6 0.9 add_pairs.1
  60.5 1.1 %collective-permute-start.7 = (bf16[32,2048]{1,0:T(8,128)(2,1)S(1)}, bf16[32,2048]{1,0:T(8,128)(2,1)S(1)}, u32[]{:S(2)}, u32[]{:S(2)}) collective-permute-start(bf16[32,2048]{1,0:T(8,128)(2,1)S(1)} %get-tuple-element.59), channel_id=1, source_target_pairs={{0,16},{16,0},{32,48},{48,32},{1,17},{17,1},{33,49},{49,33},{2,18}... | collective-permute-start | bytes 393224 | tf_op jit(solution)/shard_map/ppermute | solution.py:23
  61.6 1.6 %collective-permute-start.8 = (bf16[32,2048]{1,0:T(8,128)(2,1)S(1)}, bf16[32,2048]{1,0:T(8,128)(2,1)S(1)}, u32[]{:S(2)}, u32[]{:S(2)}) collective-permute-start(bf16[32,2048]{1,0:T(8,128)(2,1)S(1)} %get-tuple-element.60), channel_id=1, source_target_pairs={{0,32},{16,48},{32,0},{48,16},{1,33},{17,49},{33,1},{49,17},{2,34}... | collective-permute-start | bytes 393224 | tf_op jit(solution)/shard_map/ppermute | solution.py:23
  63.2 2.3 %collective-permute-start.9 = (bf16[32,2048]{1,0:T(8,128)(2,1)S(1)}, bf16[32,2048]{1,0:T(8,128)(2,1)S(1)}, u32[]{:S(2)}, u32[]{:S(2)}) collective-permute-start(bf16[32,2048]{1,0:T(8,128)(2,1)S(1)} %get-tuple-element.61), channel_id=1, source_target_pairs={{0,48},{16,32},{32,16},{48,0},{1,49},{17,33},{33,17},{49,1},{2,50}... | collective-permute-start | bytes 393224 | tf_op jit(solution)/shard_map/ppermute | solution.py:23
  65.5 1.6 %collective-permute-start.10 = (bf16[32,2048]{1,0:T(8,128)(2,1)S(1)}, bf16[32,2048]{1,0:T(8,128)(2,1)S(1)}, u32[]{:S(2)}, u32[]{:S(2)}) collective-permute-start(bf16[32,2048]{1,0:T(8,128)(2,1)S(1)} %get-tuple-element.63), channel_id=1, source_target_pairs={{0,2},{2,0},{4,6},{6,4},{1,3},{3,1},{5,7},{7,5},{8,10},{10,8},{12,... | collective-permute-start | bytes 393224 | tf_op jit(solution)/shard_map/ppermute | solution.py:23
  67.1 2.9 %collective-permute-start.11 = (bf16[32,2048]{1,0:T(8,128)(2,1)S(1)}, bf16[32,2048]{1,0:T(8,128)(2,1)S(1)}, u32[]{:S(2)}, u32[]{:S(2)}) collective-permute-start(bf16[32,2048]{1,0:T(8,128)(2,1)S(1)} %get-tuple-element.64), channel_id=1, source_target_pairs={{0,4},{2,6},{4,0},{6,2},{1,5},{3,7},{5,1},{7,3},{8,12},{10,14},{12... | collective-permute-start | bytes 393224 | tf_op jit(solution)/shard_map/ppermute | solution.py:23
  70.2 0.9 collective-permute-start.25
  71.1 1.0 %copy-done.5 = bf16[2,128,832]{2,1,0:T(8,128)(2,1)S(1)} copy-done((bf16[2,128,832]{2,1,0:T(8,128)(2,1)S(1)}, bf16[2,128,832]{2,1,0:T(8,128)(2,1)}, u32[]{:S(2)}) %copy-start.5) | copy-done | bytes 426008
  72.1 1.9 %expander.1 = (f32[16,832]{1,0:T(8,128)}, f32[16,832]{1,0:T(8,128)}) custom-call(s32[5]{0:T(128)S(1)} %copy-done.11, bf16[32,256]{1,0:T(8,128)(2,1)S(1)} %collective-permute-done.27.low_other, bf16[32,256]{1,0:T(8,128)(2,1)S(1)} %get-tuple-element.80.low_own, bf16[2,384,832]{2,1,0:T(8,128)(2,1)S(1)} %copy-done.3, bf16[2,128,832]{2,1,0:T(8,128)(2,1)S(1)} %copy-done.5, ...), custom_call_target="tpu_custom_call" | custom-call | flops 55000000 | bytes 2000000 | tf_op jit(solution)/shard_map/expander/pallas_call | solution.py:331
  74.0 2.2 %collective-permute-done.11.refs_6_ = bf16[32,2048]{1,0:T(8,128)(2,1)S(1)} collective-permute-done((bf16[32,2048]{1,0:T(8,128)(2,1)S(1)}, bf16[32,2048]{1,0:T(8,128)(2,1)S(1)}, u32[]{:S(2)}, u32[]{:S(2)}) %collective-permute-start.11) | collective-permute-done | bytes 131104 | tf_op jit(solution)/shard_map/ppermute | solution.py:23
  76.2 2.1 %collective-permute-done.12.refs_7_ = bf16[32,2048]{1,0:T(8,128)(2,1)S(1)} collective-permute-done((bf16[32,2048]{1,0:T(8,128)(2,1)S(1)}, bf16[32,2048]{1,0:T(8,128)(2,1)S(1)}, u32[]{:S(2)}, u32[]{:S(2)}) %collective-permute-start.12) | collective-permute-done | bytes 131104 | tf_op jit(solution)/shard_map/ppermute | solution.py:23
  79.7 0.9 collective-permute-start.17
  80.6 2.6 %collective-permute-start.16 = (f32[8,2048]{1,0:T(8,128)S(1)}, f32[8,2048]{1,0:T(8,128)S(1)}, u32[]{:S(2)}, u32[]{:S(2)}) collective-permute-start(f32[8,2048]{1,0:T(8,128)S(1)} %get-tuple-element.71), channel_id=1, source_target_pairs={{0,2},{2,0},{4,6},{6,4},{1,3},{3,1},{5,7},{7,5},{8,10},{10,8},{12,... | collective-permute-start | bytes 196616 | tf_op jit(solution)/shard_map/ppermute | solution.py:23
  85.5 2.1 %collective-permute-start.13 = (f32[8,2048]{1,0:T(8,128)S(1)}, f32[8,2048]{1,0:T(8,128)S(1)}, u32[]{:S(2)}, u32[]{:S(2)}) collective-permute-start(f32[8,2048]{1,0:T(8,128)S(1)} %get-tuple-element.67), channel_id=1, source_target_pairs={{0,16},{16,0},{32,48},{48,32},{1,17},{17,1},{33,49},{49,33},{2,18}... | collective-permute-start | bytes 196616 | tf_op jit(solution)/shard_map/ppermute | solution.py:23
  87.6 1.3 %collective-permute-start.19 = (bf16[8,2048]{1,0:T(8,128)(2,1)S(1)}, bf16[8,2048]{1,0:T(8,128)(2,1)S(1)}, u32[]{:S(2)}, u32[]{:S(2)}) collective-permute-start(bf16[8,2048]{1,0:T(8,128)(2,1)S(1)} %add_convert_fusion.2), channel_id=1, source_target_pairs={{0,8},{8,0},{1,9},{9,1},{2,10},{10,2},{3,11},{11,3},{4,12},{12,4},... | collective-permute-start | bytes 98312 | tf_op jit(solution)/shard_map/ppermute | solution.py:23
  91.1 4.6 %collective-permute-done.19 = bf16[8,2048]{1,0:T(8,128)(2,1)S(1)} collective-permute-done((bf16[8,2048]{1,0:T(8,128)(2,1)S(1)}, bf16[8,2048]{1,0:T(8,128)(2,1)S(1)}, u32[]{:S(2)}, u32[]{:S(2)}) %collective-permute-start.19) | collective-permute-done | bytes 32800 | tf_op jit(solution)/shard_map/ppermute | solution.py:23
  (74 shorter events, 12.6 us)
Async XLA Ops:
  3.7 5.2 %collective-permute-start.2 = (f32[8,256]{1,0:T(8,128)}, f32[8,256]{1,0:T(8,128)S(1)}, u32[]{:S(2)}, u32[]{:S(2)}) collective-permute-start(f32[8,256]{1,0:T(8,128)} %get-tuple-element.47), channel_id=1, source_target_pairs={{0,1},{1,0},{2,3},{3,2},{4,5},{5,4},{6,7},{7,6},{8,9},{9,8},{10,11... | collective-permute-start | bytes 24584 | tf_op jit(solution)/shard_map/ppermute | solution.py:23
  3.7 24.7 %collective-permute-start = (bf16[2,2,2,32,832]{4,3,2,1,0:T(8,128)(2,1)}, bf16[2,2,2,32,832]{4,3,2,1,0:T(8,128)(2,1)}, u32[]{:S(2)}, u32[]{:S(2)}) collective-permute-start(bf16[2,2,2,32,832]{4,3,2,1,0:T(8,128)(2,1)} %get-tuple-element.48.refs_0_), channel_id=1, source_target_pairs={{0,128},{64,192},{128,0},{192,64},{1,129},{65,193},{129,1},{193,65... | collective-permute-start | bytes 1277960 | tf_op jit(solution)/shard_map/ppermute | solution.py:23
  7.0 21.6 %collective-permute-start.1 = (bf16[2,2,2,32,832]{4,3,2,1,0:T(8,128)(2,1)}, bf16[2,2,2,32,832]{4,3,2,1,0:T(8,128)(2,1)}, u32[]{:S(2)}, u32[]{:S(2)}) collective-permute-start(bf16[2,2,2,32,832]{4,3,2,1,0:T(8,128)(2,1)} %get-tuple-element.48.refs_0_), channel_id=1, source_target_pairs={{0,64},{64,0},{128,192},{192,128},{1,65},{65,1},{129,193},{193,129... | collective-permute-start | bytes 1277960 | tf_op jit(solution)/shard_map/ppermute | solution.py:23
  11.2 17.8 %all-to-all-start = ((bf16[16,8,2304]{2,1,0:T(8,128)(2,1)}), bf16[16,8,2304]{2,1,0:T(8,128)(2,1)}, u32[]{:S(2)}, u32[]{:S(2)}) async-start(bf16[16,8,2304]{2,1,0:T(8,128)(2,1)} %bitcast.7), calls=%async_computation | async-start | bytes 1179648 | tf_op jit(solution)/shard_map/all_to_all | solution.py:343
  18.7 20.5 %copy-start = (bf16[2048,832]{0,1:T(8,128)(2,1)S(1)}, bf16[2048,832]{0,1:T(8,128)(2,1)}, u32[]{:S(2)}) copy-start(bf16[2048,832]{0,1:T(8,128)(2,1)} %param.14) | copy-start | bytes 10223620
  29.0 24.7 %collective-permute-start.3 = (bf16[2,2,2,32,832]{4,3,2,1,0:T(8,128)(2,1)}, bf16[2,2,2,32,832]{4,3,2,1,0:T(8,128)(2,1)S(1)}, u32[]{:S(2)}, u32[]{:S(2)}) collective-permute-start(bf16[2,2,2,32,832]{4,3,2,1,0:T(8,128)(2,1)} %get-tuple-element.48.refs_0_), channel_id=1, source_target_pairs={{64,128},{128,64},{65,129},{129,65},{66,130},{130,66},{67,131},{13... | collective-permute-start | bytes 1277960 | tf_op jit(solution)/shard_map/ppermute | solution.py:365
  29.7 24.0 %collective-permute-start.4 = (bf16[2,2,2,32,832]{4,3,2,1,0:T(8,128)(2,1)}, bf16[2,2,2,32,832]{4,3,2,1,0:T(8,128)(2,1)S(1)}, u32[]{:S(2)}, u32[]{:S(2)}) collective-permute-start(bf16[2,2,2,32,832]{4,3,2,1,0:T(8,128)(2,1)} %collective-permute-done.two.refs_2_), channel_id=1, source_target_pairs={{64,0},{128,192},{65,1},{129,193},{66,2},{130,194},{67,3},{131,195... | collective-permute-start | bytes 1277960 | tf_op jit(solution)/shard_map/ppermute | solution.py:366
  33.2 14.8 %collective-permute-start.20 = (bf16[48,256]{1,0:T(8,128)(2,1)S(1)}, bf16[48,256]{1,0:T(8,128)(2,1)S(1)}, u32[]{:S(2)}, u32[]{:S(2)}) collective-permute-start(bf16[48,256]{1,0:T(8,128)(2,1)S(1)} %narrow.1.own), channel_id=1, source_target_pairs={{0,8},{8,0},{1,9},{9,1},{2,10},{10,2},{3,11},{11,3},{4,12},{12,4},... | collective-permute-start | bytes 73736 | tf_op jit(solution)/shard_map/ppermute | solution.py:23
  48.0 9.6 %collective-permute-start.21 = (bf16[48,256]{1,0:T(8,128)(2,1)S(1)}, bf16[48,256]{1,0:T(8,128)(2,1)S(1)}, u32[]{:S(2)}, u32[]{:S(2)}) collective-permute-start(bf16[48,256]{1,0:T(8,128)(2,1)S(1)} %join_halves.1.p0), channel_id=1, source_target_pairs={{0,64},{64,0},{128,192},{192,128},{1,65},{65,1},{129,193},{193,129... | collective-permute-start | bytes 73736 | tf_op jit(solution)/shard_map/ppermute | solution.py:23
  51.2 6.5 %collective-permute-start.22 = (bf16[48,256]{1,0:T(8,128)(2,1)S(1)}, bf16[48,256]{1,0:T(8,128)(2,1)S(1)}, u32[]{:S(2)}, u32[]{:S(2)}) collective-permute-start(bf16[48,256]{1,0:T(8,128)(2,1)S(1)} %join_halves.1.p0), channel_id=1, source_target_pairs={{0,128},{64,192},{128,0},{192,64},{1,129},{65,193},{129,1},{193,65... | collective-permute-start | bytes 73736 | tf_op jit(solution)/shard_map/ppermute | solution.py:23
  51.8 5.9 %collective-permute-start.23 = (bf16[48,256]{1,0:T(8,128)(2,1)S(1)}, bf16[48,256]{1,0:T(8,128)(2,1)S(1)}, u32[]{:S(2)}, u32[]{:S(2)}) collective-permute-start(bf16[48,256]{1,0:T(8,128)(2,1)S(1)} %join_halves.1.p0), channel_id=1, source_target_pairs={{0,192},{64,128},{128,64},{192,0},{1,193},{65,129},{129,65},{193,1... | collective-permute-start | bytes 73736 | tf_op jit(solution)/shard_map/ppermute | solution.py:23
  53.7 5.9 %collective-permute-start.5 = (bf16[192,2048]{1,0:T(8,128)(2,1)S(1)}, bf16[192,2048]{1,0:T(8,128)(2,1)S(1)}, u32[]{:S(2)}, u32[]{:S(2)}) collective-permute-start(bf16[192,2048]{1,0:T(8,128)(2,1)S(1)} %get-tuple-element.53), channel_id=1, source_target_pairs={{0,1},{1,0},{2,3},{3,2},{4,5},{5,4},{6,7},{7,6},{8,9},{9,8},{10,11... | collective-permute-start | bytes 2359304 | tf_op jit(solution)/shard_map/ppermute | solution.py:23
  57.0 14.1 %copy-start.3 = (bf16[2,384,832]{2,1,0:T(8,128)(2,1)S(1)}, bf16[2,384,832]{2,1,0:T(8,128)(2,1)}, u32[]{:S(2)}) copy-start(bf16[2,384,832]{2,1,0:T(8,128)(2,1)} %copy-done.2) | copy-start | bytes 3833860
  57.1 14.1 %copy-start.9 = (f32[832]{0:T(1024)S(1)}, f32[832]{0:T(1024)}, u32[]{:S(2)}) copy-start(f32[832]{0:T(1024)} %gate_scale.3) | copy-start | bytes 9988
  57.1 2.5 %collective-permute-start.6 = (bf16[64,2048]{1,0:T(8,128)(2,1)S(1)}, bf16[64,2048]{1,0:T(8,128)(2,1)S(1)}, u32[]{:S(2)}, u32[]{:S(2)}) collective-permute-start(bf16[64,2048]{1,0:T(8,128)(2,1)S(1)} %get-tuple-element.57), channel_id=1, source_target_pairs={{0,1},{1,0},{2,3},{3,2},{4,5},{5,4},{6,7},{7,6},{8,9},{9,8},{10,11... | collective-permute-start | bytes 786440 | tf_op jit(solution)/shard_map/ppermute | solution.py:23
  59.2 7.8 %collective-permute-start.24 = (f32[16,2048]{1,0:T(8,128)S(1)}, f32[16,2048]{1,0:T(8,128)S(1)}, u32[]{:S(2)}, u32[]{:S(2)}) collective-permute-start(f32[16,2048]{1,0:T(8,128)S(1)} %get-tuple-element.79), channel_id=1, source_target_pairs={{0,1},{1,0},{2,3},{3,2},{4,5},{5,4},{6,7},{7,6},{8,9},{9,8},{10,11... | collective-permute-start | bytes 393224 | tf_op jit(solution)/shard_map/ppermute | solution.py:23
  60.5 9.5 %collective-permute-start.7 = (bf16[32,2048]{1,0:T(8,128)(2,1)S(1)}, bf16[32,2048]{1,0:T(8,128)(2,1)S(1)}, u32[]{:S(2)}, u32[]{:S(2)}) collective-permute-start(bf16[32,2048]{1,0:T(8,128)(2,1)S(1)} %get-tuple-element.59), channel_id=1, source_target_pairs={{0,16},{16,0},{32,48},{48,32},{1,17},{17,1},{33,49},{49,33},{2,18}... | collective-permute-start | bytes 393224 | tf_op jit(solution)/shard_map/ppermute | solution.py:23
  61.6 3.9 %collective-permute-start.27 = (bf16[32,256]{1,0:T(8,128)(2,1)S(1)}, bf16[32,256]{1,0:T(8,128)(2,1)S(1)}, u32[]{:S(2)}, u32[]{:S(2)}) collective-permute-start(bf16[32,256]{1,0:T(8,128)(2,1)S(1)} %get-tuple-element.80.low_own), channel_id=1, source_target_pairs={{0,1},{1,0},{2,3},{3,2},{4,5},{5,4},{6,7},{7,6},{8,9},{9,8},{10,11... | collective-permute-start | bytes 49160 | tf_op jit(solution)/shard_map/ppermute | solution.py:23
  61.6 8.6 %collective-permute-start.8 = (bf16[32,2048]{1,0:T(8,128)(2,1)S(1)}, bf16[32,2048]{1,0:T(8,128)(2,1)S(1)}, u32[]{:S(2)}, u32[]{:S(2)}) collective-permute-start(bf16[32,2048]{1,0:T(8,128)(2,1)S(1)} %get-tuple-element.60), channel_id=1, source_target_pairs={{0,32},{16,48},{32,0},{48,16},{1,33},{17,49},{33,1},{49,17},{2,34}... | collective-permute-start | bytes 393224 | tf_op jit(solution)/shard_map/ppermute | solution.py:23
  63.2 10.8 %collective-permute-start.9 = (bf16[32,2048]{1,0:T(8,128)(2,1)S(1)}, bf16[32,2048]{1,0:T(8,128)(2,1)S(1)}, u32[]{:S(2)}, u32[]{:S(2)}) collective-permute-start(bf16[32,2048]{1,0:T(8,128)(2,1)S(1)} %get-tuple-element.61), channel_id=1, source_target_pairs={{0,48},{16,32},{32,16},{48,0},{1,49},{17,33},{33,17},{49,1},{2,50}... | collective-permute-start | bytes 393224 | tf_op jit(solution)/shard_map/ppermute | solution.py:23
  65.5 8.5 %collective-permute-start.10 = (bf16[32,2048]{1,0:T(8,128)(2,1)S(1)}, bf16[32,2048]{1,0:T(8,128)(2,1)S(1)}, u32[]{:S(2)}, u32[]{:S(2)}) collective-permute-start(bf16[32,2048]{1,0:T(8,128)(2,1)S(1)} %get-tuple-element.63), channel_id=1, source_target_pairs={{0,2},{2,0},{4,6},{6,4},{1,3},{3,1},{5,7},{7,5},{8,10},{10,8},{12,... | collective-permute-start | bytes 393224 | tf_op jit(solution)/shard_map/ppermute | solution.py:23
  67.1 9.1 %collective-permute-start.11 = (bf16[32,2048]{1,0:T(8,128)(2,1)S(1)}, bf16[32,2048]{1,0:T(8,128)(2,1)S(1)}, u32[]{:S(2)}, u32[]{:S(2)}) collective-permute-start(bf16[32,2048]{1,0:T(8,128)(2,1)S(1)} %get-tuple-element.64), channel_id=1, source_target_pairs={{0,4},{2,6},{4,0},{6,2},{1,5},{3,7},{5,1},{7,3},{8,12},{10,14},{12... | collective-permute-start | bytes 393224 | tf_op jit(solution)/shard_map/ppermute | solution.py:23
  70.0 8.4 %collective-permute-start.12 = (bf16[32,2048]{1,0:T(8,128)(2,1)S(1)}, bf16[32,2048]{1,0:T(8,128)(2,1)S(1)}, u32[]{:S(2)}, u32[]{:S(2)}) collective-permute-start(bf16[32,2048]{1,0:T(8,128)(2,1)S(1)} %get-tuple-element.65), channel_id=1, source_target_pairs={{0,6},{2,4},{4,2},{6,0},{1,7},{3,5},{5,3},{7,1},{8,14},{10,12},{12... | collective-permute-start | bytes 393224 | tf_op jit(solution)/shard_map/ppermute | solution.py:23
  70.2 13.0 %collective-permute-start.25 = (bf16[16,2048]{1,0:T(8,128)(2,1)S(1)}, bf16[16,2048]{1,0:T(8,128)(2,1)S(1)}, u32[]{:S(2)}, u32[]{:S(2)}) collective-permute-start(bf16[16,2048]{1,0:T(8,128)(2,1)S(1)} %add_convert_fusion), channel_id=1, source_target_pairs={{0,8},{8,0},{1,9},{9,1},{2,10},{10,2},{3,11},{11,3},{4,12},{12,4},... | collective-permute-start | bytes 196616 | tf_op jit(solution)/shard_map/ppermute | solution.py:23
  79.1 5.6 %collective-permute-start.18 = (f32[8,2048]{1,0:T(8,128)S(1)}, f32[8,2048]{1,0:T(8,128)S(1)}, u32[]{:S(2)}, u32[]{:S(2)}) collective-permute-start(f32[8,2048]{1,0:T(8,128)S(1)} %get-tuple-element.73), channel_id=1, source_target_pairs={{0,6},{2,4},{4,2},{6,0},{1,7},{3,5},{5,3},{7,1},{8,14},{10,12},{12... | collective-permute-start | bytes 196616 | tf_op jit(solution)/shard_map/ppermute | solution.py:23
  79.7 5.8 %collective-permute-start.17 = (f32[8,2048]{1,0:T(8,128)S(1)}, f32[8,2048]{1,0:T(8,128)S(1)}, u32[]{:S(2)}, u32[]{:S(2)}) collective-permute-start(f32[8,2048]{1,0:T(8,128)S(1)} %get-tuple-element.72), channel_id=1, source_target_pairs={{0,4},{2,6},{4,0},{6,2},{1,5},{3,7},{5,1},{7,3},{8,12},{10,14},{12... | collective-permute-start | bytes 196616 | tf_op jit(solution)/shard_map/ppermute | solution.py:23
  80.6 7.0 %collective-permute-start.16 = (f32[8,2048]{1,0:T(8,128)S(1)}, f32[8,2048]{1,0:T(8,128)S(1)}, u32[]{:S(2)}, u32[]{:S(2)}) collective-permute-start(f32[8,2048]{1,0:T(8,128)S(1)} %get-tuple-element.71), channel_id=1, source_target_pairs={{0,2},{2,0},{4,6},{6,4},{1,3},{3,1},{5,7},{7,5},{8,10},{10,8},{12,... | collective-permute-start | bytes 196616 | tf_op jit(solution)/shard_map/ppermute | solution.py:23
  83.3 5.7 %collective-permute-start.26 = (f32[16,2048]{1,0:T(8,128)S(1)}, f32[16,2048]{1,0:T(8,128)S(1)}, u32[]{:S(2)}, u32[]{:S(2)}) collective-permute-start(f32[16,2048]{1,0:T(8,128)S(1)} %convert_add_fusion), channel_id=1, source_target_pairs={{0,1},{1,0},{2,3},{3,2},{4,5},{5,4},{6,7},{7,6},{8,9},{9,8},{10,11... | collective-permute-start | bytes 393224 | tf_op jit(solution)/shard_map/ppermute | solution.py:23
  83.4 7.1 %collective-permute-start.15 = (f32[8,2048]{1,0:T(8,128)S(1)}, f32[8,2048]{1,0:T(8,128)S(1)}, u32[]{:S(2)}, u32[]{:S(2)}) collective-permute-start(f32[8,2048]{1,0:T(8,128)S(1)} %get-tuple-element.69), channel_id=1, source_target_pairs={{0,48},{16,32},{32,16},{48,0},{1,49},{17,33},{33,17},{49,1},{2,50}... | collective-permute-start | bytes 196616 | tf_op jit(solution)/shard_map/ppermute | solution.py:23
  84.7 5.9 %collective-permute-start.14 = (f32[8,2048]{1,0:T(8,128)S(1)}, f32[8,2048]{1,0:T(8,128)S(1)}, u32[]{:S(2)}, u32[]{:S(2)}) collective-permute-start(f32[8,2048]{1,0:T(8,128)S(1)} %get-tuple-element.68), channel_id=1, source_target_pairs={{0,32},{16,48},{32,0},{48,16},{1,33},{17,49},{33,1},{49,17},{2,34}... | collective-permute-start | bytes 196616 | tf_op jit(solution)/shard_map/ppermute | solution.py:23
  85.5 5.6 %collective-permute-start.13 = (f32[8,2048]{1,0:T(8,128)S(1)}, f32[8,2048]{1,0:T(8,128)S(1)}, u32[]{:S(2)}, u32[]{:S(2)}) collective-permute-start(f32[8,2048]{1,0:T(8,128)S(1)} %get-tuple-element.67), channel_id=1, source_target_pairs={{0,16},{16,0},{32,48},{48,32},{1,17},{17,1},{33,49},{49,33},{2,18}... | collective-permute-start | bytes 196616 | tf_op jit(solution)/shard_map/ppermute | solution.py:23
  87.6 8.1 %collective-permute-start.19 = (bf16[8,2048]{1,0:T(8,128)(2,1)S(1)}, bf16[8,2048]{1,0:T(8,128)(2,1)S(1)}, u32[]{:S(2)}, u32[]{:S(2)}) collective-permute-start(bf16[8,2048]{1,0:T(8,128)(2,1)S(1)} %add_convert_fusion.2), channel_id=1, source_target_pairs={{0,8},{8,0},{1,9},{9,1},{2,10},{10,2},{3,11},{11,3},{4,12},{12,4},... | collective-permute-start | bytes 98312 | tf_op jit(solution)/shard_map/ppermute | solution.py:23
  (12 other events, 47.9 us)

commit v7 on v5

--- a/solution.py
+++ b/solution.py
@@ -10,7 +10,7 @@
 ADAPTER_SCALE = 2.0
 FFN = ("x", "zh", "y", "core")
 F32, BF16 = jnp.float32, jnp.bfloat16
-UNITS, FEATS, STEP = 832, 2048, 256
+UNITS, BOTH, FEATS, STEP, CHUNK = 832, 1664, 2048, 256, 512
 PLAIN = (((1,), (0,)), ((), ()))
 BY_ROWS = (((1,), (1,)), ((), ()))
 BY_COLUMNS = (((0,), (0,)), ((), ()))
@@ -50,13 +50,12 @@
         jnp.concatenate([gate_lift[...], none], 0).astype(BF16),
         jnp.concatenate([none, up_lift[...]], 0).astype(BF16),
     )
-    back = jnp.zeros((128, 32), F32)
+    back, scaled = jnp.zeros((128, 32), F32), []
     for k, (grad, scale) in enumerate(((gate, gate_scale), (up, up_scale))):
         rows = dot(order, grad[...], BY_ROWS)
         back += dot(rows.astype(BF16), lifts[k], BY_ROWS)
-        rows = (rows * scale[...].reshape(1, UNITS)).astype(BF16).reshape(2, 2, 32, UNITS)
-        both[0, k] = rows[0]
-        both[1, k] = rows[1]
+        scaled.append(rows * scale[...].reshape(1, UNITS))
+    both[...] = jnp.concatenate(scaled, 1).astype(BF16).reshape(2, 2, 32, BOTH)
 
     def packed(row):
         return row // 4 % 2 * 64 + row // 8 % 2 * 32 + row % 4 * 8 + row // 16
@@ -67,7 +66,7 @@
 
 
 def prep(place, *arrays):
-    both = jax.ShapeDtypeStruct((2, 2, 2, 32, UNITS), BF16)
+    both = jax.ShapeDtypeStruct((2, 2, 32, BOTH), BF16)
     back = jax.ShapeDtypeStruct((8, 256), F32)
     return pl.pallas_call(
         prep_kernel,
@@ -80,34 +79,39 @@
 
 
 def product_kernel(pairs, *refs):
-    blocks, (gate_codes, up_codes, other, own, grads, gate_held, up_held, sems) = refs[:-8], refs[-8:]
+    blocks, (gate_codes, up_codes, other, own, grads, held, sems) = refs[:-7], refs[-7:]
     count = len(blocks) // pairs
-    copies = []
-    for i, start in enumerate(range(0, FEATS, STEP)):
-        columns = pl.ds(start, STEP)
-        copies.append(
-            [
-                pltpu.make_async_copy(source.at[:, columns], held.at[:, columns], sems.at[k, i])
-                for k, (source, held) in enumerate(((gate_codes, gate_held), (up_codes, up_held)))
-            ]
-        )
-        for copy in copies[-1]:
-            copy.start()
-    for k in range(2):
-        for c in range(2):
-            for half in range(2):
-                for j in range(count):
-                    value = blocks[j * pairs][half, k, c]
-                    if pairs == 2:
-                        value += blocks[j * pairs + 1][half, k, c]
-                    row = ((c * 2 + half) * count + j) * 32
-                    grads[k, row : row + 32] = value
-    gate, up, cut = grads[0], grads[1], 64 * count
-    for i, start in enumerate(range(0, FEATS, STEP)):
+
+    def copies(i):
+        columns = pl.ds(i * CHUNK, CHUNK)
+        return [
+            pltpu.make_async_copy(
+                source.at[:, columns], held.at[pl.ds(k * UNITS, UNITS), columns], sems.at[k, i]
+            )
+            for k, source in enumerate((gate_codes, up_codes))
+        ]
+
+    for copy in copies(0) + copies(1):
+        copy.start()
+    for c in range(2):
+        for half in range(2):
+            for j in range(count):
+                value = blocks[j * pairs][half, c]
+                if pairs == 2:
+                    value += blocks[j * pairs + 1][half, c]
+                row = ((c * 2 + half) * count + j) * 32
+                grads[row : row + 32] = value
+    rows, cut = grads[...], 64 * count
+    for start in range(0, FEATS, STEP):
         columns = slice(start, start + STEP)
-        for copy in copies[i]:
-            copy.wait()
-        total = dot(gate, gate_held[:, columns], PLAIN) + dot(up, up_held[:, columns], PLAIN)
+        if start % CHUNK == 0:
+            i = start // CHUNK
+            for copy in copies(i):
+                copy.wait()
+            if i + 2 < FEATS // CHUNK:
+                for copy in copies(i + 2):
+                    copy.start()
+        total = dot(rows, held[:, columns], PLAIN)
         other[:, columns] = total[:cut].astype(BF16)
         own[:, columns] = total[cut:].astype(BF16)
 
@@ -118,15 +122,14 @@
     anywhere = pl.BlockSpec(memory_space=pl.ANY)
     return pl.pallas_call(
         functools.partial(product_kernel, pairs),
-        out_shape=(part, part, jax.ShapeDtypeStruct((2, 128 * count, UNITS), BF16)),
+        out_shape=(part, part, jax.ShapeDtypeStruct((128 * count, BOTH), BF16)),
         in_specs=[VMEM] * len(blocks) + [anywhere] * 2,
         out_specs=(VMEM,) * 3,
         scratch_shapes=[
-            pltpu.VMEM((UNITS, FEATS), BF16),
-            pltpu.VMEM((UNITS, FEATS), BF16),
-            pltpu.SemaphoreType.DMA((2, FEATS // STEP)),
+            pltpu.VMEM((BOTH, FEATS), BF16),
+            pltpu.SemaphoreType.DMA((2, FEATS // CHUNK)),
         ],
-        compiler_params=pltpu.CompilerParams(vmem_limit_bytes=20 << 20),
+        compiler_params=pltpu.CompilerParams(vmem_limit_bytes=44 << 20),
         cost_estimate=pl.CostEstimate(
             flops=900_000_000 * count, bytes_accessed=8_000_000, transcendentals=0
         ),
@@ -134,7 +137,7 @@
     )(*blocks, gate_codes, up_codes)
 
 
-def pairs_kernel(place, own1, theirs1, own2, theirs2, out):
+def pairs_kernel(marked, place, own1, theirs1, own2, theirs2, out):
     for j in range(4):
         halves = []
         for half in range(2):
@@ -150,7 +153,7 @@
     return pl.pallas_call(
         pairs_kernel,
         out_shape=jax.ShapeDtypeStruct((4, 4, 16, FEATS), BF16),
-        in_specs=[SMEM] + [VMEM] * 4,
+        in_specs=[pl.BlockSpec(memory_space=pl.ANY), SMEM] + [VMEM] * 4,
         out_specs=VMEM,
         compiler_params=pltpu.CompilerParams(vmem_limit_bytes=8 << 20),
         cost_estimate=pl.CostEstimate(flops=600_000, bytes_accessed=3_200_000, transcendentals=0),
@@ -158,15 +161,15 @@
     )(*arrays)
 
 
-def mark_kernel(one, two, out):
-    out[...] = jnp.zeros((8, 128), F32)
+def mark_kernel(*refs):
+    refs[-1][...] = jnp.zeros((8, 128), F32)
 
 
 def mark(*arrays):
     return pl.pallas_call(
         mark_kernel,
         out_shape=jax.ShapeDtypeStruct((8, 128), F32),
-        in_specs=[pl.BlockSpec(memory_space=pl.ANY)] * 2,
+        in_specs=[pl.BlockSpec(memory_space=pl.ANY)] * len(arrays),
         out_specs=VMEM,
         compiler_params=pltpu.CompilerParams(vmem_limit_bytes=1 << 20),
         cost_estimate=pl.CostEstimate(flops=100_000_000_000, bytes_accessed=4096, transcendentals=0),
@@ -288,9 +291,9 @@
 
     low1 = dot(low, order((0, 1, 2)), BY_ROWS).astype(BF16)
     low2 = dot(low, order((3,)), BY_ROWS).astype(BF16)
-    for k, (out, scale) in enumerate(((gate_out, gate_scale), (up_out, up_scale))):
-        total = dot(low1, grads1[k], PLAIN) + dot(low2, grads2[k], PLAIN)
-        out[...] = ADAPTER_SCALE * total[16 * k : 16 * k + 16] / scale[...].reshape(1, UNITS)
+    total = ADAPTER_SCALE * (dot(low1, grads1[...], PLAIN) + dot(low2, grads2[...], PLAIN))
+    gate_out[...] = total[:16, :UNITS] / gate_scale[...].reshape(1, UNITS)
+    up_out[...] = total[16:, UNITS:] / up_scale[...].reshape(1, UNITS)
 
 
 def expander(*arrays):
@@ -336,15 +339,19 @@
     small = narrow(marked, landed, *downs)
     small_theirs = swap(small, "zh", 1)
     other1, own1, grads1 = product((both, one, two), 1, *codes)
-    other1, middle, ends, marked = lax.optimization_barrier(
-        (other1, middle, ends, mark(middle, ends))
+    other1, middle, ends, small_theirs, marked = lax.optimization_barrier(
+        (other1, middle, ends, small_theirs, mark(middle, ends, small_theirs))
     )
     other2, own2, grads2 = product((middle, ends), 2, *codes)
-    sums = add_pairs(place, own1, swap(other1, "core", 1), own2, swap(other2, "core", 1))
+    own2, small_theirs = lax.optimization_barrier((own2, small_theirs))
+    sums = add_pairs(
+        marked, place, own1, swap(other1, "core", 1), own2, swap(other2, "core", 1)
+    )
+
+    parts = gather_over(join_halves(small, small_theirs), "hid")
+    marked, parts = lax.optimization_barrier((sums, parts))
     kept = plane(sums.reshape(256, FEATS)).astype(F32).reshape(16, 16, FEATS).sum(0)
-
-    small = join_halves(small, small_theirs)
-    low, adapter, keep, give = joined(marked, place, gather_over(small, "hid"), landed, *downs)
+    low, adapter, keep, give = joined(marked, place, parts, landed, *downs)
     low_other = swap(low, "core", 1)
     half = (keep + swap(give, "core", 1)).astype(BF16)
     mine = half.astype(F32) + swap(half, "zh", 1).astype(F32)

time: 101 us -> 95.5 us (0.946)
  Pallas kernels: 25.2 us -> 18.8 us
  local copies, waits for them, and re-layouts: 6.01 us -> 7.88 us
    pallas_call x2, Pallas kernels: 15.4 us -> 8.93 us  [product(): pl.pallas_call(functools.partial(product_kernel, pairs), out_shape=(part,...]
    ppermute x14, waiting for transfers between devices: 23.4 us -> 21.1 us  [swap(): return lax.ppermute(value, axis, [(i, i ^ mask) for i in range(size)])]
    all_to_all x2, waiting for transfers between devices: 9.08 us -> 11.2 us  [plane(): lax.all_to_all(value, ('x', 'y'), split_axis=0, concat_axis=0, tiled=True)]
    unnamed x30, local copies, waits for them, and re-layouts: 5.39 us -> 7.27 us
    all_to_all x2, starting transfers between devices: 14.8 us -> 13.8 us  [plane(): lax.all_to_all(value, ('x', 'y'), split_axis=0, concat_axis=0, tiled=True)]
  transfers between devices with their start and end apart: 18 -> 18, of which waited for: 7 -> 9; matrix products, arithmetic and copies ran while one was open for 1% -> 1% of each run, Pallas kernels for 23% -> 16%
where the time goes in v7:
time: 95.5 us; the launch traced here: 94.8 us
  starting transfers between devices  33.4 us (35%)
  waiting for transfers between devices  32.3 us (34%)
  Pallas kernels  18.8 us (20%)
  local copies, waits for them, and re-layouts  7.88 us (8%)
  other arithmetic  1.54 us (2%)
    ppermute x14, waiting for transfers between devices, swap(): return lax.ppermute(value, axis, [(i, i ^ mask) for i in range(size)])  21.1 us
    ppermute x14, starting transfers between devices, swap(): return lax.ppermute(value, axis, [(i, i ^ mask) for i in range(size)])  17.7 us
    all_to_all x2, starting transfers between devices, plane(): lax.all_to_all(value, ('x', 'y'), split_axis=0, concat_axis=0, tiled=True)  13.8 us
    all_to_all x2, waiting for transfers between devices, plane(): lax.all_to_all(value, ('x', 'y'), split_axis=0, concat_axis=0, tiled=True)  11.2 us
    pallas_call x2, Pallas kernels, product(): pl.pallas_call(functools.partial(product_kernel, pairs), out_shape=(part,...  8.93 us
    unnamed x30, local copies, waits for them, and re-layouts  7.27 us
    pallas_call x1, Pallas kernels, prep(): pl.pallas_call(prep_kernel, out_shape=(both, back, back), in_specs=[SMEM]...  2.43 us
  transfers between devices with their start and end apart: 18, of which 9 were waited for; matrix products, arithmetic and copies ran while one was open for 1% of the time, Pallas kernels for 16%

profile of v7, /device:TPU:8, one launch (start us, length us, event | category | flops | bytes accessed | tf_op | source)
XLA Modules:
  0.0 94.8 jit_solution(12187067779180071448)
XLA Ops:
  1.2 2.4 %prep.1 = (bf16[2,2,32,1664]{3,2,1,0:T(8,128)(2,1)}, f32[8,256]{1,0:T(8,128)}, f32[8,256]{1,0:T(8,128)}) custom-call(s32[5]{0:T(128)} %stack.23.place, bf16[832,128]{1,0:T(8,128)(2,1)} %bitcast.26, bf16[832,128]{1,0:T(8,128)(2,1)} %bitcast.27, f32[832]{0:T(1024)} %gate_scale.3, f32[832]{0:T(1024)} %up_scale.3, f32[16,832]{1,0:T(8,128)} %gate_lift.1, ...), custom_call_target="tpu_custom_call" | custom-call | flops 14000000 | bytes 1200000 | tf_op jit(solution)/shard_map/prep/pallas_call | solution.py:71
  3.7 3.3 %collective-permute-start = (bf16[2,2,32,1664]{3,2,1,0:T(8,128)(2,1)}, bf16[2,2,32,1664]{3,2,1,0:T(8,128)(2,1)}, u32[]{:S(2)}, u32[]{:S(2)}) collective-permute-start(bf16[2,2,32,1664]{3,2,1,0:T(8,128)(2,1)} %get-tuple-element.40.refs_0_), channel_id=1, source_target_pairs={{0,128},{64,192},{128,0},{192,64},{1,129},{65,193},{129,1},{193,65... | collective-permute-start | bytes 1277960 | tf_op jit(solution)/shard_map/ppermute | solution.py:23
  7.0 1.9 %collective-permute-start.1 = (bf16[2,2,32,1664]{3,2,1,0:T(8,128)(2,1)}, bf16[2,2,32,1664]{3,2,1,0:T(8,128)(2,1)}, u32[]{:S(2)}, u32[]{:S(2)}) collective-permute-start(bf16[2,2,32,1664]{3,2,1,0:T(8,128)(2,1)} %get-tuple-element.40.refs_0_), channel_id=1, source_target_pairs={{0,64},{64,0},{128,192},{192,128},{1,65},{65,1},{129,193},{193,129... | collective-permute-start | bytes 1277960 | tf_op jit(solution)/shard_map/ppermute | solution.py:23
  8.9 0.8 copy-done.13
  10.3 0.8 spread.1
  11.2 7.4 %all-to-all-start = ((bf16[16,8,2304]{2,1,0:T(8,128)(2,1)}), bf16[16,8,2304]{2,1,0:T(8,128)(2,1)}, u32[]{:S(2)}, u32[]{:S(2)}) async-start(bf16[16,8,2304]{2,1,0:T(8,128)(2,1)} %bitcast.7), calls=%async_computation | async-start | bytes 1179648 | tf_op jit(solution)/shard_map/all_to_all | solution.py:313
  18.6 8.4 %collective-permute-done.refs_1_.refs_2_ = bf16[2,2,32,1664]{3,2,1,0:T(8,128)(2,1)} collective-permute-done((bf16[2,2,32,1664]{3,2,1,0:T(8,128)(2,1)}, bf16[2,2,32,1664]{3,2,1,0:T(8,128)(2,1)}, u32[]{:S(2)}, u32[]{:S(2)}) %collective-permute-start) | collective-permute-done | bytes 426016 | tf_op jit(solution)/shard_map/ppermute | solution.py:23
  27.1 2.5 %all-to-all-done = bf16[16,8,2304]{2,1,0:T(8,128)(2,1)} async-done(((bf16[16,8,2304]{2,1,0:T(8,128)(2,1)}), bf16[16,8,2304]{2,1,0:T(8,128)(2,1)}, u32[]{:S(2)}, u32[]{:S(2)}) %all-to-all-start) | async-done | bytes 589856 | tf_op jit(solution)/shard_map/all_to_all | solution.py:313
  30.3 1.3 %collective-permute-start.4 = (bf16[2,2,32,1664]{3,2,1,0:T(8,128)(2,1)}, bf16[2,2,32,1664]{3,2,1,0:T(8,128)(2,1)S(1)}, u32[]{:S(2)}, u32[]{:S(2)}) collective-permute-start(bf16[2,2,32,1664]{3,2,1,0:T(8,128)(2,1)} %collective-permute-done.refs_1_.refs_2_), channel_id=1, source_target_pairs={{64,0},{128,192},{65,1},{129,193},{66,2},{130,194},{67,3},{131,195... | collective-permute-start | bytes 1277960 | tf_op jit(solution)/shard_map/ppermute | solution.py:336
  31.6 0.9 copy-done.7
  32.5 1.3 %narrow.1.own = bf16[48,256]{1,0:T(8,128)(2,1)S(1)} custom-call(f32[8,128]{1,0:T(8,128)S(1)} %mark.2.marked, bf16[128,2304]{1,0:T(8,128)(2,1)} %bitcast.8.landed, f32[16,2048]{1,0:T(8,128)S(1)} %bitcast.22, f32[16,2048]{1,0:T(8,128)S(1)} %bitcast.24), custom_call_target="tpu_custom_call" | custom-call | flops 17000000 | bytes 900000 | tf_op jit(solution)/shard_map/narrow/pallas_call | solution.py:208
  33.8 4.5 %collective-permute-start.5 = (bf16[48,256]{1,0:T(8,128)(2,1)S(1)}, bf16[48,256]{1,0:T(8,128)(2,1)S(1)}, u32[]{:S(2)}, u32[]{:S(2)}) collective-permute-start(bf16[48,256]{1,0:T(8,128)(2,1)S(1)} %narrow.1.own), channel_id=1, source_target_pairs={{0,8},{8,0},{1,9},{9,1},{2,10},{10,2},{3,11},{11,3},{4,12},{12,4},... | collective-permute-start | bytes 73736 | tf_op jit(solution)/shard_map/ppermute | solution.py:23
  38.4 1.0 %copy-done.12 = bf16[2,2,32,1664]{3,2,1,0:T(8,128)(2,1)S(1)} copy-done((bf16[2,2,32,1664]{3,2,1,0:T(8,128)(2,1)S(1)}, bf16[2,2,32,1664]{3,2,1,0:T(8,128)(2,1)}, u32[]{:S(2)}) %copy-start.12) | copy-done | bytes 426008
  39.4 6.2 %product.2 = (bf16[192,2048]{1,0:T(8,128)(2,1)S(1)}, bf16[192,2048]{1,0:T(8,128)(2,1)S(1)}, bf16[384,1664]{1,0:T(8,128)(2,1)S(1)}) custom-call(bf16[2,2,32,1664]{3,2,1,0:T(8,128)(2,1)S(1)} %copy-done.12, bf16[2,2,32,1664]{3,2,1,0:T(8,128)(2,1)} %collective-permute-done.1.refs_0_.refs_1_, bf16[2,2,32,1664]{3,2,1,0:T(8,128)(2,1)} %collective-permute-done.refs_1_.refs_2_, ...), custom_call_target="tpu_custom_call" | custom-call | flops 2700000000 | bytes 8000000 | tf_op jit(solution)/shard_map/product/pallas_call | solution.py:123
  45.6 1.1 %copy-done.2 = bf16[384,1664]{1,0:T(8,128)(2,1)} copy-done((bf16[384,1664]{1,0:T(8,128)(2,1)}, bf16[384,1664]{1,0:T(8,128)(2,1)S(1)}, u32[]{:S(2)}) %copy-start.2) | copy-done | bytes 1277976
  46.8 1.8 %copy-done.1 = bf16[2048,832]{0,1:T(8,128)(2,1)S(1)} copy-done((bf16[2048,832]{0,1:T(8,128)(2,1)S(1)}, bf16[2048,832]{0,1:T(8,128)(2,1)}, u32[]{:S(2)}) %copy-start.1) | copy-done | bytes 3407896
  48.6 2.7 %product.3 = (bf16[64,2048]{1,0:T(8,128)(2,1)S(1)}, bf16[64,2048]{1,0:T(8,128)(2,1)S(1)}, bf16[128,1664]{1,0:T(8,128)(2,1)S(1)}) custom-call(bf16[2,2,32,1664]{3,2,1,0:T(8,128)(2,1)S(1)} %collective-permute-done.3.refs_0_, bf16[2,2,32,1664]{3,2,1,0:T(8,128)(2,1)S(1)} %collective-permute-done.4.refs_1_, bf16[832,2048]{1,0:T(8,128)(2,1)S(1)} %bitcast.19, ...), custom_call_target="tpu_custom_call" | custom-call | flops 900000000 | bytes 8000000 | tf_op jit(solution)/shard_map/product/pallas_call | solution.py:123
  51.5 3.3 %collective-permute-start.9 = (bf16[48,256]{1,0:T(8,128)(2,1)S(1)}, bf16[48,256]{1,0:T(8,128)(2,1)S(1)}, u32[]{:S(2)}, u32[]{:S(2)}) collective-permute-start(bf16[48,256]{1,0:T(8,128)(2,1)S(1)} %join_halves.1.p0), channel_id=1, source_target_pairs={{0,64},{64,0},{128,192},{192,128},{1,65},{65,1},{129,193},{193,129... | collective-permute-start | bytes 73736 | tf_op jit(solution)/shard_map/ppermute | solution.py:23
  55.4 1.9 %collective-permute-start.11 = (bf16[48,256]{1,0:T(8,128)(2,1)S(1)}, bf16[48,256]{1,0:T(8,128)(2,1)S(1)}, u32[]{:S(2)}, u32[]{:S(2)}) collective-permute-start(bf16[48,256]{1,0:T(8,128)(2,1)S(1)} %join_halves.1.p0), channel_id=1, source_target_pairs={{0,192},{64,128},{128,64},{192,0},{1,193},{65,129},{129,65},{193,1... | collective-permute-start | bytes 73736 | tf_op jit(solution)/shard_map/ppermute | solution.py:23
  57.3 1.8 %add_pairs.1.marked = bf16[4,4,16,2048]{3,2,1,0:T(8,128)(2,1)} custom-call(f32[8,128]{1,0:T(8,128)S(1)} %mark.3.marked, s32[5]{0:T(128)S(1)} %copy-done.11, bf16[192,2048]{1,0:T(8,128)(2,1)S(1)} %get-tuple-element.47.own1, bf16[192,2048]{1,0:T(8,128)(2,1)S(1)} %collective-permute-done.6.theirs1, bf16[64,2048]{1,0:T(8,128)(2,1)S(1)} %get-tuple-element.53.own2, ...), custom_call_target="tpu_custom_call" | custom-call | flops 600000 | bytes 3200000 | tf_op jit(solution)/shard_map/add_pairs/pallas_call | solution.py:153
  59.7 1.3 %collective-permute-done.11.p3 = bf16[48,256]{1,0:T(8,128)(2,1)S(1)} collective-permute-done((bf16[48,256]{1,0:T(8,128)(2,1)S(1)}, bf16[48,256]{1,0:T(8,128)(2,1)S(1)}, u32[]{:S(2)}, u32[]{:S(2)}) %collective-permute-start.11) | collective-permute-done | bytes 24608 | tf_op jit(solution)/shard_map/ppermute | solution.py:23
  61.0 1.5 %joined.1 = (bf16[32,256]{1,0:T(8,128)(2,1)S(1)}, f32[8,2048]{1,0:T(8,128)S(1)}, f32[16,2048]{1,0:T(8,128)S(1)}, f32[16,2048]{1,0:T(8,128)S(1)}) custom-call(bf16[4,4,16,2048]{3,2,1,0:T(8,128)(2,1)} %add_pairs.1.marked, s32[5]{0:T(128)S(1)} %copy-done.11, bf16[48,256]{1,0:T(8,128)(2,1)S(1)} %join_halves.1.p0, bf16[48,256]{1,0:T(8,128)(2,1)S(1)} %collective-permute-done.9.p1, ...), custom_call_target="tpu_custom_call" | custom-call | flops 99999997952 | bytes 1000000 | tf_op jit(solution)/shard_map/joined/pallas_call | solution.py:260
  62.7 6.4 %all-to-all-start.1 = ((bf16[16,16,2048]{2,1,0:T(8,128)(2,1)}), bf16[16,16,2048]{2,1,0:T(8,128)(2,1)S(1)}, u32[]{:S(2)}, u32[]{:S(2)}) async-start(bf16[16,16,2048]{2,1,0:T(8,128)(2,1)} %bitcast.13), calls=%async_computation.1 | async-start | bytes 2097152 | tf_op jit(solution)/shard_map/all_to_all | solution.py:313
  69.0 0.9 collective-permute-start.13
  69.9 1.2 %collective-permute-done.15.low_other = bf16[32,256]{1,0:T(8,128)(2,1)S(1)} collective-permute-done((bf16[32,256]{1,0:T(8,128)(2,1)S(1)}, bf16[32,256]{1,0:T(8,128)(2,1)S(1)}, u32[]{:S(2)}, u32[]{:S(2)}) %collective-permute-start.15) | collective-permute-done | bytes 16416 | tf_op jit(solution)/shard_map/ppermute | solution.py:23
  71.1 1.0 %copy-done.5 = bf16[128,1664]{1,0:T(8,128)(2,1)S(1)} copy-done((bf16[128,1664]{1,0:T(8,128)(2,1)S(1)}, bf16[128,1664]{1,0:T(8,128)(2,1)}, u32[]{:S(2)}) %copy-start.5) | copy-done | bytes 426008
  72.1 1.9 %expander.1 = (f32[16,832]{1,0:T(8,128)}, f32[16,832]{1,0:T(8,128)}) custom-call(s32[5]{0:T(128)S(1)} %copy-done.11, bf16[32,256]{1,0:T(8,128)(2,1)S(1)} %collective-permute-done.15.low_other, bf16[32,256]{1,0:T(8,128)(2,1)S(1)} %get-tuple-element.64.low_own, bf16[384,1664]{1,0:T(8,128)(2,1)S(1)} %copy-done.3, bf16[128,1664]{1,0:T(8,128)(2,1)S(1)} %copy-done.5, ...), custom_call_target="tpu_custom_call" | custom-call | flops 55000000 | bytes 2000000 | tf_op jit(solution)/shard_map/expander/pallas_call | solution.py:301
  74.0 3.3 %collective-permute-done.13 = bf16[16,2048]{1,0:T(8,128)(2,1)S(1)} collective-permute-done((bf16[16,2048]{1,0:T(8,128)(2,1)S(1)}, bf16[16,2048]{1,0:T(8,128)(2,1)S(1)}, u32[]{:S(2)}, u32[]{:S(2)}) %collective-permute-start.13) | collective-permute-done | bytes 65568 | tf_op jit(solution)/shard_map/ppermute | solution.py:23
  77.4 8.7 %all-to-all-done.1 = bf16[16,16,2048]{2,1,0:T(8,128)(2,1)S(1)} async-done(((bf16[16,16,2048]{2,1,0:T(8,128)(2,1)}), bf16[16,16,2048]{2,1,0:T(8,128)(2,1)S(1)}, u32[]{:S(2)}, u32[]{:S(2)}) %all-to-all-start.1) | async-done | bytes 1048608 | tf_op jit(solution)/shard_map/all_to_all | solution.py:313
  86.3 0.9 collective-permute-start.8
  87.2 0.7 select_bitcast_fusion
  87.9 6.3 %collective-permute-done.8 = bf16[8,2048]{1,0:T(8,128)(2,1)S(1)} collective-permute-done((bf16[8,2048]{1,0:T(8,128)(2,1)S(1)}, bf16[8,2048]{1,0:T(8,128)(2,1)S(1)}, u32[]{:S(2)}, u32[]{:S(2)}) %collective-permute-start.8) | collective-permute-done | bytes 32800 | tf_op jit(solution)/shard_map/ppermute | solution.py:23
  (52 shorter events, 4.5 us)
Async XLA Ops:
  3.7 5.2 %collective-permute-start.2 = (f32[8,256]{1,0:T(8,128)}, f32[8,256]{1,0:T(8,128)S(1)}, u32[]{:S(2)}, u32[]{:S(2)}) collective-permute-start(f32[8,256]{1,0:T(8,128)} %get-tuple-element.39), channel_id=1, source_target_pairs={{0,1},{1,0},{2,3},{3,2},{4,5},{5,4},{6,7},{7,6},{8,9},{9,8},{10,11... | collective-permute-start | bytes 24584 | tf_op jit(solution)/shard_map/ppermute | solution.py:23
  3.7 23.3 %collective-permute-start = (bf16[2,2,32,1664]{3,2,1,0:T(8,128)(2,1)}, bf16[2,2,32,1664]{3,2,1,0:T(8,128)(2,1)}, u32[]{:S(2)}, u32[]{:S(2)}) collective-permute-start(bf16[2,2,32,1664]{3,2,1,0:T(8,128)(2,1)} %get-tuple-element.40.refs_0_), channel_id=1, source_target_pairs={{0,128},{64,192},{128,0},{192,64},{1,129},{65,193},{129,1},{193,65... | collective-permute-start | bytes 1277960 | tf_op jit(solution)/shard_map/ppermute | solution.py:23
  7.0 20.1 %collective-permute-start.1 = (bf16[2,2,32,1664]{3,2,1,0:T(8,128)(2,1)}, bf16[2,2,32,1664]{3,2,1,0:T(8,128)(2,1)}, u32[]{:S(2)}, u32[]{:S(2)}) collective-permute-start(bf16[2,2,32,1664]{3,2,1,0:T(8,128)(2,1)} %get-tuple-element.40.refs_0_), channel_id=1, source_target_pairs={{0,64},{64,0},{128,192},{192,128},{1,65},{65,1},{129,193},{193,129... | collective-permute-start | bytes 1277960 | tf_op jit(solution)/shard_map/ppermute | solution.py:23
  8.9 0.8 copy-start.13
  11.2 18.4 %all-to-all-start = ((bf16[16,8,2304]{2,1,0:T(8,128)(2,1)}), bf16[16,8,2304]{2,1,0:T(8,128)(2,1)}, u32[]{:S(2)}, u32[]{:S(2)}) async-start(bf16[16,8,2304]{2,1,0:T(8,128)(2,1)} %bitcast.7), calls=%async_computation | async-start | bytes 1179648 | tf_op jit(solution)/shard_map/all_to_all | solution.py:313
  18.6 13.0 %copy-start.6 = (f32[2048,16]{0,1:T(8,128)S(1)}, f32[2048,16]{0,1:T(8,128)}, u32[]{:S(2)}) copy-start(f32[2048,16]{0,1:T(8,128)} %param.18) | copy-start | bytes 393220
  18.6 19.8 %copy-start = (bf16[2048,832]{0,1:T(8,128)(2,1)S(1)}, bf16[2048,832]{0,1:T(8,128)(2,1)}, u32[]{:S(2)}) copy-start(bf16[2048,832]{0,1:T(8,128)(2,1)} %param.14) | copy-start | bytes 10223620
  29.6 17.1 %collective-permute-start.3 = (bf16[2,2,32,1664]{3,2,1,0:T(8,128)(2,1)}, bf16[2,2,32,1664]{3,2,1,0:T(8,128)(2,1)S(1)}, u32[]{:S(2)}, u32[]{:S(2)}) collective-permute-start(bf16[2,2,32,1664]{3,2,1,0:T(8,128)(2,1)} %get-tuple-element.40.refs_0_), channel_id=1, source_target_pairs={{64,128},{128,64},{65,129},{129,65},{66,130},{130,66},{67,131},{13... | collective-permute-start | bytes 1277960 | tf_op jit(solution)/shard_map/ppermute | solution.py:335
  30.3 16.4 %collective-permute-start.4 = (bf16[2,2,32,1664]{3,2,1,0:T(8,128)(2,1)}, bf16[2,2,32,1664]{3,2,1,0:T(8,128)(2,1)S(1)}, u32[]{:S(2)}, u32[]{:S(2)}) collective-permute-start(bf16[2,2,32,1664]{3,2,1,0:T(8,128)(2,1)} %collective-permute-done.refs_1_.refs_2_), channel_id=1, source_target_pairs={{64,0},{128,192},{65,1},{129,193},{66,2},{130,194},{67,3},{131,195... | collective-permute-start | bytes 1277960 | tf_op jit(solution)/shard_map/ppermute | solution.py:336
  31.6 0.9 copy-start.7
  33.8 12.8 %collective-permute-start.5 = (bf16[48,256]{1,0:T(8,128)(2,1)S(1)}, bf16[48,256]{1,0:T(8,128)(2,1)S(1)}, u32[]{:S(2)}, u32[]{:S(2)}) collective-permute-start(bf16[48,256]{1,0:T(8,128)(2,1)S(1)} %narrow.1.own), channel_id=1, source_target_pairs={{0,8},{8,0},{1,9},{9,1},{2,10},{10,2},{3,11},{11,3},{4,12},{12,4},... | collective-permute-start | bytes 73736 | tf_op jit(solution)/shard_map/ppermute | solution.py:23
  38.4 1.0 %copy-start.12 = (bf16[2,2,32,1664]{3,2,1,0:T(8,128)(2,1)S(1)}, bf16[2,2,32,1664]{3,2,1,0:T(8,128)(2,1)}, u32[]{:S(2)}) copy-start(bf16[2,2,32,1664]{3,2,1,0:T(8,128)(2,1)} %get-tuple-element.40.refs_0_) | copy-start | bytes 1277956
  45.6 1.1 %copy-start.2 = (bf16[384,1664]{1,0:T(8,128)(2,1)}, bf16[384,1664]{1,0:T(8,128)(2,1)S(1)}, u32[]{:S(2)}) copy-start(bf16[384,1664]{1,0:T(8,128)(2,1)S(1)} %get-tuple-element.65.grads1) | copy-start | bytes 3833860
  46.7 2.0 %copy-start.1 = (bf16[2048,832]{0,1:T(8,128)(2,1)S(1)}, bf16[2048,832]{0,1:T(8,128)(2,1)}, u32[]{:S(2)}) copy-start(bf16[2048,832]{0,1:T(8,128)(2,1)} %param.15) | copy-start | bytes 10223620
  46.7 10.6 %copy-start.11 = (s32[5]{0:T(128)S(1)}, s32[5]{0:T(128)}, u32[]{:S(2)}) copy-start(s32[5]{0:T(128)} %stack.23.place) | copy-start | bytes 64
  46.7 14.3 %copy-start.8 = (f32[2048,16]{0,1:T(8,128)S(1)}, f32[2048,16]{0,1:T(8,128)}, u32[]{:S(2)}) copy-start(f32[2048,16]{0,1:T(8,128)} %param.20) | copy-start | bytes 393220
  46.7 10.6 %collective-permute-start.6 = (bf16[192,2048]{1,0:T(8,128)(2,1)S(1)}, bf16[192,2048]{1,0:T(8,128)(2,1)S(1)}, u32[]{:S(2)}, u32[]{:S(2)}) collective-permute-start(bf16[192,2048]{1,0:T(8,128)(2,1)S(1)} %get-tuple-element.48), channel_id=1, source_target_pairs={{0,1},{1,0},{2,3},{3,2},{4,5},{5,4},{6,7},{7,6},{8,9},{9,8},{10,11... | collective-permute-start | bytes 2359304 | tf_op jit(solution)/shard_map/ppermute | solution.py:23
  51.4 11.2 %copy-start.4 = (bf16[128,1664]{1,0:T(8,128)(2,1)}, bf16[128,1664]{1,0:T(8,128)(2,1)S(1)}, u32[]{:S(2)}) copy-start(bf16[128,1664]{1,0:T(8,128)(2,1)S(1)} %get-tuple-element.66.grads2) | copy-start | bytes 1277956
  51.4 5.9 %collective-permute-start.7 = (bf16[64,2048]{1,0:T(8,128)(2,1)S(1)}, bf16[64,2048]{1,0:T(8,128)(2,1)S(1)}, u32[]{:S(2)}, u32[]{:S(2)}) collective-permute-start(bf16[64,2048]{1,0:T(8,128)(2,1)S(1)} %get-tuple-element.54), channel_id=1, source_target_pairs={{0,1},{1,0},{2,3},{3,2},{4,5},{5,4},{6,7},{7,6},{8,9},{9,8},{10,11... | collective-permute-start | bytes 786440 | tf_op jit(solution)/shard_map/ppermute | solution.py:23
  51.5 7.6 %collective-permute-start.9 = (bf16[48,256]{1,0:T(8,128)(2,1)S(1)}, bf16[48,256]{1,0:T(8,128)(2,1)S(1)}, u32[]{:S(2)}, u32[]{:S(2)}) collective-permute-start(bf16[48,256]{1,0:T(8,128)(2,1)S(1)} %join_halves.1.p0), channel_id=1, source_target_pairs={{0,64},{64,0},{128,192},{192,128},{1,65},{65,1},{129,193},{193,129... | collective-permute-start | bytes 73736 | tf_op jit(solution)/shard_map/ppermute | solution.py:23
  54.8 4.9 %collective-permute-start.10 = (bf16[48,256]{1,0:T(8,128)(2,1)S(1)}, bf16[48,256]{1,0:T(8,128)(2,1)S(1)}, u32[]{:S(2)}, u32[]{:S(2)}) collective-permute-start(bf16[48,256]{1,0:T(8,128)(2,1)S(1)} %join_halves.1.p0), channel_id=1, source_target_pairs={{0,128},{64,192},{128,0},{192,64},{1,129},{65,193},{129,1},{193,65... | collective-permute-start | bytes 73736 | tf_op jit(solution)/shard_map/ppermute | solution.py:23
  55.4 5.6 %collective-permute-start.11 = (bf16[48,256]{1,0:T(8,128)(2,1)S(1)}, bf16[48,256]{1,0:T(8,128)(2,1)S(1)}, u32[]{:S(2)}, u32[]{:S(2)}) collective-permute-start(bf16[48,256]{1,0:T(8,128)(2,1)S(1)} %join_halves.1.p0), channel_id=1, source_target_pairs={{0,192},{64,128},{128,64},{192,0},{1,193},{65,129},{129,65},{193,1... | collective-permute-start | bytes 73736 | tf_op jit(solution)/shard_map/ppermute | solution.py:23
  59.1 12.0 %copy-start.3 = (bf16[384,1664]{1,0:T(8,128)(2,1)S(1)}, bf16[384,1664]{1,0:T(8,128)(2,1)}, u32[]{:S(2)}) copy-start(bf16[384,1664]{1,0:T(8,128)(2,1)} %copy-done.2) | copy-start | bytes 3833860
  59.1 12.0 %copy-start.9 = (f32[832]{0:T(1024)S(1)}, f32[832]{0:T(1024)}, u32[]{:S(2)}) copy-start(f32[832]{0:T(1024)} %gate_scale.3) | copy-start | bytes 9988
  59.1 12.0 %copy-start.10 = (f32[832]{0:T(1024)S(1)}, f32[832]{0:T(1024)}, u32[]{:S(2)}) copy-start(f32[832]{0:T(1024)} %up_scale.3) | copy-start | bytes 9988
  62.6 6.5 %collective-permute-start.12 = (f32[16,2048]{1,0:T(8,128)S(1)}, f32[16,2048]{1,0:T(8,128)S(1)}, u32[]{:S(2)}, u32[]{:S(2)}) collective-permute-start(f32[16,2048]{1,0:T(8,128)S(1)} %get-tuple-element.63), channel_id=1, source_target_pairs={{0,1},{1,0},{2,3},{3,2},{4,5},{5,4},{6,7},{7,6},{8,9},{9,8},{10,11... | collective-permute-start | bytes 393224 | tf_op jit(solution)/shard_map/ppermute | solution.py:23
  62.7 23.4 %all-to-all-start.1 = ((bf16[16,16,2048]{2,1,0:T(8,128)(2,1)}), bf16[16,16,2048]{2,1,0:T(8,128)(2,1)S(1)}, u32[]{:S(2)}, u32[]{:S(2)}) async-start(bf16[16,16,2048]{2,1,0:T(8,128)(2,1)} %bitcast.13), calls=%async_computation.1 | async-start | bytes 2097152 | tf_op jit(solution)/shard_map/all_to_all | solution.py:313
  69.0 8.3 %collective-permute-start.13 = (bf16[16,2048]{1,0:T(8,128)(2,1)S(1)}, bf16[16,2048]{1,0:T(8,128)(2,1)S(1)}, u32[]{:S(2)}, u32[]{:S(2)}) collective-permute-start(bf16[16,2048]{1,0:T(8,128)(2,1)S(1)} %add_convert_fusion), channel_id=1, source_target_pairs={{0,8},{8,0},{1,9},{9,1},{2,10},{10,2},{3,11},{11,3},{4,12},{12,4},... | collective-permute-start | bytes 196616 | tf_op jit(solution)/shard_map/ppermute | solution.py:23
  69.9 1.2 %collective-permute-start.15 = (bf16[32,256]{1,0:T(8,128)(2,1)S(1)}, bf16[32,256]{1,0:T(8,128)(2,1)S(1)}, u32[]{:S(2)}, u32[]{:S(2)}) collective-permute-start(bf16[32,256]{1,0:T(8,128)(2,1)S(1)} %get-tuple-element.64.low_own), channel_id=1, source_target_pairs={{0,1},{1,0},{2,3},{3,2},{4,5},{5,4},{6,7},{7,6},{8,9},{9,8},{10,11... | collective-permute-start | bytes 49160 | tf_op jit(solution)/shard_map/ppermute | solution.py:23
  71.1 1.0 %copy-start.5 = (bf16[128,1664]{1,0:T(8,128)(2,1)S(1)}, bf16[128,1664]{1,0:T(8,128)(2,1)}, u32[]{:S(2)}) copy-start(bf16[128,1664]{1,0:T(8,128)(2,1)} %copy-done.4) | copy-start | bytes 1277956
  77.3 9.8 %collective-permute-start.14 = (f32[16,2048]{1,0:T(8,128)S(1)}, f32[16,2048]{1,0:T(8,128)S(1)}, u32[]{:S(2)}, u32[]{:S(2)}) collective-permute-start(f32[16,2048]{1,0:T(8,128)S(1)} %convert_add_fusion), channel_id=1, source_target_pairs={{0,1},{1,0},{2,3},{3,2},{4,5},{5,4},{6,7},{7,6},{8,9},{9,8},{10,11... | collective-permute-start | bytes 393224 | tf_op jit(solution)/shard_map/ppermute | solution.py:23
  86.3 7.9 %collective-permute-start.8 = (bf16[8,2048]{1,0:T(8,128)(2,1)S(1)}, bf16[8,2048]{1,0:T(8,128)(2,1)S(1)}, u32[]{:S(2)}, u32[]{:S(2)}) collective-permute-start(bf16[8,2048]{1,0:T(8,128)(2,1)S(1)} %slice.17), channel_id=1, source_target_pairs={{0,8},{8,0},{1,9},{9,1},{2,10},{10,2},{3,11},{11,3},{4,12},{12,4},... | collective-permute-start | bytes 98312 | tf_op jit(solution)/shard_map/ppermute | solution.py:23
  (1 other events, 0.7 us)

commit v8 on v7

--- a/solution.py
+++ b/solution.py
@@ -37,7 +37,7 @@
     return (column == source(row)).astype(F32).astype(BF16)
 
 
-def prep_kernel(place, gate, up, gate_scale, up_scale, gate_lift, up_lift, both, back_other, back_own):
+def prep_kernel(place, gate, up, gate_scale, up_scale, gate_lift, up_lift, both, back_sums):
     zh, core = place[0], place[1]
 
     def source(row):
@@ -61,18 +61,19 @@
         return row // 4 % 2 * 64 + row // 8 % 2 * 32 + row % 4 * 8 + row // 16
 
     back = dot(one_hot(128, 128, packed), back.astype(BF16), PLAIN)
-    back_other[...] = jnp.concatenate([back[16 * i : 16 * i + 8] for i in range(8)], 1)
-    back_own[...] = jnp.concatenate([back[16 * i + 8 : 16 * i + 16] for i in range(8)], 1)
+    for c in range(2):
+        rows = [back[16 * i + 8 * (1 - c) : 16 * i + 8 * (2 - c)] for i in range(8)]
+        back_sums[8 * c : 8 * c + 8] = jnp.concatenate(rows, 1)
 
 
 def prep(place, *arrays):
     both = jax.ShapeDtypeStruct((2, 2, 32, BOTH), BF16)
-    back = jax.ShapeDtypeStruct((8, 256), F32)
+    back = jax.ShapeDtypeStruct((16, 256), F32)
     return pl.pallas_call(
         prep_kernel,
-        out_shape=(both, back, back),
+        out_shape=(both, back),
         in_specs=[SMEM] + [VMEM] * 6,
-        out_specs=(VMEM,) * 3,
+        out_specs=(VMEM,) * 2,
         cost_estimate=pl.CostEstimate(flops=14_000_000, bytes_accessed=1_200_000, transcendentals=0),
         name="prep",
     )(place, *arrays)
@@ -177,38 +178,41 @@
     )(*arrays)
 
 
-def spread_kernel(inputs, back_own, back_theirs, out):
-    rows = jnp.concatenate([inputs[...].astype(F32), back_own[...] + back_theirs[...]], 1)
-    rows = jnp.concatenate([rows, rows], 0).astype(BF16)
-    for i in range(8):
+def spread_kernel(inputs, inputs_theirs, back, back_theirs, gate_down, up_down, out, down):
+    tokens = jnp.concatenate([inputs[...].astype(F32), inputs_theirs[...].astype(F32)], 0)
+    sums = back[...] + jnp.concatenate([back_theirs[8:], back_theirs[:8]], 0)
+    rows = jnp.concatenate([tokens, sums], 1).astype(BF16)
+    for i in range(16):
         out[16 * i : 16 * i + 16] = rows
+    down[...] = jnp.concatenate([gate_down[...], up_down[...]], 0).astype(BF16)
 
 
 def spread(*arrays):
     return pl.pallas_call(
         spread_kernel,
-        out_shape=jax.ShapeDtypeStruct((128, FEATS + 256), BF16),
-        in_specs=[VMEM] * 3,
-        out_specs=VMEM,
-        compiler_params=pltpu.CompilerParams(vmem_limit_bytes=4 << 20),
-        cost_estimate=pl.CostEstimate(flops=40_000_000_000, bytes_accessed=700_000, transcendentals=0),
+        out_shape=(
+            jax.ShapeDtypeStruct((256, FEATS + 256), BF16),
+            jax.ShapeDtypeStruct((32, FEATS), BF16),
+        ),
+        in_specs=[VMEM] * 6,
+        out_specs=(VMEM, VMEM),
+        compiler_params=pltpu.CompilerParams(vmem_limit_bytes=6 << 20),
+        cost_estimate=pl.CostEstimate(flops=40_000_000_000, bytes_accessed=1_400_000, transcendentals=0),
         name="spread",
     )(*arrays)
 
 
-def narrow_kernel(marked, landed, gate_down, up_down, out):
-    down = jnp.concatenate([gate_down[...], up_down[...]], 0).astype(BF16)
-    low = dot(down, landed[:, :FEATS], BY_ROWS)
-    back = landed[:, FEATS:].astype(F32).reshape(16, 8, 256).sum(0)
-    low = jnp.concatenate([low, jnp.zeros((32, 128), F32)], 1)
-    out[...] = jnp.concatenate([low, back, jnp.zeros((8, 256), F32)], 0).astype(BF16)
+def narrow_kernel(marked, landed, down, out):
+    low = dot(down[...], landed[:, :FEATS], BY_ROWS)
+    back = landed[:, FEATS:].astype(F32).reshape(16, 16, 256).sum(0)
+    out[...] = jnp.concatenate([low, back], 0).astype(BF16)
 
 
 def narrow(*arrays):
     return pl.pallas_call(
         narrow_kernel,
         out_shape=jax.ShapeDtypeStruct((48, 256), BF16),
-        in_specs=[pl.BlockSpec(memory_space=pl.ANY)] + [VMEM] * 3,
+        in_specs=[pl.BlockSpec(memory_space=pl.ANY)] + [VMEM] * 2,
         out_specs=VMEM,
         compiler_params=pltpu.CompilerParams(vmem_limit_bytes=6 << 20),
         cost_estimate=pl.CostEstimate(flops=17_000_000, bytes_accessed=900_000, transcendentals=0),
@@ -218,15 +222,14 @@
 
 def halves_kernel(own, theirs, out):
     mine, other = own[...].astype(F32), theirs[...].astype(F32)
-    low = jnp.concatenate([mine[:32, :128], other[:32, :128]], 1)
-    back = mine[32:40] + jnp.concatenate([other[36:40], other[32:36]], 0)
-    out[...] = jnp.concatenate([low, back, jnp.zeros((8, 256), F32)], 0).astype(BF16)
+    back = jnp.concatenate([other[start : start + 4] for start in (36, 32, 44, 40)], 0)
+    out[...] = jnp.concatenate([mine[:32], other[:32], mine[32:] + back], 0).astype(BF16)
 
 
 def join_halves(*arrays):
     return pl.pallas_call(
         halves_kernel,
-        out_shape=jax.ShapeDtypeStruct((48, 256), BF16),
+        out_shape=jax.ShapeDtypeStruct((80, 256), BF16),
         in_specs=[VMEM] * 2,
         out_specs=VMEM,
         compiler_params=pltpu.CompilerParams(vmem_limit_bytes=2 << 20),
@@ -235,54 +238,50 @@
     )(*arrays)
 
 
-def joined_kernel(marked, place, p0, p1, p2, p3, landed, gate_down, up_down, low_out, adapter, keep, give):
+def joined_kernel(marked, place, p0, p1, p2, p3, landed, down, low_out, adapter, keep):
     core, hid, x, y = place[1], place[2], place[3], place[4]
     parts = [part[...].astype(F32) for part in (p0, p1, p2, p3)]
-    low_out[...] = sum(part[:32] for part in parts).astype(BF16)
+    low_out[...] = sum(part[:64] for part in parts).astype(BF16)
     back = jnp.concatenate(
-        [part[32:40, 32 * i : 32 * i + 32] for part in parts for i in range(8)], 0
+        [part[64:80, 32 * i : 32 * i + 32] for part in parts for i in range(8)], 0
     ).astype(BF16)
 
     def source(row):
-        return ((row // 32) ^ hid) * 64 + row % 8 * 8 + 4 + row // 8 % 4
-
-    mine = dot(one_hot(16, 256, lambda row: source(x * 32 + y * 8 + row % 8)), back, PLAIN)
-    back = (ADAPTER_SCALE * dot(one_hot(128, 256, source), back, PLAIN)).astype(BF16)
-    down = jnp.concatenate([gate_down[...], up_down[...]], 0).astype(BF16)
-    adapter[...] = ADAPTER_SCALE * dot(mine.astype(BF16), down, PLAIN)[:8]
+        return ((row // 64) ^ hid) * 128 + row % 8 * 16 + row // 8 % 2 * 8 + 4 + row // 16 % 4
+
+    mine = dot(one_hot(16, 512, lambda row: source(x * 64 + y * 16 + row % 8)), back, PLAIN)
+    back = (ADAPTER_SCALE * dot(one_hot(256, 512, source), back, PLAIN)).astype(BF16)
+    adapter[...] = ADAPTER_SCALE * dot(mine.astype(BF16), down[...], PLAIN)[:8]
     reducer = dot(back, landed[:, :FEATS], BY_COLUMNS)
-    keep[...] = jnp.where(core == 0, reducer[:16], reducer[16:])
-    give[...] = jnp.where(core == 0, reducer[16:], reducer[:16])
+    keep[...] = jnp.where(core == 0, reducer[:16], reducer[16:]).astype(BF16)
 
 
 def joined(marked, place, parts, *arrays):
-    half = jax.ShapeDtypeStruct((16, FEATS), F32)
     return pl.pallas_call(
         joined_kernel,
         out_shape=(
-            jax.ShapeDtypeStruct((32, 256), BF16),
+            jax.ShapeDtypeStruct((64, 256), BF16),
             jax.ShapeDtypeStruct((8, FEATS), F32),
-            half,
-            half,
+            jax.ShapeDtypeStruct((16, FEATS), BF16),
         ),
-        in_specs=[pl.BlockSpec(memory_space=pl.ANY), SMEM] + [VMEM] * 7,
-        out_specs=(VMEM,) * 4,
-        compiler_params=pltpu.CompilerParams(vmem_limit_bytes=6 << 20),
-        cost_estimate=pl.CostEstimate(flops=100_000_000_000, bytes_accessed=1_000_000, transcendentals=0),
+        in_specs=[pl.BlockSpec(memory_space=pl.ANY), SMEM] + [VMEM] * 6,
+        out_specs=(VMEM,) * 3,
+        compiler_params=pltpu.CompilerParams(vmem_limit_bytes=8 << 20),
+        cost_estimate=pl.CostEstimate(flops=40_000_000, bytes_accessed=1_400_000, transcendentals=0),
         name="joined",
     )(marked, place, *parts, *arrays)
 
 
-def expander_kernel(place, low_other, low_own, grads1, grads2, gate_scale, up_scale, gate_out, up_out):
+def expander_kernel(place, low_halves, grads1, grads2, gate_scale, up_scale, gate_out, up_out):
     hid = place[2]
-    low = jnp.concatenate([low_other[...], low_own[...]], 1)
+    low = jnp.concatenate([low_halves[:32], low_halves[32:]], 1)
 
     def order(blocks):
         pieces = [
             one_hot(
                 32 * len(blocks),
                 512,
-                lambda row: c * 256 + (1 - half) * 128 + ((row // 32 + blocks[0]) ^ hid) * 32 + row % 32,
+                lambda row: (1 - half) * 256 + ((row // 32 + blocks[0]) ^ hid) * 64 + row // 8 % 4 * 16 + (1 - c) * 8 + row % 8,
             )
             for c in range(2)
             for half in range(2)
@@ -301,7 +300,7 @@
     return pl.pallas_call(
         expander_kernel,
         out_shape=(out, out),
-        in_specs=[SMEM] + [VMEM] * 6,
+        in_specs=[SMEM] + [VMEM] * 5,
         out_specs=(VMEM, VMEM),
         compiler_params=pltpu.CompilerParams(vmem_limit_bytes=8 << 20),
         cost_estimate=pl.CostEstimate(flops=55_000_000, bytes_accessed=2_000_000, transcendentals=0),
@@ -320,23 +319,22 @@
     hid = lax.axis_index("hid")
     x, zh, y, core = (lax.axis_index(name) for name in FFN)
     place = jnp.stack([zh, core, hid, x, y])
-    downs = gate_down.T, up_down.T
-
-    both, back_other, back_own = prep(
-        place, gate_grad.T, up_grad.T, gate_scale, up_scale, gate_lift, up_lift
-    )
+
+    inputs_theirs = swap(inputs, "core", 1)
+    both, back = prep(place, gate_grad.T, up_grad.T, gate_scale, up_scale, gate_lift, up_lift)
     two, one = swap(both, "hid", 2), swap(both, "hid", 1)
-    gathered = spread(inputs, back_own, swap(back_other, "core", 1))
+    gathered, down = spread(
+        inputs, inputs_theirs, back, swap(back, "core", 1), gate_down.T, up_down.T
+    )
 
     landed = plane(gathered)
-    both, two, one, landed, marked = lax.optimization_barrier(
-        (both, two, one, landed, mark(one, two))
-    )
+    both, two, one, marked = lax.optimization_barrier((both, two, one, mark(one, two)))
     middle = lax.ppermute(both, "hid", [(1, 2), (2, 1)])
     ends = lax.ppermute(two, "hid", [(1, 0), (2, 3)])
 
     codes = gate_codes.T, up_codes.T
-    small = narrow(marked, landed, *downs)
+    one, landed = lax.optimization_barrier((one, landed))
+    small = narrow(marked, landed, down)
     small_theirs = swap(small, "zh", 1)
     other1, own1, grads1 = product((both, one, two), 1, *codes)
     other1, middle, ends, small_theirs, marked = lax.optimization_barrier(
@@ -347,19 +345,14 @@
     sums = add_pairs(
         marked, place, own1, swap(other1, "core", 1), own2, swap(other2, "core", 1)
     )
-
     parts = gather_over(join_halves(small, small_theirs), "hid")
     marked, parts = lax.optimization_barrier((sums, parts))
     kept = plane(sums.reshape(256, FEATS)).astype(F32).reshape(16, 16, FEATS).sum(0)
-    low, adapter, keep, give = joined(marked, place, parts, landed, *downs)
-    low_other = swap(low, "core", 1)
-    half = (keep + swap(give, "core", 1)).astype(BF16)
+    low, adapter, half = joined(marked, place, parts, landed, down)
     mine = half.astype(F32) + swap(half, "zh", 1).astype(F32)
     theirs = swap(mine, "core", 1)
     gate_reducer, up_reducer = (jnp.where(core == k, mine, theirs) for k in range(2))
-    gate_expander, up_expander = expander(
-        place, low_other, low, grads1, grads2, gate_scale, up_scale
-    )
+    gate_expander, up_expander = expander(place, low, grads1, grads2, gate_scale, up_scale)
     arrived = swap(kept[:8].astype(BF16), "zh", 1)
     rows = (kept[8:] + arrived.astype(F32) + adapter).astype(BF16)
     return rows, gate_reducer.T, gate_expander, up_reducer.T, up_expander

time: 95.5 us -> 98.8 us (1.035)
  local copies, waits for them, and re-layouts: 7.88 us -> 11.8 us
  waiting for transfers between devices: 32.3 us -> 31 us
  other arithmetic: 1.54 us -> 2.75 us
    unnamed x30 -> x28, local copies, waits for them, and re-layouts: 7.27 us -> 11.2 us
    all_to_all x2, waiting for transfers between devices: 11.2 us -> 8.84 us  [plane(): lax.all_to_all(value, ('x', 'y'), split_axis=0, concat_axis=0, tiled=True)]
    reduce_sum x1, other arithmetic: 0.15 us -> 1.38 us  [per_device(): plane(sums.reshape(256, FEATS)).astype(F32).reshape(16, 16, FEATS).sum(0)]
    pallas_call x2, Pallas kernels: 8.93 us -> 9.99 us  [product(): pl.pallas_call(functools.partial(product_kernel, pairs), out_shape=(part,...]
    ppermute x14 -> x13, waiting for transfers between devices: 21.1 us -> 22.1 us  [swap(): return lax.ppermute(value, axis, [(i, i ^ mask) for i in range(size)])]
    ppermute x14 -> x13, starting transfers between devices: 17.7 us -> 17.6 us  [swap(): return lax.ppermute(value, axis, [(i, i ^ mask) for i in range(size)])]
  transfers between devices with their start and end apart: 18 -> 17, of which waited for: 9 -> 7; matrix products, arithmetic and copies ran while one was open for 1% -> 3% of each run, Pallas kernels for 16% -> 17%
where the time goes in v8:
time: 98.8 us; the launch traced here: 97.6 us
  starting transfers between devices  32.6 us (33%)
  waiting for transfers between devices  31 us (31%)
  Pallas kernels  18.8 us (19%)
  local copies, waits for them, and re-layouts  11.8 us (12%)
  other arithmetic  2.75 us (3%)
    ppermute x13, waiting for transfers between devices, swap(): return lax.ppermute(value, axis, [(i, i ^ mask) for i in range(size)])  22.1 us
    ppermute x13, starting transfers between devices, swap(): return lax.ppermute(value, axis, [(i, i ^ mask) for i in range(size)])  17.6 us
    all_to_all x2, starting transfers between devices, plane(): lax.all_to_all(value, ('x', 'y'), split_axis=0, concat_axis=0, tiled=True)  13.1 us
    unnamed x28, local copies, waits for them, and re-layouts  11.2 us
    pallas_call x2, Pallas kernels, product(): pl.pallas_call(functools.partial(product_kernel, pairs), out_shape=(part,...  9.99 us
    all_to_all x2, waiting for transfers between devices, plane(): lax.all_to_all(value, ('x', 'y'), split_axis=0, concat_axis=0, tiled=True)  8.84 us
    pallas_call x1, Pallas kernels, prep(): pl.pallas_call(prep_kernel, out_shape=(both, back), in_specs=[SMEM] + [VM...  2.44 us
  transfers between devices with their start and end apart: 17, of which 7 were waited for; matrix products, arithmetic and copies ran while one was open for 3% of the time, Pallas kernels for 17%

profile of v8, /device:TPU:8, one launch (start us, length us, event | category | flops | bytes accessed | tf_op | source)
XLA Modules:
  0.0 97.6 jit_solution(3613905703090661236)
XLA Ops:
  1.3 2.4 %prep.1 = (bf16[2,2,32,1664]{3,2,1,0:T(8,128)(2,1)}, f32[16,256]{1,0:T(8,128)}) custom-call(s32[5]{0:T(128)} %stack.23.place, bf16[832,128]{1,0:T(8,128)(2,1)} %bitcast.26, bf16[832,128]{1,0:T(8,128)(2,1)} %bitcast.27, f32[832]{0:T(1024)} %gate_scale.3, f32[832]{0:T(1024)} %up_scale.3, f32[16,832]{1,0:T(8,128)} %gate_lift.1, f32[16,832]{1,0:T(8,128)} %up_lift.1), custom_call_target="tpu_custom_call" | custom-call | flops 14000000 | bytes 1200000 | tf_op jit(solution)/shard_map/prep/pallas_call | solution.py:72
  4.3 3.3 %collective-permute-start = (bf16[2,2,32,1664]{3,2,1,0:T(8,128)(2,1)}, bf16[2,2,32,1664]{3,2,1,0:T(8,128)(2,1)}, u32[]{:S(2)}, u32[]{:S(2)}) collective-permute-start(bf16[2,2,32,1664]{3,2,1,0:T(8,128)(2,1)} %get-tuple-element.39.refs_0_), channel_id=1, source_target_pairs={{0,128},{64,192},{128,0},{192,64},{1,129},{65,193},{129,1},{193,65... | collective-permute-start | bytes 1277960 | tf_op jit(solution)/shard_map/ppermute | solution.py:23
  7.5 1.9 %collective-permute-start.1 = (bf16[2,2,32,1664]{3,2,1,0:T(8,128)(2,1)}, bf16[2,2,32,1664]{3,2,1,0:T(8,128)(2,1)S(1)}, u32[]{:S(2)}, u32[]{:S(2)}) collective-permute-start(bf16[2,2,32,1664]{3,2,1,0:T(8,128)(2,1)} %get-tuple-element.39.refs_0_), channel_id=1, source_target_pairs={{0,64},{64,0},{128,192},{192,128},{1,65},{65,1},{129,193},{193,129... | collective-permute-start | bytes 1277960 | tf_op jit(solution)/shard_map/ppermute | solution.py:23
  10.4 0.9 copy-done.11
  12.8 1.1 %spread.1 = (bf16[256,2304]{1,0:T(8,128)(2,1)}, bf16[32,2048]{1,0:T(8,128)(2,1)S(1)}) custom-call(bf16[8,2048]{1,0:T(8,128)(2,1)S(1)} %copy-done.12, bf16[8,2048]{1,0:T(8,128)(2,1)S(1)} %collective-permute-done.2.inputs_theirs, f32[16,256]{1,0:T(8,128)S(1)} %copy-done.13, f32[16,256]{1,0:T(8,128)S(1)} %collective-permute-done.3.back_theirs, ...), custom_call_target="tpu_custom_call" | custom-call | flops 40000000000 | bytes 1400000 | tf_op jit(solution)/shard_map/spread/pallas_call | solution.py:191
  13.9 7.4 %all-to-all-start = ((bf16[16,16,2304]{2,1,0:T(8,128)(2,1)}), bf16[16,16,2304]{2,1,0:T(8,128)(2,1)S(1)}, u32[]{:S(2)}, u32[]{:S(2)}) async-start(bf16[16,16,2304]{2,1,0:T(8,128)(2,1)} %bitcast.9), calls=%async_computation | async-start | bytes 2359296 | tf_op jit(solution)/shard_map/all_to_all | solution.py:312
  21.3 5.8 %collective-permute-done.refs_1_.refs_2_ = bf16[2,2,32,1664]{3,2,1,0:T(8,128)(2,1)} collective-permute-done((bf16[2,2,32,1664]{3,2,1,0:T(8,128)(2,1)}, bf16[2,2,32,1664]{3,2,1,0:T(8,128)(2,1)}, u32[]{:S(2)}, u32[]{:S(2)}) %collective-permute-start) | collective-permute-done | bytes 426016 | tf_op jit(solution)/shard_map/ppermute | solution.py:23
  28.6 1.3 %collective-permute-start.5 = (bf16[2,2,32,1664]{3,2,1,0:T(8,128)(2,1)}, bf16[2,2,32,1664]{3,2,1,0:T(8,128)(2,1)S(1)}, u32[]{:S(2)}, u32[]{:S(2)}) collective-permute-start(bf16[2,2,32,1664]{3,2,1,0:T(8,128)(2,1)} %collective-permute-done.refs_1_.refs_2_), channel_id=1, source_target_pairs={{64,0},{128,192},{65,1},{129,193},{66,2},{130,194},{67,3},{131,195... | collective-permute-start | bytes 1277960 | tf_op jit(solution)/shard_map/ppermute | solution.py:333
  29.9 8.8 %all-to-all-done = bf16[16,16,2304]{2,1,0:T(8,128)(2,1)S(1)} async-done(((bf16[16,16,2304]{2,1,0:T(8,128)(2,1)}), bf16[16,16,2304]{2,1,0:T(8,128)(2,1)S(1)}, u32[]{:S(2)}, u32[]{:S(2)}) %all-to-all-start) | async-done | bytes 1179680 | tf_op jit(solution)/shard_map/all_to_all | solution.py:312
  39.1 4.5 %collective-permute-start.6 = (bf16[48,256]{1,0:T(8,128)(2,1)S(1)}, bf16[48,256]{1,0:T(8,128)(2,1)S(1)}, u32[]{:S(2)}, u32[]{:S(2)}) collective-permute-start(bf16[48,256]{1,0:T(8,128)(2,1)S(1)} %narrow.1.own), channel_id=1, source_target_pairs={{0,8},{8,0},{1,9},{9,1},{2,10},{10,2},{3,11},{11,3},{4,12},{12,4},... | collective-permute-start | bytes 73736 | tf_op jit(solution)/shard_map/ppermute | solution.py:23
  43.6 2.0 %copy-done = bf16[2048,832]{0,1:T(8,128)(2,1)S(1)} copy-done((bf16[2048,832]{0,1:T(8,128)(2,1)S(1)}, bf16[2048,832]{0,1:T(8,128)(2,1)}, u32[]{:S(2)}) %copy-start) | copy-done | bytes 3407896
  45.6 1.0 %copy-done.9 = bf16[2,2,32,1664]{3,2,1,0:T(8,128)(2,1)S(1)} copy-done((bf16[2,2,32,1664]{3,2,1,0:T(8,128)(2,1)S(1)}, bf16[2,2,32,1664]{3,2,1,0:T(8,128)(2,1)}, u32[]{:S(2)}) %copy-start.9) | copy-done | bytes 426008
  46.6 6.5 %product.2 = (bf16[192,2048]{1,0:T(8,128)(2,1)S(1)}, bf16[192,2048]{1,0:T(8,128)(2,1)S(1)}, bf16[384,1664]{1,0:T(8,128)(2,1)S(1)}) custom-call(bf16[2,2,32,1664]{3,2,1,0:T(8,128)(2,1)} %get-tuple-element.39.refs_0_, bf16[2,2,32,1664]{3,2,1,0:T(8,128)(2,1)S(1)} %copy-done.9, bf16[2,2,32,1664]{3,2,1,0:T(8,128)(2,1)} %collective-permute-done.refs_1_.refs_2_, ...), custom_call_target="tpu_custom_call" | custom-call | flops 2700000000 | bytes 8000000 | tf_op jit(solution)/shard_map/product/pallas_call | solution.py:124
  53.9 1.4 %copy-done.1 = bf16[2048,832]{0,1:T(8,128)(2,1)S(1)} copy-done((bf16[2048,832]{0,1:T(8,128)(2,1)S(1)}, bf16[2048,832]{0,1:T(8,128)(2,1)}, u32[]{:S(2)}) %copy-start.1) | copy-done | bytes 3407896
  55.3 1.0 %copy-done.2 = bf16[2048,832]{0,1:T(8,128)(2,1)S(1)} copy-done((bf16[2048,832]{0,1:T(8,128)(2,1)S(1)}, bf16[2048,832]{0,1:T(8,128)(2,1)}, u32[]{:S(2)}) %copy-start.2) | copy-done | bytes 3407896
  56.3 1.0 %copy-done.4 = bf16[2,2,32,1664]{3,2,1,0:T(8,128)(2,1)S(1)} copy-done((bf16[2,2,32,1664]{3,2,1,0:T(8,128)(2,1)S(1)}, bf16[2,2,32,1664]{3,2,1,0:T(8,128)(2,1)}, u32[]{:S(2)}) %copy-start.4) | copy-done | bytes 426008
  57.3 3.5 %product.3 = (bf16[64,2048]{1,0:T(8,128)(2,1)S(1)}, bf16[64,2048]{1,0:T(8,128)(2,1)S(1)}, bf16[128,1664]{1,0:T(8,128)(2,1)S(1)}) custom-call(bf16[2,2,32,1664]{3,2,1,0:T(8,128)(2,1)S(1)} %collective-permute-done.4.refs_0_, bf16[2,2,32,1664]{3,2,1,0:T(8,128)(2,1)S(1)} %copy-done.4, bf16[832,2048]{1,0:T(8,128)(2,1)S(1)} %bitcast.21, bf16[832,2048]{1,0:T(8,128)(2,1)S(1)} %bitcast.23), custom_call_target="tpu_custom_call" | custom-call | flops 900000000 | bytes 8000000 | tf_op jit(solution)/shard_map/product/pallas_call | solution.py:124
  60.9 1.5 %collective-permute-done.8.theirs2 = bf16[64,2048]{1,0:T(8,128)(2,1)S(1)} collective-permute-done((bf16[64,2048]{1,0:T(8,128)(2,1)S(1)}, bf16[64,2048]{1,0:T(8,128)(2,1)S(1)}, u32[]{:S(2)}, u32[]{:S(2)}) %collective-permute-start.8) | collective-permute-done | bytes 262176 | tf_op jit(solution)/shard_map/ppermute | solution.py:23
  62.4 1.7 %add_pairs.1.marked = bf16[4,4,16,2048]{3,2,1,0:T(8,128)(2,1)} custom-call(f32[8,128]{1,0:T(8,128)S(1)} %mark.3.marked, s32[5]{0:T(128)S(1)} %copy-done.7, bf16[192,2048]{1,0:T(8,128)(2,1)S(1)} %get-tuple-element.50.own1, bf16[192,2048]{1,0:T(8,128)(2,1)S(1)} %collective-permute-done.7.theirs1, bf16[64,2048]{1,0:T(8,128)(2,1)S(1)} %get-tuple-element.56.own2, ...), custom_call_target="tpu_custom_call" | custom-call | flops 600000 | bytes 3200000 | tf_op jit(solution)/shard_map/add_pairs/pallas_call | solution.py:154
  64.2 5.7 %all-to-all-start.1 = ((bf16[16,16,2048]{2,1,0:T(8,128)(2,1)}), bf16[16,16,2048]{2,1,0:T(8,128)(2,1)}, u32[]{:S(2)}, u32[]{:S(2)}) async-start(bf16[16,16,2048]{2,1,0:T(8,128)(2,1)} %bitcast.13), calls=%async_computation.1 | async-start | bytes 2097152 | tf_op jit(solution)/shard_map/all_to_all | solution.py:312
  69.8 1.1 %collective-permute-start.10 = (bf16[80,256]{1,0:T(8,128)(2,1)S(1)}, bf16[80,256]{1,0:T(8,128)(2,1)S(1)}, u32[]{:S(2)}, u32[]{:S(2)}) collective-permute-start(bf16[80,256]{1,0:T(8,128)(2,1)S(1)} %join_halves.1.p0), channel_id=1, source_target_pairs={{0,64},{64,0},{128,192},{192,128},{1,65},{65,1},{129,193},{193,129... | collective-permute-start | bytes 122888 | tf_op jit(solution)/shard_map/ppermute | solution.py:23
  70.9 1.4 %collective-permute-start.11 = (bf16[80,256]{1,0:T(8,128)(2,1)S(1)}, bf16[80,256]{1,0:T(8,128)(2,1)S(1)}, u32[]{:S(2)}, u32[]{:S(2)}) collective-permute-start(bf16[80,256]{1,0:T(8,128)(2,1)S(1)} %join_halves.1.p0), channel_id=1, source_target_pairs={{0,128},{64,192},{128,0},{192,64},{1,129},{65,193},{129,1},{193,65... | collective-permute-start | bytes 122888 | tf_op jit(solution)/shard_map/ppermute | solution.py:23
  72.4 1.9 %collective-permute-start.12 = (bf16[80,256]{1,0:T(8,128)(2,1)S(1)}, bf16[80,256]{1,0:T(8,128)(2,1)S(1)}, u32[]{:S(2)}, u32[]{:S(2)}) collective-permute-start(bf16[80,256]{1,0:T(8,128)(2,1)S(1)} %join_halves.1.p0), channel_id=1, source_target_pairs={{0,192},{64,128},{128,64},{192,0},{1,193},{65,129},{129,65},{193,1... | collective-permute-start | bytes 122888 | tf_op jit(solution)/shard_map/ppermute | solution.py:23
  74.3 1.6 %collective-permute-done.11.p2 = bf16[80,256]{1,0:T(8,128)(2,1)S(1)} collective-permute-done((bf16[80,256]{1,0:T(8,128)(2,1)S(1)}, bf16[80,256]{1,0:T(8,128)(2,1)S(1)}, u32[]{:S(2)}, u32[]{:S(2)}) %collective-permute-start.11) | collective-permute-done | bytes 40992 | tf_op jit(solution)/shard_map/ppermute | solution.py:23
  75.9 2.3 %collective-permute-done.12.p3 = bf16[80,256]{1,0:T(8,128)(2,1)S(1)} collective-permute-done((bf16[80,256]{1,0:T(8,128)(2,1)S(1)}, bf16[80,256]{1,0:T(8,128)(2,1)S(1)}, u32[]{:S(2)}, u32[]{:S(2)}) %collective-permute-start.12) | collective-permute-done | bytes 40992 | tf_op jit(solution)/shard_map/ppermute | solution.py:23
  78.2 1.1 %joined.1 = (bf16[64,256]{1,0:T(8,128)(2,1)S(1)}, f32[8,2048]{1,0:T(8,128)S(1)}, bf16[16,2048]{1,0:T(8,128)(2,1)S(1)}) custom-call(bf16[4,4,16,2048]{3,2,1,0:T(8,128)(2,1)} %add_pairs.1.marked, s32[5]{0:T(128)S(1)} %copy-done.7, bf16[80,256]{1,0:T(8,128)(2,1)S(1)} %join_halves.1.p0, bf16[80,256]{1,0:T(8,128)(2,1)S(1)} %collective-permute-done.10.p1, ...), custom_call_target="tpu_custom_call" | custom-call | flops 40000000 | bytes 1400000 | tf_op jit(solution)/shard_map/joined/pallas_call | solution.py:260
  79.3 1.1 %collective-permute-start.13 = (bf16[16,2048]{1,0:T(8,128)(2,1)S(1)}, bf16[16,2048]{1,0:T(8,128)(2,1)S(1)}, u32[]{:S(2)}, u32[]{:S(2)}) collective-permute-start(bf16[16,2048]{1,0:T(8,128)(2,1)S(1)} %get-tuple-element.65), channel_id=1, source_target_pairs={{0,8},{8,0},{1,9},{9,1},{2,10},{10,2},{3,11},{11,3},{4,12},{12,4},... | collective-permute-start | bytes 196616 | tf_op jit(solution)/shard_map/ppermute | solution.py:23
  80.5 1.9 %expander.1 = (f32[16,832]{1,0:T(8,128)}, f32[16,832]{1,0:T(8,128)}) custom-call(s32[5]{0:T(128)S(1)} %copy-done.7, bf16[64,256]{1,0:T(8,128)(2,1)S(1)} %get-tuple-element.66.low_halves, bf16[384,1664]{1,0:T(8,128)(2,1)S(1)} %get-tuple-element.67.grads1, bf16[128,1664]{1,0:T(8,128)(2,1)S(1)} %get-tuple-element.68.grads2, f32[832]{0:T(1024)S(1)} %copy-done.5, ...), custom_call_target="tpu_custom_call" | custom-call | flops 55000000 | bytes 2000000 | tf_op jit(solution)/shard_map/expander/pallas_call | solution.py:300
  82.4 5.2 %collective-permute-done.13 = bf16[16,2048]{1,0:T(8,128)(2,1)S(1)} collective-permute-done((bf16[16,2048]{1,0:T(8,128)(2,1)S(1)}, bf16[16,2048]{1,0:T(8,128)(2,1)S(1)}, u32[]{:S(2)}, u32[]{:S(2)}) %collective-permute-start.13) | collective-permute-done | bytes 65568 | tf_op jit(solution)/shard_map/ppermute | solution.py:23
  87.7 1.4 %convert_reduce_fusion = f32[16,2048]{1,0:T(8,128)S(1)} fusion(bf16[16,16,2048]{2,1,0:T(8,128)(2,1)} %all-to-all-done.1), kind=kLoop, calls=%fused_computation | loop fusion | flops 1015808 | bytes 1179648 | tf_op jit(solution)/shard_map/reduce_sum | solution.py:350
  89.1 1.5 %collective-permute-start.9 = (bf16[8,2048]{1,0:T(8,128)(2,1)S(1)}, bf16[8,2048]{1,0:T(8,128)(2,1)S(1)}, u32[]{:S(2)}, u32[]{:S(2)}) collective-permute-start(bf16[8,2048]{1,0:T(8,128)(2,1)S(1)} %slice.17), channel_id=1, source_target_pairs={{0,8},{8,0},{1,9},{9,1},{2,10},{10,2},{3,11},{11,3},{4,12},{12,4},... | collective-permute-start | bytes 98312 | tf_op jit(solution)/shard_map/ppermute | solution.py:23
  91.3 5.7 %collective-permute-done.9 = bf16[8,2048]{1,0:T(8,128)(2,1)S(1)} collective-permute-done((bf16[8,2048]{1,0:T(8,128)(2,1)S(1)}, bf16[8,2048]{1,0:T(8,128)(2,1)S(1)}, u32[]{:S(2)}, u32[]{:S(2)}) %collective-permute-start.9) | collective-permute-done | bytes 32800 | tf_op jit(solution)/shard_map/ppermute | solution.py:23
  (47 shorter events, 7.7 us)
Async XLA Ops:
  0.6 8.8 %collective-permute-start.2 = (bf16[8,2048]{1,0:T(8,128)(2,1)}, bf16[8,2048]{1,0:T(8,128)(2,1)S(1)}, u32[]{:S(2)}, u32[]{:S(2)}) collective-permute-start(bf16[8,2048]{1,0:T(8,128)(2,1)} %inputs.1), channel_id=1, source_target_pairs={{0,1},{1,0},{2,3},{3,2},{4,5},{5,4},{6,7},{7,6},{8,9},{9,8},{10,11... | collective-permute-start | bytes 98312 | tf_op jit(solution)/shard_map/ppermute | solution.py:23
  3.8 5.7 %collective-permute-start.3 = (f32[16,256]{1,0:T(8,128)}, f32[16,256]{1,0:T(8,128)S(1)}, u32[]{:S(2)}, u32[]{:S(2)}) collective-permute-start(f32[16,256]{1,0:T(8,128)} %get-tuple-element.41.back), channel_id=1, source_target_pairs={{0,1},{1,0},{2,3},{3,2},{4,5},{5,4},{6,7},{7,6},{8,9},{9,8},{10,11... | collective-permute-start | bytes 49160 | tf_op jit(solution)/shard_map/ppermute | solution.py:23
  4.3 22.8 %collective-permute-start = (bf16[2,2,32,1664]{3,2,1,0:T(8,128)(2,1)}, bf16[2,2,32,1664]{3,2,1,0:T(8,128)(2,1)}, u32[]{:S(2)}, u32[]{:S(2)}) collective-permute-start(bf16[2,2,32,1664]{3,2,1,0:T(8,128)(2,1)} %get-tuple-element.39.refs_0_), channel_id=1, source_target_pairs={{0,128},{64,192},{128,0},{192,64},{1,129},{65,193},{129,1},{193,65... | collective-permute-start | bytes 1277960 | tf_op jit(solution)/shard_map/ppermute | solution.py:23
  7.5 19.6 %collective-permute-start.1 = (bf16[2,2,32,1664]{3,2,1,0:T(8,128)(2,1)}, bf16[2,2,32,1664]{3,2,1,0:T(8,128)(2,1)S(1)}, u32[]{:S(2)}, u32[]{:S(2)}) collective-permute-start(bf16[2,2,32,1664]{3,2,1,0:T(8,128)(2,1)} %get-tuple-element.39.refs_0_), channel_id=1, source_target_pairs={{0,64},{64,0},{128,192},{192,128},{1,65},{65,1},{129,193},{193,129... | collective-permute-start | bytes 1277960 | tf_op jit(solution)/shard_map/ppermute | solution.py:23
  9.5 0.9 copy-start.10
  10.4 0.9 copy-start.11
  11.3 0.8 copy-start.12
  12.0 0.7 copy-start.13
  13.9 24.8 %all-to-all-start = ((bf16[16,16,2304]{2,1,0:T(8,128)(2,1)}), bf16[16,16,2304]{2,1,0:T(8,128)(2,1)S(1)}, u32[]{:S(2)}, u32[]{:S(2)}) async-start(bf16[16,16,2304]{2,1,0:T(8,128)(2,1)} %bitcast.9), calls=%async_computation | async-start | bytes 2359296 | tf_op jit(solution)/shard_map/all_to_all | solution.py:312
  27.1 0.8 copy-start.8
  27.9 25.3 %collective-permute-start.4 = (bf16[2,2,32,1664]{3,2,1,0:T(8,128)(2,1)}, bf16[2,2,32,1664]{3,2,1,0:T(8,128)(2,1)S(1)}, u32[]{:S(2)}, u32[]{:S(2)}) collective-permute-start(bf16[2,2,32,1664]{3,2,1,0:T(8,128)(2,1)} %get-tuple-element.39.refs_0_), channel_id=1, source_target_pairs={{64,128},{128,64},{65,129},{129,65},{66,130},{130,66},{67,131},{13... | collective-permute-start | bytes 1277960 | tf_op jit(solution)/shard_map/ppermute | solution.py:332
  28.6 24.6 %collective-permute-start.5 = (bf16[2,2,32,1664]{3,2,1,0:T(8,128)(2,1)}, bf16[2,2,32,1664]{3,2,1,0:T(8,128)(2,1)S(1)}, u32[]{:S(2)}, u32[]{:S(2)}) collective-permute-start(bf16[2,2,32,1664]{3,2,1,0:T(8,128)(2,1)} %collective-permute-done.refs_1_.refs_2_), channel_id=1, source_target_pairs={{64,0},{128,192},{65,1},{129,193},{66,2},{130,194},{67,3},{131,195... | collective-permute-start | bytes 1277960 | tf_op jit(solution)/shard_map/ppermute | solution.py:333
  39.1 14.1 %collective-permute-start.6 = (bf16[48,256]{1,0:T(8,128)(2,1)S(1)}, bf16[48,256]{1,0:T(8,128)(2,1)S(1)}, u32[]{:S(2)}, u32[]{:S(2)}) collective-permute-start(bf16[48,256]{1,0:T(8,128)(2,1)S(1)} %narrow.1.own), channel_id=1, source_target_pairs={{0,8},{8,0},{1,9},{9,1},{2,10},{10,2},{3,11},{11,3},{4,12},{12,4},... | collective-permute-start | bytes 73736 | tf_op jit(solution)/shard_map/ppermute | solution.py:23
  43.6 2.0 %copy-start = (bf16[2048,832]{0,1:T(8,128)(2,1)S(1)}, bf16[2048,832]{0,1:T(8,128)(2,1)}, u32[]{:S(2)}) copy-start(bf16[2048,832]{0,1:T(8,128)(2,1)} %param.14) | copy-start | bytes 10223620
  45.6 1.0 %copy-start.9 = (bf16[2,2,32,1664]{3,2,1,0:T(8,128)(2,1)S(1)}, bf16[2,2,32,1664]{3,2,1,0:T(8,128)(2,1)}, u32[]{:S(2)}) copy-start(bf16[2,2,32,1664]{3,2,1,0:T(8,128)(2,1)} %copy-done.8) | copy-start | bytes 1277956
  53.1 0.8 copy-start.3
  53.2 2.1 %copy-start.1 = (bf16[2048,832]{0,1:T(8,128)(2,1)S(1)}, bf16[2048,832]{0,1:T(8,128)(2,1)}, u32[]{:S(2)}) copy-start(bf16[2048,832]{0,1:T(8,128)(2,1)} %param.14) | copy-start | bytes 10223620
  53.2 3.1 %copy-start.2 = (bf16[2048,832]{0,1:T(8,128)(2,1)S(1)}, bf16[2048,832]{0,1:T(8,128)(2,1)}, u32[]{:S(2)}) copy-start(bf16[2048,832]{0,1:T(8,128)(2,1)} %param.15) | copy-start | bytes 10223620
  53.9 8.5 %collective-permute-start.7 = (bf16[192,2048]{1,0:T(8,128)(2,1)S(1)}, bf16[192,2048]{1,0:T(8,128)(2,1)S(1)}, u32[]{:S(2)}, u32[]{:S(2)}) collective-permute-start(bf16[192,2048]{1,0:T(8,128)(2,1)S(1)} %get-tuple-element.51), channel_id=1, source_target_pairs={{0,1},{1,0},{2,3},{3,2},{4,5},{5,4},{6,7},{7,6},{8,9},{9,8},{10,11... | collective-permute-start | bytes 2359304 | tf_op jit(solution)/shard_map/ppermute | solution.py:23
  56.3 1.0 %copy-start.4 = (bf16[2,2,32,1664]{3,2,1,0:T(8,128)(2,1)S(1)}, bf16[2,2,32,1664]{3,2,1,0:T(8,128)(2,1)}, u32[]{:S(2)}) copy-start(bf16[2,2,32,1664]{3,2,1,0:T(8,128)(2,1)} %copy-done.3) | copy-start | bytes 1277956
  57.3 5.1 %copy-start.7 = (s32[5]{0:T(128)S(1)}, s32[5]{0:T(128)}, u32[]{:S(2)}) copy-start(s32[5]{0:T(128)} %stack.23.place) | copy-start | bytes 64
  60.8 1.6 %collective-permute-start.8 = (bf16[64,2048]{1,0:T(8,128)(2,1)S(1)}, bf16[64,2048]{1,0:T(8,128)(2,1)S(1)}, u32[]{:S(2)}, u32[]{:S(2)}) collective-permute-start(bf16[64,2048]{1,0:T(8,128)(2,1)S(1)} %get-tuple-element.57), channel_id=1, source_target_pairs={{0,1},{1,0},{2,3},{3,2},{4,5},{5,4},{6,7},{7,6},{8,9},{9,8},{10,11... | collective-permute-start | bytes 786440 | tf_op jit(solution)/shard_map/ppermute | solution.py:23
  64.2 16.3 %copy-start.5 = (f32[832]{0:T(1024)S(1)}, f32[832]{0:T(1024)}, u32[]{:S(2)}) copy-start(f32[832]{0:T(1024)} %gate_scale.3) | copy-start | bytes 9988
  64.2 16.3 %copy-start.6 = (f32[832]{0:T(1024)S(1)}, f32[832]{0:T(1024)}, u32[]{:S(2)}) copy-start(f32[832]{0:T(1024)} %up_scale.3) | copy-start | bytes 9988
  64.2 23.5 %all-to-all-start.1 = ((bf16[16,16,2048]{2,1,0:T(8,128)(2,1)}), bf16[16,16,2048]{2,1,0:T(8,128)(2,1)}, u32[]{:S(2)}, u32[]{:S(2)}) async-start(bf16[16,16,2048]{2,1,0:T(8,128)(2,1)} %bitcast.13), calls=%async_computation.1 | async-start | bytes 2097152 | tf_op jit(solution)/shard_map/all_to_all | solution.py:312
  69.8 4.5 %collective-permute-start.10 = (bf16[80,256]{1,0:T(8,128)(2,1)S(1)}, bf16[80,256]{1,0:T(8,128)(2,1)S(1)}, u32[]{:S(2)}, u32[]{:S(2)}) collective-permute-start(bf16[80,256]{1,0:T(8,128)(2,1)S(1)} %join_halves.1.p0), channel_id=1, source_target_pairs={{0,64},{64,0},{128,192},{192,128},{1,65},{65,1},{129,193},{193,129... | collective-permute-start | bytes 122888 | tf_op jit(solution)/shard_map/ppermute | solution.py:23
  70.9 5.0 %collective-permute-start.11 = (bf16[80,256]{1,0:T(8,128)(2,1)S(1)}, bf16[80,256]{1,0:T(8,128)(2,1)S(1)}, u32[]{:S(2)}, u32[]{:S(2)}) collective-permute-start(bf16[80,256]{1,0:T(8,128)(2,1)S(1)} %join_halves.1.p0), channel_id=1, source_target_pairs={{0,128},{64,192},{128,0},{192,64},{1,129},{65,193},{129,1},{193,65... | collective-permute-start | bytes 122888 | tf_op jit(solution)/shard_map/ppermute | solution.py:23
  72.4 5.8 %collective-permute-start.12 = (bf16[80,256]{1,0:T(8,128)(2,1)S(1)}, bf16[80,256]{1,0:T(8,128)(2,1)S(1)}, u32[]{:S(2)}, u32[]{:S(2)}) collective-permute-start(bf16[80,256]{1,0:T(8,128)(2,1)S(1)} %join_halves.1.p0), channel_id=1, source_target_pairs={{0,192},{64,128},{128,64},{192,0},{1,193},{65,129},{129,65},{193,1... | collective-permute-start | bytes 122888 | tf_op jit(solution)/shard_map/ppermute | solution.py:23
  79.3 8.3 %collective-permute-start.13 = (bf16[16,2048]{1,0:T(8,128)(2,1)S(1)}, bf16[16,2048]{1,0:T(8,128)(2,1)S(1)}, u32[]{:S(2)}, u32[]{:S(2)}) collective-permute-start(bf16[16,2048]{1,0:T(8,128)(2,1)S(1)} %get-tuple-element.65), channel_id=1, source_target_pairs={{0,8},{8,0},{1,9},{9,1},{2,10},{10,2},{3,11},{11,3},{4,12},{12,4},... | collective-permute-start | bytes 196616 | tf_op jit(solution)/shard_map/ppermute | solution.py:23
  87.6 3.0 %collective-permute-start.14 = (f32[16,2048]{1,0:T(8,128)S(1)}, f32[16,2048]{1,0:T(8,128)S(1)}, u32[]{:S(2)}, u32[]{:S(2)}) collective-permute-start(f32[16,2048]{1,0:T(8,128)S(1)} %convert_add_fusion), channel_id=1, source_target_pairs={{0,1},{1,0},{2,3},{3,2},{4,5},{5,4},{6,7},{7,6},{8,9},{9,8},{10,11... | collective-permute-start | bytes 393224 | tf_op jit(solution)/shard_map/ppermute | solution.py:23
  89.1 7.9 %collective-permute-start.9 = (bf16[8,2048]{1,0:T(8,128)(2,1)S(1)}, bf16[8,2048]{1,0:T(8,128)(2,1)S(1)}, u32[]{:S(2)}, u32[]{:S(2)}) collective-permute-start(bf16[8,2048]{1,0:T(8,128)(2,1)S(1)} %slice.17), channel_id=1, source_target_pairs={{0,8},{8,0},{1,9},{9,1},{2,10},{10,2},{3,11},{11,3},{4,12},{12,4},... | collective-permute-start | bytes 98312 | tf_op jit(solution)/shard_map/ppermute | solution.py:23

commit v9 on v8

--- a/solution.py
+++ b/solution.py
@@ -333,12 +333,12 @@
     ends = lax.ppermute(two, "hid", [(1, 0), (2, 3)])
 
     codes = gate_codes.T, up_codes.T
-    one, landed = lax.optimization_barrier((one, landed))
+    other1, own1, grads1 = product((both, one, two), 1, *codes)
+    landed, grads1 = lax.optimization_barrier((landed, grads1))
     small = narrow(marked, landed, down)
     small_theirs = swap(small, "zh", 1)
-    other1, own1, grads1 = product((both, one, two), 1, *codes)
-    other1, middle, ends, small_theirs, marked = lax.optimization_barrier(
-        (other1, middle, ends, small_theirs, mark(middle, ends, small_theirs))
+    middle, ends, small_theirs, marked = lax.optimization_barrier(
+        (middle, ends, small_theirs, mark(middle, ends, small_theirs))
     )
     other2, own2, grads2 = product((middle, ends), 2, *codes)
     own2, small_theirs = lax.optimization_barrier((own2, small_theirs))
@@ -349,7 +349,9 @@
     marked, parts = lax.optimization_barrier((sums, parts))
     kept = plane(sums.reshape(256, FEATS)).astype(F32).reshape(16, 16, FEATS).sum(0)
     low, adapter, half = joined(marked, place, parts, landed, down)
-    mine = half.astype(F32) + swap(half, "zh", 1).astype(F32)
+    half_theirs = swap(half, "zh", 1)
+    half_theirs, kept = lax.optimization_barrier((half_theirs, kept))
+    mine = half.astype(F32) + half_theirs.astype(F32)
     theirs = swap(mine, "core", 1)
     gate_reducer, up_reducer = (jnp.where(core == k, mine, theirs) for k in range(2))
     gate_expander, up_expander = expander(place, low, grads1, grads2, gate_scale, up_scale)

time: 98.8 us -> 96.6 us (0.978)
  waiting for transfers between devices: 31 us -> 17.5 us
  starting transfers between devices: 32.6 us -> 45.8 us
  local copies, waits for them, and re-layouts: 11.8 us -> 9.55 us
    ppermute x13, starting transfers between devices: 17.6 us -> 28.2 us  [swap(): return lax.ppermute(value, axis, [(i, i ^ mask) for i in range(size)])]
    all_to_all x2, waiting for transfers between devices: 8.84 us -> 0.01 us  [plane(): lax.all_to_all(value, ('x', 'y'), split_axis=0, concat_axis=0, tiled=True)]
    ppermute x13, waiting for transfers between devices: 22.1 us -> 17.5 us  [swap(): return lax.ppermute(value, axis, [(i, i ^ mask) for i in range(size)])]
    unnamed x28 -> x30, local copies, waits for them, and re-layouts: 11.2 us -> 8.94 us
    all_to_all x2, starting transfers between devices: 13.1 us -> 14.9 us  [plane(): lax.all_to_all(value, ('x', 'y'), split_axis=0, concat_axis=0, tiled=True)]
  transfers between devices with their start and end apart: 17 -> 17, of which waited for: 7 -> 7; matrix products, arithmetic and copies ran while one was open for 3% -> 3% of each run, Pallas kernels for 17% -> 18%
where the time goes in v9:
time: 96.6 us; the launch traced here: 95.6 us
  starting transfers between devices  45.8 us (47%)
  Pallas kernels  19.2 us (20%)
  waiting for transfers between devices  17.5 us (18%)
  local copies, waits for them, and re-layouts  9.55 us (10%)
  other arithmetic  2.75 us (3%)
    ppermute x13, starting transfers between devices, swap(): return lax.ppermute(value, axis, [(i, i ^ mask) for i in range(size)])  28.2 us
    ppermute x13, waiting for transfers between devices, swap(): return lax.ppermute(value, axis, [(i, i ^ mask) for i in range(size)])  17.5 us
    all_to_all x2, starting transfers between devices, plane(): lax.all_to_all(value, ('x', 'y'), split_axis=0, concat_axis=0, tiled=True)  14.9 us
    pallas_call x2, Pallas kernels, product(): pl.pallas_call(functools.partial(product_kernel, pairs), out_shape=(part,...  10.4 us
    unnamed x30, local copies, waits for them, and re-layouts  8.94 us
    pallas_call x1, Pallas kernels, prep(): pl.pallas_call(prep_kernel, out_shape=(both, back), in_specs=[SMEM] + [VM...  2.44 us
  transfers between devices with their start and end apart: 17, of which 7 were waited for; matrix products, arithmetic and copies ran while one was open for 3% of the time, Pallas kernels for 18%

profile of v9, /device:TPU:8, one launch (start us, length us, event | category | flops | bytes accessed | tf_op | source)
XLA Modules:
  0.0 95.6 jit_solution(2050791279268920879)
XLA Ops:
  1.3 2.4 %prep.1 = (bf16[2,2,32,1664]{3,2,1,0:T(8,128)(2,1)}, f32[16,256]{1,0:T(8,128)}) custom-call(s32[5]{0:T(128)} %stack.23.place, bf16[832,128]{1,0:T(8,128)(2,1)} %bitcast.26, bf16[832,128]{1,0:T(8,128)(2,1)} %bitcast.27, f32[832]{0:T(1024)} %gate_scale.3, f32[832]{0:T(1024)} %up_scale.3, f32[16,832]{1,0:T(8,128)} %gate_lift.1, f32[16,832]{1,0:T(8,128)} %up_lift.1), custom_call_target="tpu_custom_call" | custom-call | flops 14000000 | bytes 1200000 | tf_op jit(solution)/shard_map/prep/pallas_call | solution.py:72
  4.3 3.3 %collective-permute-start = (bf16[2,2,32,1664]{3,2,1,0:T(8,128)(2,1)}, bf16[2,2,32,1664]{3,2,1,0:T(8,128)(2,1)}, u32[]{:S(2)}, u32[]{:S(2)}) collective-permute-start(bf16[2,2,32,1664]{3,2,1,0:T(8,128)(2,1)} %get-tuple-element.40.refs_0_), channel_id=1, source_target_pairs={{0,128},{64,192},{128,0},{192,64},{1,129},{65,193},{129,1},{193,65... | collective-permute-start | bytes 1277960 | tf_op jit(solution)/shard_map/ppermute | solution.py:23
  7.5 1.9 %collective-permute-start.1 = (bf16[2,2,32,1664]{3,2,1,0:T(8,128)(2,1)}, bf16[2,2,32,1664]{3,2,1,0:T(8,128)(2,1)S(1)}, u32[]{:S(2)}, u32[]{:S(2)}) collective-permute-start(bf16[2,2,32,1664]{3,2,1,0:T(8,128)(2,1)} %get-tuple-element.40.refs_0_), channel_id=1, source_target_pairs={{0,64},{64,0},{128,192},{192,128},{1,65},{65,1},{129,193},{193,129... | collective-permute-start | bytes 1277960 | tf_op jit(solution)/shard_map/ppermute | solution.py:23
  9.5 0.9 copy-done.11
  10.4 0.9 copy-done.12
  12.8 1.1 %spread.1 = (bf16[256,2304]{1,0:T(8,128)(2,1)}, bf16[32,2048]{1,0:T(8,128)(2,1)S(1)}) custom-call(bf16[8,2048]{1,0:T(8,128)(2,1)S(1)} %copy-done.13, bf16[8,2048]{1,0:T(8,128)(2,1)S(1)} %collective-permute-done.4.inputs_theirs, f32[16,256]{1,0:T(8,128)S(1)} %copy-done.14, f32[16,256]{1,0:T(8,128)S(1)} %collective-permute-done.5.back_theirs, ...), custom_call_target="tpu_custom_call" | custom-call | flops 40000000000 | bytes 1400000 | tf_op jit(solution)/shard_map/spread/pallas_call | solution.py:191
  13.9 7.4 %all-to-all-start = ((bf16[16,16,2304]{2,1,0:T(8,128)(2,1)}), bf16[16,16,2304]{2,1,0:T(8,128)(2,1)S(1)}, u32[]{:S(2)}, u32[]{:S(2)}) async-start(bf16[16,16,2304]{2,1,0:T(8,128)(2,1)} %bitcast.9), calls=%async_computation | async-start | bytes 2359296 | tf_op jit(solution)/shard_map/all_to_all | solution.py:312
  21.3 5.8 %collective-permute-done.refs_1_.refs_2_ = bf16[2,2,32,1664]{3,2,1,0:T(8,128)(2,1)} collective-permute-done((bf16[2,2,32,1664]{3,2,1,0:T(8,128)(2,1)}, bf16[2,2,32,1664]{3,2,1,0:T(8,128)(2,1)}, u32[]{:S(2)}, u32[]{:S(2)}) %collective-permute-start) | collective-permute-done | bytes 426016 | tf_op jit(solution)/shard_map/ppermute | solution.py:23
  27.9 1.4 %collective-permute-start.2 = (bf16[2,2,32,1664]{3,2,1,0:T(8,128)(2,1)}, bf16[2,2,32,1664]{3,2,1,0:T(8,128)(2,1)}, u32[]{:S(2)}, u32[]{:S(2)}) collective-permute-start(bf16[2,2,32,1664]{3,2,1,0:T(8,128)(2,1)} %get-tuple-element.40.refs_0_), channel_id=1, source_target_pairs={{64,128},{128,64},{65,129},{129,65},{66,130},{130,66},{67,131},{13... | collective-permute-start | bytes 1277960 | tf_op jit(solution)/shard_map/ppermute | solution.py:332
  29.3 1.3 %collective-permute-start.3 = (bf16[2,2,32,1664]{3,2,1,0:T(8,128)(2,1)}, bf16[2,2,32,1664]{3,2,1,0:T(8,128)(2,1)}, u32[]{:S(2)}, u32[]{:S(2)}) collective-permute-start(bf16[2,2,32,1664]{3,2,1,0:T(8,128)(2,1)} %collective-permute-done.refs_1_.refs_2_), channel_id=1, source_target_pairs={{64,0},{128,192},{65,1},{129,193},{66,2},{130,194},{67,3},{131,195... | collective-permute-start | bytes 1277960 | tf_op jit(solution)/shard_map/ppermute | solution.py:333
  30.6 1.0 %copy-done.10 = bf16[2,2,32,1664]{3,2,1,0:T(8,128)(2,1)S(1)} copy-done((bf16[2,2,32,1664]{3,2,1,0:T(8,128)(2,1)S(1)}, bf16[2,2,32,1664]{3,2,1,0:T(8,128)(2,1)}, u32[]{:S(2)}) %copy-start.10) | copy-done | bytes 426008
  31.6 6.5 %product.2 = (bf16[192,2048]{1,0:T(8,128)(2,1)S(1)}, bf16[192,2048]{1,0:T(8,128)(2,1)S(1)}, bf16[384,1664]{1,0:T(8,128)(2,1)S(1)}) custom-call(bf16[2,2,32,1664]{3,2,1,0:T(8,128)(2,1)} %get-tuple-element.40.refs_0_, bf16[2,2,32,1664]{3,2,1,0:T(8,128)(2,1)S(1)} %copy-done.10, bf16[2,2,32,1664]{3,2,1,0:T(8,128)(2,1)} %collective-permute-done.refs_1_.refs_2_, ...), custom_call_target="tpu_custom_call" | custom-call | flops 2700000000 | bytes 8000000 | tf_op jit(solution)/shard_map/product/pallas_call | solution.py:124
  38.1 0.9 copy-done.8
  39.4 6.5 %collective-permute-start.6 = (bf16[48,256]{1,0:T(8,128)(2,1)S(1)}, bf16[48,256]{1,0:T(8,128)(2,1)S(1)}, u32[]{:S(2)}, u32[]{:S(2)}) collective-permute-start(bf16[48,256]{1,0:T(8,128)(2,1)S(1)} %narrow.1.own), channel_id=1, source_target_pairs={{0,8},{8,0},{1,9},{9,1},{2,10},{10,2},{3,11},{11,3},{4,12},{12,4},... | collective-permute-start | bytes 73736 | tf_op jit(solution)/shard_map/ppermute | solution.py:23
  45.9 1.9 %collective-permute-done.6.refs_2_.theirs = bf16[48,256]{1,0:T(8,128)(2,1)S(1)} collective-permute-done((bf16[48,256]{1,0:T(8,128)(2,1)S(1)}, bf16[48,256]{1,0:T(8,128)(2,1)S(1)}, u32[]{:S(2)}, u32[]{:S(2)}) %collective-permute-start.6) | collective-permute-done | bytes 24608 | tf_op jit(solution)/shard_map/ppermute | solution.py:23
  47.8 2.0 %copy-done.1 = bf16[2048,832]{0,1:T(8,128)(2,1)S(1)} copy-done((bf16[2048,832]{0,1:T(8,128)(2,1)S(1)}, bf16[2048,832]{0,1:T(8,128)(2,1)}, u32[]{:S(2)}) %copy-start.1) | copy-done | bytes 3407896
  49.8 1.0 %copy-done.2 = bf16[2048,832]{0,1:T(8,128)(2,1)S(1)} copy-done((bf16[2048,832]{0,1:T(8,128)(2,1)S(1)}, bf16[2048,832]{0,1:T(8,128)(2,1)}, u32[]{:S(2)}) %copy-start.2) | copy-done | bytes 3407896
  50.8 3.8 %product.3 = (bf16[64,2048]{1,0:T(8,128)(2,1)S(1)}, bf16[64,2048]{1,0:T(8,128)(2,1)S(1)}, bf16[128,1664]{1,0:T(8,128)(2,1)S(1)}) custom-call(bf16[2,2,32,1664]{3,2,1,0:T(8,128)(2,1)} %collective-permute-done.2.refs_0_, bf16[2,2,32,1664]{3,2,1,0:T(8,128)(2,1)} %collective-permute-done.3.refs_1_, bf16[832,2048]{1,0:T(8,128)(2,1)S(1)} %bitcast.21, ...), custom_call_target="tpu_custom_call" | custom-call | flops 900000000 | bytes 8000000 | tf_op jit(solution)/shard_map/product/pallas_call | solution.py:124
  54.8 1.5 %collective-permute-done.8.theirs2 = bf16[64,2048]{1,0:T(8,128)(2,1)S(1)} collective-permute-done((bf16[64,2048]{1,0:T(8,128)(2,1)S(1)}, bf16[64,2048]{1,0:T(8,128)(2,1)S(1)}, u32[]{:S(2)}, u32[]{:S(2)}) %collective-permute-start.8) | collective-permute-done | bytes 262176 | tf_op jit(solution)/shard_map/ppermute | solution.py:23
  56.3 1.8 %add_pairs.1.marked = bf16[4,4,16,2048]{3,2,1,0:T(8,128)(2,1)} custom-call(f32[8,128]{1,0:T(8,128)S(1)} %mark.3.marked, s32[5]{0:T(128)S(1)} %copy-done.7, bf16[192,2048]{1,0:T(8,128)(2,1)S(1)} %get-tuple-element.50.own1, bf16[192,2048]{1,0:T(8,128)(2,1)S(1)} %collective-permute-done.7.theirs1, bf16[64,2048]{1,0:T(8,128)(2,1)S(1)} %get-tuple-element.56.own2, ...), custom_call_target="tpu_custom_call" | custom-call | flops 600000 | bytes 3200000 | tf_op jit(solution)/shard_map/add_pairs/pallas_call | solution.py:154
  58.0 7.5 %all-to-all-start.1 = ((bf16[16,16,2048]{2,1,0:T(8,128)(2,1)}), bf16[16,16,2048]{2,1,0:T(8,128)(2,1)}, u32[]{:S(2)}, u32[]{:S(2)}) async-start(bf16[16,16,2048]{2,1,0:T(8,128)(2,1)} %bitcast.13), calls=%async_computation.1 | async-start | bytes 2097152 | tf_op jit(solution)/shard_map/all_to_all | solution.py:312
  65.6 3.4 %collective-permute-start.9 = (bf16[80,256]{1,0:T(8,128)(2,1)S(1)}, bf16[80,256]{1,0:T(8,128)(2,1)S(1)}, u32[]{:S(2)}, u32[]{:S(2)}) collective-permute-start(bf16[80,256]{1,0:T(8,128)(2,1)S(1)} %join_halves.1.p0), channel_id=1, source_target_pairs={{0,64},{64,0},{128,192},{192,128},{1,65},{65,1},{129,193},{193,129... | collective-permute-start | bytes 122888 | tf_op jit(solution)/shard_map/ppermute | solution.py:23
  69.0 1.6 %collective-permute-start.10 = (bf16[80,256]{1,0:T(8,128)(2,1)S(1)}, bf16[80,256]{1,0:T(8,128)(2,1)S(1)}, u32[]{:S(2)}, u32[]{:S(2)}) collective-permute-start(bf16[80,256]{1,0:T(8,128)(2,1)S(1)} %join_halves.1.p0), channel_id=1, source_target_pairs={{0,128},{64,192},{128,0},{192,64},{1,129},{65,193},{129,1},{193,65... | collective-permute-start | bytes 122888 | tf_op jit(solution)/shard_map/ppermute | solution.py:23
  70.6 1.4 %collective-permute-start.11 = (bf16[80,256]{1,0:T(8,128)(2,1)S(1)}, bf16[80,256]{1,0:T(8,128)(2,1)S(1)}, u32[]{:S(2)}, u32[]{:S(2)}) collective-permute-start(bf16[80,256]{1,0:T(8,128)(2,1)S(1)} %join_halves.1.p0), channel_id=1, source_target_pairs={{0,192},{64,128},{128,64},{192,0},{1,193},{65,129},{129,65},{193,1... | collective-permute-start | bytes 122888 | tf_op jit(solution)/shard_map/ppermute | solution.py:23
  71.9 3.2 %collective-permute-done.10.p2 = bf16[80,256]{1,0:T(8,128)(2,1)S(1)} collective-permute-done((bf16[80,256]{1,0:T(8,128)(2,1)S(1)}, bf16[80,256]{1,0:T(8,128)(2,1)S(1)}, u32[]{:S(2)}, u32[]{:S(2)}) %collective-permute-start.10) | collective-permute-done | bytes 40992 | tf_op jit(solution)/shard_map/ppermute | solution.py:23
  75.2 1.2 %collective-permute-done.11.p3 = bf16[80,256]{1,0:T(8,128)(2,1)S(1)} collective-permute-done((bf16[80,256]{1,0:T(8,128)(2,1)S(1)}, bf16[80,256]{1,0:T(8,128)(2,1)S(1)}, u32[]{:S(2)}, u32[]{:S(2)}) %collective-permute-start.11) | collective-permute-done | bytes 40992 | tf_op jit(solution)/shard_map/ppermute | solution.py:23
  76.4 1.1 %joined.1 = (bf16[64,256]{1,0:T(8,128)(2,1)S(1)}, f32[8,2048]{1,0:T(8,128)S(1)}, bf16[16,2048]{1,0:T(8,128)(2,1)S(1)}) custom-call(bf16[4,4,16,2048]{3,2,1,0:T(8,128)(2,1)} %add_pairs.1.marked, s32[5]{0:T(128)S(1)} %copy-done.7, bf16[80,256]{1,0:T(8,128)(2,1)S(1)} %join_halves.1.p0, bf16[80,256]{1,0:T(8,128)(2,1)S(1)} %collective-permute-done.9.p1, ...), custom_call_target="tpu_custom_call" | custom-call | flops 40000000 | bytes 1400000 | tf_op jit(solution)/shard_map/joined/pallas_call | solution.py:260
  77.5 5.0 %collective-permute-start.12 = (bf16[16,2048]{1,0:T(8,128)(2,1)S(1)}, bf16[16,2048]{1,0:T(8,128)(2,1)S(1)}, u32[]{:S(2)}, u32[]{:S(2)}) collective-permute-start(bf16[16,2048]{1,0:T(8,128)(2,1)S(1)} %get-tuple-element.64), channel_id=1, source_target_pairs={{0,8},{8,0},{1,9},{9,1},{2,10},{10,2},{3,11},{11,3},{4,12},{12,4},... | collective-permute-start | bytes 196616 | tf_op jit(solution)/shard_map/ppermute | solution.py:23
  82.5 1.9 %expander.1 = (f32[16,832]{1,0:T(8,128)}, f32[16,832]{1,0:T(8,128)}) custom-call(s32[5]{0:T(128)S(1)} %copy-done.7, bf16[64,256]{1,0:T(8,128)(2,1)S(1)} %get-tuple-element.68.low_halves, bf16[384,1664]{1,0:T(8,128)(2,1)S(1)} %get-tuple-element.69.grads1, bf16[128,1664]{1,0:T(8,128)(2,1)S(1)} %copy-done.4, f32[832]{0:T(1024)S(1)} %copy-done.5, f32[832]{0:T(1024)S(1)} %copy-done.6), custom_call_target="tpu_custom_call" | custom-call | flops 55000000 | bytes 2000000 | tf_op jit(solution)/shard_map/expander/pallas_call | solution.py:300
  84.5 1.4 %convert_reduce_fusion = f32[16,2048]{1,0:T(8,128)S(1)} fusion(bf16[16,16,2048]{2,1,0:T(8,128)(2,1)} %all-to-all-done.1), kind=kLoop, calls=%fused_computation | loop fusion | flops 1015808 | bytes 1179648 | tf_op jit(solution)/shard_map/reduce_sum | solution.py:350
  86.3 4.4 %collective-permute-start.13 = (bf16[8,2048]{1,0:T(8,128)(2,1)S(1)}, bf16[8,2048]{1,0:T(8,128)(2,1)S(1)}, u32[]{:S(2)}, u32[]{:S(2)}) collective-permute-start(bf16[8,2048]{1,0:T(8,128)(2,1)S(1)} %slice.12), channel_id=1, source_target_pairs={{0,8},{8,0},{1,9},{9,1},{2,10},{10,2},{3,11},{11,3},{4,12},{12,4},... | collective-permute-start | bytes 98312 | tf_op jit(solution)/shard_map/ppermute | solution.py:23
  90.8 3.4 %collective-permute-done.13 = bf16[8,2048]{1,0:T(8,128)(2,1)S(1)} collective-permute-done((bf16[8,2048]{1,0:T(8,128)(2,1)S(1)}, bf16[8,2048]{1,0:T(8,128)(2,1)S(1)}, u32[]{:S(2)}, u32[]{:S(2)}) %collective-permute-start.13) | collective-permute-done | bytes 32800 | tf_op jit(solution)/shard_map/ppermute | solution.py:23
  (49 shorter events, 5.9 us)
Async XLA Ops:
  0.6 8.8 %collective-permute-start.4 = (bf16[8,2048]{1,0:T(8,128)(2,1)}, bf16[8,2048]{1,0:T(8,128)(2,1)S(1)}, u32[]{:S(2)}, u32[]{:S(2)}) collective-permute-start(bf16[8,2048]{1,0:T(8,128)(2,1)} %inputs.1), channel_id=1, source_target_pairs={{0,1},{1,0},{2,3},{3,2},{4,5},{5,4},{6,7},{7,6},{8,9},{9,8},{10,11... | collective-permute-start | bytes 98312 | tf_op jit(solution)/shard_map/ppermute | solution.py:23
  3.8 5.7 %collective-permute-start.5 = (f32[16,256]{1,0:T(8,128)}, f32[16,256]{1,0:T(8,128)S(1)}, u32[]{:S(2)}, u32[]{:S(2)}) collective-permute-start(f32[16,256]{1,0:T(8,128)} %get-tuple-element.43.back), channel_id=1, source_target_pairs={{0,1},{1,0},{2,3},{3,2},{4,5},{5,4},{6,7},{7,6},{8,9},{9,8},{10,11... | collective-permute-start | bytes 49160 | tf_op jit(solution)/shard_map/ppermute | solution.py:23
  4.3 22.8 %collective-permute-start = (bf16[2,2,32,1664]{3,2,1,0:T(8,128)(2,1)}, bf16[2,2,32,1664]{3,2,1,0:T(8,128)(2,1)}, u32[]{:S(2)}, u32[]{:S(2)}) collective-permute-start(bf16[2,2,32,1664]{3,2,1,0:T(8,128)(2,1)} %get-tuple-element.40.refs_0_), channel_id=1, source_target_pairs={{0,128},{64,192},{128,0},{192,64},{1,129},{65,193},{129,1},{193,65... | collective-permute-start | bytes 1277960 | tf_op jit(solution)/shard_map/ppermute | solution.py:23
  7.5 19.6 %collective-permute-start.1 = (bf16[2,2,32,1664]{3,2,1,0:T(8,128)(2,1)}, bf16[2,2,32,1664]{3,2,1,0:T(8,128)(2,1)S(1)}, u32[]{:S(2)}, u32[]{:S(2)}) collective-permute-start(bf16[2,2,32,1664]{3,2,1,0:T(8,128)(2,1)} %get-tuple-element.40.refs_0_), channel_id=1, source_target_pairs={{0,64},{64,0},{128,192},{192,128},{1,65},{65,1},{129,193},{193,129... | collective-permute-start | bytes 1277960 | tf_op jit(solution)/shard_map/ppermute | solution.py:23
  9.5 0.9 copy-start.11
  10.4 0.9 copy-start.12
  11.3 0.8 copy-start.13
  12.0 0.7 copy-start.14
  13.9 25.1 %all-to-all-start = ((bf16[16,16,2304]{2,1,0:T(8,128)(2,1)}), bf16[16,16,2304]{2,1,0:T(8,128)(2,1)S(1)}, u32[]{:S(2)}, u32[]{:S(2)}) async-start(bf16[16,16,2304]{2,1,0:T(8,128)(2,1)} %bitcast.9), calls=%async_computation | async-start | bytes 2359296 | tf_op jit(solution)/shard_map/all_to_all | solution.py:312
  21.3 9.3 %copy-start = (bf16[2048,832]{0,1:T(8,128)(2,1)S(1)}, bf16[2048,832]{0,1:T(8,128)(2,1)}, u32[]{:S(2)}) copy-start(bf16[2048,832]{0,1:T(8,128)(2,1)} %param.14) | copy-start | bytes 10223620
  27.1 0.8 copy-start.9
  27.9 18.1 %collective-permute-start.2 = (bf16[2,2,32,1664]{3,2,1,0:T(8,128)(2,1)}, bf16[2,2,32,1664]{3,2,1,0:T(8,128)(2,1)}, u32[]{:S(2)}, u32[]{:S(2)}) collective-permute-start(bf16[2,2,32,1664]{3,2,1,0:T(8,128)(2,1)} %get-tuple-element.40.refs_0_), channel_id=1, source_target_pairs={{64,128},{128,64},{65,129},{129,65},{66,130},{130,66},{67,131},{13... | collective-permute-start | bytes 1277960 | tf_op jit(solution)/shard_map/ppermute | solution.py:332
  29.3 16.6 %collective-permute-start.3 = (bf16[2,2,32,1664]{3,2,1,0:T(8,128)(2,1)}, bf16[2,2,32,1664]{3,2,1,0:T(8,128)(2,1)}, u32[]{:S(2)}, u32[]{:S(2)}) collective-permute-start(bf16[2,2,32,1664]{3,2,1,0:T(8,128)(2,1)} %collective-permute-done.refs_1_.refs_2_), channel_id=1, source_target_pairs={{64,0},{128,192},{65,1},{129,193},{66,2},{130,194},{67,3},{131,195... | collective-permute-start | bytes 1277960 | tf_op jit(solution)/shard_map/ppermute | solution.py:333
  30.6 1.0 %copy-start.10 = (bf16[2,2,32,1664]{3,2,1,0:T(8,128)(2,1)S(1)}, bf16[2,2,32,1664]{3,2,1,0:T(8,128)(2,1)}, u32[]{:S(2)}) copy-start(bf16[2,2,32,1664]{3,2,1,0:T(8,128)(2,1)} %copy-done.9) | copy-start | bytes 1277956
  38.1 0.9 copy-start.8
  39.4 8.4 %collective-permute-start.6 = (bf16[48,256]{1,0:T(8,128)(2,1)S(1)}, bf16[48,256]{1,0:T(8,128)(2,1)S(1)}, u32[]{:S(2)}, u32[]{:S(2)}) collective-permute-start(bf16[48,256]{1,0:T(8,128)(2,1)S(1)} %narrow.1.own), channel_id=1, source_target_pairs={{0,8},{8,0},{1,9},{9,1},{2,10},{10,2},{3,11},{11,3},{4,12},{12,4},... | collective-permute-start | bytes 73736 | tf_op jit(solution)/shard_map/ppermute | solution.py:23
  45.9 8.8 %collective-permute-start.7 = (bf16[192,2048]{1,0:T(8,128)(2,1)}, bf16[192,2048]{1,0:T(8,128)(2,1)S(1)}, u32[]{:S(2)}, u32[]{:S(2)}) collective-permute-start(bf16[192,2048]{1,0:T(8,128)(2,1)} %copy-done.8), channel_id=1, source_target_pairs={{0,1},{1,0},{2,3},{3,2},{4,5},{5,4},{6,7},{7,6},{8,9},{9,8},{10,11... | collective-permute-start | bytes 2359304 | tf_op jit(solution)/shard_map/ppermute | solution.py:23
  47.8 2.0 %copy-start.1 = (bf16[2048,832]{0,1:T(8,128)(2,1)S(1)}, bf16[2048,832]{0,1:T(8,128)(2,1)}, u32[]{:S(2)}) copy-start(bf16[2048,832]{0,1:T(8,128)(2,1)} %param.14) | copy-start | bytes 10223620
  47.8 3.0 %copy-start.2 = (bf16[2048,832]{0,1:T(8,128)(2,1)S(1)}, bf16[2048,832]{0,1:T(8,128)(2,1)}, u32[]{:S(2)}) copy-start(bf16[2048,832]{0,1:T(8,128)(2,1)} %param.15) | copy-start | bytes 10223620
  50.8 5.5 %copy-start.7 = (s32[5]{0:T(128)S(1)}, s32[5]{0:T(128)}, u32[]{:S(2)}) copy-start(s32[5]{0:T(128)} %stack.23.place) | copy-start | bytes 64
  54.6 3.4 %copy-start.3 = (bf16[128,1664]{1,0:T(8,128)(2,1)}, bf16[128,1664]{1,0:T(8,128)(2,1)S(1)}, u32[]{:S(2)}) copy-start(bf16[128,1664]{1,0:T(8,128)(2,1)S(1)} %get-tuple-element.70.grads2) | copy-start | bytes 1277956
  54.6 1.6 %collective-permute-start.8 = (bf16[64,2048]{1,0:T(8,128)(2,1)S(1)}, bf16[64,2048]{1,0:T(8,128)(2,1)S(1)}, u32[]{:S(2)}, u32[]{:S(2)}) collective-permute-start(bf16[64,2048]{1,0:T(8,128)(2,1)S(1)} %get-tuple-element.57), channel_id=1, source_target_pairs={{0,1},{1,0},{2,3},{3,2},{4,5},{5,4},{6,7},{7,6},{8,9},{9,8},{10,11... | collective-permute-start | bytes 786440 | tf_op jit(solution)/shard_map/ppermute | solution.py:23
  58.0 24.5 %copy-start.4 = (bf16[128,1664]{1,0:T(8,128)(2,1)S(1)}, bf16[128,1664]{1,0:T(8,128)(2,1)}, u32[]{:S(2)}) copy-start(bf16[128,1664]{1,0:T(8,128)(2,1)} %copy-done.3) | copy-start | bytes 1277956
  58.0 24.5 %copy-start.5 = (f32[832]{0:T(1024)S(1)}, f32[832]{0:T(1024)}, u32[]{:S(2)}) copy-start(f32[832]{0:T(1024)} %gate_scale.3) | copy-start | bytes 9988
  58.0 24.5 %copy-start.6 = (f32[832]{0:T(1024)S(1)}, f32[832]{0:T(1024)}, u32[]{:S(2)}) copy-start(f32[832]{0:T(1024)} %up_scale.3) | copy-start | bytes 9988
  58.0 26.4 %all-to-all-start.1 = ((bf16[16,16,2048]{2,1,0:T(8,128)(2,1)}), bf16[16,16,2048]{2,1,0:T(8,128)(2,1)}, u32[]{:S(2)}, u32[]{:S(2)}) async-start(bf16[16,16,2048]{2,1,0:T(8,128)(2,1)} %bitcast.13), calls=%async_computation.1 | async-start | bytes 2097152 | tf_op jit(solution)/shard_map/all_to_all | solution.py:312
  65.6 6.3 %collective-permute-start.9 = (bf16[80,256]{1,0:T(8,128)(2,1)S(1)}, bf16[80,256]{1,0:T(8,128)(2,1)S(1)}, u32[]{:S(2)}, u32[]{:S(2)}) collective-permute-start(bf16[80,256]{1,0:T(8,128)(2,1)S(1)} %join_halves.1.p0), channel_id=1, source_target_pairs={{0,64},{64,0},{128,192},{192,128},{1,65},{65,1},{129,193},{193,129... | collective-permute-start | bytes 122888 | tf_op jit(solution)/shard_map/ppermute | solution.py:23
  69.0 6.2 %collective-permute-start.10 = (bf16[80,256]{1,0:T(8,128)(2,1)S(1)}, bf16[80,256]{1,0:T(8,128)(2,1)S(1)}, u32[]{:S(2)}, u32[]{:S(2)}) collective-permute-start(bf16[80,256]{1,0:T(8,128)(2,1)S(1)} %join_halves.1.p0), channel_id=1, source_target_pairs={{0,128},{64,192},{128,0},{192,64},{1,129},{65,193},{129,1},{193,65... | collective-permute-start | bytes 122888 | tf_op jit(solution)/shard_map/ppermute | solution.py:23
  70.6 5.8 %collective-permute-start.11 = (bf16[80,256]{1,0:T(8,128)(2,1)S(1)}, bf16[80,256]{1,0:T(8,128)(2,1)S(1)}, u32[]{:S(2)}, u32[]{:S(2)}) collective-permute-start(bf16[80,256]{1,0:T(8,128)(2,1)S(1)} %join_halves.1.p0), channel_id=1, source_target_pairs={{0,192},{64,128},{128,64},{192,0},{1,193},{65,129},{129,65},{193,1... | collective-permute-start | bytes 122888 | tf_op jit(solution)/shard_map/ppermute | solution.py:23
  77.5 8.8 %collective-permute-start.12 = (bf16[16,2048]{1,0:T(8,128)(2,1)S(1)}, bf16[16,2048]{1,0:T(8,128)(2,1)S(1)}, u32[]{:S(2)}, u32[]{:S(2)}) collective-permute-start(bf16[16,2048]{1,0:T(8,128)(2,1)S(1)} %get-tuple-element.64), channel_id=1, source_target_pairs={{0,8},{8,0},{1,9},{9,1},{2,10},{10,2},{3,11},{11,3},{4,12},{12,4},... | collective-permute-start | bytes 196616 | tf_op jit(solution)/shard_map/ppermute | solution.py:23
  86.3 7.9 %collective-permute-start.13 = (bf16[8,2048]{1,0:T(8,128)(2,1)S(1)}, bf16[8,2048]{1,0:T(8,128)(2,1)S(1)}, u32[]{:S(2)}, u32[]{:S(2)}) collective-permute-start(bf16[8,2048]{1,0:T(8,128)(2,1)S(1)} %slice.12), channel_id=1, source_target_pairs={{0,8},{8,0},{1,9},{9,1},{2,10},{10,2},{3,11},{11,3},{4,12},{12,4},... | collective-permute-start | bytes 98312 | tf_op jit(solution)/shard_map/ppermute | solution.py:23
  90.7 4.1 %collective-permute-start.14 = (f32[16,2048]{1,0:T(8,128)S(1)}, f32[16,2048]{1,0:T(8,128)S(1)}, u32[]{:S(2)}, u32[]{:S(2)}) collective-permute-start(f32[16,2048]{1,0:T(8,128)S(1)} %convert_add_fusion), channel_id=1, source_target_pairs={{0,1},{1,0},{2,3},{3,2},{4,5},{5,4},{6,7},{7,6},{8,9},{9,8},{10,11... | collective-permute-start | bytes 393224 | tf_op jit(solution)/shard_map/ppermute | solution.py:23

commit v10 on v7

--- a/solution.py
+++ b/solution.py
@@ -177,28 +177,31 @@
     )(*arrays)
 
 
-def spread_kernel(inputs, back_own, back_theirs, out):
+def spread_kernel(inputs, back_own, back_theirs, gate_down, up_down, out, down):
     rows = jnp.concatenate([inputs[...].astype(F32), back_own[...] + back_theirs[...]], 1)
     rows = jnp.concatenate([rows, rows], 0).astype(BF16)
     for i in range(8):
         out[16 * i : 16 * i + 16] = rows
+    down[...] = jnp.concatenate([gate_down[...], up_down[...]], 0).astype(BF16)
 
 
 def spread(*arrays):
     return pl.pallas_call(
         spread_kernel,
-        out_shape=jax.ShapeDtypeStruct((128, FEATS + 256), BF16),
-        in_specs=[VMEM] * 3,
-        out_specs=VMEM,
+        out_shape=(
+            jax.ShapeDtypeStruct((128, FEATS + 256), BF16),
+            jax.ShapeDtypeStruct((32, FEATS), BF16),
+        ),
+        in_specs=[VMEM] * 5,
+        out_specs=(VMEM, VMEM),
         compiler_params=pltpu.CompilerParams(vmem_limit_bytes=4 << 20),
         cost_estimate=pl.CostEstimate(flops=40_000_000_000, bytes_accessed=700_000, transcendentals=0),
         name="spread",
     )(*arrays)
 
 
-def narrow_kernel(marked, landed, gate_down, up_down, out):
-    down = jnp.concatenate([gate_down[...], up_down[...]], 0).astype(BF16)
-    low = dot(down, landed[:, :FEATS], BY_ROWS)
+def narrow_kernel(marked, landed, down, out):
+    low = dot(down[...], landed[:, :FEATS], BY_ROWS)
     back = landed[:, FEATS:].astype(F32).reshape(16, 8, 256).sum(0)
     low = jnp.concatenate([low, jnp.zeros((32, 128), F32)], 1)
     out[...] = jnp.concatenate([low, back, jnp.zeros((8, 256), F32)], 0).astype(BF16)
@@ -208,7 +211,7 @@
     return pl.pallas_call(
         narrow_kernel,
         out_shape=jax.ShapeDtypeStruct((48, 256), BF16),
-        in_specs=[pl.BlockSpec(memory_space=pl.ANY)] + [VMEM] * 3,
+        in_specs=[pl.BlockSpec(memory_space=pl.ANY)] + [VMEM] * 2,
         out_specs=VMEM,
         compiler_params=pltpu.CompilerParams(vmem_limit_bytes=6 << 20),
         cost_estimate=pl.CostEstimate(flops=17_000_000, bytes_accessed=900_000, transcendentals=0),
@@ -235,7 +238,7 @@
     )(*arrays)
 
 
-def joined_kernel(marked, place, p0, p1, p2, p3, landed, gate_down, up_down, low_out, adapter, keep, give):
+def joined_kernel(marked, place, p0, p1, p2, p3, landed, down, low_out, adapter, keep, give):
     core, hid, x, y = place[1], place[2], place[3], place[4]
     parts = [part[...].astype(F32) for part in (p0, p1, p2, p3)]
     low_out[...] = sum(part[:32] for part in parts).astype(BF16)
@@ -248,8 +251,7 @@
 
     mine = dot(one_hot(16, 256, lambda row: source(x * 32 + y * 8 + row % 8)), back, PLAIN)
     back = (ADAPTER_SCALE * dot(one_hot(128, 256, source), back, PLAIN)).astype(BF16)
-    down = jnp.concatenate([gate_down[...], up_down[...]], 0).astype(BF16)
-    adapter[...] = ADAPTER_SCALE * dot(mine.astype(BF16), down, PLAIN)[:8]
+    adapter[...] = ADAPTER_SCALE * dot(mine.astype(BF16), down[...], PLAIN)[:8]
     reducer = dot(back, landed[:, :FEATS], BY_COLUMNS)
     keep[...] = jnp.where(core == 0, reducer[:16], reducer[16:])
     give[...] = jnp.where(core == 0, reducer[16:], reducer[:16])
@@ -265,7 +267,7 @@
             half,
             half,
         ),
-        in_specs=[pl.BlockSpec(memory_space=pl.ANY), SMEM] + [VMEM] * 7,
+        in_specs=[pl.BlockSpec(memory_space=pl.ANY), SMEM] + [VMEM] * 6,
         out_specs=(VMEM,) * 4,
         compiler_params=pltpu.CompilerParams(vmem_limit_bytes=6 << 20),
         cost_estimate=pl.CostEstimate(flops=100_000_000_000, bytes_accessed=1_000_000, transcendentals=0),
@@ -320,13 +322,14 @@
     hid = lax.axis_index("hid")
     x, zh, y, core = (lax.axis_index(name) for name in FFN)
     place = jnp.stack([zh, core, hid, x, y])
-    downs = gate_down.T, up_down.T
 
     both, back_other, back_own = prep(
         place, gate_grad.T, up_grad.T, gate_scale, up_scale, gate_lift, up_lift
     )
     two, one = swap(both, "hid", 2), swap(both, "hid", 1)
-    gathered = spread(inputs, back_own, swap(back_other, "core", 1))
+    gathered, down = spread(
+        inputs, back_own, swap(back_other, "core", 1), gate_down.T, up_down.T
+    )
 
     landed = plane(gathered)
     both, two, one, landed, marked = lax.optimization_barrier(
@@ -336,11 +339,11 @@
     ends = lax.ppermute(two, "hid", [(1, 0), (2, 3)])
 
     codes = gate_codes.T, up_codes.T
-    small = narrow(marked, landed, *downs)
+    small = narrow(marked, landed, down)
     small_theirs = swap(small, "zh", 1)
     other1, own1, grads1 = product((both, one, two), 1, *codes)
-    other1, middle, ends, small_theirs, marked = lax.optimization_barrier(
-        (other1, middle, ends, small_theirs, mark(middle, ends, small_theirs))
+    middle, ends, small_theirs, marked = lax.optimization_barrier(
+        (middle, ends, small_theirs, mark(middle, ends, small_theirs))
     )
     other2, own2, grads2 = product((middle, ends), 2, *codes)
     own2, small_theirs = lax.optimization_barrier((own2, small_theirs))
@@ -351,7 +354,7 @@
     parts = gather_over(join_halves(small, small_theirs), "hid")
     marked, parts = lax.optimization_barrier((sums, parts))
     kept = plane(sums.reshape(256, FEATS)).astype(F32).reshape(16, 16, FEATS).sum(0)
-    low, adapter, keep, give = joined(marked, place, parts, landed, *downs)
+    low, adapter, keep, give = joined(marked, place, parts, landed, down)
     low_other = swap(low, "core", 1)
     half = (keep + swap(give, "core", 1)).astype(BF16)
     mine = half.astype(F32) + swap(half, "zh", 1).astype(F32)

time: 95.5 us -> 96 us (level)
  starting transfers between devices: 33.4 us -> 31.7 us
  local copies, waits for them, and re-layouts: 7.88 us -> 8.89 us
    all_to_all x2, waiting for transfers between devices: 11.2 us -> 13.6 us  [plane(): lax.all_to_all(value, ('x', 'y'), split_axis=0, concat_axis=0, tiled=True)]
    ppermute x14, waiting for transfers between devices: 21.1 us -> 19.5 us  [swap(): return lax.ppermute(value, axis, [(i, i ^ mask) for i in range(size)])]
    all_to_all x2, starting transfers between devices: 13.8 us -> 12.3 us  [plane(): lax.all_to_all(value, ('x', 'y'), split_axis=0, concat_axis=0, tiled=True)]
    unnamed x30 -> x28, local copies, waits for them, and re-layouts: 7.27 us -> 8.28 us
where the time goes in v10:
time: 96 us; the launch traced here: 94.8 us
  waiting for transfers between devices  33.1 us (34%)
  starting transfers between devices  31.7 us (33%)
  Pallas kernels  18.7 us (19%)
  local copies, waits for them, and re-layouts  8.89 us (9%)
  other arithmetic  1.54 us (2%)
    ppermute x14, waiting for transfers between devices, swap(): return lax.ppermute(value, axis, [(i, i ^ mask) for i in range(size)])  19.5 us
    ppermute x14, starting transfers between devices, swap(): return lax.ppermute(value, axis, [(i, i ^ mask) for i in range(size)])  17.4 us
    all_to_all x2, waiting for transfers between devices, plane(): lax.all_to_all(value, ('x', 'y'), split_axis=0, concat_axis=0, tiled=True)  13.6 us
    all_to_all x2, starting transfers between devices, plane(): lax.all_to_all(value, ('x', 'y'), split_axis=0, concat_axis=0, tiled=True)  12.3 us
    pallas_call x2, Pallas kernels, product(): pl.pallas_call(functools.partial(product_kernel, pairs), out_shape=(part,...  8.93 us
    unnamed x28, local copies, waits for them, and re-layouts  8.28 us
    pallas_call x1, Pallas kernels, prep(): pl.pallas_call(prep_kernel, out_shape=(both, back, back), in_specs=[SMEM]...  2.43 us
  transfers between devices with their start and end apart: 18, of which 9 were waited for; matrix products, arithmetic and copies ran while one was open for 1% of the time, Pallas kernels for 16%

profile of v10, /device:TPU:8, one launch (start us, length us, event | category | flops | bytes accessed | tf_op | source)
XLA Modules:
  0.0 94.8 jit_solution(15023591804915580381)
XLA Ops:
  1.2 2.4 %prep.1 = (bf16[2,2,32,1664]{3,2,1,0:T(8,128)(2,1)}, f32[8,256]{1,0:T(8,128)}, f32[8,256]{1,0:T(8,128)}) custom-call(s32[5]{0:T(128)} %stack.23.place, bf16[832,128]{1,0:T(8,128)(2,1)} %bitcast.24, bf16[832,128]{1,0:T(8,128)(2,1)} %bitcast.25, f32[832]{0:T(1024)} %gate_scale.3, f32[832]{0:T(1024)} %up_scale.3, f32[16,832]{1,0:T(8,128)} %gate_lift.1, ...), custom_call_target="tpu_custom_call" | custom-call | flops 14000000 | bytes 1200000 | tf_op jit(solution)/shard_map/prep/pallas_call | solution.py:71
  3.7 3.3 %collective-permute-start = (bf16[2,2,32,1664]{3,2,1,0:T(8,128)(2,1)}, bf16[2,2,32,1664]{3,2,1,0:T(8,128)(2,1)}, u32[]{:S(2)}, u32[]{:S(2)}) collective-permute-start(bf16[2,2,32,1664]{3,2,1,0:T(8,128)(2,1)} %get-tuple-element.42.refs_0_), channel_id=1, source_target_pairs={{0,128},{64,192},{128,0},{192,64},{1,129},{65,193},{129,1},{193,65... | collective-permute-start | bytes 1277960 | tf_op jit(solution)/shard_map/ppermute | solution.py:23
  7.0 1.9 %collective-permute-start.1 = (bf16[2,2,32,1664]{3,2,1,0:T(8,128)(2,1)}, bf16[2,2,32,1664]{3,2,1,0:T(8,128)(2,1)}, u32[]{:S(2)}, u32[]{:S(2)}) collective-permute-start(bf16[2,2,32,1664]{3,2,1,0:T(8,128)(2,1)} %get-tuple-element.42.refs_0_), channel_id=1, source_target_pairs={{0,64},{64,0},{128,192},{192,128},{1,65},{65,1},{129,193},{193,129... | collective-permute-start | bytes 1277960 | tf_op jit(solution)/shard_map/ppermute | solution.py:23
  8.9 0.9 copy-done.10
  9.8 0.9 copy-done.11
  10.7 0.8 copy-done.12
  12.1 0.9 spread.1
  13.0 7.4 %all-to-all-start = ((bf16[16,8,2304]{2,1,0:T(8,128)(2,1)}), bf16[16,8,2304]{2,1,0:T(8,128)(2,1)}, u32[]{:S(2)}, u32[]{:S(2)}) async-start(bf16[16,8,2304]{2,1,0:T(8,128)(2,1)} %bitcast.9), calls=%async_computation | async-start | bytes 1179648 | tf_op jit(solution)/shard_map/all_to_all | solution.py:315
  20.4 6.6 %collective-permute-done.refs_1_.refs_2_ = bf16[2,2,32,1664]{3,2,1,0:T(8,128)(2,1)} collective-permute-done((bf16[2,2,32,1664]{3,2,1,0:T(8,128)(2,1)}, bf16[2,2,32,1664]{3,2,1,0:T(8,128)(2,1)}, u32[]{:S(2)}, u32[]{:S(2)}) %collective-permute-start) | collective-permute-done | bytes 426016 | tf_op jit(solution)/shard_map/ppermute | solution.py:23
  27.1 4.3 %all-to-all-done = bf16[16,8,2304]{2,1,0:T(8,128)(2,1)} async-done(((bf16[16,8,2304]{2,1,0:T(8,128)(2,1)}), bf16[16,8,2304]{2,1,0:T(8,128)(2,1)}, u32[]{:S(2)}, u32[]{:S(2)}) %all-to-all-start) | async-done | bytes 589856 | tf_op jit(solution)/shard_map/all_to_all | solution.py:315
  32.1 1.3 %collective-permute-start.4 = (bf16[2,2,32,1664]{3,2,1,0:T(8,128)(2,1)}, bf16[2,2,32,1664]{3,2,1,0:T(8,128)(2,1)S(1)}, u32[]{:S(2)}, u32[]{:S(2)}) collective-permute-start(bf16[2,2,32,1664]{3,2,1,0:T(8,128)(2,1)} %collective-permute-done.refs_1_.refs_2_), channel_id=1, source_target_pairs={{64,0},{128,192},{65,1},{129,193},{66,2},{130,194},{67,3},{131,195... | collective-permute-start | bytes 1277960 | tf_op jit(solution)/shard_map/ppermute | solution.py:339
  33.4 1.3 %narrow.1.own = bf16[48,256]{1,0:T(8,128)(2,1)S(1)} custom-call(f32[8,128]{1,0:T(8,128)S(1)} %mark.2.marked, bf16[128,2304]{1,0:T(8,128)(2,1)} %bitcast.10.landed, bf16[32,2048]{1,0:T(8,128)(2,1)S(1)} %get-tuple-element.46.down), custom_call_target="tpu_custom_call" | custom-call | flops 17000000 | bytes 900000 | tf_op jit(solution)/shard_map/narrow/pallas_call | solution.py:211
  34.7 4.5 %collective-permute-start.5 = (bf16[48,256]{1,0:T(8,128)(2,1)S(1)}, bf16[48,256]{1,0:T(8,128)(2,1)S(1)}, u32[]{:S(2)}, u32[]{:S(2)}) collective-permute-start(bf16[48,256]{1,0:T(8,128)(2,1)S(1)} %narrow.1.own), channel_id=1, source_target_pairs={{0,8},{8,0},{1,9},{9,1},{2,10},{10,2},{3,11},{11,3},{4,12},{12,4},... | collective-permute-start | bytes 73736 | tf_op jit(solution)/shard_map/ppermute | solution.py:23
  39.3 1.0 %copy-done.9 = bf16[2,2,32,1664]{3,2,1,0:T(8,128)(2,1)S(1)} copy-done((bf16[2,2,32,1664]{3,2,1,0:T(8,128)(2,1)S(1)}, bf16[2,2,32,1664]{3,2,1,0:T(8,128)(2,1)}, u32[]{:S(2)}) %copy-start.9) | copy-done | bytes 426008
  40.3 6.2 %product.2 = (bf16[192,2048]{1,0:T(8,128)(2,1)S(1)}, bf16[192,2048]{1,0:T(8,128)(2,1)S(1)}, bf16[384,1664]{1,0:T(8,128)(2,1)S(1)}) custom-call(bf16[2,2,32,1664]{3,2,1,0:T(8,128)(2,1)S(1)} %copy-done.9, bf16[2,2,32,1664]{3,2,1,0:T(8,128)(2,1)} %collective-permute-done.1.refs_0_.refs_1_, bf16[2,2,32,1664]{3,2,1,0:T(8,128)(2,1)} %collective-permute-done.refs_1_.refs_2_, ...), custom_call_target="tpu_custom_call" | custom-call | flops 2700000000 | bytes 8000000 | tf_op jit(solution)/shard_map/product/pallas_call | solution.py:123
  46.5 1.1 %copy-done.2 = bf16[384,1664]{1,0:T(8,128)(2,1)} copy-done((bf16[384,1664]{1,0:T(8,128)(2,1)}, bf16[384,1664]{1,0:T(8,128)(2,1)S(1)}, u32[]{:S(2)}) %copy-start.2) | copy-done | bytes 1277976
  47.6 1.9 %copy-done.1 = bf16[2048,832]{0,1:T(8,128)(2,1)S(1)} copy-done((bf16[2048,832]{0,1:T(8,128)(2,1)S(1)}, bf16[2048,832]{0,1:T(8,128)(2,1)}, u32[]{:S(2)}) %copy-start.1) | copy-done | bytes 3407896
  49.5 2.7 %product.3 = (bf16[64,2048]{1,0:T(8,128)(2,1)S(1)}, bf16[64,2048]{1,0:T(8,128)(2,1)S(1)}, bf16[128,1664]{1,0:T(8,128)(2,1)S(1)}) custom-call(bf16[2,2,32,1664]{3,2,1,0:T(8,128)(2,1)S(1)} %collective-permute-done.3.refs_0_, bf16[2,2,32,1664]{3,2,1,0:T(8,128)(2,1)S(1)} %collective-permute-done.4.refs_1_, bf16[832,2048]{1,0:T(8,128)(2,1)S(1)} %bitcast.19, ...), custom_call_target="tpu_custom_call" | custom-call | flops 900000000 | bytes 8000000 | tf_op jit(solution)/shard_map/product/pallas_call | solution.py:123
  52.4 3.3 %collective-permute-start.9 = (bf16[48,256]{1,0:T(8,128)(2,1)S(1)}, bf16[48,256]{1,0:T(8,128)(2,1)S(1)}, u32[]{:S(2)}, u32[]{:S(2)}) collective-permute-start(bf16[48,256]{1,0:T(8,128)(2,1)S(1)} %join_halves.1.p0), channel_id=1, source_target_pairs={{0,64},{64,0},{128,192},{192,128},{1,65},{65,1},{129,193},{193,129... | collective-permute-start | bytes 73736 | tf_op jit(solution)/shard_map/ppermute | solution.py:23
  56.3 1.9 %collective-permute-start.11 = (bf16[48,256]{1,0:T(8,128)(2,1)S(1)}, bf16[48,256]{1,0:T(8,128)(2,1)S(1)}, u32[]{:S(2)}, u32[]{:S(2)}) collective-permute-start(bf16[48,256]{1,0:T(8,128)(2,1)S(1)} %join_halves.1.p0), channel_id=1, source_target_pairs={{0,192},{64,128},{128,64},{192,0},{1,193},{65,129},{129,65},{193,1... | collective-permute-start | bytes 73736 | tf_op jit(solution)/shard_map/ppermute | solution.py:23
  58.2 1.8 %add_pairs.1.marked = bf16[4,4,16,2048]{3,2,1,0:T(8,128)(2,1)} custom-call(f32[8,128]{1,0:T(8,128)S(1)} %mark.3.marked, s32[5]{0:T(128)S(1)} %copy-done.8, bf16[192,2048]{1,0:T(8,128)(2,1)S(1)} %get-tuple-element.49.own1, bf16[192,2048]{1,0:T(8,128)(2,1)S(1)} %collective-permute-done.6.theirs1, bf16[64,2048]{1,0:T(8,128)(2,1)S(1)} %get-tuple-element.55.own2, ...), custom_call_target="tpu_custom_call" | custom-call | flops 600000 | bytes 3200000 | tf_op jit(solution)/shard_map/add_pairs/pallas_call | solution.py:153
  60.6 1.3 %collective-permute-done.11.p3 = bf16[48,256]{1,0:T(8,128)(2,1)S(1)} collective-permute-done((bf16[48,256]{1,0:T(8,128)(2,1)S(1)}, bf16[48,256]{1,0:T(8,128)(2,1)S(1)}, u32[]{:S(2)}, u32[]{:S(2)}) %collective-permute-start.11) | collective-permute-done | bytes 24608 | tf_op jit(solution)/shard_map/ppermute | solution.py:23
  61.9 1.5 %joined.1 = (bf16[32,256]{1,0:T(8,128)(2,1)S(1)}, f32[8,2048]{1,0:T(8,128)S(1)}, f32[16,2048]{1,0:T(8,128)S(1)}, f32[16,2048]{1,0:T(8,128)S(1)}) custom-call(bf16[4,4,16,2048]{3,2,1,0:T(8,128)(2,1)} %add_pairs.1.marked, s32[5]{0:T(128)S(1)} %copy-done.8, bf16[48,256]{1,0:T(8,128)(2,1)S(1)} %join_halves.1.p0, bf16[48,256]{1,0:T(8,128)(2,1)S(1)} %collective-permute-done.9.p1, ...), custom_call_target="tpu_custom_call" | custom-call | flops 99999997952 | bytes 1000000 | tf_op jit(solution)/shard_map/joined/pallas_call | solution.py:262
  63.6 4.9 %all-to-all-start.1 = ((bf16[16,16,2048]{2,1,0:T(8,128)(2,1)}), bf16[16,16,2048]{2,1,0:T(8,128)(2,1)S(1)}, u32[]{:S(2)}, u32[]{:S(2)}) async-start(bf16[16,16,2048]{2,1,0:T(8,128)(2,1)} %bitcast.13), calls=%async_computation.1 | async-start | bytes 2097152 | tf_op jit(solution)/shard_map/all_to_all | solution.py:315
  68.5 0.8 collective-permute-start.13
  69.3 1.2 %collective-permute-done.15.low_other = bf16[32,256]{1,0:T(8,128)(2,1)S(1)} collective-permute-done((bf16[32,256]{1,0:T(8,128)(2,1)S(1)}, bf16[32,256]{1,0:T(8,128)(2,1)S(1)}, u32[]{:S(2)}, u32[]{:S(2)}) %collective-permute-start.15) | collective-permute-done | bytes 16416 | tf_op jit(solution)/shard_map/ppermute | solution.py:23
  70.5 1.0 %copy-done.5 = bf16[128,1664]{1,0:T(8,128)(2,1)S(1)} copy-done((bf16[128,1664]{1,0:T(8,128)(2,1)S(1)}, bf16[128,1664]{1,0:T(8,128)(2,1)}, u32[]{:S(2)}) %copy-start.5) | copy-done | bytes 426008
  71.5 1.9 %expander.1 = (f32[16,832]{1,0:T(8,128)}, f32[16,832]{1,0:T(8,128)}) custom-call(s32[5]{0:T(128)S(1)} %copy-done.8, bf16[32,256]{1,0:T(8,128)(2,1)S(1)} %collective-permute-done.15.low_other, bf16[32,256]{1,0:T(8,128)(2,1)S(1)} %get-tuple-element.66.low_own, bf16[384,1664]{1,0:T(8,128)(2,1)S(1)} %copy-done.3, bf16[128,1664]{1,0:T(8,128)(2,1)S(1)} %copy-done.5, ...), custom_call_target="tpu_custom_call" | custom-call | flops 55000000 | bytes 2000000 | tf_op jit(solution)/shard_map/expander/pallas_call | solution.py:303
  73.4 3.3 %collective-permute-done.13 = bf16[16,2048]{1,0:T(8,128)(2,1)S(1)} collective-permute-done((bf16[16,2048]{1,0:T(8,128)(2,1)S(1)}, bf16[16,2048]{1,0:T(8,128)(2,1)S(1)}, u32[]{:S(2)}, u32[]{:S(2)}) %collective-permute-start.13) | collective-permute-done | bytes 65568 | tf_op jit(solution)/shard_map/ppermute | solution.py:23
  76.9 9.3 %all-to-all-done.1 = bf16[16,16,2048]{2,1,0:T(8,128)(2,1)S(1)} async-done(((bf16[16,16,2048]{2,1,0:T(8,128)(2,1)}), bf16[16,16,2048]{2,1,0:T(8,128)(2,1)S(1)}, u32[]{:S(2)}, u32[]{:S(2)}) %all-to-all-start.1) | async-done | bytes 1048608 | tf_op jit(solution)/shard_map/all_to_all | solution.py:315
  86.3 0.8 collective-permute-start.8
  87.9 6.4 %collective-permute-done.8 = bf16[8,2048]{1,0:T(8,128)(2,1)S(1)} collective-permute-done((bf16[8,2048]{1,0:T(8,128)(2,1)S(1)}, bf16[8,2048]{1,0:T(8,128)(2,1)S(1)}, u32[]{:S(2)}, u32[]{:S(2)}) %collective-permute-start.8) | collective-permute-done | bytes 32800 | tf_op jit(solution)/shard_map/ppermute | solution.py:23
  (50 shorter events, 5.2 us)
Async XLA Ops:
  3.7 5.2 %collective-permute-start.2 = (f32[8,256]{1,0:T(8,128)}, f32[8,256]{1,0:T(8,128)S(1)}, u32[]{:S(2)}, u32[]{:S(2)}) collective-permute-start(f32[8,256]{1,0:T(8,128)} %get-tuple-element.40), channel_id=1, source_target_pairs={{0,1},{1,0},{2,3},{3,2},{4,5},{5,4},{6,7},{7,6},{8,9},{9,8},{10,11... | collective-permute-start | bytes 24584 | tf_op jit(solution)/shard_map/ppermute | solution.py:23
  3.7 23.3 %collective-permute-start = (bf16[2,2,32,1664]{3,2,1,0:T(8,128)(2,1)}, bf16[2,2,32,1664]{3,2,1,0:T(8,128)(2,1)}, u32[]{:S(2)}, u32[]{:S(2)}) collective-permute-start(bf16[2,2,32,1664]{3,2,1,0:T(8,128)(2,1)} %get-tuple-element.42.refs_0_), channel_id=1, source_target_pairs={{0,128},{64,192},{128,0},{192,64},{1,129},{65,193},{129,1},{193,65... | collective-permute-start | bytes 1277960 | tf_op jit(solution)/shard_map/ppermute | solution.py:23
  7.0 20.1 %collective-permute-start.1 = (bf16[2,2,32,1664]{3,2,1,0:T(8,128)(2,1)}, bf16[2,2,32,1664]{3,2,1,0:T(8,128)(2,1)}, u32[]{:S(2)}, u32[]{:S(2)}) collective-permute-start(bf16[2,2,32,1664]{3,2,1,0:T(8,128)(2,1)} %get-tuple-element.42.refs_0_), channel_id=1, source_target_pairs={{0,64},{64,0},{128,192},{192,128},{1,65},{65,1},{129,193},{193,129... | collective-permute-start | bytes 1277960 | tf_op jit(solution)/shard_map/ppermute | solution.py:23
  8.9 0.9 copy-start.10
  9.8 0.9 copy-start.11
  10.7 0.8 copy-start.12
  11.4 0.7 copy-start.13
  13.0 18.4 %all-to-all-start = ((bf16[16,8,2304]{2,1,0:T(8,128)(2,1)}), bf16[16,8,2304]{2,1,0:T(8,128)(2,1)}, u32[]{:S(2)}, u32[]{:S(2)}) async-start(bf16[16,8,2304]{2,1,0:T(8,128)(2,1)} %bitcast.9), calls=%async_computation | async-start | bytes 1179648 | tf_op jit(solution)/shard_map/all_to_all | solution.py:315
  20.4 18.9 %copy-start = (bf16[2048,832]{0,1:T(8,128)(2,1)S(1)}, bf16[2048,832]{0,1:T(8,128)(2,1)}, u32[]{:S(2)}) copy-start(bf16[2048,832]{0,1:T(8,128)(2,1)} %param.14) | copy-start | bytes 10223620
  31.4 16.2 %collective-permute-start.3 = (bf16[2,2,32,1664]{3,2,1,0:T(8,128)(2,1)}, bf16[2,2,32,1664]{3,2,1,0:T(8,128)(2,1)S(1)}, u32[]{:S(2)}, u32[]{:S(2)}) collective-permute-start(bf16[2,2,32,1664]{3,2,1,0:T(8,128)(2,1)} %get-tuple-element.42.refs_0_), channel_id=1, source_target_pairs={{64,128},{128,64},{65,129},{129,65},{66,130},{130,66},{67,131},{13... | collective-permute-start | bytes 1277960 | tf_op jit(solution)/shard_map/ppermute | solution.py:338
  32.1 15.5 %collective-permute-start.4 = (bf16[2,2,32,1664]{3,2,1,0:T(8,128)(2,1)}, bf16[2,2,32,1664]{3,2,1,0:T(8,128)(2,1)S(1)}, u32[]{:S(2)}, u32[]{:S(2)}) collective-permute-start(bf16[2,2,32,1664]{3,2,1,0:T(8,128)(2,1)} %collective-permute-done.refs_1_.refs_2_), channel_id=1, source_target_pairs={{64,0},{128,192},{65,1},{129,193},{66,2},{130,194},{67,3},{131,195... | collective-permute-start | bytes 1277960 | tf_op jit(solution)/shard_map/ppermute | solution.py:339
  34.7 12.9 %collective-permute-start.5 = (bf16[48,256]{1,0:T(8,128)(2,1)S(1)}, bf16[48,256]{1,0:T(8,128)(2,1)S(1)}, u32[]{:S(2)}, u32[]{:S(2)}) collective-permute-start(bf16[48,256]{1,0:T(8,128)(2,1)S(1)} %narrow.1.own), channel_id=1, source_target_pairs={{0,8},{8,0},{1,9},{9,1},{2,10},{10,2},{3,11},{11,3},{4,12},{12,4},... | collective-permute-start | bytes 73736 | tf_op jit(solution)/shard_map/ppermute | solution.py:23
  39.3 1.0 %copy-start.9 = (bf16[2,2,32,1664]{3,2,1,0:T(8,128)(2,1)S(1)}, bf16[2,2,32,1664]{3,2,1,0:T(8,128)(2,1)}, u32[]{:S(2)}) copy-start(bf16[2,2,32,1664]{3,2,1,0:T(8,128)(2,1)} %get-tuple-element.42.refs_0_) | copy-start | bytes 1277956
  46.5 1.1 %copy-start.2 = (bf16[384,1664]{1,0:T(8,128)(2,1)}, bf16[384,1664]{1,0:T(8,128)(2,1)S(1)}, u32[]{:S(2)}) copy-start(bf16[384,1664]{1,0:T(8,128)(2,1)S(1)} %get-tuple-element.67.grads1) | copy-start | bytes 3833860
  47.6 2.0 %copy-start.1 = (bf16[2048,832]{0,1:T(8,128)(2,1)S(1)}, bf16[2048,832]{0,1:T(8,128)(2,1)}, u32[]{:S(2)}) copy-start(bf16[2048,832]{0,1:T(8,128)(2,1)} %param.15) | copy-start | bytes 10223620
  47.6 10.6 %collective-permute-start.6 = (bf16[192,2048]{1,0:T(8,128)(2,1)S(1)}, bf16[192,2048]{1,0:T(8,128)(2,1)S(1)}, u32[]{:S(2)}, u32[]{:S(2)}) collective-permute-start(bf16[192,2048]{1,0:T(8,128)(2,1)S(1)} %get-tuple-element.50), channel_id=1, source_target_pairs={{0,1},{1,0},{2,3},{3,2},{4,5},{5,4},{6,7},{7,6},{8,9},{9,8},{10,11... | collective-permute-start | bytes 2359304 | tf_op jit(solution)/shard_map/ppermute | solution.py:23
  49.5 8.7 %copy-start.8 = (s32[5]{0:T(128)S(1)}, s32[5]{0:T(128)}, u32[]{:S(2)}) copy-start(s32[5]{0:T(128)} %stack.23.place) | copy-start | bytes 64
  52.3 11.2 %copy-start.4 = (bf16[128,1664]{1,0:T(8,128)(2,1)}, bf16[128,1664]{1,0:T(8,128)(2,1)S(1)}, u32[]{:S(2)}) copy-start(bf16[128,1664]{1,0:T(8,128)(2,1)S(1)} %get-tuple-element.68.grads2) | copy-start | bytes 1277956
  52.3 5.9 %collective-permute-start.7 = (bf16[64,2048]{1,0:T(8,128)(2,1)S(1)}, bf16[64,2048]{1,0:T(8,128)(2,1)S(1)}, u32[]{:S(2)}, u32[]{:S(2)}) collective-permute-start(bf16[64,2048]{1,0:T(8,128)(2,1)S(1)} %get-tuple-element.56), channel_id=1, source_target_pairs={{0,1},{1,0},{2,3},{3,2},{4,5},{5,4},{6,7},{7,6},{8,9},{9,8},{10,11... | collective-permute-start | bytes 786440 | tf_op jit(solution)/shard_map/ppermute | solution.py:23
  52.4 7.6 %collective-permute-start.9 = (bf16[48,256]{1,0:T(8,128)(2,1)S(1)}, bf16[48,256]{1,0:T(8,128)(2,1)S(1)}, u32[]{:S(2)}, u32[]{:S(2)}) collective-permute-start(bf16[48,256]{1,0:T(8,128)(2,1)S(1)} %join_halves.1.p0), channel_id=1, source_target_pairs={{0,64},{64,0},{128,192},{192,128},{1,65},{65,1},{129,193},{193,129... | collective-permute-start | bytes 73736 | tf_op jit(solution)/shard_map/ppermute | solution.py:23
  55.7 4.9 %collective-permute-start.10 = (bf16[48,256]{1,0:T(8,128)(2,1)S(1)}, bf16[48,256]{1,0:T(8,128)(2,1)S(1)}, u32[]{:S(2)}, u32[]{:S(2)}) collective-permute-start(bf16[48,256]{1,0:T(8,128)(2,1)S(1)} %join_halves.1.p0), channel_id=1, source_target_pairs={{0,128},{64,192},{128,0},{192,64},{1,129},{65,193},{129,1},{193,65... | collective-permute-start | bytes 73736 | tf_op jit(solution)/shard_map/ppermute | solution.py:23
  56.3 5.6 %collective-permute-start.11 = (bf16[48,256]{1,0:T(8,128)(2,1)S(1)}, bf16[48,256]{1,0:T(8,128)(2,1)S(1)}, u32[]{:S(2)}, u32[]{:S(2)}) collective-permute-start(bf16[48,256]{1,0:T(8,128)(2,1)S(1)} %join_halves.1.p0), channel_id=1, source_target_pairs={{0,192},{64,128},{128,64},{192,0},{1,193},{65,129},{129,65},{193,1... | collective-permute-start | bytes 73736 | tf_op jit(solution)/shard_map/ppermute | solution.py:23
  60.0 10.5 %copy-start.3 = (bf16[384,1664]{1,0:T(8,128)(2,1)S(1)}, bf16[384,1664]{1,0:T(8,128)(2,1)}, u32[]{:S(2)}) copy-start(bf16[384,1664]{1,0:T(8,128)(2,1)} %copy-done.2) | copy-start | bytes 3833860
  60.0 10.5 %copy-start.6 = (f32[832]{0:T(1024)S(1)}, f32[832]{0:T(1024)}, u32[]{:S(2)}) copy-start(f32[832]{0:T(1024)} %gate_scale.3) | copy-start | bytes 9988
  60.0 10.5 %copy-start.7 = (f32[832]{0:T(1024)S(1)}, f32[832]{0:T(1024)}, u32[]{:S(2)}) copy-start(f32[832]{0:T(1024)} %up_scale.3) | copy-start | bytes 9988
  63.5 5.0 %collective-permute-start.12 = (f32[16,2048]{1,0:T(8,128)S(1)}, f32[16,2048]{1,0:T(8,128)S(1)}, u32[]{:S(2)}, u32[]{:S(2)}) collective-permute-start(f32[16,2048]{1,0:T(8,128)S(1)} %get-tuple-element.65), channel_id=1, source_target_pairs={{0,1},{1,0},{2,3},{3,2},{4,5},{5,4},{6,7},{7,6},{8,9},{9,8},{10,11... | collective-permute-start | bytes 393224 | tf_op jit(solution)/shard_map/ppermute | solution.py:23
  63.6 22.6 %all-to-all-start.1 = ((bf16[16,16,2048]{2,1,0:T(8,128)(2,1)}), bf16[16,16,2048]{2,1,0:T(8,128)(2,1)S(1)}, u32[]{:S(2)}, u32[]{:S(2)}) async-start(bf16[16,16,2048]{2,1,0:T(8,128)(2,1)} %bitcast.13), calls=%async_computation.1 | async-start | bytes 2097152 | tf_op jit(solution)/shard_map/all_to_all | solution.py:315
  68.5 8.3 %collective-permute-start.13 = (bf16[16,2048]{1,0:T(8,128)(2,1)S(1)}, bf16[16,2048]{1,0:T(8,128)(2,1)S(1)}, u32[]{:S(2)}, u32[]{:S(2)}) collective-permute-start(bf16[16,2048]{1,0:T(8,128)(2,1)S(1)} %add_convert_fusion), channel_id=1, source_target_pairs={{0,8},{8,0},{1,9},{9,1},{2,10},{10,2},{3,11},{11,3},{4,12},{12,4},... | collective-permute-start | bytes 196616 | tf_op jit(solution)/shard_map/ppermute | solution.py:23
  69.3 1.2 %collective-permute-start.15 = (bf16[32,256]{1,0:T(8,128)(2,1)S(1)}, bf16[32,256]{1,0:T(8,128)(2,1)S(1)}, u32[]{:S(2)}, u32[]{:S(2)}) collective-permute-start(bf16[32,256]{1,0:T(8,128)(2,1)S(1)} %get-tuple-element.66.low_own), channel_id=1, source_target_pairs={{0,1},{1,0},{2,3},{3,2},{4,5},{5,4},{6,7},{7,6},{8,9},{9,8},{10,11... | collective-permute-start | bytes 49160 | tf_op jit(solution)/shard_map/ppermute | solution.py:23
  70.5 1.0 %copy-start.5 = (bf16[128,1664]{1,0:T(8,128)(2,1)S(1)}, bf16[128,1664]{1,0:T(8,128)(2,1)}, u32[]{:S(2)}) copy-start(bf16[128,1664]{1,0:T(8,128)(2,1)} %copy-done.4) | copy-start | bytes 1277956
  76.8 10.3 %collective-permute-start.14 = (f32[16,2048]{1,0:T(8,128)S(1)}, f32[16,2048]{1,0:T(8,128)S(1)}, u32[]{:S(2)}, u32[]{:S(2)}) collective-permute-start(f32[16,2048]{1,0:T(8,128)S(1)} %convert_add_fusion), channel_id=1, source_target_pairs={{0,1},{1,0},{2,3},{3,2},{4,5},{5,4},{6,7},{7,6},{8,9},{9,8},{10,11... | collective-permute-start | bytes 393224 | tf_op jit(solution)/shard_map/ppermute | solution.py:23
  86.3 7.9 %collective-permute-start.8 = (bf16[8,2048]{1,0:T(8,128)(2,1)S(1)}, bf16[8,2048]{1,0:T(8,128)(2,1)S(1)}, u32[]{:S(2)}, u32[]{:S(2)}) collective-permute-start(bf16[8,2048]{1,0:T(8,128)(2,1)S(1)} %slice.17), channel_id=1, source_target_pairs={{0,8},{8,0},{1,9},{9,1},{2,10},{10,2},{3,11},{11,3},{4,12},{12,4},... | collective-permute-start | bytes 98312 | tf_op jit(solution)/shard_map/ppermute | solution.py:23
